TPU v7x, 32 devices: a whole 2x2x4 slice. The times are simulated.
32 devices in a mesh: ctx: 8 (over z, core), head: 4 (over y, x).
Axes of the slice: x: 2, y: 2, z: 4, core: 2. Of those that a mesh axis runs over, the one named last changes fastest.
Arguments:
- hidden: bfloat16 [2048, 2048], P('ctx'), may hold values from -6 to 6
- w_query: bfloat16 [2048, 2048], P('head'), may hold values from -0.125 to 0.125
- w_key: bfloat16 [2048, 2048], P('head'), may hold values from -0.125 to 0.125
- payload_projection_matrix: bfloat16 [2048, 4096], P('head'), may hold values from -0.125 to 0.125
- conv_weight: bfloat16 [4, 8192], replicated, may hold values from -3 to 3
- log_decay: float32 [32, 2048], P('head', 'ctx'), may hold values from -1.6 to 0
- beta_rate: float32 [32, 2048], P('head', 'ctx'), may hold values from 0 to 1
- norm_gain: float32 [128], replicated, may hold values from 0.25 to 1.75
- head_order: int32 [16], replicated, may hold values from 0 to 15, each once
- block_starts: int32 [8], P('ctx'), may hold values 0 or 1
Outputs:
- mixed: bfloat16 [2048, 4096], P('ctx', 'head')
Inputs may be any that keep to these rules, and one draw needn't show every extreme that they name: Index j of the head axis serves serving key head j (logical key head head_order[j * 4]) and serving value heads 2j and 2j + 1.
All inputs are finite; a program needn't handle non-finite values. No bound on the sum of `block_starts` on one device may be relied on, other than what follows from the above.
Results may differ from a plain program's by a relative error of at most 0.0046.
Values may be sent and summed in bfloat16 or wider, within the bound.
No kernel may reach another device: no remote copies, remote signals or barrier semaphores. Data moves between devices by JAX's collectives and lax.ppermute only.
A program may use at most 128 MiB of HBM per device.

v0:
```python
import jax
import jax.numpy as jnp
from jax import lax
from jax.sharding import PartitionSpec as P

DK = 128
VALUE_HEAD_SIZE = 128
KCONV = 4
GROUP = 64


HIGH_PRECISION = lax.Precision.HIGHEST
eps = 1e-06


def from_behind(value, axis, steps):
    count = lax.axis_size(axis)
    initial, last = (max(0, -steps), min(count, count - steps))
    return lax.ppermute(value, axis, [(source, source + steps) for source in range(initial, last)])


def carried_in(value, axis, combine, identity):
    size, place = (lax.axis_size(axis), lax.axis_index(axis))
    everything = jax.tree.map(lambda part: lax.all_gather(part, axis), value)
    start = jax.tree.map(
        lambda part, zero: jnp.broadcast_to(jnp.asarray(zero, part.dtype), part.shape),
        value,
        identity,
    )

    def turn(k, before):
        reached = k < place
        new = combine(before, jax.tree.map(lambda part: part[k], everything))
        return jax.tree.map(lambda a, b: jnp.where(reached, a, b), new, before)

    return lax.fori_loop(0, size, turn, start)


def lower_solve(system, right):
    return lax.linalg.triangular_solve(
        system, right, left_side=True, lower=True, unit_diagonal=True
    )


def arrange(weight, width, head_order):
    rows = weight.shape[0]
    blocks = weight.reshape(rows, weight.shape[1] // width, width)
    return jnp.take(blocks, head_order, axis=1).reshape(rows, weight.shape[1])


def convolve(extended, weight, taps):
    proj = jnp.dot(extended, weight, preferred_element_type=jnp.float32).astype(jnp.bfloat16)
    count = proj.shape[0] - (KCONV - 1)
    total = taps[KCONV - 1].astype(jnp.float32) * proj[KCONV - 1 :].astype(jnp.float32)
    for lag in range(1, KCONV):
        offset = KCONV - 1 - lag
        total = total + taps[offset].astype(jnp.float32) * proj[offset : offset + count].astype(
            jnp.float32
        )
    return jax.nn.silu(total)


def unit_rows(values):
    return values * lax.rsqrt(jnp.sum(values * values, axis=-1, keepdims=True) + eps)


def to_blocks(values):
    count, heads, width = values.shape
    return values.reshape(count // GROUP, GROUP, heads, width).transpose(0, 2, 1, 3)


def key_phase(key_vec, decay, delta_writing_strength):
    size_c = decay.shape[-1]
    cumulative_decay = jnp.cumsum(decay, axis=-1)
    rows = lax.broadcasted_iota(jnp.int32, (size_c, size_c), 0)
    cols = lax.broadcasted_iota(jnp.int32, (size_c, size_c), 1)
    spread = cumulative_decay[..., :, None] - cumulative_decay[..., None, :]
    strict_w = jnp.where(cols < rows, jnp.exp(jnp.where(cols < rows, spread, 0.0)), 0.0)
    incl_w = jnp.where(cols <= rows, jnp.exp(jnp.where(cols <= rows, spread, 0.0)), 0.0)
    key_key = jnp.einsum("nhtd,nhsd->nhts", key_vec, key_vec, precision=HIGH_PRECISION)
    system = (
        jnp.eye(size_c, dtype=jnp.float32)
        + delta_writing_strength[..., :, None] * strict_w * key_key
    )
    decay_growth = jnp.exp(cumulative_decay)
    write_k = lower_solve(system, (delta_writing_strength * decay_growth)[..., None] * key_vec)
    trailing_keys = jnp.exp(cumulative_decay[..., -1:] - cumulative_decay)[..., None] * key_vec
    eye_k = jnp.eye(DK, dtype=jnp.float32)
    trans_a = jnp.exp(cumulative_decay[..., -1])[..., None, None] * eye_k - jnp.einsum(
        "nhsk,nhsj->nhkj", trailing_keys, write_k, precision=HIGH_PRECISION
    )

    def key_chain(acc, step_a):
        return (jnp.einsum("hij,hjk->hik", step_a, acc, precision=HIGH_PRECISION), acc)

    start = jnp.broadcast_to(eye_k, (key_vec.shape[1], DK, DK))
    dev_a, enter_a = lax.scan(key_chain, start, trans_a)
    return (key_vec, decay_growth, incl_w, system, write_k, trailing_keys, trans_a, enter_a, dev_a)


def value_phase(query_vector, value, delta_writing_strength, keyed):
    key_vec, decay_growth, incl_w, system, write_k, trailing_keys, trans_a, enter_a, dev_a = keyed
    write_v = lower_solve(system, delta_writing_strength[..., None] * value)
    attend = incl_w * jnp.einsum("nhtd,nhsd->nhts", query_vector, key_vec, precision=HIGH_PRECISION)
    inner = jnp.einsum("nhts,nhsv->nhtv", attend, write_v, precision=HIGH_PRECISION)
    qeff = decay_growth[..., None] * query_vector - jnp.einsum(
        "nhts,nhsk->nhtk", attend, write_k, precision=HIGH_PRECISION
    )
    trans_b = jnp.einsum("nhsk,nhsv->nhkv", trailing_keys, write_v, precision=HIGH_PRECISION)

    def value_chain(acc, pair):
        return (jnp.einsum("hij,hjv->hiv", pair[0], acc, precision=HIGH_PRECISION) + pair[1], acc)

    start = jnp.zeros((value.shape[1], DK, VALUE_HEAD_SIZE), jnp.float32)
    dev_b, enter_b = lax.scan(value_chain, start, (trans_a, trans_b))
    return (inner, qeff, enter_b, dev_b)


def combine(earlier, later):
    joined_a = jnp.einsum("hij,hjk->hik", later[0], earlier[0], precision=HIGH_PRECISION)
    joined_b = jnp.einsum("hij,hjv->hiv", later[0], earlier[1], precision=HIGH_PRECISION) + later[1]
    return (joined_a, joined_b)


def per_device(
    hidden,
    w_query,
    w_key,
    payload_projection_matrix,
    conv_weight,
    log_decay,
    beta_rate,
    norm_gain,
    head_order,
    block_starts,
):
    count = hidden.shape[0]
    key_heads = head_order.shape[0] // lax.axis_size("head")
    heads = 2 * key_heads
    serve = lax.axis_index("head")
    mine = lax.dynamic_slice_in_dim(head_order, serve * key_heads, key_heads)
    key_cols = (mine[:, None] * DK + jnp.arange(DK, dtype=jnp.int32)[None, :]).reshape(-1)
    value_cols = (
        mine[:, None] * (2 * VALUE_HEAD_SIZE)
        + jnp.arange(2 * VALUE_HEAD_SIZE, dtype=jnp.int32)[None, :]
    ).reshape(-1)
    key_total = head_order.shape[0] * DK
    question_filter_weights = jnp.take(conv_weight, key_cols, axis=1)
    taps_k = jnp.take(conv_weight, key_total + key_cols, axis=1)
    taps_v = jnp.take(conv_weight, 2 * key_total + value_cols, axis=1)
    keep = (1 - block_starts[0]).astype(jnp.float32)
    rim = from_behind(hidden[count - (KCONV - 1) :], "ctx", 1)
    extended = jnp.concatenate([rim * keep.astype(jnp.bfloat16), hidden], axis=0)
    decay = log_decay.reshape(heads, count // GROUP, GROUP).transpose(1, 0, 2)
    delta_writing_strength = beta_rate.reshape(heads, count // GROUP, GROUP).transpose(1, 0, 2)
    cols_q, cols_k, cols_v = (
        lax.all_to_all(
            arrange(w_query, DK, head_order), "head", split_axis=1, concat_axis=0, tiled=True
        ),
        lax.all_to_all(
            arrange(w_key, DK, head_order), "head", split_axis=1, concat_axis=0, tiled=True
        ),
        lax.all_to_all(
            arrange(payload_projection_matrix, 2 * VALUE_HEAD_SIZE, head_order),
            "head",
            split_axis=1,
            concat_axis=0,
            tiled=True,
        ),
    )
    key_act = convolve(extended, cols_k, taps_k)
    key_vec = to_blocks(jnp.repeat(unit_rows(key_act.reshape(count, key_heads, DK)), 2, axis=1))
    keyed = key_phase(key_vec, decay, delta_writing_strength)
    query_act = convolve(extended, cols_q, question_filter_weights)
    value_act = convolve(extended, cols_v, taps_v)
    query_vector = to_blocks(
        jnp.repeat(unit_rows(query_act.reshape(count, key_heads, DK)), 2, axis=1)
    )
    value = to_blocks(value_act.reshape(count, heads, VALUE_HEAD_SIZE))
    inner, qeff, enter_b, dev_b = value_phase(query_vector, value, delta_writing_strength, keyed)
    enter_a = keyed[7]
    dev_a = keyed[8]
    identity = (
        jnp.broadcast_to(jnp.eye(DK, dtype=jnp.float32), dev_a.shape),
        jnp.zeros_like(dev_b),
    )
    prior_a, prior_b = carried_in((dev_a * keep, dev_b), "ctx", combine, identity)
    state_in = prior_b * keep
    entering = jnp.einsum("nhij,hjv->nhiv", enter_a, state_in, precision=HIGH_PRECISION) + enter_b
    reads = inner + jnp.einsum("nhtk,nhkv->nhtv", qeff, entering, precision=HIGH_PRECISION)
    reads = reads.transpose(0, 2, 1, 3).reshape(count, heads, VALUE_HEAD_SIZE)
    scaled = reads * lax.rsqrt(jnp.mean(reads * reads, axis=-1, keepdims=True) + eps) * norm_gain
    return scaled.reshape(count, heads * VALUE_HEAD_SIZE).astype(jnp.bfloat16)


def solution(mesh):
    return jax.shard_map(
        per_device,
        mesh=mesh,
        in_specs=(
            P("ctx", None),
            P("head", None),
            P("head", None),
            P("head", None),
            P(),
            P("head", "ctx"),
            P("head", "ctx"),
            P(),
            P(),
            P("ctx"),
        ),
        out_specs=P("ctx", "head"),
        check_vma=False,
    )
```

profile of v0, /device:TPU:0, one launch (start us, length us, event | category | flops | bytes accessed | tf_op | source)
XLA Modules:
  0.0 432.1 jit_solution(12944830623792190916)
XLA Ops:
  7.3 2.4 collective-permute-start
  11.0 3.9 copy.130
  14.9 3.0 copy.131
  18.0 3.9 copy.124
  21.9 3.9 copy.125
  25.9 2.1 gather_fusion.5
  28.0 3.9 gather_fusion.3
  31.9 4.2 select_bitcast_fusion.1
  36.1 3.9 copy.132
  40.0 4.7 %all-to-all-start.1 = ((bf16[512,4,512]{0,2,1:T(8,128)(2,1)}), bf16[512,4,512]{0,2,1:T(8,128)(2,1)S(1)}, u32[]{:S(2)}, u32[]{:S(2)}) async-start(bf16[512,4,512]{0,2,1:T(8,128)(2,1)} %bitcast.169), calls=%async_computation.1 | async-start | bytes 4194304 | tf_op jit(solution)/shard_map/all_to_all | solution.py:160
  45.1 1.9 copy.123
  47.1 0.9 reduce_window_sum.11
  48.1 2.9 gather_fusion.4
  52.5 6.6 %copy.142 = bf16[512,4096]{0,1:T(8,128)(2,1)} copy(bf16[512,4096]{1,0:T(8,128)(2,1)} %param.25) | data formatting | bytes 8388608 | tf_op args[3]
  59.1 6.4 %copy.143 = bf16[512,16,256]{2,0,1:T(8,128)(2,1)} copy(bf16[512,16,256]{0,2,1:T(8,128)(2,1)} %bitcast.161) | data formatting | bytes 8388608 | tf_op jit(solution)/shard_map/reshape | solution.py:47
  65.5 5.0 %gather_fusion.1 = bf16[16,512,256]{2,1,0:T(8,128)(2,1)} fusion(bf16[512,16,256]{2,0,1:T(8,128)(2,1)} %copy.143, s32[1024]{0:T(1024)S(1)} %pad_clamp_fusion.1), kind=kCustom, calls=%fused_computation.5 | custom fusion | bytes 8388672 | tf_op jit(solution)/shard_map/jit(_take)/gather | solution.py:48
  70.5 6.4 %copy.144 = bf16[512,16,256]{0,2,1:T(8,128)(2,1)} copy(bf16[512,16,256]{2,0,1:T(8,128)(2,1)} %bitcast.160) | data formatting | bytes 8388608 | tf_op jit(solution)/shard_map/jit(_take)/gather | solution.py:48
  76.9 2.4 copy.133
  79.3 2.6 convolution_convert_fusion.1
  83.4 2.8 fusion.25
  86.2 158.5 %custom-call.6 = f32[4,8,1,64,64]{3,4,2,1,0:T(8,128)S(1)} custom-call(f32[4,8,1,64,64]{4,3,2,1,0:T(8,128)} %fusion.25), custom_call_target="InvertDiagBlocksLowerTriangular" | custom-call | tf_op jit(solution)/shard_map/triangular_solve/custom-call.1 | solution.py:40
  245.3 1.9 fusion.34
  247.3 3.7 multiply_subtract_fusion
  251.1 6.3 %while.39 = (s32[]{:T(128)}, f32[8,128,128]{2,1,0:T(8,128)S(1)}, f32[4,8,128,128]{3,2,1,0:T(8,128)}, f32[4,8,128,128]{3,2,1,0:T(8,128)S(1)}, s32[]{:T(128)}) while((s32[]{:T(128)}, f32[8,128,128]{2,1,0:T(8,128)S(1)}, f32[4,8,128,128]{3,2,1,0:T(8,128)}, f32[4,8,128,128]{3,2,1,0:T(8,128)S(1)}, s32[]{:T(128)}) %tuple.91), condition=%wide.region_4.8_spmd, body=%wide.region_3.7_spmd.sunk | while | flops 201326592 | bytes 3670093 | solution.py:97
  257.4 0.9 broadcast_multiply_fusion.2
  258.3 3.9 bitcast_select_fusion
  262.2 4.8 %all-to-all-start.2 = ((bf16[512,4,1024]{0,2,1:T(8,128)(2,1)}), bf16[512,4,1024]{0,2,1:T(8,128)(2,1)}, u32[]{:S(2)}, u32[]{:S(2)}) async-start(bf16[512,4,1024]{0,2,1:T(8,128)(2,1)} %bitcast_select_fusion), calls=%async_computation.2 | async-start | bytes 8388608 | tf_op jit(solution)/shard_map/all_to_all | solution.py:163
  267.3 5.0 %gather_fusion = bf16[1024,4]{1,0:T(8,128)(2,1)S(1)} fusion(bf16[4,8192]{0,1:T(8,128)(2,1)} %copy.123, s32[1024]{0:T(1024)S(1)} %broadcast_clamp_fusion), kind=kCustom, calls=%fused_computation.4 | custom fusion | bytes 20480 | tf_op jit(solution)/shard_map/jit(_take)/gather | solution.py:150
  273.1 41.9 %all-to-all-done.2 = bf16[512,4,1024]{0,2,1:T(8,128)(2,1)} async-done(((bf16[512,4,1024]{0,2,1:T(8,128)(2,1)}), bf16[512,4,1024]{0,2,1:T(8,128)(2,1)}, u32[]{:S(2)}, u32[]{:S(2)}) %all-to-all-start.2) | async-done | bytes 4194336 | tf_op jit(solution)/shard_map/all_to_all | solution.py:163
  315.1 6.4 %copy.145 = bf16[4,512,1024]{2,1,0:T(8,128)(2,1)} copy(bf16[4,512,1024]{1,2,0:T(8,128)(2,1)} %bitcast.31) | data formatting | bytes 8388608 | tf_op jit(solution)/shard_map/all_to_all | solution.py:163
  321.4 3.8 convolution_convert_fusion
  326.5 2.1 fusion.33
  328.6 4.8 %fusion.43 = f32[4,8,128,128]{3,2,1,0:T(8,128)} fusion(f32[4,8,64,128]{3,2,1,0:T(8,128)S(1)} %fusion.33, f32[4,8,64,128]{3,2,0,1:T(8,128)S(1)} %copy-done.8), kind=kOutput, calls=%fused_computation.72 | convolution fusion | flops 402653184 | bytes 4194304 | tf_op jit(solution)/shard_map/nhsk,nhsv->nhkv/dot_general | solution.py:109
  333.4 18.5 %while.40 = (s32[]{:T(128)}, f32[8,128,128]{2,1,0:T(8,128)}, f32[4,8,128,128]{2,3,1,0:T(8,128)}, f32[4,8,128,128]{3,2,1,0:T(8,128)S(1)}, f32[4,8,128,128]{3,2,1,0:T(8,128)}, /*index=5*/s32[]{:T(128)}, s32[]{:T(128)}) while((s32[]{:T(128)}, f32[8,128,128]{2,1,0:T(8,128)}, f32[4,8,128,128]{2,3,1,0:T(8,128)}, ...), condition=%wide.region_6.10_spmd.clone, body=%wide.region_5.9_spmd.clone.sunk | while | flops 201719808 | bytes 6293091 | solution.py:115
  333.4 1.0 copy.250
  334.5 2.5 convolution_add_fusion.3
  338.0 1.0 copy.250
  339.1 2.5 convolution_add_fusion.3
  342.6 1.0 copy.250
  343.7 2.5 convolution_add_fusion.3
  347.2 1.0 copy.250
  348.3 2.5 convolution_add_fusion.3
  351.9 3.9 copy.126
  355.8 3.8 all-to-all-start
  359.7 3.2 gather_fusion.2
  363.4 22.1 %all-to-all-done = bf16[512,4,512]{0,2,1:T(8,128)(2,1)S(1)} async-done(((bf16[512,4,512]{0,2,1:T(8,128)(2,1)}), bf16[512,4,512]{0,2,1:T(8,128)(2,1)S(1)}, u32[]{:S(2)}, u32[]{:S(2)}) %all-to-all-start) | async-done | bytes 2097184 | tf_op jit(solution)/shard_map/all_to_all | solution.py:157
  385.6 2.4 copy.127
  388.0 2.6 convolution_convert_fusion.2
  392.8 1.8 convolution_multiply_fusion.1
  394.6 1.3 convolution_subtract_fusion
  395.9 1.2 fusion.67
  397.1 1.8 all-gather.7.cloned.1.call-done
  398.9 16.0 %while.41 = (s32[]{:T(128)}, f32[8,128,128]{2,1,0:T(8,128)S(1)}, s32[]{:T(128)}, f32[8,8,128,128]{3,2,1,0:T(8,128)}, f32[8,8,128,128]{3,2,1,0:T(8,128)}, /*index=5*/s32[]{:T(128)}, s32[]{:T(128)}) while((s32[]{:T(128)}, f32[8,128,128]{2,1,0:T(8,128)S(1)}, s32[]{:T(128)}, f32[8,8,128,128]{3,2,1,0:T(8,128)}, ...), condition=%wide.region_8.12_spmd.clone, body=%wide.region_7.11_spmd.clone.sunk | while | flops 201850880 | bytes 3672679 | solution.py:36
  399.0 1.9 fusion.92
  400.9 1.9 fusion.92
  402.9 1.9 fusion.92
  404.9 1.9 fusion.92
  406.8 1.9 fusion.92
  408.8 1.9 fusion.92
  410.8 1.9 fusion.92
  412.7 1.9 fusion.92
  414.9 3.7 fusion.48
  418.6 4.2 multiply_reduce_fusion
  423.9 1.1 fusion.32
  (141 shorter events, 22.2 us)
Async XLA Ops:
  6.5 356.9 %copy-start = (f32[128]{0:T(128)S(1)}, f32[128]{0:T(128)}, u32[]{:S(2)}) copy-start(f32[128]{0:T(128)} %param.29) | copy-start | bytes 1540
  7.3 69.6 %collective-permute-start = (bf16[3,2048]{1,0:T(4,128)(2,1)S(1)}, bf16[3,2048]{1,0:T(4,128)(2,1)S(1)}, u32[]{:S(2)}, u32[]{:S(2)}) collective-permute-start(bf16[3,2048]{1,0:T(4,128)(2,1)S(1)} %slice.82), channel_id=1, source_target_pairs={{0,4},{4,8},{8,12},{12,16},{16,20},{20,24},{24,28},{1,5},{5,9},{9,... | collective-permute-start | bytes 36872 | tf_op jit(solution)/shard_map/ppermute | solution.py:19
  28.0 3.9 copy-start.9
  40.0 4.7 %copy-start.16 = (s32[16]{0:T(128)S(1)}, s32[16]{0:T(128)}, u32[]{:S(2)}) copy-start(s32[16]{0:T(128)} %param.30) | copy-start | bytes 196
  40.0 5.1 %copy-start.13 = (bf16[4,8192]{1,0:T(4,128)(2,1)S(1)}, bf16[4,8192]{1,0:T(4,128)(2,1)}, u32[]{:S(2)}) copy-start(bf16[4,8192]{1,0:T(4,128)(2,1)} %param.26) | copy-start | bytes 196612
  40.0 36.9 %all-to-all-start.1 = ((bf16[512,4,512]{0,2,1:T(8,128)(2,1)}), bf16[512,4,512]{0,2,1:T(8,128)(2,1)S(1)}, u32[]{:S(2)}, u32[]{:S(2)}) async-start(bf16[512,4,512]{0,2,1:T(8,128)(2,1)} %bitcast.169), calls=%async_computation.1 | async-start | bytes 4194304 | tf_op jit(solution)/shard_map/all_to_all | solution.py:160
  44.7 2.3 copy-start.14
  44.7 2.4 copy-start.15
  44.7 352.4 %all-gather.5.cloned.1.call-start = ((), (), s32[]{:S(2)}) async-start(), calls=%async_computation.3 | async-start | bytes 4718592 | tf_op jit(solution)/shard_map/all_gather | solution.py:24
  83.4 162.0 %copy-start.1 = (f32[256,4,2,128]{3,0,2,1:T(8,128)}, f32[256,4,2,128]{3,0,2,1:T(8,128)S(1)}, u32[]{:S(2)}) copy-start(f32[256,4,2,128]{3,0,2,1:T(8,128)S(1)} %broadcast_in_dim.115) | copy-start | bytes 3145732
  244.7 2.5 copy-start.10
  245.3 5.7 %copy-start.7 = (f32[4,8,64,128]{3,2,0,1:T(8,128)}, f32[4,8,64,128]{3,2,0,1:T(8,128)S(1)}, u32[]{:S(2)}) copy-start(f32[4,8,64,128]{3,2,0,1:T(8,128)S(1)} %get-tuple-element.234) | copy-start | bytes 3145732
  247.3 3.7 copy-start.5
  262.2 52.8 %all-to-all-start.2 = ((bf16[512,4,1024]{0,2,1:T(8,128)(2,1)}), bf16[512,4,1024]{0,2,1:T(8,128)(2,1)}, u32[]{:S(2)}, u32[]{:S(2)}) async-start(bf16[512,4,1024]{0,2,1:T(8,128)(2,1)} %bitcast_select_fusion), calls=%async_computation.2 | async-start | bytes 8388608 | tf_op jit(solution)/shard_map/all_to_all | solution.py:163
  267.1 131.8 %all-gather.7.cloned.1.call-start = ((), (), s32[]{:S(2)}) async-start(), calls=%async_computation.4 | async-start | bytes 4718592 | tf_op jit(solution)/shard_map/all_gather | solution.py:24
  325.2 1.2 copy-start.11
  326.1 2.4 copy-start.8
  328.6 4.8 %copy-start.3 = (f32[4,8,64,128]{3,2,1,0:T(8,128)}, f32[4,8,64,128]{3,2,1,0:T(8,128)S(1)}, u32[]{:S(2)}) copy-start(f32[4,8,64,128]{3,2,1,0:T(8,128)S(1)} %fusion.33) | copy-start | bytes 3145732
  355.8 29.8 %all-to-all-start = ((bf16[512,4,512]{0,2,1:T(8,128)(2,1)}), bf16[512,4,512]{0,2,1:T(8,128)(2,1)S(1)}, u32[]{:S(2)}, u32[]{:S(2)}) async-start(bf16[512,4,512]{0,2,1:T(8,128)(2,1)} %bitcast.171), calls=%async_computation | async-start | bytes 4194304 | tf_op jit(solution)/shard_map/all_to_all | solution.py:157
  391.5 1.2 copy-start.2
  392.0 2.6 copy-start.6
  394.6 1.3 copy-start.4
  414.9 3.7 copy-start.12
Sparse Core Ops, SparseCore 0:
  258.4 48.9 all-gather.4
  352.0 46.8 all-gather.6
where the time goes:
time: 441 us; the launch traced here: 432 us
  other arithmetic  177 us (40%)
  local copies, waits for them, and re-layouts  93.6 us (21%)
  waiting for transfers between devices  66 us (15%)
  matrix products  64.4 us (15%)
  starting transfers between devices  15.8 us (4%)
  between operations  15 us (3%)
    another operation x3, other arithmetic, lower_solve(): lax.linalg.triangular_solve(system, right, left_side=True, lower=True, un...  159 us
    all_to_all x1, waiting for transfers between devices, per_device(): lax.all_to_all(arrange(payload_projection_matrix, 2 * VALUE_HEAD_SIZE, he...  41.9 us
    all_to_all x1, waiting for transfers between devices, per_device(): lax.all_to_all(arrange(w_query, DK, head_order), 'head', split_axis=1, co...  22.1 us
    unnamed x45, local copies, waits for them, and re-layouts  17.7 us
    gather x4, local copies, waits for them, and re-layouts, arrange(): return jnp.take(blocks, head_order, axis=1).reshape(rows, weight.shape[1])  17.4 us
    dot_general x8, matrix products, combine(): jnp.einsum('hij,hjv->hiv', later[0], earlier[1], precision=HIGH_PRECISION)  15.1 us
    reshape x3, local copies, waits for them, and re-layouts, arrange(): blocks = weight.reshape(rows, weight.shape[1] // width, width)  13.3 us
    dot_general x4, matrix products, value_chain(): jnp.einsum('hij,hjv->hiv', pair[0], acc, precision=HIGH_PRECISION) + pair[1]  9.94 us
  transfers between devices with their start and end apart: 6, of which 3 were waited for; matrix products, arithmetic and copies ran while one was open for 29% of the time, Pallas kernels for 0%

commit v1 on v0

v1 whole, which is shorter than its diff:
```python
import functools

import jax
import jax.numpy as jnp
from jax import lax
from jax.experimental import pallas as pl
from jax.experimental.pallas import tpu as pltpu
from jax.sharding import PartitionSpec as P

HEAD = 128
TAPS = 4
RIM = 16
EPS = 1e-06
VMEM_BYTES = 40 * 1024 * 1024
F32 = jnp.float32
BF16 = jnp.bfloat16

NN = (((1,), (0,)), ((), ()))
NT = (((1,), (1,)), ((), ()))


def dot1(a, b, dims=NN):
    return lax.dot_general(
        a.astype(BF16), b.astype(BF16), dims, preferred_element_type=F32
    )


def split(a):
    high = a.astype(BF16)
    return high, (a - high.astype(F32)).astype(BF16)


def dot3s(a, b, dims=NN):
    (ah, al), (bh, bl) = a, b
    one = functools.partial(lax.dot_general, dimension_numbers=dims, preferred_element_type=F32)
    return one(ah, bh) + (one(ah, bl) + one(al, bh))


def dot3(a, b, dims=NN):
    return dot3s(split(a), split(b), dims)


def dot_full(a, b, dims=NN):
    return lax.dot_general(
        a, b, dims, precision=lax.Precision.HIGHEST, preferred_element_type=F32
    )


def whole(array):
    zeros = (0,) * array.ndim
    return pl.BlockSpec(array.shape, lambda i, sp: zeros)


def call(body, sp, inputs, specs, outs, scratch=(), flops=10**7):
    return pl.pallas_call(
        body,
        grid_spec=pltpu.PrefetchScalarGridSpec(
            num_scalar_prefetch=1,
            grid=(1,),
            in_specs=specs,
            out_specs=[whole(out) for out in outs],
            scratch_shapes=list(scratch),
        ),
        out_shape=[jax.ShapeDtypeStruct(out.shape, out.dtype) for out in outs],
        compiler_params=pltpu.CompilerParams(vmem_limit_bytes=VMEM_BYTES),
        cost_estimate=pl.CostEstimate(flops=flops, bytes_accessed=2**20, transcendentals=0),
    )(sp, *inputs)


class Plan:
    def __init__(self, ranks, key_heads):
        bits = [1 << i for i in range(ranks.bit_length() - 1)]
        self.orders = (bits, bits[::-1])
        self.stages = len(bits)
        self.key_heads = key_heads

    def offsets(self, route, stage):
        out = [0]
        for bit in self.orders[route][stage + 1 :]:
            out = out + [o ^ bit for o in out]
        return out

    def weight_spec(self, rows, width, unit, head):
        heads = self.key_heads
        return pl.BlockSpec(
            (rows, width), lambda i, sp: (0, sp[2 + (sp[0] ^ unit) * heads + head])
        )

    def tap_spec(self, width, base, head):
        heads = self.key_heads
        return pl.BlockSpec(
            (TAPS, width), lambda i, sp: (0, base + sp[2 + sp[0] * heads + head])
        )


def hidden_spec(hidden, rows):
    return pl.BlockSpec((hidden.shape[0], rows), lambda i, sp: (0, sp[0]))


def send_stage(plan, stage, chunk, hidden, rim, weight, received, sp):
    rows, count = weight.shape[0], hidden.shape[0]
    width = chunk["width"]
    inputs, specs = [hidden, rim], [hidden_spec(hidden, rows), whole(rim)]
    jobs, outs, places = [], [], {}
    for route, heads in enumerate(chunk["heads"]):
        if not heads:
            continue
        offsets = plan.offsets(route, stage)
        for before in range(stage):
            places[route, before] = len(inputs)
            inputs.append(received[route][before])
            specs.append(whole(received[route][before]))
        for slot, offset in enumerate(offsets):
            unit = offset ^ plan.orders[route][stage]
            sources = [
                (places[route, before], plan.offsets(route, before).index(unit))
                for before in range(stage)
            ]
            for at, head in enumerate(heads):
                jobs.append((len(inputs), sources, len(outs), slot, at))
                inputs.append(weight)
                specs.append(plan.weight_spec(rows, width, unit, head))
        outs.append(
            jax.ShapeDtypeStruct((len(offsets), RIM + count, width * len(heads)), BF16)
        )
    total = len(inputs)

    def body(sp_ref, *refs):
        tokens, edge = refs[0][...], refs[1][...]
        for place, sources, out, slot, at in jobs:
            held = refs[place][...]
            cols = slice(at * width, (at + 1) * width)
            for left, span in ((edge, slice(0, RIM)), (tokens, slice(RIM, RIM + count))):
                part = jnp.dot(left, held, preferred_element_type=F32)
                for source, index in sources:
                    part = part + refs[source][index, span, cols].astype(F32)
                refs[total + out][slot, span, cols] = part.astype(BF16)

    sent = call(body, sp, inputs, specs, outs)
    result, at = [], 0
    for heads in chunk["heads"]:
        result.append(sent[at] if heads else None)
        at += 1 if heads else 0
    return result


def exchange(plan, stage, sent):
    ranks = lax.axis_size("head")
    return [
        None
        if part is None
        else lax.ppermute(
            part, "head", [(i, i ^ plan.orders[route][stage]) for i in range(ranks)]
        )
        for route, part in enumerate(sent)
    ]


def gather_specs(plan, chunk, heads, hidden, rim, weight, taps, base, received):
    rows, width = weight.shape[0], chunk["width"]
    inputs, specs = [hidden, rim], [hidden_spec(hidden, rows), whole(rim)]
    places, jobs = {}, []
    for head in heads:
        route = [head in group for group in chunk["heads"]].index(True)
        if route not in places:
            places[route] = []
            for part in received[route]:
                places[route].append(len(inputs))
                inputs.append(part)
                specs.append(pl.BlockSpec((1,) + part.shape[1:], lambda i, sp: (0, 0, 0)))
        at = chunk["heads"][route].index(head)
        jobs.append((len(inputs), places[route], slice(at * width, (at + 1) * width)))
        inputs += [weight, taps]
        specs += [plan.weight_spec(rows, width, 0, head), plan.tap_spec(width, base, head)]
    return inputs, specs, jobs


def activate(refs, job, scratch):
    place, sources, cols = job
    held, taps = refs[place][...], refs[place + 1][...].astype(F32)
    count = refs[0].shape[0]
    for left, span in ((refs[1], slice(0, RIM)), (refs[0], slice(RIM, RIM + count))):
        part = jnp.dot(left[...], held, preferred_element_type=F32)
        for source in sources:
            part = part + refs[source][0, span, cols].astype(F32)
        scratch[span, :] = part
    total = None
    for tap in range(TAPS):
        first = RIM - (TAPS - 1) + tap
        term = taps[tap : tap + 1] * scratch[first : first + count, :]
        total = term if total is None else total + term
    return total / (1.0 + jnp.exp(-total))


def unit_rows(values):
    return values * lax.rsqrt(jnp.sum(values * values, axis=-1, keepdims=True) + EPS)


def iotas(size):
    return (
        lax.broadcasted_iota(jnp.int32, (size, size), 0),
        lax.broadcasted_iota(jnp.int32, (size, size), 1),
    )


def running(decay):
    size = decay.shape[1]
    rows, cols = iotas(size)
    upper = (rows <= cols).astype(F32)
    lower = (cols <= rows).astype(F32)
    return dot_full(decay, upper), dot_full(lower, decay, NT)


def as_columns(values):
    rows, cols = iotas(values.shape[1])
    return dot_full((rows == cols).astype(F32), values, NT)


def inverses(systems):
    size = systems[0].shape[0]
    rows, cols = iotas(size)
    eye = (rows == cols).astype(F32)
    near = [jnp.where((rows >> 3) == (cols >> 3), low, 0.0) for low in systems]
    cut = [split(n) for n in near]
    square = [dot3s(c, c) for c in cut]
    cut2 = [split(s) for s in square]
    cube = [dot3s(c, c2) for c, c2 in zip(cut, cut2)]
    inv = [eye - n + s - c for n, s, c in zip(near, square, cube)]
    fourth = [split(dot3s(c2, c2)) for c2 in cut2]
    inv = [x + dot3s(split(x), f) for x, f in zip(inv, fourth)]
    shift = 3
    while (1 << shift) < size:
        inside = ((rows >> (shift + 1)) == (cols >> (shift + 1))) & (
            (rows >> shift) != (cols >> shift)
        )
        parts = [split(x) for x in inv]
        lower = [split(jnp.where(inside, low, 0.0)) for low in systems]
        middle = [split(dot3s(low, x)) for low, x in zip(lower, parts)]
        inv = [x - dot3s(p, m) for x, p, m in zip(inv, parts, middle)]
        shift += 1
    return inv


def key_phase(plan, chunk, heads, hidden, rim, weight, taps, base, received, decay, beta, sp):
    inputs, specs, jobs = gather_specs(
        plan, chunk, heads, hidden, rim, weight, taps, base, received
    )
    at = len(inputs)
    inputs += [decay, beta]
    specs += [whole(decay), whole(beta)]
    count, number = hidden.shape[0], 2 * len(heads)
    half = count // 2
    first = 2 * heads[0]
    outs = [
        jax.ShapeDtypeStruct((len(heads), count, HEAD), F32),
        jax.ShapeDtypeStruct((len(heads), HEAD, count), F32),
        jax.ShapeDtypeStruct((number, 3, half, half), F32),
        jax.ShapeDtypeStruct((number, count, HEAD), F32),
        jax.ShapeDtypeStruct((number, HEAD, HEAD), F32),
    ]
    total = len(inputs)

    def body(sp_ref, *refs):
        key_ref, turned_ref, solve_ref, write_ref, trans_ref, scratch = refs[total:]
        sums, sums_col = running(refs[at][...])
        beta_col = as_columns(refs[at + 1][...])
        rows, cols = iotas(half)
        keys, systems, crosses = [], [], []
        for i, job in enumerate(jobs):
            key = unit_rows(activate(refs, job, scratch))
            keys.append(key)
            key_ref[i] = key
            turned_ref[i] = key.T
            low, high = split(key[:half]), split(key[half:])
            alike = (dot3s(low, low, NT), dot3s(high, high, NT), dot3s(high, low, NT))
            for r in (first + 2 * i, first + 2 * i + 1):
                row, col, rate = sums[r : r + 1], sums_col[:, r : r + 1], beta_col[:, r : r + 1]
                for b, span in enumerate((slice(0, half), slice(half, count))):
                    fade = jnp.exp(jnp.minimum(col[span] - row[:, span], 0.0))
                    systems.append(jnp.where(cols < rows, rate[span] * fade * alike[b], 0.0))
                fade = jnp.exp(jnp.minimum(col[half:] - row[:, :half], 0.0))
                crosses.append(rate[half:] * fade * alike[2])
        solved = [split(x) for x in inverses(systems)]
        middle = [
            split(dot3s(split(c), solved[2 * j])) for j, c in enumerate(crosses)
        ]
        corner = [-dot3s(solved[2 * j + 1], m) for j, m in enumerate(middle)]
        keep = sp_ref[1].astype(F32)
        eye = (lax.broadcasted_iota(jnp.int32, (HEAD, HEAD), 0)
               == lax.broadcasted_iota(jnp.int32, (HEAD, HEAD), 1)).astype(F32)
        for j in range(number):
            r, key = first + j, keys[j // 2]
            row, col, rate = sums[r : r + 1], sums_col[:, r : r + 1], beta_col[:, r : r + 1]
            top, bottom, side = solved[2 * j], solved[2 * j + 1], split(corner[j])
            for place, part in enumerate((top, bottom, side)):
                solve_ref[j, place] = part[0].astype(F32) + part[1].astype(F32)
            right = (rate * jnp.exp(col)) * key
            right_low, right_high = split(right[:half]), split(right[half:])
            write_low = dot3s(top, right_low)
            write_high = dot3s(side, right_low) + dot3s(bottom, right_high)
            write_ref[j, :half] = write_low
            write_ref[j, half:] = write_high
            tail = jnp.exp(row[:, count - 1 :] - row)
            trailing = turned_ref[j // 2] * tail
            moved = dot3(trailing[:, :half], write_low) + dot3(trailing[:, half:], write_high)
            gone = jnp.exp(row[:, count - 1 :])
            trans_ref[j] = keep * (gone * eye - moved)

    return call(
        body, sp, inputs, specs, outs, [pltpu.VMEM((RIM + count, HEAD), F32)], flops=4 * 10**9
    )


def value_phase(
    plan, chunk, heads, hidden, rim, weight, taps, base, received, decay, beta, turned, solve, sp
):
    inputs, specs, jobs = gather_specs(
        plan, chunk, heads, hidden, rim, weight, taps, base, received
    )
    at = len(inputs)
    inputs += [decay, beta, turned, solve]
    specs += [whole(decay), whole(beta), whole(turned), whole(solve)]
    count, number = hidden.shape[0], 2 * len(heads)
    half = count // 2
    first = 2 * heads[0]
    outs = [
        jax.ShapeDtypeStruct((number, count, HEAD), F32),
        jax.ShapeDtypeStruct((number, HEAD, HEAD), F32),
    ]
    total = len(inputs)

    def body(sp_ref, *refs):
        write_ref, trans_ref, scratch = refs[total:]
        turned_ref, solve_ref = refs[at + 2], refs[at + 3]
        sums, _ = running(refs[at][...])
        beta_col = as_columns(refs[at + 1][...])
        for i, job in enumerate(jobs):
            values = activate(refs, job, scratch)
            for j in (2 * i, 2 * i + 1):
                r = first + j
                row, rate = sums[r : r + 1], beta_col[:, r : r + 1]
                right = rate * values[:, (j % 2) * HEAD : (j % 2 + 1) * HEAD]
                low, high = split(right[:half]), split(right[half:])
                write_low = dot3s(split(solve_ref[j, 0]), low)
                write_high = dot3s(split(solve_ref[j, 2]), low) + dot3s(
                    split(solve_ref[j, 1]), high
                )
                write_ref[j, :half] = write_low
                write_ref[j, half:] = write_high
                trailing = turned_ref[i] * jnp.exp(row[:, count - 1 :] - row)
                trans_ref[j] = dot3(trailing[:, :half], write_low) + dot3(
                    trailing[:, half:], write_high
                )

    return call(
        body, sp, inputs, specs, outs, [pltpu.VMEM((RIM + count, 2 * HEAD), F32)], flops=10**9
    )


def query_phase(
    plan, chunk, heads, hidden, rim, weight, taps, base, received, decay, keys, write_k, write_v, sp
):
    inputs, specs, jobs = gather_specs(
        plan, chunk, heads, hidden, rim, weight, taps, base, received
    )
    at = len(inputs)
    inputs += [decay, keys, write_k, write_v]
    specs += [whole(decay), whole(keys), whole(write_k), whole(write_v)]
    count, number = hidden.shape[0], 2 * len(heads)
    first = 2 * heads[0]
    outs = [
        jax.ShapeDtypeStruct((number, count, HEAD), F32),
        jax.ShapeDtypeStruct((number, count, HEAD), F32),
    ]
    total = len(inputs)

    def body(sp_ref, *refs):
        inner_ref, query_ref, scratch = refs[total:]
        key_ref, write_k_ref, write_v_ref = refs[at + 1 : at + 4]
        sums, sums_col = running(refs[at][...])
        rows, cols = iotas(count)
        for i, job in enumerate(jobs):
            query = unit_rows(activate(refs, job, scratch))
            alike = dot3(query, key_ref[i], NT)
            for j in (2 * i, 2 * i + 1):
                r = first + j
                row, col = sums[r : r + 1], sums_col[:, r : r + 1]
                fade = jnp.exp(jnp.minimum(col - row, 0.0))
                attend = jnp.where(cols <= rows, fade * alike, 0.0)
                attend = split(attend)
                inner_ref[j] = dot3s(attend, split(write_v_ref[j]))
                query_ref[j] = jnp.exp(col) * query - dot3s(attend, split(write_k_ref[j]))

    return call(
        body, sp, inputs, specs, outs, [pltpu.VMEM((RIM + count, HEAD), F32)], flops=10**9
    )


def join_pair(mine_a, mine_b, other_a, other_b, sp, place):
    number = mine_a.shape[0]
    half = number // 2
    inputs = [mine_a, mine_b, other_a, other_b]
    out = jax.ShapeDtypeStruct((2, half, HEAD, HEAD), BF16)

    def body(sp_ref, mine_a_ref, mine_b_ref, other_a_ref, other_b_ref, out_ref):
        core = sp_ref[place]
        for i in range(half):
            h = core * half + i
            pair = [
                (mine_a_ref[h], other_a_ref[h].astype(F32)),
                (mine_b_ref[h], other_b_ref[h].astype(F32)),
            ]
            early_a, early_b = [jnp.where(core == 0, p[0], p[1]) for p in pair]
            late_a, late_b = [jnp.where(core == 0, p[1], p[0]) for p in pair]
            late = split(late_a)
            out_ref[0, i] = dot3s(late, split(early_a)).astype(BF16)
            out_ref[1, i] = (dot3s(late, split(early_b)) + late_b).astype(BF16)

    return call(body, sp, inputs, [whole(a) for a in inputs], [out])[0]


def run_chain(parts, sp):
    half = parts[0].shape[1]
    out = jax.ShapeDtypeStruct((half, HEAD, HEAD), BF16)

    def body(sp_ref, *refs):
        for i in range(half):
            state = refs[0][1, i].astype(F32)
            for part in refs[1:-1]:
                high, low = split(state)
                left = part[0, i]
                state = (
                    jnp.dot(left, high, preferred_element_type=F32)
                    + jnp.dot(left, low, preferred_element_type=F32)
                    + part[1, i].astype(F32)
                )
            refs[-1][i] = state.astype(BF16)

    return call(body, sp, parts, [whole(a) for a in parts], [out])[0]


def shifted(value, steps):
    count = lax.axis_size("ctx")
    return lax.ppermute(value, "ctx", [(i, i + steps) for i in range(count - steps)])


def swapped(value):
    count = lax.axis_size("ctx")
    return lax.ppermute(value, "ctx", [(i, i ^ 1) for i in range(count)])


def enter_chip(joined, sp):
    chips = lax.axis_size("ctx") // 2
    if chips == 1:
        return jnp.zeros(joined.shape[1:], BF16)
    if chips <= 4:
        parts = [shifted(joined, 2 * d) for d in range(chips - 1, 0, -1)]
        return run_chain(parts, sp)
    joined = shifted(joined, 2)
    step = 1
    while step < chips:
        early = shifted(joined, 2 * step).astype(F32)
        late = joined.astype(F32)
        both = jnp.einsum(
            "hij,xhjk->xhik", late[0], early, precision=lax.Precision.HIGHEST
        )
        joined = (both + late * jnp.array([0.0, 1.0], F32)[:, None, None, None]).astype(BF16)
        step *= 2
    return joined[1]


def finish(groups, gain, sp, place, count):
    inputs = [gain]
    for group in groups:
        inputs += list(group)
    heads = sum(group[0].shape[0] for group in groups)
    out = jax.ShapeDtypeStruct((count, heads * HEAD), BF16)

    def body(sp_ref, gain_ref, *refs):
        out_ref = refs[-1]
        core = sp_ref[place]
        keep = sp_ref[1].astype(F32)
        at = 0
        for g in range(len(groups)):
            inner, query, mine, other, early_a, early_b = refs[6 * g : 6 * g + 6]
            number = inner.shape[0]
            half = number // 2
            for j in range(number):
                low_half = j < half
                i = j % half
                own, far = mine[i].astype(F32), other[i].astype(F32)
                state = jnp.where((core == 0) == low_half, own, far)
                stepped = dot3(early_a[j].astype(F32), state) + early_b[j].astype(F32)
                state = keep * jnp.where(core == 0, state, stepped)
                read = inner[j] + dot3(query[j], state)
                scale = lax.rsqrt(jnp.mean(read * read, axis=-1, keepdims=True) + EPS)
                cols = slice(at * HEAD, (at + 1) * HEAD)
                out_ref[:, cols] = (read * scale * gain_ref[...]).astype(BF16)
                at += 1

    return call(body, sp, inputs, [whole(a) for a in inputs], [out], flops=10**8)[0]


def per_device(
    hidden,
    w_query,
    w_key,
    payload_projection_matrix,
    conv_weight,
    log_decay,
    beta_rate,
    norm_gain,
    head_order,
    block_starts,
):
    count = hidden.shape[0]
    ranks = lax.axis_size("head")
    total_heads = head_order.shape[0]
    key_heads = total_heads // ranks
    plan = Plan(ranks, key_heads)
    serve = lax.axis_index("head")
    core = lax.axis_index("ctx") % 2
    rows = w_key.shape[0]
    keep = 1 - block_starts[0]
    place = 2 + total_heads
    sp = jnp.concatenate(
        [jnp.stack([serve, keep]), head_order, jnp.stack([core])]
    ).astype(jnp.int32)

    edge = lax.dynamic_slice(hidden, (count - RIM, serve * rows), (RIM, rows))
    rim = shifted(edge, 1) * keep.astype(BF16)

    cut = (key_heads + 1) // 2
    every = [list(range(cut)), list(range(cut, key_heads))]
    groups = [list(range(i, min(i + 2, key_heads))) for i in range(0, key_heads, 2)]
    narrow = {"width": HEAD, "heads": every}
    wide = [{"width": 2 * HEAD, "heads": [g[:1], g[1:]]} for g in groups]
    chunks = [(narrow, w_key)] + [(w, payload_projection_matrix) for w in wide]
    chunks.append((narrow, w_query))

    arrived = []
    for chunk, weight in chunks:
        received = [[], []]
        for stage in range(plan.stages):
            sent = send_stage(plan, stage, chunk, hidden, rim, weight, received, sp)
            for route, part in enumerate(exchange(plan, stage, sent)):
                if part is not None:
                    received[route].append(part)
        arrived.append(received)

    gain = norm_gain[None, :]
    results = []
    for g, heads in enumerate(groups):
        keys, turned, solve, write_k, trans_a = key_phase(
            plan, narrow, heads, hidden, rim, w_key, conv_weight, total_heads,
            arrived[0], log_decay, beta_rate, sp,
        )
        write_v, trans_b = value_phase(
            plan, wide[g], heads, hidden, rim, payload_projection_matrix, conv_weight,
            total_heads, arrived[1 + g], log_decay, beta_rate, turned, solve, sp,
        )
        other_a, other_b = swapped(trans_a), swapped(trans_b)
        joined = join_pair(trans_a, trans_b, other_a, other_b, sp, place)
        mine = enter_chip(joined, sp)
        other = swapped(mine)
        inner, query = query_phase(
            plan, narrow, heads, hidden, rim, w_query, conv_weight, 0,
            arrived[-1], log_decay, keys, write_k, write_v, sp,
        )
        results.append((inner, query, mine, other, other_a, other_b))
    return finish(results, gain, sp, place, count)


def solution(mesh):
    return jax.shard_map(
        per_device,
        mesh=mesh,
        in_specs=(
            P("ctx", None),
            P("head", None),
            P("head", None),
            P("head", None),
            P(),
            P("head", "ctx"),
            P("head", "ctx"),
            P(),
            P(),
            P("ctx"),
        ),
        out_specs=P("ctx", "head"),
        check_vma=False,
    )
```

time: 441 us -> 97.7 us (0.22); the launches traced: 432 us -> 97.4 us
  other arithmetic: 177 us -> 0.74 us
  local copies, waits for them, and re-layouts: 93.6 us -> 3.56 us
  matrix products: 64.4 us -> 0 us
  waiting for transfers between devices: 66 us -> 1.82 us
  Pallas kernels: 0 us -> 40.6 us
  starting transfers between devices: 15.8 us -> 49.7 us
  between operations: 15 us -> 1.02 us
    another operation x6 -> x0, other arithmetic: 159 us -> none  [the longest x3 159 us: lower_solve(): lax.linalg.triangular_solve(system, right, left_side=True, lower=True, un...]
    all_to_all x3 -> x0, waiting for transfers between devices: 64.1 us -> none  [the longest x1 41.9 us: per_device(): lax.all_to_all(arrange(payload_projection_matrix, 2 * VALUE_HEAD_SIZE, he...]
    dot_general x27 -> x0, matrix products: 60.4 us -> none  [the longest x8 15.1 us: combine(): jnp.einsum('hij,hjv->hiv', later[0], earlier[1], precision=HIGH_PRECISION)]
    ppermute x1 -> x29, starting transfers between devices: 2.36 us -> 49.7 us  [the longest x7 26 us: shifted(): lax.ppermute(value, 'ctx', [(i, i + steps) for i in range(count - steps)])]
    pallas_call x0 -> x19, Pallas kernels: none -> 40.6 us  [call(): pl.pallas_call(body, grid_spec=pltpu.PrefetchScalarGridSpec(num_scalar_pr...]
    gather x7 -> x0, local copies, waits for them, and re-layouts: 28.5 us -> none  [the longest x4 17.4 us: arrange(): return jnp.take(blocks, head_order, axis=1).reshape(rows, weight.shape[1])]
    unnamed x45 -> x20, local copies, waits for them, and re-layouts: 17.7 us -> 2.84 us
    reshape x9 -> x0, local copies, waits for them, and re-layouts: 13.9 us -> none  [the longest x3 13.3 us: arrange(): blocks = weight.reshape(rows, weight.shape[1] // width, width)]
  transfers between devices with their start and end apart: 6 -> 29, of which waited for: 3 -> 4; matrix products, arithmetic and copies ran while one was open for 29% -> 1% of each run, Pallas kernels for 0% -> 37%
where the time goes in v1:
time: 97.7 us; the launch traced here: 97.4 us
  starting transfers between devices  49.7 us (51%)
  Pallas kernels  40.6 us (42%)
  local copies, waits for them, and re-layouts  3.56 us (4%)
  waiting for transfers between devices  1.82 us (2%)
  between operations  1.02 us (1%)
    pallas_call x19, Pallas kernels, call(): pl.pallas_call(body, grid_spec=pltpu.PrefetchScalarGridSpec(num_scalar_pr...  40.6 us
    ppermute x7, starting transfers between devices, shifted(): lax.ppermute(value, 'ctx', [(i, i + steps) for i in range(count - steps)])  26 us
    ppermute x16, starting transfers between devices, exchange(): lax.ppermute(part, 'head', [(i, i ^ plan.orders[route][stage]) for i in r...  21.8 us
    unnamed x20, local copies, waits for them, and re-layouts  2.84 us
  transfers between devices with their start and end apart: 29, of which 4 were waited for; matrix products, arithmetic and copies ran while one was open for 1% of the time, Pallas kernels for 37%

profile of v1, /device:TPU:0, one launch (start us, length us, event | category | flops | bytes accessed | tf_op | source)
XLA Modules:
  0.0 97.4 jit_solution(17805771563400909776)
XLA Ops:
  0.0 0.7 constant_dynamic-slice_fusion
  0.7 2.3 %collective-permute-start = (bf16[16,512]{1,0:T(8,128)(2,1)S(1)}, bf16[16,512]{1,0:T(8,128)(2,1)S(1)}, u32[]{:S(2)}, u32[]{:S(2)}) collective-permute-start(bf16[16,512]{1,0:T(8,128)(2,1)S(1)} %constant_dynamic-slice_fusion), channel_id=1, source_target_pairs={{0,4},{4,8},{8,12},{12,16},{16,20},{20,24},{24,28},{1,5},{5,9},{9,... | collective-permute-start | bytes 49160 | tf_op jit(solution)/shard_map/ppermute | solution.py:444
  3.7 0.7 pad_add_fusion.sp_ref
  4.5 0.0 copy-start.2
  4.5 1.6 %copy-done.2 = bf16[512,2048]{1,0:T(8,128)(2,1)S(1)} copy-done((bf16[512,2048]{1,0:T(8,128)(2,1)S(1)}, bf16[512,2048]{1,0:T(8,128)(2,1)}, u32[]{:S(2)}) %copy-start.2) | copy-done | bytes 2097176
  6.1 1.2 %copy-done.4 = bf16[256,2048]{1,0:T(8,128)(2,1)S(1)} copy-done((bf16[256,2048]{1,0:T(8,128)(2,1)S(1)}, bf16[256,2048]{1,0:T(8,128)(2,1)}, u32[]{:S(2)}) %copy-start.4) | copy-done | bytes 1048600
  7.3 1.6 %shard_map.102 = (bf16[2,272,256]{2,1,0:T(8,128)(2,1)S(1)}, bf16[2,272,256]{2,1,0:T(8,128)(2,1)S(1)}) custom-call(s32[19]{0:T(128)S(1)} %pad_add_fusion.sp_ref, bf16[256,2048]{1,0:T(8,128)(2,1)S(1)} %copy-done.4, bf16[16,512]{1,0:T(8,128)(2,1)S(1)} %broadcast_multiply_fusion.refs_1_, bf16[512,2048]{1,0:T(8,128)(2,1)S(1)} %copy-done.2, ...), custom_call_target="tpu_custom_call" | custom-call | flops 10000000 | bytes 1048576 | tf_op jit(solution)/shard_map/pallas_call | solution.py:55
  8.9 2.4 %collective-permute-start.4 = (bf16[2,272,256]{2,1,0:T(8,128)(2,1)S(1)}, bf16[2,272,256]{2,1,0:T(8,128)(2,1)S(1)}, u32[]{:S(2)}, u32[]{:S(2)}) collective-permute-start(bf16[2,272,256]{2,1,0:T(8,128)(2,1)S(1)} %get-tuple-element.42), channel_id=1, source_target_pairs={{0,1},{1,0},{2,3},{3,2},{4,5},{5,4},{6,7},{7,6},{8,9},{9,8},{10,11... | collective-permute-start | bytes 835592 | tf_op jit(solution)/shard_map/ppermute | solution.py:152
  11.2 1.5 %collective-permute-start.5 = (bf16[2,272,256]{2,1,0:T(8,128)(2,1)S(1)}, bf16[2,272,256]{2,1,0:T(8,128)(2,1)S(1)}, u32[]{:S(2)}, u32[]{:S(2)}) collective-permute-start(bf16[2,272,256]{2,1,0:T(8,128)(2,1)S(1)} %get-tuple-element.43), channel_id=1, source_target_pairs={{0,2},{1,3},{2,0},{3,1},{4,6},{5,7},{6,4},{7,5},{8,10},{9,11},{10,... | collective-permute-start | bytes 835592 | tf_op jit(solution)/shard_map/ppermute | solution.py:152
  12.8 1.1 %shard_map.112 = (bf16[2,272,256]{2,1,0:T(8,128)(2,1)S(1)}, bf16[2,272,256]{2,1,0:T(8,128)(2,1)S(1)}) custom-call(s32[19]{0:T(128)S(1)} %pad_add_fusion.sp_ref, bf16[256,2048]{1,0:T(8,128)(2,1)S(1)} %copy-done.4, bf16[16,512]{1,0:T(8,128)(2,1)S(1)} %broadcast_multiply_fusion.refs_1_, bf16[512,4096]{1,0:T(8,128)(2,1)S(1)} %copy-done, ...), custom_call_target="tpu_custom_call" | custom-call | flops 10000000 | bytes 1048576 | tf_op jit(solution)/shard_map/pallas_call | solution.py:55
  13.9 0.6 collective-permute-start.19
  14.5 0.0 collective-permute-start.20
  14.6 1.1 %shard_map.105 = (bf16[2,272,256]{2,1,0:T(8,128)(2,1)S(1)}, bf16[2,272,256]{2,1,0:T(8,128)(2,1)S(1)}) custom-call(s32[19]{0:T(128)S(1)} %pad_add_fusion.sp_ref, bf16[256,2048]{1,0:T(8,128)(2,1)S(1)} %copy-done.4, bf16[16,512]{1,0:T(8,128)(2,1)S(1)} %broadcast_multiply_fusion.refs_1_, bf16[512,4096]{1,0:T(8,128)(2,1)S(1)} %copy-done, ...), custom_call_target="tpu_custom_call" | custom-call | flops 10000000 | bytes 1048576 | tf_op jit(solution)/shard_map/pallas_call | solution.py:55
  15.7 2.0 %collective-permute-start.7 = (bf16[2,272,256]{2,1,0:T(8,128)(2,1)S(1)}, bf16[2,272,256]{2,1,0:T(8,128)(2,1)S(1)}, u32[]{:S(2)}, u32[]{:S(2)}) collective-permute-start(bf16[2,272,256]{2,1,0:T(8,128)(2,1)S(1)} %get-tuple-element.47), channel_id=1, source_target_pairs={{0,1},{1,0},{2,3},{3,2},{4,5},{5,4},{6,7},{7,6},{8,9},{9,8},{10,11... | collective-permute-start | bytes 835592 | tf_op jit(solution)/shard_map/ppermute | solution.py:152
  17.7 0.0 collective-permute-done.4.refs_2_
  17.7 2.2 %collective-permute-start.8 = (bf16[2,272,256]{2,1,0:T(8,128)(2,1)S(1)}, bf16[2,272,256]{2,1,0:T(8,128)(2,1)S(1)}, u32[]{:S(2)}, u32[]{:S(2)}) collective-permute-start(bf16[2,272,256]{2,1,0:T(8,128)(2,1)S(1)} %get-tuple-element.48), channel_id=1, source_target_pairs={{0,2},{1,3},{2,0},{3,1},{4,6},{5,7},{6,4},{7,5},{8,10},{9,11},{10,... | collective-permute-start | bytes 835592 | tf_op jit(solution)/shard_map/ppermute | solution.py:152
  19.9 0.3 collective-permute-done.5.refs_5_.refs_2_
  20.2 1.1 %shard_map.103 = (bf16[1,272,256]{2,1,0:T(8,128)(2,1)S(1)}, bf16[1,272,256]{2,1,0:T(8,128)(2,1)S(1)}) custom-call(s32[19]{0:T(128)S(1)} %pad_add_fusion.sp_ref, bf16[256,2048]{1,0:T(8,128)(2,1)S(1)} %copy-done.4, bf16[16,512]{1,0:T(8,128)(2,1)S(1)} %broadcast_multiply_fusion.refs_1_, bf16[2,272,256]{2,1,0:T(8,128)(2,1)S(1)} %collective-permute-done.4.refs_2_, ...), custom_call_target="tpu_custom_call" | custom-call | flops 10000000 | bytes 1048576 | tf_op jit(solution)/shard_map/pallas_call | solution.py:55
  21.4 1.3 %collective-permute-start.18 = (bf16[1,272,256]{2,1,0:T(8,128)(2,1)S(1)}, bf16[1,272,256]{2,1,0:T(8,128)(2,1)S(1)}, u32[]{:S(2)}, u32[]{:S(2)}) collective-permute-start(bf16[1,272,256]{2,1,0:T(8,128)(2,1)S(1)} %get-tuple-element.59), channel_id=1, source_target_pairs={{0,1},{1,0},{2,3},{3,2},{4,5},{5,4},{6,7},{7,6},{8,9},{9,8},{10,11... | collective-permute-start | bytes 417800 | tf_op jit(solution)/shard_map/ppermute | solution.py:152
  22.6 1.6 %shard_map.100 = (bf16[2,272,256]{2,1,0:T(8,128)(2,1)S(1)}, bf16[2,272,256]{2,1,0:T(8,128)(2,1)S(1)}) custom-call(s32[19]{0:T(128)S(1)} %pad_add_fusion.sp_ref, bf16[256,2048]{1,0:T(8,128)(2,1)S(1)} %copy-done.4, bf16[16,512]{1,0:T(8,128)(2,1)S(1)} %broadcast_multiply_fusion.refs_1_, bf16[512,2048]{1,0:T(8,128)(2,1)S(1)} %copy-done.1, ...), custom_call_target="tpu_custom_call" | custom-call | flops 10000000 | bytes 1048576 | tf_op jit(solution)/shard_map/pallas_call | solution.py:55
  24.2 0.0 collective-permute-done.19.refs_2_
  24.2 1.7 %collective-permute-start.1 = (bf16[2,272,256]{2,1,0:T(8,128)(2,1)S(1)}, bf16[2,272,256]{2,1,0:T(8,128)(2,1)S(1)}, u32[]{:S(2)}, u32[]{:S(2)}) collective-permute-start(bf16[2,272,256]{2,1,0:T(8,128)(2,1)S(1)} %get-tuple-element.39), channel_id=1, source_target_pairs={{0,1},{1,0},{2,3},{3,2},{4,5},{5,4},{6,7},{7,6},{8,9},{9,8},{10,11... | collective-permute-start | bytes 835592 | tf_op jit(solution)/shard_map/ppermute | solution.py:152
  25.9 0.3 collective-permute-done.20.refs_4_.refs_6_
  26.2 0.9 shard_map.113
  27.1 1.6 %collective-permute-start.21 = (bf16[1,272,256]{2,1,0:T(8,128)(2,1)S(1)}, bf16[1,272,256]{2,1,0:T(8,128)(2,1)S(1)}, u32[]{:S(2)}, u32[]{:S(2)}) collective-permute-start(bf16[1,272,256]{2,1,0:T(8,128)(2,1)S(1)} %get-tuple-element.64), channel_id=1, source_target_pairs={{0,2},{1,3},{2,0},{3,1},{4,6},{5,7},{6,4},{7,5},{8,10},{9,11},{10,... | collective-permute-start | bytes 417800 | tf_op jit(solution)/shard_map/ppermute | solution.py:152
  28.7 0.9 collective-permute-done.7.refs_2_
  29.5 2.3 %collective-permute-start.22 = (bf16[1,272,256]{2,1,0:T(8,128)(2,1)S(1)}, bf16[1,272,256]{2,1,0:T(8,128)(2,1)S(1)}, u32[]{:S(2)}, u32[]{:S(2)}) collective-permute-start(bf16[1,272,256]{2,1,0:T(8,128)(2,1)S(1)} %get-tuple-element.65), channel_id=1, source_target_pairs={{0,1},{1,0},{2,3},{3,2},{4,5},{5,4},{6,7},{7,6},{8,9},{9,8},{10,11... | collective-permute-start | bytes 417800 | tf_op jit(solution)/shard_map/ppermute | solution.py:152
  31.8 0.3 collective-permute-done.8.refs_4_.refs_6_
  32.2 0.9 shard_map.106
  33.1 1.6 %collective-permute-start.9 = (bf16[1,272,256]{2,1,0:T(8,128)(2,1)S(1)}, bf16[1,272,256]{2,1,0:T(8,128)(2,1)S(1)}, u32[]{:S(2)}, u32[]{:S(2)}) collective-permute-start(bf16[1,272,256]{2,1,0:T(8,128)(2,1)S(1)} %get-tuple-element.49), channel_id=1, source_target_pairs={{0,2},{1,3},{2,0},{3,1},{4,6},{5,7},{6,4},{7,5},{8,10},{9,11},{10,... | collective-permute-start | bytes 417800 | tf_op jit(solution)/shard_map/ppermute | solution.py:152
  34.6 0.5 collective-permute-start.6
  35.2 6.4 %shard_map.111 = (f32[2,256,128]{2,1,0:T(8,128)S(1)}, f32[2,128,256]{2,1,0:T(8,128)S(1)}, f32[4,3,128,128]{3,2,1,0:T(8,128)S(1)}, f32[4,256,128]{2,1,0:T(8,128)S(1)}, f32[4,128,128]{2,1,0:T(8,128)S(1)}) custom-call(s32[19]{0:T(128)S(1)} %pad_add_fusion.sp_ref, bf16[256,2048]{1,0:T(8,128)(2,1)S(1)} %copy-done.4, ...), custom_call_target="tpu_custom_call" | custom-call | flops 4000000000 | bytes 1048576 | tf_op jit(solution)/shard_map/pallas_call | solution.py:55
  41.5 0.0 collective-permute-done.21.refs_3_
  41.6 1.6 %collective-permute-start.2 = (bf16[2,272,256]{2,1,0:T(8,128)(2,1)S(1)}, bf16[2,272,256]{2,1,0:T(8,128)(2,1)S(1)}, u32[]{:S(2)}, u32[]{:S(2)}) collective-permute-start(bf16[2,272,256]{2,1,0:T(8,128)(2,1)S(1)} %get-tuple-element.40), channel_id=1, source_target_pairs={{0,2},{1,3},{2,0},{3,1},{4,6},{5,7},{6,4},{7,5},{8,10},{9,11},{10,... | collective-permute-start | bytes 835592 | tf_op jit(solution)/shard_map/ppermute | solution.py:152
  43.1 0.0 collective-permute-done.22.refs_7_
  43.1 0.6 collective-permute-start.10
  43.8 2.8 %shard_map.114 = (f32[4,256,128]{2,1,0:T(8,128)S(1)}, f32[4,128,128]{2,1,0:T(8,128)S(1)}) custom-call(s32[19]{0:T(128)S(1)} %pad_add_fusion.sp_ref, bf16[256,2048]{1,0:T(8,128)(2,1)S(1)} %copy-done.4, bf16[16,512]{1,0:T(8,128)(2,1)S(1)} %broadcast_multiply_fusion.refs_1_, bf16[2,272,256]{2,1,0:T(8,128)(2,1)S(1)} %collective-permute-done.19.refs_2_, ...), custom_call_target="tpu_custom_call" | custom-call | flops 1000000000 | bytes 1048576 | tf_op jit(solution)/shard_map/pallas_call | solution.py:55
  46.6 0.6 collective-permute-start.24
  47.2 0.1 collective-permute-start.23
  47.3 6.6 %shard_map.104 = (f32[2,256,128]{2,1,0:T(8,128)S(1)}, f32[2,128,256]{2,1,0:T(8,128)S(1)}, f32[4,3,128,128]{3,2,1,0:T(8,128)S(1)}, f32[4,256,128]{2,1,0:T(8,128)S(1)}, f32[4,128,128]{2,1,0:T(8,128)S(1)}) custom-call(s32[19]{0:T(128)S(1)} %pad_add_fusion.sp_ref, bf16[256,2048]{1,0:T(8,128)(2,1)S(1)} %copy-done.4, ...), custom_call_target="tpu_custom_call" | custom-call | flops 4000000000 | bytes 1048576 | tf_op jit(solution)/shard_map/pallas_call | solution.py:55
  53.9 0.0 collective-permute-done.10.refs_7_
  53.9 2.8 %shard_map.107 = (f32[4,256,128]{2,1,0:T(8,128)S(1)}, f32[4,128,128]{2,1,0:T(8,128)S(1)}) custom-call(s32[19]{0:T(128)S(1)} %pad_add_fusion.sp_ref, bf16[256,2048]{1,0:T(8,128)(2,1)S(1)} %copy-done.4, bf16[16,512]{1,0:T(8,128)(2,1)S(1)} %broadcast_multiply_fusion.refs_1_, bf16[2,272,256]{2,1,0:T(8,128)(2,1)S(1)} %collective-permute-done.7.refs_2_, ...), custom_call_target="tpu_custom_call" | custom-call | flops 1000000000 | bytes 1048576 | tf_op jit(solution)/shard_map/pallas_call | solution.py:55
  56.7 0.5 collective-permute-start.12
  57.2 0.1 collective-permute-start.11
  57.2 1.1 %shard_map.101 = (bf16[1,272,256]{2,1,0:T(8,128)(2,1)S(1)}, bf16[1,272,256]{2,1,0:T(8,128)(2,1)S(1)}) custom-call(s32[19]{0:T(128)S(1)} %pad_add_fusion.sp_ref, bf16[256,2048]{1,0:T(8,128)(2,1)S(1)} %copy-done.4, bf16[16,512]{1,0:T(8,128)(2,1)S(1)} %broadcast_multiply_fusion.refs_1_, bf16[2,272,256]{2,1,0:T(8,128)(2,1)S(1)} %collective-permute-done.1.refs_2_, ...), custom_call_target="tpu_custom_call" | custom-call | flops 10000000 | bytes 1048576 | tf_op jit(solution)/shard_map/pallas_call | solution.py:55
  58.4 0.0 copy-start.5
  58.4 1.3 %collective-permute-start.17 = (bf16[1,272,256]{2,1,0:T(8,128)(2,1)S(1)}, bf16[1,272,256]{2,1,0:T(8,128)(2,1)S(1)}, u32[]{:S(2)}, u32[]{:S(2)}) collective-permute-start(bf16[1,272,256]{2,1,0:T(8,128)(2,1)S(1)} %get-tuple-element.58), channel_id=1, source_target_pairs={{0,1},{1,0},{2,3},{3,2},{4,5},{5,4},{6,7},{7,6},{8,9},{9,8},{10,11... | collective-permute-start | bytes 417800 | tf_op jit(solution)/shard_map/ppermute | solution.py:152
  59.7 0.0 collective-permute-done.24.other_b_ref.refs_11_
  59.7 0.8 shard_map.116
  60.6 6.0 %collective-permute-start.27 = (bf16[2,2,128,128]{3,2,1,0:T(8,128)(2,1)S(1)}, bf16[2,2,128,128]{3,2,1,0:T(8,128)(2,1)S(1)}, u32[]{:S(2)}, u32[]{:S(2)}) collective-permute-start(bf16[2,2,128,128]{3,2,1,0:T(8,128)(2,1)S(1)} %shard_map.116), channel_id=1, source_target_pairs={{0,8},{4,12},{8,16},{12,20},{16,24},{20,28},{1,9},{5,13},{9,17},{1... | collective-permute-start | bytes 393224 | tf_op jit(solution)/shard_map/ppermute | solution.py:444
  66.6 4.5 %collective-permute-start.26 = (bf16[2,2,128,128]{3,2,1,0:T(8,128)(2,1)S(1)}, bf16[2,2,128,128]{3,2,1,0:T(8,128)(2,1)S(1)}, u32[]{:S(2)}, u32[]{:S(2)}) collective-permute-start(bf16[2,2,128,128]{3,2,1,0:T(8,128)(2,1)S(1)} %shard_map.116), channel_id=1, source_target_pairs={{0,16},{4,20},{8,24},{12,28},{1,17},{5,21},{9,25},{13,29},{2,18},{... | collective-permute-start | bytes 393224 | tf_op jit(solution)/shard_map/ppermute | solution.py:444
  71.1 0.5 collective-permute-start.3
  71.7 1.3 %collective-permute-start.25 = (bf16[2,2,128,128]{3,2,1,0:T(8,128)(2,1)S(1)}, bf16[2,2,128,128]{3,2,1,0:T(8,128)(2,1)S(1)}, u32[]{:S(2)}, u32[]{:S(2)}) collective-permute-start(bf16[2,2,128,128]{3,2,1,0:T(8,128)(2,1)S(1)} %shard_map.116), channel_id=1, source_target_pairs={{0,24},{4,28},{1,25},{5,29},{2,26},{6,30},{3,27},{7,31}} | collective-permute-start | bytes 393224 | tf_op jit(solution)/shard_map/ppermute | solution.py:444
  73.0 0.8 shard_map.109
  73.8 1.3 %collective-permute-start.15 = (bf16[2,2,128,128]{3,2,1,0:T(8,128)(2,1)S(1)}, bf16[2,2,128,128]{3,2,1,0:T(8,128)(2,1)S(1)}, u32[]{:S(2)}, u32[]{:S(2)}) collective-permute-start(bf16[2,2,128,128]{3,2,1,0:T(8,128)(2,1)S(1)} %shard_map.109), channel_id=1, source_target_pairs={{0,8},{4,12},{8,16},{12,20},{16,24},{20,28},{1,9},{5,13},{9,17},{1... | collective-permute-start | bytes 393224 | tf_op jit(solution)/shard_map/ppermute | solution.py:444
  75.1 1.3 %collective-permute-start.14 = (bf16[2,2,128,128]{3,2,1,0:T(8,128)(2,1)S(1)}, bf16[2,2,128,128]{3,2,1,0:T(8,128)(2,1)S(1)}, u32[]{:S(2)}, u32[]{:S(2)}) collective-permute-start(bf16[2,2,128,128]{3,2,1,0:T(8,128)(2,1)S(1)} %shard_map.109), channel_id=1, source_target_pairs={{0,16},{4,20},{8,24},{12,28},{1,17},{5,21},{9,25},{13,29},{2,18},{... | collective-permute-start | bytes 393224 | tf_op jit(solution)/shard_map/ppermute | solution.py:444
  76.4 9.2 %collective-permute-start.13 = (bf16[2,2,128,128]{3,2,1,0:T(8,128)(2,1)S(1)}, bf16[2,2,128,128]{3,2,1,0:T(8,128)(2,1)S(1)}, u32[]{:S(2)}, u32[]{:S(2)}) collective-permute-start(bf16[2,2,128,128]{3,2,1,0:T(8,128)(2,1)S(1)} %shard_map.109), channel_id=1, source_target_pairs={{0,24},{4,28},{1,25},{5,29},{2,26},{6,30},{3,27},{7,31}} | collective-permute-start | bytes 393224 | tf_op jit(solution)/shard_map/ppermute | solution.py:444
  85.7 3.2 %shard_map.115 = (f32[4,256,128]{2,1,0:T(8,128)S(1)}, f32[4,256,128]{2,1,0:T(8,128)S(1)}) custom-call(s32[19]{0:T(128)S(1)} %pad_add_fusion.sp_ref, bf16[256,2048]{1,0:T(8,128)(2,1)S(1)} %copy-done.5, bf16[16,512]{1,0:T(8,128)(2,1)S(1)} %broadcast_multiply_fusion.refs_1_, bf16[2,272,256]{2,1,0:T(8,128)(2,1)S(1)} %collective-permute-done.2.refs_5_.refs_2_, ...), custom_call_target="tpu_custom_call" | custom-call | flops 1000000000 | bytes 1048576 | tf_op jit(solution)/shard_map/pallas_call | solution.py:55
  88.9 0.9 shard_map.117.refs_8_
  89.8 0.1 collective-permute-start.28
  89.9 0.9 shard_map.110.refs_2_
  90.8 0.5 collective-permute-start.16
  91.4 3.2 %shard_map.108 = (f32[4,256,128]{2,1,0:T(8,128)S(1)}, f32[4,256,128]{2,1,0:T(8,128)S(1)}) custom-call(s32[19]{0:T(128)S(1)} %pad_add_fusion.sp_ref, bf16[256,2048]{1,0:T(8,128)(2,1)S(1)} %copy-done.5, bf16[16,512]{1,0:T(8,128)(2,1)S(1)} %broadcast_multiply_fusion.refs_1_, bf16[2,272,256]{2,1,0:T(8,128)(2,1)S(1)} %collective-permute-done.1.refs_2_, ...), custom_call_target="tpu_custom_call" | custom-call | flops 1000000000 | bytes 1048576 | tf_op jit(solution)/shard_map/pallas_call | solution.py:55
  94.6 2.8 %shard_map.118 = bf16[256,1024]{1,0:T(8,128)(2,1)} custom-call(s32[19]{0:T(128)S(1)} %pad_add_fusion.sp_ref, f32[1,128]{1,0:T(1,128)S(1)} %bitcast.4, f32[4,256,128]{2,1,0:T(8,128)S(1)} %get-tuple-element.54.refs_0_, f32[4,256,128]{2,1,0:T(8,128)S(1)} %get-tuple-element.55.refs_1_, bf16[2,128,128]{2,1,0:T(8,128)(2,1)S(1)} %shard_map.110.refs_2_, ...), custom_call_target="tpu_custom_call" | custom-call | flops 100000000 | bytes 1048576 | tf_op jit(solution)/shard_map/pallas_call | solution.py:55
  (36 shorter events, 0.1 us)
Async XLA Ops:
  0.7 3.7 %collective-permute-start = (bf16[16,512]{1,0:T(8,128)(2,1)S(1)}, bf16[16,512]{1,0:T(8,128)(2,1)S(1)}, u32[]{:S(2)}, u32[]{:S(2)}) collective-permute-start(bf16[16,512]{1,0:T(8,128)(2,1)S(1)} %constant_dynamic-slice_fusion), channel_id=1, source_target_pairs={{0,4},{4,8},{8,12},{12,16},{16,20},{20,24},{24,28},{1,5},{5,9},{9,... | collective-permute-start | bytes 49160 | tf_op jit(solution)/shard_map/ppermute | solution.py:444
  4.5 1.6 %copy-start.2 = (bf16[512,2048]{1,0:T(8,128)(2,1)S(1)}, bf16[512,2048]{1,0:T(8,128)(2,1)}, u32[]{:S(2)}) copy-start(bf16[512,2048]{1,0:T(8,128)(2,1)} %refs_6_.14) | copy-start | bytes 6291460
  6.1 1.2 %copy-start.4 = (bf16[256,2048]{1,0:T(8,128)(2,1)S(1)}, bf16[256,2048]{1,0:T(8,128)(2,1)}, u32[]{:S(2)}) copy-start(bf16[256,2048]{1,0:T(8,128)(2,1)} %refs_0_.27) | copy-start | bytes 3145732
  7.3 5.5 %copy-start = (bf16[512,4096]{1,0:T(8,128)(2,1)S(1)}, bf16[512,4096]{1,0:T(8,128)(2,1)}, u32[]{:S(2)}) copy-start(bf16[512,4096]{1,0:T(8,128)(2,1)} %refs_8_.14) | copy-start | bytes 12582916
  8.9 8.8 %collective-permute-start.4 = (bf16[2,272,256]{2,1,0:T(8,128)(2,1)S(1)}, bf16[2,272,256]{2,1,0:T(8,128)(2,1)S(1)}, u32[]{:S(2)}, u32[]{:S(2)}) collective-permute-start(bf16[2,272,256]{2,1,0:T(8,128)(2,1)S(1)} %get-tuple-element.42), channel_id=1, source_target_pairs={{0,1},{1,0},{2,3},{3,2},{4,5},{5,4},{6,7},{7,6},{8,9},{9,8},{10,11... | collective-permute-start | bytes 835592 | tf_op jit(solution)/shard_map/ppermute | solution.py:152
  11.2 9.0 %collective-permute-start.5 = (bf16[2,272,256]{2,1,0:T(8,128)(2,1)S(1)}, bf16[2,272,256]{2,1,0:T(8,128)(2,1)S(1)}, u32[]{:S(2)}, u32[]{:S(2)}) collective-permute-start(bf16[2,272,256]{2,1,0:T(8,128)(2,1)S(1)} %get-tuple-element.43), channel_id=1, source_target_pairs={{0,2},{1,3},{2,0},{3,1},{4,6},{5,7},{6,4},{7,5},{8,10},{9,11},{10,... | collective-permute-start | bytes 835592 | tf_op jit(solution)/shard_map/ppermute | solution.py:152
  13.9 10.3 %collective-permute-start.19 = (bf16[2,272,256]{2,1,0:T(8,128)(2,1)S(1)}, bf16[2,272,256]{2,1,0:T(8,128)(2,1)S(1)}, u32[]{:S(2)}, u32[]{:S(2)}) collective-permute-start(bf16[2,272,256]{2,1,0:T(8,128)(2,1)S(1)} %get-tuple-element.62), channel_id=1, source_target_pairs={{0,1},{1,0},{2,3},{3,2},{4,5},{5,4},{6,7},{7,6},{8,9},{9,8},{10,11... | collective-permute-start | bytes 835592 | tf_op jit(solution)/shard_map/ppermute | solution.py:152
  14.5 11.7 %collective-permute-start.20 = (bf16[2,272,256]{2,1,0:T(8,128)(2,1)S(1)}, bf16[2,272,256]{2,1,0:T(8,128)(2,1)S(1)}, u32[]{:S(2)}, u32[]{:S(2)}) collective-permute-start(bf16[2,272,256]{2,1,0:T(8,128)(2,1)S(1)} %get-tuple-element.63), channel_id=1, source_target_pairs={{0,2},{1,3},{2,0},{3,1},{4,6},{5,7},{6,4},{7,5},{8,10},{9,11},{10,... | collective-permute-start | bytes 835592 | tf_op jit(solution)/shard_map/ppermute | solution.py:152
  15.7 13.8 %collective-permute-start.7 = (bf16[2,272,256]{2,1,0:T(8,128)(2,1)S(1)}, bf16[2,272,256]{2,1,0:T(8,128)(2,1)S(1)}, u32[]{:S(2)}, u32[]{:S(2)}) collective-permute-start(bf16[2,272,256]{2,1,0:T(8,128)(2,1)S(1)} %get-tuple-element.47), channel_id=1, source_target_pairs={{0,1},{1,0},{2,3},{3,2},{4,5},{5,4},{6,7},{7,6},{8,9},{9,8},{10,11... | collective-permute-start | bytes 835592 | tf_op jit(solution)/shard_map/ppermute | solution.py:152
  17.7 4.9 %copy-start.1 = (bf16[512,2048]{1,0:T(8,128)(2,1)S(1)}, bf16[512,2048]{1,0:T(8,128)(2,1)}, u32[]{:S(2)}) copy-start(bf16[512,2048]{1,0:T(8,128)(2,1)} %refs_6_.15) | copy-start | bytes 6291460
  17.7 14.4 %collective-permute-start.8 = (bf16[2,272,256]{2,1,0:T(8,128)(2,1)S(1)}, bf16[2,272,256]{2,1,0:T(8,128)(2,1)S(1)}, u32[]{:S(2)}, u32[]{:S(2)}) collective-permute-start(bf16[2,272,256]{2,1,0:T(8,128)(2,1)S(1)} %get-tuple-element.48), channel_id=1, source_target_pairs={{0,2},{1,3},{2,0},{3,1},{4,6},{5,7},{6,4},{7,5},{8,10},{9,11},{10,... | collective-permute-start | bytes 835592 | tf_op jit(solution)/shard_map/ppermute | solution.py:152
  21.4 13.3 %collective-permute-start.18 = (bf16[1,272,256]{2,1,0:T(8,128)(2,1)S(1)}, bf16[1,272,256]{2,1,0:T(8,128)(2,1)S(1)}, u32[]{:S(2)}, u32[]{:S(2)}) collective-permute-start(bf16[1,272,256]{2,1,0:T(8,128)(2,1)S(1)} %get-tuple-element.59), channel_id=1, source_target_pairs={{0,1},{1,0},{2,3},{3,2},{4,5},{5,4},{6,7},{7,6},{8,9},{9,8},{10,11... | collective-permute-start | bytes 417800 | tf_op jit(solution)/shard_map/ppermute | solution.py:152
  24.2 33.0 %collective-permute-start.1 = (bf16[2,272,256]{2,1,0:T(8,128)(2,1)S(1)}, bf16[2,272,256]{2,1,0:T(8,128)(2,1)S(1)}, u32[]{:S(2)}, u32[]{:S(2)}) collective-permute-start(bf16[2,272,256]{2,1,0:T(8,128)(2,1)S(1)} %get-tuple-element.39), channel_id=1, source_target_pairs={{0,1},{1,0},{2,3},{3,2},{4,5},{5,4},{6,7},{7,6},{8,9},{9,8},{10,11... | collective-permute-start | bytes 835592 | tf_op jit(solution)/shard_map/ppermute | solution.py:152
  27.1 14.4 %collective-permute-start.21 = (bf16[1,272,256]{2,1,0:T(8,128)(2,1)S(1)}, bf16[1,272,256]{2,1,0:T(8,128)(2,1)S(1)}, u32[]{:S(2)}, u32[]{:S(2)}) collective-permute-start(bf16[1,272,256]{2,1,0:T(8,128)(2,1)S(1)} %get-tuple-element.64), channel_id=1, source_target_pairs={{0,2},{1,3},{2,0},{3,1},{4,6},{5,7},{6,4},{7,5},{8,10},{9,11},{10,... | collective-permute-start | bytes 417800 | tf_op jit(solution)/shard_map/ppermute | solution.py:152
  29.5 5.6 %copy-start.6 = (bf16[4,8192]{1,0:T(4,128)(2,1)S(1)}, bf16[4,8192]{1,0:T(4,128)(2,1)}, u32[]{:S(2)}) copy-start(bf16[4,8192]{1,0:T(4,128)(2,1)} %refs_7_.15) | copy-start | bytes 196612
  29.5 5.6 %copy-start.7 = (f32[8,256]{1,0:T(8,128)S(1)}, f32[8,256]{1,0:T(8,128)}, u32[]{:S(2)}) copy-start(f32[8,256]{1,0:T(8,128)} %refs_8_.15) | copy-start | bytes 24580
  29.5 5.6 %copy-start.8 = (f32[8,256]{1,0:T(8,128)S(1)}, f32[8,256]{1,0:T(8,128)}, u32[]{:S(2)}) copy-start(f32[8,256]{1,0:T(8,128)} %refs_11_.3) | copy-start | bytes 24580
  29.5 13.6 %collective-permute-start.22 = (bf16[1,272,256]{2,1,0:T(8,128)(2,1)S(1)}, bf16[1,272,256]{2,1,0:T(8,128)(2,1)S(1)}, u32[]{:S(2)}, u32[]{:S(2)}) collective-permute-start(bf16[1,272,256]{2,1,0:T(8,128)(2,1)S(1)} %get-tuple-element.65), channel_id=1, source_target_pairs={{0,1},{1,0},{2,3},{3,2},{4,5},{5,4},{6,7},{7,6},{8,9},{9,8},{10,11... | collective-permute-start | bytes 417800 | tf_op jit(solution)/shard_map/ppermute | solution.py:152
  33.1 13.5 %collective-permute-start.9 = (bf16[1,272,256]{2,1,0:T(8,128)(2,1)S(1)}, bf16[1,272,256]{2,1,0:T(8,128)(2,1)S(1)}, u32[]{:S(2)}, u32[]{:S(2)}) collective-permute-start(bf16[1,272,256]{2,1,0:T(8,128)(2,1)S(1)} %get-tuple-element.49), channel_id=1, source_target_pairs={{0,2},{1,3},{2,0},{3,1},{4,6},{5,7},{6,4},{7,5},{8,10},{9,11},{10,... | collective-permute-start | bytes 417800 | tf_op jit(solution)/shard_map/ppermute | solution.py:152
  34.6 12.6 %collective-permute-start.6 = (bf16[1,272,256]{2,1,0:T(8,128)(2,1)S(1)}, bf16[1,272,256]{2,1,0:T(8,128)(2,1)S(1)}, u32[]{:S(2)}, u32[]{:S(2)}) collective-permute-start(bf16[1,272,256]{2,1,0:T(8,128)(2,1)S(1)} %get-tuple-element.44), channel_id=1, source_target_pairs={{0,2},{1,3},{2,0},{3,1},{4,6},{5,7},{6,4},{7,5},{8,10},{9,11},{10,... | collective-permute-start | bytes 417800 | tf_op jit(solution)/shard_map/ppermute | solution.py:152
  41.6 15.7 %collective-permute-start.2 = (bf16[2,272,256]{2,1,0:T(8,128)(2,1)S(1)}, bf16[2,272,256]{2,1,0:T(8,128)(2,1)S(1)}, u32[]{:S(2)}, u32[]{:S(2)}) collective-permute-start(bf16[2,272,256]{2,1,0:T(8,128)(2,1)S(1)} %get-tuple-element.40), channel_id=1, source_target_pairs={{0,2},{1,3},{2,0},{3,1},{4,6},{5,7},{6,4},{7,5},{8,10},{9,11},{10,... | collective-permute-start | bytes 835592 | tf_op jit(solution)/shard_map/ppermute | solution.py:152
  43.1 10.7 %collective-permute-start.10 = (bf16[1,272,256]{2,1,0:T(8,128)(2,1)S(1)}, bf16[1,272,256]{2,1,0:T(8,128)(2,1)S(1)}, u32[]{:S(2)}, u32[]{:S(2)}) collective-permute-start(bf16[1,272,256]{2,1,0:T(8,128)(2,1)S(1)} %get-tuple-element.50), channel_id=1, source_target_pairs={{0,1},{1,0},{2,3},{3,2},{4,5},{5,4},{6,7},{7,6},{8,9},{9,8},{10,11... | collective-permute-start | bytes 417800 | tf_op jit(solution)/shard_map/ppermute | solution.py:152
  43.8 3.5 %copy-start.3 = (bf16[512,2048]{1,0:T(8,128)(2,1)S(1)}, bf16[512,2048]{1,0:T(8,128)(2,1)}, u32[]{:S(2)}) copy-start(bf16[512,2048]{1,0:T(8,128)(2,1)} %refs_6_.14) | copy-start | bytes 6291460
  46.6 13.2 %collective-permute-start.24 = (f32[4,128,128]{2,1,0:T(8,128)S(1)}, f32[4,128,128]{2,1,0:T(8,128)S(1)}, u32[]{:S(2)}, u32[]{:S(2)}) collective-permute-start(f32[4,128,128]{2,1,0:T(8,128)S(1)} %get-tuple-element.72.mine_b_ref), channel_id=1, source_target_pairs={{0,4},{4,0},{8,12},{12,8},{16,20},{20,16},{24,28},{28,24},{1,5},{5... | collective-permute-start | bytes 786440 | tf_op jit(solution)/shard_map/ppermute | solution.py:449
  47.2 12.5 %collective-permute-start.23 = (f32[4,128,128]{2,1,0:T(8,128)S(1)}, f32[4,128,128]{2,1,0:T(8,128)S(1)}, u32[]{:S(2)}, u32[]{:S(2)}) collective-permute-start(f32[4,128,128]{2,1,0:T(8,128)S(1)} %get-tuple-element.71.mine_a_ref), channel_id=1, source_target_pairs={{0,4},{4,0},{8,12},{12,8},{16,20},{20,16},{24,28},{28,24},{1,5},{5... | collective-permute-start | bytes 786440 | tf_op jit(solution)/shard_map/ppermute | solution.py:449
  56.7 14.5 %collective-permute-start.12 = (f32[4,128,128]{2,1,0:T(8,128)S(1)}, f32[4,128,128]{2,1,0:T(8,128)S(1)}, u32[]{:S(2)}, u32[]{:S(2)}) collective-permute-start(f32[4,128,128]{2,1,0:T(8,128)S(1)} %get-tuple-element.57.mine_b_ref), channel_id=1, source_target_pairs={{0,4},{4,0},{8,12},{12,8},{16,20},{20,16},{24,28},{28,24},{1,5},{5... | collective-permute-start | bytes 786440 | tf_op jit(solution)/shard_map/ppermute | solution.py:449
  57.2 14.5 %collective-permute-start.11 = (f32[4,128,128]{2,1,0:T(8,128)S(1)}, f32[4,128,128]{2,1,0:T(8,128)S(1)}, u32[]{:S(2)}, u32[]{:S(2)}) collective-permute-start(f32[4,128,128]{2,1,0:T(8,128)S(1)} %get-tuple-element.56.mine_a_ref), channel_id=1, source_target_pairs={{0,4},{4,0},{8,12},{12,8},{16,20},{20,16},{24,28},{28,24},{1,5},{5... | collective-permute-start | bytes 786440 | tf_op jit(solution)/shard_map/ppermute | solution.py:449
  58.4 27.3 %copy-start.5 = (bf16[256,2048]{1,0:T(8,128)(2,1)S(1)}, bf16[256,2048]{1,0:T(8,128)(2,1)}, u32[]{:S(2)}) copy-start(bf16[256,2048]{1,0:T(8,128)(2,1)} %refs_0_.27) | copy-start | bytes 3145732
  58.4 15.4 %collective-permute-start.17 = (bf16[1,272,256]{2,1,0:T(8,128)(2,1)S(1)}, bf16[1,272,256]{2,1,0:T(8,128)(2,1)S(1)}, u32[]{:S(2)}, u32[]{:S(2)}) collective-permute-start(bf16[1,272,256]{2,1,0:T(8,128)(2,1)S(1)} %get-tuple-element.58), channel_id=1, source_target_pairs={{0,1},{1,0},{2,3},{3,2},{4,5},{5,4},{6,7},{7,6},{8,9},{9,8},{10,11... | collective-permute-start | bytes 417800 | tf_op jit(solution)/shard_map/ppermute | solution.py:152
  60.6 14.6 %collective-permute-start.27 = (bf16[2,2,128,128]{3,2,1,0:T(8,128)(2,1)S(1)}, bf16[2,2,128,128]{3,2,1,0:T(8,128)(2,1)S(1)}, u32[]{:S(2)}, u32[]{:S(2)}) collective-permute-start(bf16[2,2,128,128]{3,2,1,0:T(8,128)(2,1)S(1)} %shard_map.116), channel_id=1, source_target_pairs={{0,8},{4,12},{8,16},{12,20},{16,24},{20,28},{1,9},{5,13},{9,17},{1... | collective-permute-start | bytes 393224 | tf_op jit(solution)/shard_map/ppermute | solution.py:444
  66.6 9.9 %collective-permute-start.26 = (bf16[2,2,128,128]{3,2,1,0:T(8,128)(2,1)S(1)}, bf16[2,2,128,128]{3,2,1,0:T(8,128)(2,1)S(1)}, u32[]{:S(2)}, u32[]{:S(2)}) collective-permute-start(bf16[2,2,128,128]{3,2,1,0:T(8,128)(2,1)S(1)} %shard_map.116), channel_id=1, source_target_pairs={{0,16},{4,20},{8,24},{12,28},{1,17},{5,21},{9,25},{13,29},{2,18},{... | collective-permute-start | bytes 393224 | tf_op jit(solution)/shard_map/ppermute | solution.py:444
  71.1 20.2 %collective-permute-start.3 = (bf16[1,272,256]{2,1,0:T(8,128)(2,1)S(1)}, bf16[1,272,256]{2,1,0:T(8,128)(2,1)S(1)}, u32[]{:S(2)}, u32[]{:S(2)}) collective-permute-start(bf16[1,272,256]{2,1,0:T(8,128)(2,1)S(1)} %get-tuple-element.41), channel_id=1, source_target_pairs={{0,2},{1,3},{2,0},{3,1},{4,6},{5,7},{6,4},{7,5},{8,10},{9,11},{10,... | collective-permute-start | bytes 417800 | tf_op jit(solution)/shard_map/ppermute | solution.py:152
  71.7 17.2 %collective-permute-start.25 = (bf16[2,2,128,128]{3,2,1,0:T(8,128)(2,1)S(1)}, bf16[2,2,128,128]{3,2,1,0:T(8,128)(2,1)S(1)}, u32[]{:S(2)}, u32[]{:S(2)}) collective-permute-start(bf16[2,2,128,128]{3,2,1,0:T(8,128)(2,1)S(1)} %shard_map.116), channel_id=1, source_target_pairs={{0,24},{4,28},{1,25},{5,29},{2,26},{6,30},{3,27},{7,31}} | collective-permute-start | bytes 393224 | tf_op jit(solution)/shard_map/ppermute | solution.py:444
  73.8 16.1 %collective-permute-start.15 = (bf16[2,2,128,128]{3,2,1,0:T(8,128)(2,1)S(1)}, bf16[2,2,128,128]{3,2,1,0:T(8,128)(2,1)S(1)}, u32[]{:S(2)}, u32[]{:S(2)}) collective-permute-start(bf16[2,2,128,128]{3,2,1,0:T(8,128)(2,1)S(1)} %shard_map.109), channel_id=1, source_target_pairs={{0,8},{4,12},{8,16},{12,20},{16,24},{20,28},{1,9},{5,13},{9,17},{1... | collective-permute-start | bytes 393224 | tf_op jit(solution)/shard_map/ppermute | solution.py:444
  75.1 14.8 %collective-permute-start.14 = (bf16[2,2,128,128]{3,2,1,0:T(8,128)(2,1)S(1)}, bf16[2,2,128,128]{3,2,1,0:T(8,128)(2,1)S(1)}, u32[]{:S(2)}, u32[]{:S(2)}) collective-permute-start(bf16[2,2,128,128]{3,2,1,0:T(8,128)(2,1)S(1)} %shard_map.109), channel_id=1, source_target_pairs={{0,16},{4,20},{8,24},{12,28},{1,17},{5,21},{9,25},{13,29},{2,18},{... | collective-permute-start | bytes 393224 | tf_op jit(solution)/shard_map/ppermute | solution.py:444
  76.4 13.5 %collective-permute-start.13 = (bf16[2,2,128,128]{3,2,1,0:T(8,128)(2,1)S(1)}, bf16[2,2,128,128]{3,2,1,0:T(8,128)(2,1)S(1)}, u32[]{:S(2)}, u32[]{:S(2)}) collective-permute-start(bf16[2,2,128,128]{3,2,1,0:T(8,128)(2,1)S(1)} %shard_map.109), channel_id=1, source_target_pairs={{0,24},{4,28},{1,25},{5,29},{2,26},{6,30},{3,27},{7,31}} | collective-permute-start | bytes 393224 | tf_op jit(solution)/shard_map/ppermute | solution.py:444
  89.8 4.8 %collective-permute-start.28 = (bf16[2,128,128]{2,1,0:T(8,128)(2,1)S(1)}, bf16[2,128,128]{2,1,0:T(8,128)(2,1)S(1)}, u32[]{:S(2)}, u32[]{:S(2)}) collective-permute-start(bf16[2,128,128]{2,1,0:T(8,128)(2,1)S(1)} %shard_map.117.refs_8_), channel_id=1, source_target_pairs={{0,4},{4,0},{8,12},{12,8},{16,20},{20,16},{24,28},{28,24},{1,5},{5... | collective-permute-start | bytes 196616 | tf_op jit(solution)/shard_map/ppermute | solution.py:449
  90.8 3.8 %collective-permute-start.16 = (bf16[2,128,128]{2,1,0:T(8,128)(2,1)S(1)}, bf16[2,128,128]{2,1,0:T(8,128)(2,1)S(1)}, u32[]{:S(2)}, u32[]{:S(2)}) collective-permute-start(bf16[2,128,128]{2,1,0:T(8,128)(2,1)S(1)} %shard_map.110.refs_2_), channel_id=1, source_target_pairs={{0,4},{4,0},{8,12},{12,8},{16,20},{20,16},{24,28},{28,24},{1,5},{5... | collective-permute-start | bytes 196616 | tf_op jit(solution)/shard_map/ppermute | solution.py:449
  91.4 3.2 %copy-start.9 = (f32[128]{0:T(128)S(1)}, f32[128]{0:T(128)}, u32[]{:S(2)}) copy-start(f32[128]{0:T(128)} %param.17) | copy-start | bytes 1540

commit v2 on v1

v2 whole, which is shorter than its diff:
```python
import functools

import jax
import jax.numpy as jnp
from jax import lax
from jax.experimental import pallas as pl
from jax.experimental.pallas import tpu as pltpu
from jax.sharding import PartitionSpec as P

HEAD = 128
TAPS = 4
RIM = 16
EPS = 1e-06
VMEM_BYTES = 40 * 1024 * 1024
F32 = jnp.float32
BF16 = jnp.bfloat16

NN = (((1,), (0,)), ((), ()))
NT = (((1,), (1,)), ((), ()))


def dot1(a, b, dims=NN):
    return lax.dot_general(
        a.astype(BF16), b.astype(BF16), dims, preferred_element_type=F32
    )


def split(a):
    high = a.astype(BF16)
    return high, (a - high.astype(F32)).astype(BF16)


def dot3s(a, b, dims=NN):
    (ah, al), (bh, bl) = a, b
    one = functools.partial(lax.dot_general, dimension_numbers=dims, preferred_element_type=F32)
    return one(ah, bh) + (one(ah, bl) + one(al, bh))


def dot3(a, b, dims=NN):
    return dot3s(split(a), split(b), dims)


def packed_left(parts):
    return jnp.concatenate(parts, axis=1)


def packed_right(parts):
    wide = jnp.concatenate(parts, axis=1)
    return jnp.concatenate([wide, wide], axis=0)


def packed_turned(parts):
    tall = jnp.concatenate(parts, axis=0)
    return jnp.concatenate([tall, tall], axis=1)


def fold(left, right, dims=NN):
    both = lax.dot_general(left, right, dims, preferred_element_type=F32)
    width = both.shape[1] // 2
    return both[:, :width] + both[:, width:]


def mul(a, b):
    return fold(packed_left(split(a)), packed_right(split(b)))


def dot_full(a, b, dims=NN):
    return lax.dot_general(
        a, b, dims, precision=lax.Precision.HIGHEST, preferred_element_type=F32
    )


def whole(array):
    zeros = (0,) * array.ndim
    return pl.BlockSpec(array.shape, lambda i, sp: zeros)


def call(body, sp, inputs, specs, outs, scratch=(), flops=10**7, after=()):
    number = len(inputs)
    specs = list(specs) + [pl.BlockSpec(memory_space=pl.ANY) for _ in after]

    def inner(sp_ref, *refs):
        body(sp_ref, *refs[:number], *refs[number + len(after) :])

    return pl.pallas_call(
        inner,
        grid_spec=pltpu.PrefetchScalarGridSpec(
            num_scalar_prefetch=1,
            grid=(1,),
            in_specs=specs,
            out_specs=[whole(out) for out in outs],
            scratch_shapes=list(scratch),
        ),
        out_shape=[jax.ShapeDtypeStruct(out.shape, out.dtype) for out in outs],
        compiler_params=pltpu.CompilerParams(vmem_limit_bytes=VMEM_BYTES),
        cost_estimate=pl.CostEstimate(flops=flops, bytes_accessed=2**20, transcendentals=0),
    )(sp, *inputs, *after)


class Plan:
    def __init__(self, ranks, key_heads):
        bits = [1 << i for i in range(ranks.bit_length() - 1)]
        self.orders = (bits, bits[::-1])
        self.stages = len(bits)
        self.key_heads = key_heads

    def offsets(self, route, stage):
        out = [0]
        for bit in self.orders[route][stage + 1 :]:
            out = out + [o ^ bit for o in out]
        return out

    def weight_spec(self, rows, width, unit, head):
        heads = self.key_heads
        return pl.BlockSpec(
            (rows, width), lambda i, sp: (0, sp[2 + (sp[0] ^ unit) * heads + head])
        )

    def tap_spec(self, width, base, head):
        heads = self.key_heads
        return pl.BlockSpec(
            (TAPS, width), lambda i, sp: (0, base + sp[2 + sp[0] * heads + head])
        )


def hidden_spec(hidden, rows):
    return pl.BlockSpec((hidden.shape[0], rows), lambda i, sp: (0, sp[0]))


def send_stage(plan, stage, chunk, hidden, rim, weight, received, sp, after=()):
    rows, count = weight.shape[0], hidden.shape[0]
    width = chunk["width"]
    inputs, specs = [hidden], [hidden_spec(hidden, rows)]
    lead = 0
    if rim is not None:
        lead = RIM
        inputs, specs = inputs + [rim], specs + [whole(rim)]
    jobs, outs, places = [], [], {}
    for route, heads in enumerate(chunk["heads"]):
        if not heads:
            continue
        offsets = plan.offsets(route, stage)
        for before in range(stage):
            places[route, before] = len(inputs)
            inputs.append(received[route][before])
            specs.append(whole(received[route][before]))
        for slot, offset in enumerate(offsets):
            unit = offset ^ plan.orders[route][stage]
            sources = [
                (places[route, before], plan.offsets(route, before).index(unit))
                for before in range(stage)
            ]
            for at, head in enumerate(heads):
                jobs.append((len(inputs), sources, len(outs), slot, at))
                inputs.append(weight)
                specs.append(plan.weight_spec(rows, width, unit, head))
        outs.append(
            jax.ShapeDtypeStruct((len(offsets), lead + count, width * len(heads)), BF16)
        )
    total = len(inputs)

    def body(sp_ref, *refs):
        lefts = [(refs[0][...], slice(lead, lead + count))]
        if lead:
            lefts.append((refs[1][...], slice(0, lead)))
        for place, sources, out, slot, at in jobs:
            held = refs[place][...]
            cols = slice(at * width, (at + 1) * width)
            for left, span in lefts:
                part = jnp.dot(left, held, preferred_element_type=F32)
                for source, index in sources:
                    part = part + refs[source][index, span, cols].astype(F32)
                refs[total + out][slot, span, cols] = part.astype(BF16)

    sent = call(body, sp, inputs, specs, outs, after=after)
    result, at = [], 0
    for heads in chunk["heads"]:
        result.append(sent[at] if heads else None)
        at += 1 if heads else 0
    return result


def rim_products(plan, rim, weight, ranks, sp, after=()):
    rows, heads = weight.shape[0], plan.key_heads
    number = ranks * heads
    out = jax.ShapeDtypeStruct((ranks, RIM, heads * HEAD), BF16)
    specs = [whole(rim)] + [
        pl.BlockSpec((rows, HEAD), lambda i, sp, s=s: (0, sp[2 + s])) for s in range(number)
    ]

    def body(sp_ref, rim_ref, *refs):
        for s in range(number):
            cols = slice((s % heads) * HEAD, (s % heads + 1) * HEAD)
            part = jnp.dot(rim_ref[...], refs[s][...], preferred_element_type=F32)
            refs[-1][s // heads, :, cols] = part.astype(BF16)

    return call(body, sp, [rim] + [weight] * number, specs, [out], after=after)[0]


def exchange(plan, stage, sent):
    ranks = lax.axis_size("head")
    return [
        None
        if part is None
        else lax.ppermute(
            part, "head", [(i, i ^ plan.orders[route][stage]) for i in range(ranks)]
        )
        for route, part in enumerate(sent)
    ]


def gather_specs(plan, chunk, heads, hidden, rim, weight, taps, base, received, rim_parts=None):
    rows, width = weight.shape[0], chunk["width"]
    inputs, specs = [hidden], [hidden_spec(hidden, rows)]
    edge = rim if rim_parts is None else rim_parts
    inputs, specs = inputs + [edge], specs + [whole(edge)]
    places, jobs = {}, []
    for head in heads:
        route = [head in group for group in chunk["heads"]].index(True)
        if route not in places:
            places[route] = []
            for part in received[route]:
                places[route].append(len(inputs))
                inputs.append(part)
                specs.append(pl.BlockSpec((1,) + part.shape[1:], lambda i, sp: (0, 0, 0)))
        at = chunk["heads"][route].index(head)
        cols = slice(at * width, (at + 1) * width)
        summed = None if rim_parts is None else slice(head * width, (head + 1) * width)
        jobs.append((len(inputs), places[route], cols, summed))
        inputs += [weight, taps]
        specs += [plan.weight_spec(rows, width, 0, head), plan.tap_spec(width, base, head)]
    return inputs, specs, jobs


def activate(refs, job, scratch):
    place, sources, cols, summed = job
    held, taps = refs[place][...], refs[place + 1][...].astype(F32)
    count = refs[0].shape[0]
    lead = 0 if summed is not None else RIM
    lefts = [(refs[0], slice(RIM, RIM + count), slice(lead, lead + count))]
    if summed is None:
        lefts.append((refs[1], slice(0, RIM), slice(0, RIM)))
    else:
        edge = refs[1][0, :, summed].astype(F32)
        for rank in range(1, refs[1].shape[0]):
            edge = edge + refs[1][rank, :, summed].astype(F32)
        scratch[0:RIM, :] = edge
    for left, span, source_span in lefts:
        part = jnp.dot(left[...], held, preferred_element_type=F32)
        for source in sources:
            part = part + refs[source][0, source_span, cols].astype(F32)
        scratch[span, :] = part
    total = None
    for tap in range(TAPS):
        first = RIM - (TAPS - 1) + tap
        term = taps[tap : tap + 1] * scratch[first : first + count, :]
        total = term if total is None else total + term
    return total / (1.0 + jnp.exp(-total))


def unit_rows(values):
    return values * lax.rsqrt(jnp.sum(values * values, axis=-1, keepdims=True) + EPS)


def iotas(size):
    return (
        lax.broadcasted_iota(jnp.int32, (size, size), 0),
        lax.broadcasted_iota(jnp.int32, (size, size), 1),
    )


def prepare(decay, beta, sp, after=()):
    heads, count = decay.shape
    outs = [
        jax.ShapeDtypeStruct((heads, count), F32),
        jax.ShapeDtypeStruct((count, heads), F32),
        jax.ShapeDtypeStruct((count, heads), F32),
    ]

    def body(sp_ref, decay_ref, beta_ref, row_ref, col_ref, rate_ref):
        rows, cols = iotas(count)
        row_ref[...] = dot_full(decay_ref[...], (rows <= cols).astype(F32))
        col_ref[...] = dot_full((cols <= rows).astype(F32), decay_ref[...], NT)
        rate_ref[...] = dot_full((rows == cols).astype(F32), beta_ref[...], NT)

    return call(body, sp, [decay, beta], [whole(decay), whole(beta)], outs, after=after)


def inverses(systems):
    size = systems[0].shape[0]
    rows, cols = iotas(size)
    eye = (rows == cols).astype(F32)
    near = [jnp.where((rows >> 3) == (cols >> 3), low, 0.0) for low in systems]
    cut = [split(n) for n in near]
    left = [packed_left(c) for c in cut]
    square = [fold(l, packed_right(c)) for l, c in zip(left, cut)]
    cut2 = [split(s) for s in square]
    right2 = [packed_right(c) for c in cut2]
    cube = [fold(l, r) for l, r in zip(left, right2)]
    inv = [eye - n + s - c for n, s, c in zip(near, square, cube)]
    fourth = [packed_right(split(fold(packed_left(c), r))) for c, r in zip(cut2, right2)]
    inv = [x + fold(packed_left(split(x)), f) for x, f in zip(inv, fourth)]
    shift = 3
    while (1 << shift) < size:
        inside = ((rows >> (shift + 1)) == (cols >> (shift + 1))) & (
            (rows >> shift) != (cols >> shift)
        )
        parts = [split(x) for x in inv]
        lower = [packed_left(split(jnp.where(inside, low, 0.0))) for low in systems]
        middle = [fold(low, packed_right(p)) for low, p in zip(lower, parts)]
        middle = [packed_right(split(m)) for m in middle]
        inv = [x - fold(packed_left(p), m) for x, p, m in zip(inv, parts, middle)]
        shift += 1
    return inv


def key_phase(
    plan, chunk, heads, hidden, rim_parts, weight, taps, base, received, tables, sp, after=()
):
    inputs, specs, jobs = gather_specs(
        plan, chunk, heads, hidden, None, weight, taps, base, received, rim_parts
    )
    at = len(inputs)
    inputs += tables
    specs += [whole(table) for table in tables]
    count, number = hidden.shape[0], 2 * len(heads)
    half = count // 2
    first = 2 * heads[0]
    outs = [
        jax.ShapeDtypeStruct((len(heads), count, HEAD), F32),
        jax.ShapeDtypeStruct((len(heads), HEAD, count), F32),
        jax.ShapeDtypeStruct((number, 3, half, half), F32),
        jax.ShapeDtypeStruct((number, count, HEAD), F32),
        jax.ShapeDtypeStruct((number, HEAD, HEAD), F32),
    ]
    total = len(inputs)

    def body(sp_ref, *refs):
        key_ref, turned_ref, solve_ref, write_ref, trans_ref, scratch = refs[total:]
        sums, sums_col, beta_col = (ref[...] for ref in refs[at : at + 3])
        rows, cols = iotas(half)
        keys, systems, crosses = [], [], []
        for i, job in enumerate(jobs):
            key = unit_rows(activate(refs, job, scratch))
            keys.append(key)
            key_ref[i] = key
            turned_ref[i] = key.T
            low, high = split(key[:half]), split(key[half:])
            low_left, high_left = packed_left(low), packed_left(high)
            low_right, high_right = packed_turned(low), packed_turned(high)
            alike = (
                fold(low_left, low_right, NT),
                fold(high_left, high_right, NT),
                fold(high_left, low_right, NT),
            )
            for r in (first + 2 * i, first + 2 * i + 1):
                row, col, rate = sums[r : r + 1], sums_col[:, r : r + 1], beta_col[:, r : r + 1]
                for b, span in enumerate((slice(0, half), slice(half, count))):
                    fade = jnp.exp(jnp.minimum(col[span] - row[:, span], 0.0))
                    systems.append(jnp.where(cols < rows, rate[span] * fade * alike[b], 0.0))
                fade = jnp.exp(jnp.minimum(col[half:] - row[:, :half], 0.0))
                crosses.append(rate[half:] * fade * alike[2])
        solved = inverses(systems)
        left = [packed_left(split(x)) for x in solved]
        middle = [
            mul(cross, solved[2 * j]) for j, cross in enumerate(crosses)
        ]
        corner = [
            -fold(left[2 * j + 1], packed_right(split(m))) for j, m in enumerate(middle)
        ]
        keep = sp_ref[1].astype(F32)
        eye = (lax.broadcasted_iota(jnp.int32, (HEAD, HEAD), 0)
               == lax.broadcasted_iota(jnp.int32, (HEAD, HEAD), 1)).astype(F32)
        for j in range(number):
            r, key = first + j, keys[j // 2]
            row, col, rate = sums[r : r + 1], sums_col[:, r : r + 1], beta_col[:, r : r + 1]
            for place, part in enumerate((solved[2 * j], solved[2 * j + 1], corner[j])):
                solve_ref[j, place] = part
            right = (rate * jnp.exp(col)) * key
            right_low = packed_right(split(right[:half]))
            right_high = packed_right(split(right[half:]))
            write_low = fold(left[2 * j], right_low)
            write_high = fold(packed_left(split(corner[j])), right_low) + fold(
                left[2 * j + 1], right_high
            )
            write_ref[j, :half] = write_low
            write_ref[j, half:] = write_high
            tail = jnp.exp(row[:, count - 1 :] - row)
            trailing = turned_ref[j // 2] * tail
            moved = mul(trailing[:, :half], write_low) + mul(trailing[:, half:], write_high)
            gone = jnp.exp(row[:, count - 1 :])
            trans_ref[j] = keep * (gone * eye - moved)

    return call(
        body, sp, inputs, specs, outs, [pltpu.VMEM((RIM + count, HEAD), F32)],
        flops=4 * 10**9, after=after,
    )


def value_phase(
    plan, chunk, heads, hidden, rim, weight, taps, base, received, tables, parts, sp, after=()
):
    inputs, specs, jobs = gather_specs(
        plan, chunk, heads, hidden, rim, weight, taps, base, received
    )
    at = len(inputs)
    inputs += tables
    for turned, solve in parts:
        inputs += [turned, solve]
    specs += [whole(a) for a in inputs[at:]]
    count, number = hidden.shape[0], 2 * len(heads)
    half = count // 2
    outs = [
        jax.ShapeDtypeStruct((number, count, HEAD), F32),
        jax.ShapeDtypeStruct((number, HEAD, HEAD), BF16),
    ]
    total = len(inputs)
    group = parts[0][0].shape[0]

    def body(sp_ref, *refs):
        write_ref, trans_ref, scratch = refs[total:]
        sums, beta_col = refs[at][...], refs[at + 2][...]
        for i, job in enumerate(jobs):
            values = activate(refs, job, scratch)
            turned_ref, solve_ref = refs[at + 3 + 2 * (i // group) : at + 5 + 2 * (i // group)]
            for j in (2 * i, 2 * i + 1):
                row, rate = sums[j : j + 1], beta_col[:, j : j + 1]
                right = rate * values[:, (j % 2) * HEAD : (j % 2 + 1) * HEAD]
                low = packed_right(split(right[:half]))
                high = packed_right(split(right[half:]))
                top, bottom, side = [
                    packed_left(split(solve_ref[j % (2 * group), place])) for place in range(3)
                ]
                write_low = fold(top, low)
                write_high = fold(side, low) + fold(bottom, high)
                write_ref[j, :half] = write_low
                write_ref[j, half:] = write_high
                trailing = turned_ref[i % group] * jnp.exp(row[:, count - 1 :] - row)
                trans_ref[j] = (
                    mul(trailing[:, :half], write_low) + mul(trailing[:, half:], write_high)
                ).astype(BF16)

    return call(
        body, sp, inputs, specs, outs, [pltpu.VMEM((RIM + count, 2 * HEAD), F32)],
        flops=2 * 10**9, after=after,
    )


def query_phase(
    plan, chunk, heads, hidden, rim, weight, taps, base, received, tables, parts, write_v, sp,
    after=(),
):
    inputs, specs, jobs = gather_specs(
        plan, chunk, heads, hidden, rim, weight, taps, base, received
    )
    at = len(inputs)
    inputs += tables + [write_v]
    for key, write_k in parts:
        inputs += [key, write_k]
    specs += [whole(a) for a in inputs[at:]]
    count, number = hidden.shape[0], 2 * len(heads)
    half = count // 2
    outs = [
        jax.ShapeDtypeStruct((number, count, HEAD), F32),
        jax.ShapeDtypeStruct((number, count, HEAD), F32),
    ]
    total = len(inputs)
    group = parts[0][0].shape[0]

    def body(sp_ref, *refs):
        inner_ref, query_ref, scratch = refs[total:]
        sums, sums_col = refs[at][...], refs[at + 1][...]
        write_v_ref = refs[at + 3]
        rows, cols = iotas(half)
        low, high = slice(0, half), slice(half, count)
        for i, job in enumerate(jobs):
            key_ref, write_k_ref = refs[at + 4 + 2 * (i // group) : at + 6 + 2 * (i // group)]
            query = unit_rows(activate(refs, job, scratch))
            key = key_ref[i % group]
            left = [packed_left(split(query[span])) for span in (low, high)]
            right = [packed_turned(split(key[span])) for span in (low, high)]
            alike = {
                (0, 0): fold(left[0], right[0], NT),
                (1, 1): fold(left[1], right[1], NT),
                (1, 0): fold(left[1], right[0], NT),
            }
            for j in (2 * i, 2 * i + 1):
                row, col = sums[j : j + 1], sums_col[:, j : j + 1]
                wrote = [
                    split(
                        jnp.concatenate(
                            [write_v_ref[j, span], write_k_ref[j % (2 * group), span]], axis=1
                        )
                    )
                    for span in (low, high)
                ]
                tall = [jnp.concatenate([w[0], w[0]], axis=0) for w in wrote]
                read = [None, None]
                for (t, s), product in alike.items():
                    fade = jnp.exp(
                        jnp.minimum(col[(low, high)[t]] - row[:, (low, high)[s]], 0.0)
                    )
                    attend = fade * product
                    if t == s:
                        attend = jnp.where(cols <= rows, attend, 0.0)
                    attend = split(attend)
                    part = jnp.dot(
                        packed_left(attend), tall[s], preferred_element_type=F32
                    ) + jnp.dot(attend[0], wrote[s][1], preferred_element_type=F32)
                    read[t] = part if read[t] is None else read[t] + part
                for t, span in enumerate((low, high)):
                    inner_ref[j, span] = read[t][:, :HEAD]
                    query_ref[j, span] = jnp.exp(col[span]) * query[span] - read[t][:, HEAD:]

    return call(
        body, sp, inputs, specs, outs, [pltpu.VMEM((RIM + count, HEAD), F32)],
        flops=2 * 10**9, after=after,
    )


def halves(groups):
    return [(g, i) for g, part in enumerate(groups) for i in range(part.shape[0] // 2)]


def join_transitions(mine, other, sp, place):
    served = halves(mine)
    out = jax.ShapeDtypeStruct((len(served), HEAD, HEAD), BF16)
    inputs, number = [*mine, *other], len(mine)

    def body(sp_ref, *refs):
        core = sp_ref[place]
        for slot, (g, i) in enumerate(served):
            h = core * (refs[g].shape[0] // 2) + i
            pair = (refs[g][h], refs[number + g][h])
            early = jnp.where(core == 0, pair[0], pair[1])
            late = jnp.where(core == 0, pair[1], pair[0])
            refs[-1][slot] = mul(late, early).astype(BF16)

    return call(body, sp, inputs, [whole(a) for a in inputs], [out])[0]


def join_writes(mine_a, other_a, mine, other, sp, place):
    served = halves(mine_a)
    out = jax.ShapeDtypeStruct((len(served), HEAD, HEAD), BF16)
    inputs, number = [*mine_a, *other_a, mine, other], len(mine_a)

    def body(sp_ref, *refs):
        core = sp_ref[place]
        for slot, (g, i) in enumerate(served):
            size = refs[g].shape[0]
            h = core * (size // 2) + i
            pair = (refs[-3][g * size + h].astype(F32), refs[-2][g * size + h].astype(F32))
            early = jnp.where(core == 0, pair[0], pair[1])
            late = jnp.where(core == 0, pair[1], pair[0])
            late_a = jnp.where(core == 0, refs[number + g][h], refs[g][h])
            refs[-1][slot] = (mul(late_a, early) + late).astype(BF16)

    return call(body, sp, inputs, [whole(a) for a in inputs], [out])[0]


def run_chain(trans, writes, sp):
    half = writes[0].shape[0]
    out = jax.ShapeDtypeStruct((half, HEAD, HEAD), BF16)
    inputs = [*trans, *writes]

    def body(sp_ref, *refs):
        for i in range(half):
            state = refs[len(trans)][i].astype(F32)
            for step in range(len(trans)):
                left = refs[step][i]
                state = fold(
                    packed_left((left, jnp.zeros_like(left))), packed_right(split(state))
                ) + refs[len(trans) + 1 + step][i].astype(F32)
            refs[-1][i] = state.astype(BF16)

    return call(body, sp, inputs, [whole(a) for a in inputs], [out])[0]


def shifted(value, steps):
    count = lax.axis_size("ctx")
    return lax.ppermute(value, "ctx", [(i, i + steps) for i in range(count - steps)])


def swapped(value):
    count = lax.axis_size("ctx")
    return lax.ppermute(value, "ctx", [(i, i ^ 1) for i in range(count)])


def enter_far(trans, writes):
    chips = lax.axis_size("ctx") // 2
    trans, writes = shifted(trans, 2), shifted(writes, 2)
    step = 1
    while step < chips:
        early_a, early_b = shifted(trans, 2 * step), shifted(writes, 2 * step)
        late = trans.astype(F32)
        join = functools.partial(
            jnp.einsum, "hij,hjk->hik", late, precision=lax.Precision.HIGHEST
        )
        writes = (join(early_b.astype(F32)) + writes.astype(F32)).astype(BF16)
        trans = join(early_a.astype(F32)).astype(BF16)
        step *= 2
    return writes


def finish(inner, query, mine, other, early_a, early_b, gain, sp, place):
    inputs = [inner, query, mine, other, *early_a, early_b, gain]
    number, count = inner.shape[:2]
    group = early_a[0].shape[0]
    half = group // 2
    out = jax.ShapeDtypeStruct((count, number * HEAD), BF16)

    def body(sp_ref, *refs):
        inner_ref, query_ref, mine_ref, other_ref = refs[:4]
        early_b_ref, gain_ref, out_ref = refs[-3:]
        core = sp_ref[place]
        keep = sp_ref[1].astype(F32)
        for j in range(number):
            slot = (j // group) * half + j % half
            own, far = mine_ref[slot].astype(F32), other_ref[slot].astype(F32)
            state = jnp.where((core == 0) == (j % group < half), own, far)
            stepped = mul(refs[4 + j // group][j % group], state) + early_b_ref[j].astype(F32)
            state = keep * jnp.where(core == 0, state, stepped)
            read = inner_ref[j] + mul(query_ref[j], state)
            scale = lax.rsqrt(jnp.mean(read * read, axis=-1, keepdims=True) + EPS)
            cols = slice(j * HEAD, (j + 1) * HEAD)
            out_ref[:, cols] = (read * scale * gain_ref[...]).astype(BF16)

    return call(body, sp, inputs, [whole(a) for a in inputs], [out], flops=10**8)[0]


def per_device(
    hidden,
    w_query,
    w_key,
    payload_projection_matrix,
    conv_weight,
    log_decay,
    beta_rate,
    norm_gain,
    head_order,
    block_starts,
):
    count = hidden.shape[0]
    ranks = lax.axis_size("head")
    chips = lax.axis_size("ctx") // 2
    total_heads = head_order.shape[0]
    key_heads = total_heads // ranks
    plan = Plan(ranks, key_heads)
    serve = lax.axis_index("head")
    core = lax.axis_index("ctx") % 2
    rows = w_key.shape[0]
    keep = 1 - block_starts[0]
    place = 2 + total_heads
    sp = jnp.concatenate(
        [jnp.stack([serve, keep]), head_order, jnp.stack([core])]
    ).astype(jnp.int32)
    w_value = payload_projection_matrix

    cut = (key_heads + 1) // 2
    routes = [list(range(cut)), list(range(cut, key_heads))]
    everyone = list(range(key_heads))
    groups = [heads for heads in routes if heads]
    narrow = {"width": HEAD, "heads": routes}
    wide = {"width": 2 * HEAD, "heads": routes}

    def send(stage, chunk, rim, weight, received, after=()):
        sent = send_stage(plan, stage, chunk, hidden, rim, weight, received, sp, after)
        for route, part in enumerate(exchange(plan, stage, sent)):
            if part is not None:
                received[route].append(part)
        return [part for part in sent if part is not None]

    got_k, got_v, got_q = [[], []], [[], []], [[], []]
    sent = send(0, narrow, None, w_key, got_k)
    edge = lax.dynamic_slice(hidden, (count - RIM, serve * rows), (RIM, rows))
    rim = shifted(edge, 1) * keep.astype(BF16)
    rim_parts = lax.all_to_all(
        rim_products(plan, rim, w_key, ranks, sp, after=sent), "head", 0, 0, tiled=True
    )
    sent = send(0, wide, rim, w_value, got_v, after=sent)
    tables = list(prepare(log_decay, beta_rate, sp, after=sent))
    for stage in range(1, plan.stages):
        sent = send(stage, narrow, None, w_key, got_k, after=sent)

    keyed = []
    for at, heads in enumerate(groups):
        keyed.append(
            key_phase(
                plan, narrow, heads, hidden, rim_parts, w_key, conv_weight, total_heads,
                got_k, tables, sp, after=sent,
            )
        )
        if at == 0:
            for stage in range(1, plan.stages):
                sent = send(stage, wide, rim, w_value, got_v, after=[keyed[0][4]])
            sent = send(0, narrow, rim, w_query, got_q, after=sent)
    for stage in range(1, plan.stages):
        send(stage, narrow, rim, w_query, got_q, after=[keyed[-1][4]])

    trans = [group[4] for group in keyed]
    other_trans = [swapped(part) for part in trans]
    joined_a = join_transitions(trans, other_trans, sp, place)
    write_v, trans_b = value_phase(
        plan, wide, everyone, hidden, rim, w_value, conv_weight, total_heads, got_v, tables,
        [(group[1], group[2]) for group in keyed], sp,
    )
    other_b = swapped(trans_b)
    joined_b = join_writes(trans, other_trans, trans_b, other_b, sp, place)
    if chips <= 4:
        far_a = [shifted(joined_a, 2 * d) for d in range(chips - 2, 0, -1)]
        far_b = [shifted(joined_b, 2 * d) for d in range(chips - 1, 0, -1)]
        mine = run_chain(far_a, far_b, sp)
    else:
        mine = enter_far(joined_a, joined_b)
    other = swapped(mine)
    inner, query = query_phase(
        plan, narrow, everyone, hidden, rim, w_query, conv_weight, 0, got_q, tables,
        [(group[0], group[3]) for group in keyed], write_v, sp,
    )
    return finish(
        inner, query, mine, other, other_trans, other_b, norm_gain[None, :], sp, place
    )


def solution(mesh):
    return jax.shard_map(
        per_device,
        mesh=mesh,
        in_specs=(
            P("ctx", None),
            P("head", None),
            P("head", None),
            P("head", None),
            P(),
            P("head", "ctx"),
            P("head", "ctx"),
            P(),
            P(),
            P("ctx"),
        ),
        out_specs=P("ctx", "head"),
        check_vma=False,
    )
```

time: 97.7 us -> 98.7 us (1.010); the launches traced: 97.4 us -> 97.1 us
  starting transfers between devices: 49.7 us -> 40.4 us
  waiting for transfers between devices: 1.82 us -> 8.92 us
  local copies, waits for them, and re-layouts: 3.56 us -> 6.07 us
    ppermute x16 -> x12, starting transfers between devices: 21.8 us -> 13.5 us  [exchange(): lax.ppermute(part, 'head', [(i, i ^ plan.orders[route][stage]) for i in r...]
    ppermute x7 -> x6, starting transfers between devices: 26 us -> 21.4 us  [shifted(): lax.ppermute(value, 'ctx', [(i, i + steps) for i in range(count - steps)])]
    all_to_all x0 -> x1, starting transfers between devices: none -> 4.07 us  [per_device(): lax.all_to_all(rim_products(plan, rim, w_key, ranks, sp, after=sent), 'he...]
    unnamed x20 -> x34, local copies, waits for them, and re-layouts: 2.84 us -> 5.36 us
    all_to_all x0 -> x1, waiting for transfers between devices: none -> 2.48 us  [per_device(): lax.all_to_all(rim_products(plan, rim, w_key, ranks, sp, after=sent), 'he...]
    ppermute x7 -> x6, waiting for transfers between devices: 0.02 us -> 2.49 us  [shifted(): lax.ppermute(value, 'ctx', [(i, i + steps) for i in range(count - steps)])]
    ppermute x16 -> x12, waiting for transfers between devices: 1.79 us -> 3.94 us  [exchange(): lax.ppermute(part, 'head', [(i, i ^ plan.orders[route][stage]) for i in r...]
    pallas_call x19 -> x16, Pallas kernels: 40.6 us -> 40 us  [call(): pl.pallas_call(inner, grid_spec=pltpu.PrefetchScalarGridSpec(num_scalar_p...]
  transfers between devices with their start and end apart: 29 -> 23, of which waited for: 4 -> 4; matrix products, arithmetic and copies ran while one was open for 1% -> 1% of each run, Pallas kernels for 37% -> 38%
where the time goes in v2:
time: 98.7 us; the launch traced here: 97.1 us
  starting transfers between devices  40.4 us (41%)
  Pallas kernels  40 us (41%)
  waiting for transfers between devices  8.92 us (9%)
  local copies, waits for them, and re-layouts  6.07 us (6%)
  between operations  0.99 us (1%)
    pallas_call x16, Pallas kernels, call(): pl.pallas_call(inner, grid_spec=pltpu.PrefetchScalarGridSpec(num_scalar_p...  40 us
    ppermute x6, starting transfers between devices, shifted(): lax.ppermute(value, 'ctx', [(i, i + steps) for i in range(count - steps)])  21.4 us
    ppermute x12, starting transfers between devices, exchange(): lax.ppermute(part, 'head', [(i, i ^ plan.orders[route][stage]) for i in r...  13.5 us
    unnamed x34, local copies, waits for them, and re-layouts  5.36 us
    all_to_all x1, starting transfers between devices, per_device(): lax.all_to_all(rim_products(plan, rim, w_key, ranks, sp, after=sent), 'he...  4.07 us
    ppermute x12, waiting for transfers between devices, exchange(): lax.ppermute(part, 'head', [(i, i ^ plan.orders[route][stage]) for i in r...  3.94 us
    ppermute x6, waiting for transfers between devices, shifted(): lax.ppermute(value, 'ctx', [(i, i + steps) for i in range(count - steps)])  2.49 us
    all_to_all x1, waiting for transfers between devices, per_device(): lax.all_to_all(rim_products(plan, rim, w_key, ranks, sp, after=sent), 'he...  2.48 us
  transfers between devices with their start and end apart: 23, of which 4 were waited for; matrix products, arithmetic and copies ran while one was open for 1% of the time, Pallas kernels for 38%

profile of v2, /device:TPU:0, one launch (start us, length us, event | category | flops | bytes accessed | tf_op | source)
XLA Modules:
  0.0 97.1 jit_solution(2673737562349087794)
XLA Ops:
  0.0 0.7 constant_dynamic-slice_fusion
  0.7 2.3 %collective-permute-start = (bf16[16,512]{1,0:T(8,128)(2,1)S(1)}, bf16[16,512]{1,0:T(8,128)(2,1)S(1)}, u32[]{:S(2)}, u32[]{:S(2)}) collective-permute-start(bf16[16,512]{1,0:T(8,128)(2,1)S(1)} %constant_dynamic-slice_fusion), channel_id=1, source_target_pairs={{0,4},{4,8},{8,12},{12,16},{16,20},{20,24},{24,28},{1,5},{5,9},{9,... | collective-permute-start | bytes 49160 | tf_op jit(solution)/shard_map/ppermute | solution.py:581
  3.7 0.7 pad_add_fusion.sp_ref
  4.5 1.6 %copy-done = bf16[512,2048]{1,0:T(8,128)(2,1)S(1)} copy-done((bf16[512,2048]{1,0:T(8,128)(2,1)S(1)}, bf16[512,2048]{1,0:T(8,128)(2,1)}, u32[]{:S(2)}) %copy-start) | copy-done | bytes 2097176
  6.1 1.2 %copy-done.5 = bf16[256,2048]{1,0:T(8,128)(2,1)S(1)} copy-done((bf16[256,2048]{1,0:T(8,128)(2,1)S(1)}, bf16[256,2048]{1,0:T(8,128)(2,1)}, u32[]{:S(2)}) %copy-start.5) | copy-done | bytes 1048600
  7.3 1.3 %shard_map.100 = (bf16[2,256,256]{2,1,0:T(8,128)(2,1)S(1)}, bf16[2,256,256]{2,1,0:T(8,128)(2,1)S(1)}) custom-call(s32[19]{0:T(128)S(1)} %pad_add_fusion.sp_ref, bf16[256,2048]{1,0:T(8,128)(2,1)S(1)} %copy-done.5, bf16[512,2048]{1,0:T(8,128)(2,1)S(1)} %copy-done, bf16[512,2048]{1,0:T(8,128)(2,1)S(1)} %copy-done, bf16[512,2048]{1,0:T(8,128)(2,1)S(1)} %copy-done, ...), custom_call_target="tpu_custom_call" | custom-call | flops 10000000 | bytes 1048576 | tf_op jit(solution)/shard_map/pallas_call | solution.py:85
  8.6 2.4 %collective-permute-start.3 = (bf16[2,256,256]{2,1,0:T(8,128)(2,1)S(1)}, bf16[2,256,256]{2,1,0:T(8,128)(2,1)S(1)}, u32[]{:S(2)}, u32[]{:S(2)}) collective-permute-start(bf16[2,256,256]{2,1,0:T(8,128)(2,1)S(1)} %get-tuple-element.34.refs_10_.refs_17_), channel_id=1, source_target_pairs={{0,1},{1,0},{2,3},{3,2},{4,5},{5,4},{6,7},{7,6},{8,9},{9,8},{10,11... | collective-permute-start | bytes 786440 | tf_op jit(solution)/shard_map/ppermute | solution.py:205
  11.0 1.5 %collective-permute-start.4 = (bf16[2,256,256]{2,1,0:T(8,128)(2,1)S(1)}, bf16[2,256,256]{2,1,0:T(8,128)(2,1)S(1)}, u32[]{:S(2)}, u32[]{:S(2)}) collective-permute-start(bf16[2,256,256]{2,1,0:T(8,128)(2,1)S(1)} %get-tuple-element.35.refs_11_.refs_18_), channel_id=1, source_target_pairs={{0,2},{1,3},{2,0},{3,1},{4,6},{5,7},{6,4},{7,5},{8,10},{9,11},{10,... | collective-permute-start | bytes 786440 | tf_op jit(solution)/shard_map/ppermute | solution.py:205
  12.5 0.0 copy-start.1
  12.5 2.4 %shard_map.101 = (bf16[2,272,512]{2,1,0:T(8,128)(2,1)}, bf16[2,272,512]{2,1,0:T(8,128)(2,1)}) custom-call(s32[19]{0:T(128)S(1)} %pad_add_fusion.sp_ref, bf16[256,2048]{1,0:T(8,128)(2,1)S(1)} %copy-done.5, bf16[16,512]{1,0:T(8,128)(2,1)S(1)} %broadcast_multiply_fusion.refs_1_.refs_0_, bf16[512,4096]{1,0:T(8,128)(2,1)S(1)} %copy-done.2, ...), custom_call_target="tpu_custom_call" | custom-call | flops 10000000 | bytes 1048576 | tf_op jit(solution)/shard_map/pallas_call | solution.py:85
  14.9 0.5 collective-permute-start.1
  15.5 0.2 collective-permute-start.2
  15.7 1.1 %collective-permute-done.3.refs_1_.refs_2_ = bf16[2,256,256]{2,1,0:T(8,128)(2,1)S(1)} collective-permute-done((bf16[2,256,256]{2,1,0:T(8,128)(2,1)S(1)}, bf16[2,256,256]{2,1,0:T(8,128)(2,1)S(1)}, u32[]{:S(2)}, u32[]{:S(2)}) %collective-permute-start.3) | collective-permute-done | bytes 262176 | tf_op jit(solution)/shard_map/ppermute | solution.py:205
  16.8 2.8 %collective-permute-done.4.refs_4_.refs_2_ = bf16[2,256,256]{2,1,0:T(8,128)(2,1)S(1)} collective-permute-done((bf16[2,256,256]{2,1,0:T(8,128)(2,1)S(1)}, bf16[2,256,256]{2,1,0:T(8,128)(2,1)S(1)}, u32[]{:S(2)}, u32[]{:S(2)}) %collective-permute-start.4) | collective-permute-done | bytes 262176 | tf_op jit(solution)/shard_map/ppermute | solution.py:205
  19.6 1.6 %shard_map.103 = (bf16[1,256,256]{2,1,0:T(8,128)(2,1)}, bf16[1,256,256]{2,1,0:T(8,128)(2,1)S(1)}) custom-call(s32[19]{0:T(128)S(1)} %pad_add_fusion.sp_ref, bf16[256,2048]{1,0:T(8,128)(2,1)S(1)} %copy-done.5, bf16[2,256,256]{2,1,0:T(8,128)(2,1)S(1)} %collective-permute-done.3.refs_1_.refs_2_, bf16[512,2048]{1,0:T(8,128)(2,1)S(1)} %copy-done.1, ...), custom_call_target="tpu_custom_call" | custom-call | flops 10000000 | bytes 1048576 | tf_op jit(solution)/shard_map/pallas_call | solution.py:85
  21.2 0.6 copy-done.15
  21.8 1.6 %collective-permute-start.5 = (bf16[1,256,256]{2,1,0:T(8,128)(2,1)}, bf16[1,256,256]{2,1,0:T(8,128)(2,1)}, u32[]{:S(2)}, u32[]{:S(2)}) collective-permute-start(bf16[1,256,256]{2,1,0:T(8,128)(2,1)} %get-tuple-element.38.refs_11_), channel_id=1, source_target_pairs={{0,2},{1,3},{2,0},{3,1},{4,6},{5,7},{6,4},{7,5},{8,10},{9,11},{10,... | collective-permute-start | bytes 393224 | tf_op jit(solution)/shard_map/ppermute | solution.py:205
  23.4 2.1 %shard_map.102 = bf16[4,16,512]{2,1,0:T(8,128)(2,1)} custom-call(s32[19]{0:T(128)S(1)} %pad_add_fusion.sp_ref, bf16[16,512]{1,0:T(8,128)(2,1)S(1)} %broadcast_multiply_fusion.refs_1_.refs_0_, bf16[512,2048]{1,0:T(8,128)(2,1)S(1)} %copy-done.1, bf16[512,2048]{1,0:T(8,128)(2,1)S(1)} %copy-done.1, bf16[512,2048]{1,0:T(8,128)(2,1)S(1)} %copy-done.1, ...), custom_call_target="tpu_custom_call" | custom-call | flops 10000000 | bytes 1048576 | tf_op jit(solution)/shard_map/pallas_call | solution.py:85
  25.6 4.1 %all-to-all-start = ((bf16[4,16,512]{2,1,0:T(8,128)(2,1)}), bf16[4,16,512]{2,1,0:T(8,128)(2,1)}, u32[]{:S(2)}, u32[]{:S(2)}) async-start(bf16[4,16,512]{2,1,0:T(8,128)(2,1)} %shard_map.102), calls=%async_computation | async-start | bytes 131072 | tf_op jit(solution)/shard_map/all_to_all | solution.py:677
  29.7 1.2 %shard_map.104 = (f32[8,256]{1,0:T(8,128)S(1)}, f32[256,8]{1,0:T(8,128)S(1)}, f32[256,8]{1,0:T(8,128)S(1)}) custom-call(s32[19]{0:T(128)S(1)} %pad_add_fusion.sp_ref, f32[8,256]{1,0:T(8,128)S(1)} %copy-done.12, f32[8,256]{1,0:T(8,128)S(1)} %copy-done.13, bf16[2,272,512]{2,1,0:T(8,128)(2,1)} %get-tuple-element.36.refs_7_.refs_2_, ...), custom_call_target="tpu_custom_call" | custom-call | flops 10000000 | bytes 1048576 | tf_op jit(solution)/shard_map/pallas_call | solution.py:85
  30.9 1.8 %collective-permute-start.8 = (bf16[1,256,256]{2,1,0:T(8,128)(2,1)}, bf16[1,256,256]{2,1,0:T(8,128)(2,1)}, u32[]{:S(2)}, u32[]{:S(2)}) collective-permute-start(bf16[1,256,256]{2,1,0:T(8,128)(2,1)} %copy-done.15), channel_id=1, source_target_pairs={{0,1},{1,0},{2,3},{3,2},{4,5},{5,4},{6,7},{7,6},{8,9},{9,8},{10,11... | collective-permute-start | bytes 393224 | tf_op jit(solution)/shard_map/ppermute | solution.py:205
  32.7 2.5 %all-to-all-done.refs_1_ = bf16[4,16,512]{2,1,0:T(8,128)(2,1)} async-done(((bf16[4,16,512]{2,1,0:T(8,128)(2,1)}), bf16[4,16,512]{2,1,0:T(8,128)(2,1)}, u32[]{:S(2)}, u32[]{:S(2)}) %all-to-all-start) | async-done | bytes 65568 | tf_op jit(solution)/shard_map/all_to_all | solution.py:677
  35.2 0.0 collective-permute-done.5.refs_3_
  35.2 0.0 copy-start.11
  35.2 0.9 copy-done.11
  36.1 0.9 copy-done.16
  37.0 6.2 %shard_map.105 = (f32[2,256,128]{2,1,0:T(8,128)S(1)}, f32[2,128,256]{2,1,0:T(8,128)S(1)}, f32[4,3,128,128]{3,2,1,0:T(8,128)S(1)}, f32[4,256,128]{2,1,0:T(8,128)S(1)}, f32[4,128,128]{2,1,0:T(8,128)S(1)}) custom-call(s32[19]{0:T(128)S(1)} %pad_add_fusion.sp_ref, bf16[256,2048]{1,0:T(8,128)(2,1)S(1)} %copy-done.6, bf16[4,16,512]{2,1,0:T(8,128)(2,1)} %all-to-all-done.refs_1_, ...), custom_call_target="tpu_custom_call" | custom-call | flops 4000000000 | bytes 1048576 | tf_op jit(solution)/shard_map/pallas_call | solution.py:85
  43.2 0.0 copy-start.4
  43.3 0.7 collective-permute-start.13
  44.0 0.0 collective-permute-done.1.refs_2_
  44.0 0.0 collective-permute-done.2.refs_5_.refs_8_
  44.0 2.4 %shard_map.106 = (bf16[1,272,512]{2,1,0:T(8,128)(2,1)S(1)}, bf16[1,272,512]{2,1,0:T(8,128)(2,1)S(1)}) custom-call(s32[19]{0:T(128)S(1)} %pad_add_fusion.sp_ref, bf16[256,2048]{1,0:T(8,128)(2,1)S(1)} %copy-done.6, bf16[16,512]{1,0:T(8,128)(2,1)S(1)} %broadcast_multiply_fusion.refs_1_.refs_0_, bf16[2,272,512]{2,1,0:T(8,128)(2,1)} %collective-permute-done.1.refs_2_, ...), custom_call_target="tpu_custom_call" | custom-call | flops 10000000 | bytes 1048576 | tf_op jit(solution)/shard_map/pallas_call | solution.py:85
  46.4 1.6 %collective-permute-start.11 = (bf16[1,272,512]{2,1,0:T(8,128)(2,1)S(1)}, bf16[1,272,512]{2,1,0:T(8,128)(2,1)S(1)}, u32[]{:S(2)}, u32[]{:S(2)}) collective-permute-start(bf16[1,272,512]{2,1,0:T(8,128)(2,1)S(1)} %get-tuple-element.44.refs_10_), channel_id=1, source_target_pairs={{0,2},{1,3},{2,0},{3,1},{4,6},{5,7},{6,4},{7,5},{8,10},{9,11},{10,... | collective-permute-start | bytes 835592 | tf_op jit(solution)/shard_map/ppermute | solution.py:205
  48.0 0.2 collective-permute-start.12
  48.2 1.5 %shard_map.107 = (bf16[2,272,256]{2,1,0:T(8,128)(2,1)S(1)}, bf16[2,272,256]{2,1,0:T(8,128)(2,1)S(1)}) custom-call(s32[19]{0:T(128)S(1)} %pad_add_fusion.sp_ref, bf16[256,2048]{1,0:T(8,128)(2,1)S(1)} %copy-done.6, bf16[16,512]{1,0:T(8,128)(2,1)S(1)} %broadcast_multiply_fusion.refs_1_.refs_0_, bf16[512,2048]{1,0:T(8,128)(2,1)S(1)} %copy-done.4, ...), custom_call_target="tpu_custom_call" | custom-call | flops 10000000 | bytes 1048576 | tf_op jit(solution)/shard_map/pallas_call | solution.py:85
  49.7 1.9 %collective-permute-start.6 = (bf16[2,272,256]{2,1,0:T(8,128)(2,1)S(1)}, bf16[2,272,256]{2,1,0:T(8,128)(2,1)S(1)}, u32[]{:S(2)}, u32[]{:S(2)}) collective-permute-start(bf16[2,272,256]{2,1,0:T(8,128)(2,1)S(1)} %get-tuple-element.46.refs_11_), channel_id=1, source_target_pairs={{0,1},{1,0},{2,3},{3,2},{4,5},{5,4},{6,7},{7,6},{8,9},{9,8},{10,11... | collective-permute-start | bytes 835592 | tf_op jit(solution)/shard_map/ppermute | solution.py:205
  51.6 0.0 collective-permute-done.8.refs_3_
  51.6 0.5 collective-permute-start.7
  52.1 5.9 %shard_map.108 = (f32[2,256,128]{2,1,0:T(8,128)S(1)}, f32[2,128,256]{2,1,0:T(8,128)S(1)}, f32[4,3,128,128]{3,2,1,0:T(8,128)S(1)}, f32[4,256,128]{2,1,0:T(8,128)S(1)}, f32[4,128,128]{2,1,0:T(8,128)S(1)}) custom-call(s32[19]{0:T(128)S(1)} %pad_add_fusion.sp_ref, bf16[256,2048]{1,0:T(8,128)(2,1)S(1)} %copy-done.6, bf16[4,16,512]{2,1,0:T(8,128)(2,1)} %all-to-all-done.refs_1_, ...), custom_call_target="tpu_custom_call" | custom-call | flops 4000000000 | bytes 1048576 | tf_op jit(solution)/shard_map/pallas_call | solution.py:85
  58.0 0.0 collective-permute-done.11.refs_3_
  58.0 0.1 collective-permute-start.14
  58.1 0.0 collective-permute-done.12.refs_9_
  58.1 5.3 %shard_map.110 = (f32[8,256,128]{2,1,0:T(8,128)S(1)}, bf16[8,128,128]{2,1,0:T(8,128)(2,1)S(1)}) custom-call(s32[19]{0:T(128)S(1)} %pad_add_fusion.sp_ref, bf16[256,2048]{1,0:T(8,128)(2,1)S(1)} %copy-done.6, bf16[16,512]{1,0:T(8,128)(2,1)S(1)} %broadcast_multiply_fusion.refs_1_.refs_0_, bf16[2,272,512]{2,1,0:T(8,128)(2,1)} %collective-permute-done.1.refs_2_, ...), custom_call_target="tpu_custom_call" | custom-call | flops 2000000000 | bytes 1048576 | tf_op jit(solution)/shard_map/pallas_call | solution.py:85
  63.5 0.5 collective-permute-start.17
  64.0 0.0 collective-permute-done.13.refs_2_.refs_4_
  64.0 0.0 collective-permute-done.14.refs_3_.refs_5_
  64.0 0.8 shard_map.112
  64.8 4.7 %collective-permute-start.15 = (bf16[4,128,128]{2,1,0:T(8,128)(2,1)S(1)}, bf16[4,128,128]{2,1,0:T(8,128)(2,1)S(1)}, u32[]{:S(2)}, u32[]{:S(2)}) collective-permute-start(bf16[4,128,128]{2,1,0:T(8,128)(2,1)S(1)} %shard_map.112), channel_id=1, source_target_pairs={{0,16},{4,20},{8,24},{12,28},{1,17},{5,21},{9,25},{13,29},{2,18},{... | collective-permute-start | bytes 393224 | tf_op jit(solution)/shard_map/ppermute | solution.py:581
  69.5 2.7 %collective-permute-start.16 = (bf16[4,128,128]{2,1,0:T(8,128)(2,1)S(1)}, bf16[4,128,128]{2,1,0:T(8,128)(2,1)S(1)}, u32[]{:S(2)}, u32[]{:S(2)}) collective-permute-start(bf16[4,128,128]{2,1,0:T(8,128)(2,1)S(1)} %shard_map.112), channel_id=1, source_target_pairs={{0,8},{4,12},{8,16},{12,20},{16,24},{20,28},{1,9},{5,13},{9,17},{1... | collective-permute-start | bytes 393224 | tf_op jit(solution)/shard_map/ppermute | solution.py:581
  72.2 0.0 collective-permute-done.6.refs_2_
  72.2 0.0 collective-permute-done.7.refs_5_.refs_8_
  72.2 1.1 %shard_map.109 = (bf16[1,272,256]{2,1,0:T(8,128)(2,1)S(1)}, bf16[1,272,256]{2,1,0:T(8,128)(2,1)S(1)}) custom-call(s32[19]{0:T(128)S(1)} %pad_add_fusion.sp_ref, bf16[256,2048]{1,0:T(8,128)(2,1)S(1)} %copy-done.6, bf16[16,512]{1,0:T(8,128)(2,1)S(1)} %broadcast_multiply_fusion.refs_1_.refs_0_, bf16[2,272,256]{2,1,0:T(8,128)(2,1)S(1)} %collective-permute-done.6.refs_2_, ...), custom_call_target="tpu_custom_call" | custom-call | flops 10000000 | bytes 1048576 | tf_op jit(solution)/shard_map/pallas_call | solution.py:85
  73.3 0.8 collective-permute-start.10
  74.1 0.4 collective-permute-start.9
  74.5 0.8 shard_map.113
  75.3 1.3 %collective-permute-start.18 = (bf16[4,128,128]{2,1,0:T(8,128)(2,1)S(1)}, bf16[4,128,128]{2,1,0:T(8,128)(2,1)S(1)}, u32[]{:S(2)}, u32[]{:S(2)}) collective-permute-start(bf16[4,128,128]{2,1,0:T(8,128)(2,1)S(1)} %shard_map.113), channel_id=1, source_target_pairs={{0,24},{4,28},{1,25},{5,29},{2,26},{6,30},{3,27},{7,31}} | collective-permute-start | bytes 393224 | tf_op jit(solution)/shard_map/ppermute | solution.py:581
  76.7 1.5 %collective-permute-start.19 = (bf16[4,128,128]{2,1,0:T(8,128)(2,1)S(1)}, bf16[4,128,128]{2,1,0:T(8,128)(2,1)S(1)}, u32[]{:S(2)}, u32[]{:S(2)}) collective-permute-start(bf16[4,128,128]{2,1,0:T(8,128)(2,1)S(1)} %shard_map.113), channel_id=1, source_target_pairs={{0,16},{4,20},{8,24},{12,28},{1,17},{5,21},{9,25},{13,29},{2,18},{... | collective-permute-start | bytes 393224 | tf_op jit(solution)/shard_map/ppermute | solution.py:581
  78.2 8.9 %collective-permute-start.20 = (bf16[4,128,128]{2,1,0:T(8,128)(2,1)S(1)}, bf16[4,128,128]{2,1,0:T(8,128)(2,1)S(1)}, u32[]{:S(2)}, u32[]{:S(2)}) collective-permute-start(bf16[4,128,128]{2,1,0:T(8,128)(2,1)S(1)} %shard_map.113), channel_id=1, source_target_pairs={{0,8},{4,12},{8,16},{12,20},{16,24},{20,28},{1,9},{5,13},{9,17},{1... | collective-permute-start | bytes 393224 | tf_op jit(solution)/shard_map/ppermute | solution.py:581
  87.1 2.5 %collective-permute-done.20.refs_4_ = bf16[4,128,128]{2,1,0:T(8,128)(2,1)S(1)} collective-permute-done((bf16[4,128,128]{2,1,0:T(8,128)(2,1)S(1)}, bf16[4,128,128]{2,1,0:T(8,128)(2,1)S(1)}, u32[]{:S(2)}, u32[]{:S(2)}) %collective-permute-start.20) | collective-permute-done | bytes 131104 | tf_op jit(solution)/shard_map/ppermute | solution.py:581
  89.6 1.0 %shard_map.114.refs_2_ = bf16[4,128,128]{2,1,0:T(8,128)(2,1)S(1)} custom-call(s32[19]{0:T(128)S(1)} %pad_add_fusion.sp_ref, bf16[4,128,128]{2,1,0:T(8,128)(2,1)S(1)} %collective-permute-done.15.refs_0_, bf16[4,128,128]{2,1,0:T(8,128)(2,1)S(1)} %collective-permute-done.16.refs_1_, bf16[4,128,128]{2,1,0:T(8,128)(2,1)S(1)} %collective-permute-done.18.refs_2_, ...), custom_call_target="tpu_custom_call" | custom-call | flops 10000000 | bytes 1048576 | tf_op jit(solution)/shard_map/pallas_call | solution.py:85
  90.6 0.1 collective-permute-start.21
  90.7 0.0 copy-start.14
  90.7 3.7 %shard_map.111 = (f32[8,256,128]{2,1,0:T(8,128)S(1)}, f32[8,256,128]{2,1,0:T(8,128)S(1)}) custom-call(s32[19]{0:T(128)S(1)} %pad_add_fusion.sp_ref, bf16[256,2048]{1,0:T(8,128)(2,1)S(1)} %copy-done.6, bf16[16,512]{1,0:T(8,128)(2,1)S(1)} %broadcast_multiply_fusion.refs_1_.refs_0_, bf16[2,272,256]{2,1,0:T(8,128)(2,1)S(1)} %collective-permute-done.6.refs_2_, ...), custom_call_target="tpu_custom_call" | custom-call | flops 2000000000 | bytes 1048576 | tf_op jit(solution)/shard_map/pallas_call | solution.py:85
  94.4 2.7 %shard_map.115 = bf16[256,1024]{1,0:T(8,128)(2,1)} custom-call(s32[19]{0:T(128)S(1)} %pad_add_fusion.sp_ref, f32[8,256,128]{2,1,0:T(8,128)S(1)} %get-tuple-element.60.refs_0_, f32[8,256,128]{2,1,0:T(8,128)S(1)} %get-tuple-element.61.refs_1_, bf16[4,128,128]{2,1,0:T(8,128)(2,1)S(1)} %shard_map.114.refs_2_, ...), custom_call_target="tpu_custom_call" | custom-call | flops 100000000 | bytes 1048576 | tf_op jit(solution)/shard_map/pallas_call | solution.py:85
  (35 shorter events, 0.1 us)
Async XLA Ops:
  0.7 11.8 %collective-permute-start = (bf16[16,512]{1,0:T(8,128)(2,1)S(1)}, bf16[16,512]{1,0:T(8,128)(2,1)S(1)}, u32[]{:S(2)}, u32[]{:S(2)}) collective-permute-start(bf16[16,512]{1,0:T(8,128)(2,1)S(1)} %constant_dynamic-slice_fusion), channel_id=1, source_target_pairs={{0,4},{4,8},{8,12},{12,16},{16,20},{20,24},{24,28},{1,5},{5,9},{9,... | collective-permute-start | bytes 49160 | tf_op jit(solution)/shard_map/ppermute | solution.py:581
  4.5 1.6 %copy-start = (bf16[512,2048]{1,0:T(8,128)(2,1)S(1)}, bf16[512,2048]{1,0:T(8,128)(2,1)}, u32[]{:S(2)}) copy-start(bf16[512,2048]{1,0:T(8,128)(2,1)} %refs_6_.18) | copy-start | bytes 6291460
  6.1 1.2 %copy-start.5 = (bf16[256,2048]{1,0:T(8,128)(2,1)S(1)}, bf16[256,2048]{1,0:T(8,128)(2,1)}, u32[]{:S(2)}) copy-start(bf16[256,2048]{1,0:T(8,128)(2,1)} %refs_0_.21) | copy-start | bytes 3145732
  7.3 5.2 %copy-start.2 = (bf16[512,4096]{1,0:T(8,128)(2,1)S(1)}, bf16[512,4096]{1,0:T(8,128)(2,1)}, u32[]{:S(2)}) copy-start(bf16[512,4096]{1,0:T(8,128)(2,1)} %refs_12_.4) | copy-start | bytes 12582916
  8.6 8.2 %collective-permute-start.3 = (bf16[2,256,256]{2,1,0:T(8,128)(2,1)S(1)}, bf16[2,256,256]{2,1,0:T(8,128)(2,1)S(1)}, u32[]{:S(2)}, u32[]{:S(2)}) collective-permute-start(bf16[2,256,256]{2,1,0:T(8,128)(2,1)S(1)} %get-tuple-element.34.refs_10_.refs_17_), channel_id=1, source_target_pairs={{0,1},{1,0},{2,3},{3,2},{4,5},{5,4},{6,7},{7,6},{8,9},{9,8},{10,11... | collective-permute-start | bytes 786440 | tf_op jit(solution)/shard_map/ppermute | solution.py:205
  11.0 8.6 %collective-permute-start.4 = (bf16[2,256,256]{2,1,0:T(8,128)(2,1)S(1)}, bf16[2,256,256]{2,1,0:T(8,128)(2,1)S(1)}, u32[]{:S(2)}, u32[]{:S(2)}) collective-permute-start(bf16[2,256,256]{2,1,0:T(8,128)(2,1)S(1)} %get-tuple-element.35.refs_11_.refs_18_), channel_id=1, source_target_pairs={{0,2},{1,3},{2,0},{3,1},{4,6},{5,7},{6,4},{7,5},{8,10},{9,11},{10,... | collective-permute-start | bytes 786440 | tf_op jit(solution)/shard_map/ppermute | solution.py:205
  12.5 7.1 %copy-start.1 = (bf16[512,2048]{1,0:T(8,128)(2,1)S(1)}, bf16[512,2048]{1,0:T(8,128)(2,1)}, u32[]{:S(2)}) copy-start(bf16[512,2048]{1,0:T(8,128)(2,1)} %refs_6_.18) | copy-start | bytes 6291460
  14.9 29.1 %collective-permute-start.1 = (bf16[2,272,512]{2,1,0:T(8,128)(2,1)}, bf16[2,272,512]{2,1,0:T(8,128)(2,1)}, u32[]{:S(2)}, u32[]{:S(2)}) collective-permute-start(bf16[2,272,512]{2,1,0:T(8,128)(2,1)} %get-tuple-element.36.refs_7_.refs_2_), channel_id=1, source_target_pairs={{0,1},{1,0},{2,3},{3,2},{4,5},{5,4},{6,7},{7,6},{8,9},{9,8},{10,11... | collective-permute-start | bytes 1671176 | tf_op jit(solution)/shard_map/ppermute | solution.py:205
  15.5 28.5 %collective-permute-start.2 = (bf16[2,272,512]{2,1,0:T(8,128)(2,1)}, bf16[2,272,512]{2,1,0:T(8,128)(2,1)}, u32[]{:S(2)}, u32[]{:S(2)}) collective-permute-start(bf16[2,272,512]{2,1,0:T(8,128)(2,1)} %get-tuple-element.37.refs_8_.refs_3_), channel_id=1, source_target_pairs={{0,2},{1,3},{2,0},{3,1},{4,6},{5,7},{6,4},{7,5},{8,10},{9,11},{10,... | collective-permute-start | bytes 1671176 | tf_op jit(solution)/shard_map/ppermute | solution.py:205
  16.8 4.4 %copy-start.10 = (bf16[2,256,256]{2,1,0:T(8,128)(2,1)}, bf16[2,256,256]{2,1,0:T(8,128)(2,1)S(1)}, u32[]{:S(2)}) copy-start(bf16[2,256,256]{2,1,0:T(8,128)(2,1)S(1)} %collective-permute-done.3.refs_1_.refs_2_) | copy-start | bytes 786436
  19.6 1.6 %copy-start.8 = (bf16[2,256,256]{2,1,0:T(8,128)(2,1)}, bf16[2,256,256]{2,1,0:T(8,128)(2,1)S(1)}, u32[]{:S(2)}) copy-start(bf16[2,256,256]{2,1,0:T(8,128)(2,1)S(1)} %collective-permute-done.4.refs_4_.refs_2_) | copy-start | bytes 786436
  21.2 0.6 copy-start.15
  21.8 7.8 %copy-start.12 = (f32[8,256]{1,0:T(8,128)S(1)}, f32[8,256]{1,0:T(8,128)}, u32[]{:S(2)}) copy-start(f32[8,256]{1,0:T(8,128)} %refs_0_.14) | copy-start | bytes 24580
  21.8 7.8 %copy-start.13 = (f32[8,256]{1,0:T(8,128)S(1)}, f32[8,256]{1,0:T(8,128)}, u32[]{:S(2)}) copy-start(f32[8,256]{1,0:T(8,128)} %refs_1_.5) | copy-start | bytes 24580
  21.8 13.3 %copy-start.6 = (bf16[256,2048]{1,0:T(8,128)(2,1)S(1)}, bf16[256,2048]{1,0:T(8,128)(2,1)}, u32[]{:S(2)}) copy-start(bf16[256,2048]{1,0:T(8,128)(2,1)} %refs_0_.21) | copy-start | bytes 3145732
  21.8 13.3 %copy-start.7 = (bf16[4,8192]{1,0:T(4,128)(2,1)S(1)}, bf16[4,8192]{1,0:T(4,128)(2,1)}, u32[]{:S(2)}) copy-start(bf16[4,8192]{1,0:T(4,128)(2,1)} %refs_13_.5) | copy-start | bytes 196612
  21.8 13.3 %collective-permute-start.5 = (bf16[1,256,256]{2,1,0:T(8,128)(2,1)}, bf16[1,256,256]{2,1,0:T(8,128)(2,1)}, u32[]{:S(2)}, u32[]{:S(2)}) collective-permute-start(bf16[1,256,256]{2,1,0:T(8,128)(2,1)} %get-tuple-element.38.refs_11_), channel_id=1, source_target_pairs={{0,2},{1,3},{2,0},{3,1},{4,6},{5,7},{6,4},{7,5},{8,10},{9,11},{10,... | collective-permute-start | bytes 393224 | tf_op jit(solution)/shard_map/ppermute | solution.py:205
  25.6 9.6 %all-to-all-start = ((bf16[4,16,512]{2,1,0:T(8,128)(2,1)}), bf16[4,16,512]{2,1,0:T(8,128)(2,1)}, u32[]{:S(2)}, u32[]{:S(2)}) async-start(bf16[4,16,512]{2,1,0:T(8,128)(2,1)} %shard_map.102), calls=%async_computation | async-start | bytes 131072 | tf_op jit(solution)/shard_map/all_to_all | solution.py:677
  30.9 20.7 %collective-permute-start.8 = (bf16[1,256,256]{2,1,0:T(8,128)(2,1)}, bf16[1,256,256]{2,1,0:T(8,128)(2,1)}, u32[]{:S(2)}, u32[]{:S(2)}) collective-permute-start(bf16[1,256,256]{2,1,0:T(8,128)(2,1)} %copy-done.15), channel_id=1, source_target_pairs={{0,1},{1,0},{2,3},{3,2},{4,5},{5,4},{6,7},{7,6},{8,9},{9,8},{10,11... | collective-permute-start | bytes 393224 | tf_op jit(solution)/shard_map/ppermute | solution.py:205
  35.2 1.0 copy-start.11
  36.1 0.9 copy-start.16
  37.0 7.0 %copy-start.3 = (bf16[512,4096]{1,0:T(8,128)(2,1)S(1)}, bf16[512,4096]{1,0:T(8,128)(2,1)}, u32[]{:S(2)}) copy-start(bf16[512,4096]{1,0:T(8,128)(2,1)} %refs_12_.4) | copy-start | bytes 12582916
  43.2 4.9 %copy-start.4 = (bf16[512,2048]{1,0:T(8,128)(2,1)S(1)}, bf16[512,2048]{1,0:T(8,128)(2,1)}, u32[]{:S(2)}) copy-start(bf16[512,2048]{1,0:T(8,128)(2,1)} %refs_12_.5) | copy-start | bytes 6291460
  43.3 20.7 %collective-permute-start.13 = (f32[4,128,128]{2,1,0:T(8,128)S(1)}, f32[4,128,128]{2,1,0:T(8,128)S(1)}, u32[]{:S(2)}, u32[]{:S(2)}) collective-permute-start(f32[4,128,128]{2,1,0:T(8,128)S(1)} %get-tuple-element.43.refs_8_.refs_0_), channel_id=1, source_target_pairs={{0,4},{4,0},{8,12},{12,8},{16,20},{20,16},{24,28},{28,24},{1,5},{5... | collective-permute-start | bytes 786440 | tf_op jit(solution)/shard_map/ppermute | solution.py:586
  46.4 11.7 %collective-permute-start.11 = (bf16[1,272,512]{2,1,0:T(8,128)(2,1)S(1)}, bf16[1,272,512]{2,1,0:T(8,128)(2,1)S(1)}, u32[]{:S(2)}, u32[]{:S(2)}) collective-permute-start(bf16[1,272,512]{2,1,0:T(8,128)(2,1)S(1)} %get-tuple-element.44.refs_10_), channel_id=1, source_target_pairs={{0,2},{1,3},{2,0},{3,1},{4,6},{5,7},{6,4},{7,5},{8,10},{9,11},{10,... | collective-permute-start | bytes 835592 | tf_op jit(solution)/shard_map/ppermute | solution.py:205
  47.9 4.1 %copy-start.9 = (bf16[2,256,256]{2,1,0:T(8,128)(2,1)S(1)}, bf16[2,256,256]{2,1,0:T(8,128)(2,1)}, u32[]{:S(2)}) copy-start(bf16[2,256,256]{2,1,0:T(8,128)(2,1)} %copy-done.8) | copy-start | bytes 786436
  48.0 10.2 %collective-permute-start.12 = (bf16[1,272,512]{2,1,0:T(8,128)(2,1)S(1)}, bf16[1,272,512]{2,1,0:T(8,128)(2,1)S(1)}, u32[]{:S(2)}, u32[]{:S(2)}) collective-permute-start(bf16[1,272,512]{2,1,0:T(8,128)(2,1)S(1)} %get-tuple-element.45.refs_11_), channel_id=1, source_target_pairs={{0,1},{1,0},{2,3},{3,2},{4,5},{5,4},{6,7},{7,6},{8,9},{9,8},{10,11... | collective-permute-start | bytes 835592 | tf_op jit(solution)/shard_map/ppermute | solution.py:205
  49.7 22.4 %collective-permute-start.6 = (bf16[2,272,256]{2,1,0:T(8,128)(2,1)S(1)}, bf16[2,272,256]{2,1,0:T(8,128)(2,1)S(1)}, u32[]{:S(2)}, u32[]{:S(2)}) collective-permute-start(bf16[2,272,256]{2,1,0:T(8,128)(2,1)S(1)} %get-tuple-element.46.refs_11_), channel_id=1, source_target_pairs={{0,1},{1,0},{2,3},{3,2},{4,5},{5,4},{6,7},{7,6},{8,9},{9,8},{10,11... | collective-permute-start | bytes 835592 | tf_op jit(solution)/shard_map/ppermute | solution.py:205
  51.6 20.6 %collective-permute-start.7 = (bf16[2,272,256]{2,1,0:T(8,128)(2,1)S(1)}, bf16[2,272,256]{2,1,0:T(8,128)(2,1)S(1)}, u32[]{:S(2)}, u32[]{:S(2)}) collective-permute-start(bf16[2,272,256]{2,1,0:T(8,128)(2,1)S(1)} %get-tuple-element.47.refs_12_), channel_id=1, source_target_pairs={{0,2},{1,3},{2,0},{3,1},{4,6},{5,7},{6,4},{7,5},{8,10},{9,11},{10,... | collective-permute-start | bytes 835592 | tf_op jit(solution)/shard_map/ppermute | solution.py:205
  58.0 6.0 %collective-permute-start.14 = (f32[4,128,128]{2,1,0:T(8,128)S(1)}, f32[4,128,128]{2,1,0:T(8,128)S(1)}, u32[]{:S(2)}, u32[]{:S(2)}) collective-permute-start(f32[4,128,128]{2,1,0:T(8,128)S(1)} %get-tuple-element.48.refs_8_.refs_1_), channel_id=1, source_target_pairs={{0,4},{4,0},{8,12},{12,8},{16,20},{20,16},{24,28},{28,24},{1,5},{5... | collective-permute-start | bytes 786440 | tf_op jit(solution)/shard_map/ppermute | solution.py:586
  63.5 11.1 %collective-permute-start.17 = (bf16[8,128,128]{2,1,0:T(8,128)(2,1)S(1)}, bf16[8,128,128]{2,1,0:T(8,128)(2,1)S(1)}, u32[]{:S(2)}, u32[]{:S(2)}) collective-permute-start(bf16[8,128,128]{2,1,0:T(8,128)(2,1)S(1)} %get-tuple-element.62.refs_4_), channel_id=1, source_target_pairs={{0,4},{4,0},{8,12},{12,8},{16,20},{20,16},{24,28},{28,24},{1,5},{5... | collective-permute-start | bytes 786440 | tf_op jit(solution)/shard_map/ppermute | solution.py:586
  64.8 11.8 %collective-permute-start.15 = (bf16[4,128,128]{2,1,0:T(8,128)(2,1)S(1)}, bf16[4,128,128]{2,1,0:T(8,128)(2,1)S(1)}, u32[]{:S(2)}, u32[]{:S(2)}) collective-permute-start(bf16[4,128,128]{2,1,0:T(8,128)(2,1)S(1)} %shard_map.112), channel_id=1, source_target_pairs={{0,16},{4,20},{8,24},{12,28},{1,17},{5,21},{9,25},{13,29},{2,18},{... | collective-permute-start | bytes 393224 | tf_op jit(solution)/shard_map/ppermute | solution.py:581
  69.5 8.7 %collective-permute-start.16 = (bf16[4,128,128]{2,1,0:T(8,128)(2,1)S(1)}, bf16[4,128,128]{2,1,0:T(8,128)(2,1)S(1)}, u32[]{:S(2)}, u32[]{:S(2)}) collective-permute-start(bf16[4,128,128]{2,1,0:T(8,128)(2,1)S(1)} %shard_map.112), channel_id=1, source_target_pairs={{0,8},{4,12},{8,16},{12,20},{16,24},{20,28},{1,9},{5,13},{9,17},{1... | collective-permute-start | bytes 393224 | tf_op jit(solution)/shard_map/ppermute | solution.py:581
  73.3 17.4 %collective-permute-start.10 = (bf16[1,272,256]{2,1,0:T(8,128)(2,1)S(1)}, bf16[1,272,256]{2,1,0:T(8,128)(2,1)S(1)}, u32[]{:S(2)}, u32[]{:S(2)}) collective-permute-start(bf16[1,272,256]{2,1,0:T(8,128)(2,1)S(1)} %get-tuple-element.50), channel_id=1, source_target_pairs={{0,1},{1,0},{2,3},{3,2},{4,5},{5,4},{6,7},{7,6},{8,9},{9,8},{10,11... | collective-permute-start | bytes 417800 | tf_op jit(solution)/shard_map/ppermute | solution.py:205
  74.1 16.6 %collective-permute-start.9 = (bf16[1,272,256]{2,1,0:T(8,128)(2,1)S(1)}, bf16[1,272,256]{2,1,0:T(8,128)(2,1)S(1)}, u32[]{:S(2)}, u32[]{:S(2)}) collective-permute-start(bf16[1,272,256]{2,1,0:T(8,128)(2,1)S(1)} %get-tuple-element.49), channel_id=1, source_target_pairs={{0,2},{1,3},{2,0},{3,1},{4,6},{5,7},{6,4},{7,5},{8,10},{9,11},{10,... | collective-permute-start | bytes 417800 | tf_op jit(solution)/shard_map/ppermute | solution.py:205
  75.3 11.8 %collective-permute-start.18 = (bf16[4,128,128]{2,1,0:T(8,128)(2,1)S(1)}, bf16[4,128,128]{2,1,0:T(8,128)(2,1)S(1)}, u32[]{:S(2)}, u32[]{:S(2)}) collective-permute-start(bf16[4,128,128]{2,1,0:T(8,128)(2,1)S(1)} %shard_map.113), channel_id=1, source_target_pairs={{0,24},{4,28},{1,25},{5,29},{2,26},{6,30},{3,27},{7,31}} | collective-permute-start | bytes 393224 | tf_op jit(solution)/shard_map/ppermute | solution.py:581
  76.7 10.5 %collective-permute-start.19 = (bf16[4,128,128]{2,1,0:T(8,128)(2,1)S(1)}, bf16[4,128,128]{2,1,0:T(8,128)(2,1)S(1)}, u32[]{:S(2)}, u32[]{:S(2)}) collective-permute-start(bf16[4,128,128]{2,1,0:T(8,128)(2,1)S(1)} %shard_map.113), channel_id=1, source_target_pairs={{0,16},{4,20},{8,24},{12,28},{1,17},{5,21},{9,25},{13,29},{2,18},{... | collective-permute-start | bytes 393224 | tf_op jit(solution)/shard_map/ppermute | solution.py:581
  78.2 11.4 %collective-permute-start.20 = (bf16[4,128,128]{2,1,0:T(8,128)(2,1)S(1)}, bf16[4,128,128]{2,1,0:T(8,128)(2,1)S(1)}, u32[]{:S(2)}, u32[]{:S(2)}) collective-permute-start(bf16[4,128,128]{2,1,0:T(8,128)(2,1)S(1)} %shard_map.113), channel_id=1, source_target_pairs={{0,8},{4,12},{8,16},{12,20},{16,24},{20,28},{1,9},{5,13},{9,17},{1... | collective-permute-start | bytes 393224 | tf_op jit(solution)/shard_map/ppermute | solution.py:581
  90.6 3.8 %collective-permute-start.21 = (bf16[4,128,128]{2,1,0:T(8,128)(2,1)S(1)}, bf16[4,128,128]{2,1,0:T(8,128)(2,1)S(1)}, u32[]{:S(2)}, u32[]{:S(2)}) collective-permute-start(bf16[4,128,128]{2,1,0:T(8,128)(2,1)S(1)} %shard_map.114.refs_2_), channel_id=1, source_target_pairs={{0,4},{4,0},{8,12},{12,8},{16,20},{20,16},{24,28},{28,24},{1,5},{5... | collective-permute-start | bytes 393224 | tf_op jit(solution)/shard_map/ppermute | solution.py:586
  90.7 3.7 %copy-start.14 = (f32[128]{0:T(128)S(1)}, f32[128]{0:T(128)}, u32[]{:S(2)}) copy-start(f32[128]{0:T(128)} %param.17) | copy-start | bytes 1540

commit v3 on v2

v3 whole, which is shorter than its diff:
```python
import functools

import jax
import jax.numpy as jnp
from jax import lax
from jax.experimental import pallas as pl
from jax.experimental.pallas import tpu as pltpu
from jax.sharding import PartitionSpec as P

HEAD = 128
TAPS = 4
RIM = 16
EPS = 1e-06
VMEM_BYTES = 20 * 1024 * 1024
F32 = jnp.float32
BF16 = jnp.bfloat16

NN = (((1,), (0,)), ((), ()))
NT = (((1,), (1,)), ((), ()))


def dot1(a, b, dims=NN):
    return lax.dot_general(
        a.astype(BF16), b.astype(BF16), dims, preferred_element_type=F32
    )


def split(a):
    high = a.astype(BF16)
    return high, (a - high.astype(F32)).astype(BF16)


def dot3s(a, b, dims=NN):
    (ah, al), (bh, bl) = a, b
    one = functools.partial(lax.dot_general, dimension_numbers=dims, preferred_element_type=F32)
    return one(ah, bh) + (one(ah, bl) + one(al, bh))


def dot3(a, b, dims=NN):
    return dot3s(split(a), split(b), dims)


def packed_left(parts):
    return jnp.concatenate(parts, axis=1)


def packed_right(parts):
    wide = jnp.concatenate(parts, axis=1)
    return jnp.concatenate([wide, wide], axis=0)


def packed_turned(parts):
    tall = jnp.concatenate(parts, axis=0)
    return jnp.concatenate([tall, tall], axis=1)


def fold(left, right, dims=NN):
    both = lax.dot_general(left, right, dims, preferred_element_type=F32)
    width = both.shape[1] // 2
    return both[:, :width] + both[:, width:]


def mul(a, b):
    return fold(packed_left(split(a)), packed_right(split(b)))


def dot_full(a, b, dims=NN):
    return lax.dot_general(
        a, b, dims, precision=lax.Precision.HIGHEST, preferred_element_type=F32
    )


def whole(array):
    zeros = (0,) * array.ndim
    return pl.BlockSpec(array.shape, lambda i, sp: zeros)


def call(body, sp, inputs, specs, outs, scratch=(), after=()):
    number = len(inputs)
    specs = list(specs) + [pl.BlockSpec(memory_space=pl.ANY) for _ in after]

    def inner(sp_ref, *refs):
        body(sp_ref, *refs[:number], *refs[number + len(after) :])

    return pl.pallas_call(
        inner,
        grid_spec=pltpu.PrefetchScalarGridSpec(
            num_scalar_prefetch=1,
            grid=(1,),
            in_specs=specs,
            out_specs=[whole(out) for out in outs],
            scratch_shapes=list(scratch),
        ),
        out_shape=[jax.ShapeDtypeStruct(out.shape, out.dtype) for out in outs],
        compiler_params=pltpu.CompilerParams(vmem_limit_bytes=VMEM_BYTES),
        cost_estimate=pl.CostEstimate(flops=1000, bytes_accessed=1000, transcendentals=0),
    )(sp, *inputs, *after)


def weight_spec(key_heads, rows, width, unit, head):
    return pl.BlockSpec(
        (rows, width), lambda i, sp: (0, sp[2 + (sp[0] ^ unit) * key_heads + head])
    )


def tap_spec(key_heads, width, base, head):
    return pl.BlockSpec(
        (TAPS, width), lambda i, sp: (0, base + sp[2 + sp[0] * key_heads + head])
    )


def hidden_spec(hidden, rows):
    return pl.BlockSpec((hidden.shape[0], rows), lambda i, sp: (0, sp[0]))


def partial_sums(key_heads, ranks, heads, width, hidden, rim, weight, sp, after=()):
    rows, count = weight.shape[0], hidden.shape[0]
    inputs, specs = [hidden, rim], [hidden_spec(hidden, rows), hidden_spec(rim, rows)]
    for unit in range(1, ranks):
        for head in heads:
            inputs.append(weight)
            specs.append(weight_spec(key_heads, rows, width, unit, head))
    outs = [jax.ShapeDtypeStruct((RIM + count, width * len(heads)), BF16)] * (ranks - 1)

    def body(sp_ref, hidden_ref, rim_ref, *refs):
        for unit in range(ranks - 1):
            out = refs[(ranks - 1) * len(heads) + unit]
            for at in range(len(heads)):
                held = refs[unit * len(heads) + at][...]
                cols = slice(at * width, (at + 1) * width)
                out[RIM:, cols] = plain(hidden_ref[...], held).astype(BF16)
                out[:RIM, cols] = plain(rim_ref[...], held).astype(BF16)

    return call(body, sp, inputs, specs, outs, after=after)


def exchange(parts):
    ranks = len(parts) + 1
    return [
        lax.ppermute(part, "head", [(i, i ^ (unit + 1)) for i in range(ranks)])
        for unit, part in enumerate(parts)
    ]


def gather_specs(key_heads, heads, width, hidden, rim, weight, taps, base, received):
    rows = weight.shape[0]
    inputs = [hidden, rim]
    specs = [hidden_spec(hidden, rows), hidden_spec(rim, rows)]
    jobs = []
    for head, at in heads:
        jobs.append(len(inputs))
        inputs += [weight, taps]
        specs += [
            weight_spec(key_heads, rows, width, 0, head), tap_spec(key_heads, width, base, head)
        ]
        for part in received:
            inputs.append(part)
            specs.append(pl.BlockSpec((part.shape[0], width), lambda i, sp, at=at: (0, at)))
    return inputs, specs, jobs


def activate(refs, job, number, scratch):
    held, taps = refs[job][...], refs[job + 1][...].astype(F32)
    count = refs[0].shape[0]
    for left, span in ((refs[0], slice(RIM, RIM + count)), (refs[1], slice(0, RIM))):
        part = plain(left[...], held)
        for source in range(job + 2, job + 2 + number):
            part = part + refs[source][span, :].astype(F32)
        scratch[span, :] = part
    total = None
    for tap in range(TAPS):
        first = RIM - (TAPS - 1) + tap
        term = taps[tap : tap + 1] * scratch[first : first + count, :]
        total = term if total is None else total + term
    return total / (1.0 + jnp.exp(-total))


def plain(a, b):
    return jnp.dot(a, b, preferred_element_type=F32)


def unit_rows(values):
    return values * lax.rsqrt(jnp.sum(values * values, axis=-1, keepdims=True) + EPS)


def iotas(size):
    return (
        lax.broadcasted_iota(jnp.int32, (size, size), 0),
        lax.broadcasted_iota(jnp.int32, (size, size), 1),
    )


def prepare(decay, beta, sp, after=()):
    heads, count = decay.shape
    outs = [
        jax.ShapeDtypeStruct((heads, count), F32),
        jax.ShapeDtypeStruct((count, heads), F32),
        jax.ShapeDtypeStruct((count, heads), F32),
    ]

    def body(sp_ref, decay_ref, beta_ref, row_ref, col_ref, rate_ref):
        rows, cols = iotas(count)
        row_ref[...] = dot_full(decay_ref[...], (rows <= cols).astype(F32))
        col_ref[...] = dot_full((cols <= rows).astype(F32), decay_ref[...], NT)
        rate_ref[...] = dot_full((rows == cols).astype(F32), beta_ref[...], NT)

    return call(body, sp, [decay, beta], [whole(decay), whole(beta)], outs, after=after)


def inverses(systems):
    size = systems[0].shape[0]
    rows, cols = iotas(size)
    eye = (rows == cols).astype(F32)
    cut = [split(low) for low in systems]
    mask = ((rows >> 2) == (cols >> 2)).astype(F32).astype(BF16)
    near = [c[0] * mask for c in cut]
    square = [plain(n, n) for n in near]
    cube = [plain(n, s.astype(BF16)) for n, s in zip(near, square)]
    inv = [
        (eye - n.astype(F32) + s - c).astype(BF16) for n, s, c in zip(near, square, cube)
    ]
    shift = 2
    while (1 << shift) < size:
        inside = ((rows >> (shift + 1)) == (cols >> (shift + 1))) & (
            (rows >> shift) != (cols >> shift)
        )
        mask = inside.astype(F32).astype(BF16)
        middle = [plain(c[0] * mask, x).astype(BF16) for c, x in zip(cut, inv)]
        inv = [x - plain(x, m).astype(BF16) for x, m in zip(inv, middle)]
        shift += 1
    rest = [
        eye - x.astype(F32) - plain(packed_left(c), jnp.concatenate([x, x], axis=0))
        for c, x in zip(cut, inv)
    ]
    return [x.astype(F32) + plain(x, r.astype(BF16)) for x, r in zip(inv, rest)]


def key_phase(gathered, first, number, count, tables, sp, after=()):
    inputs, specs, jobs = gathered
    received = (len(inputs) - 2) // len(jobs) - 2
    at = len(inputs)
    inputs = inputs + tables
    specs = specs + [whole(table) for table in tables]
    half = count // 2
    heads = range(number // 2)
    outs = [
        jax.ShapeDtypeStruct((len(heads), count, HEAD), F32),
        jax.ShapeDtypeStruct((len(heads), HEAD, count), F32),
        jax.ShapeDtypeStruct((number, 3, half, half), F32),
        jax.ShapeDtypeStruct((number, count, HEAD), F32),
        jax.ShapeDtypeStruct((number, HEAD, HEAD), F32),
    ]
    total = len(inputs)

    def body(sp_ref, *refs):
        key_ref, turned_ref, solve_ref, write_ref, trans_ref, scratch = refs[total:]
        sums, sums_col, beta_col = (ref[...] for ref in refs[at : at + 3])
        rows, cols = iotas(half)
        keys, systems, crosses = [], [], []
        for i, job in enumerate(jobs):
            key = unit_rows(activate(refs, job, received, scratch))
            keys.append(key)
            key_ref[i] = key
            turned_ref[i] = key.T
            low, high = split(key[:half]), split(key[half:])
            low_left, high_left = packed_left(low), packed_left(high)
            low_right, high_right = packed_turned(low), packed_turned(high)
            alike = (
                fold(low_left, low_right, NT),
                fold(high_left, high_right, NT),
                fold(high_left, low_right, NT),
            )
            for r in (first + 2 * i, first + 2 * i + 1):
                row, col, rate = sums[r : r + 1], sums_col[:, r : r + 1], beta_col[:, r : r + 1]
                for b, span in enumerate((slice(0, half), slice(half, count))):
                    fade = jnp.exp(jnp.minimum(col[span] - row[:, span], 0.0))
                    systems.append(jnp.where(cols < rows, rate[span] * fade * alike[b], 0.0))
                fade = jnp.exp(jnp.minimum(col[half:] - row[:, :half], 0.0))
                crosses.append(rate[half:] * fade * alike[2])
        solved = inverses(systems)
        left = [packed_left(split(x)) for x in solved]
        middle = [
            mul(cross, solved[2 * j]) for j, cross in enumerate(crosses)
        ]
        corner = [
            -fold(left[2 * j + 1], packed_right(split(m))) for j, m in enumerate(middle)
        ]
        keep = sp_ref[1].astype(F32)
        eye = (lax.broadcasted_iota(jnp.int32, (HEAD, HEAD), 0)
               == lax.broadcasted_iota(jnp.int32, (HEAD, HEAD), 1)).astype(F32)
        for j in range(number):
            r, key = first + j, keys[j // 2]
            row, col, rate = sums[r : r + 1], sums_col[:, r : r + 1], beta_col[:, r : r + 1]
            for which, part in enumerate((solved[2 * j], solved[2 * j + 1], corner[j])):
                solve_ref[j, which] = part
            right = (rate * jnp.exp(col)) * key
            right_low = packed_right(split(right[:half]))
            right_high = packed_right(split(right[half:]))
            write_low = fold(left[2 * j], right_low)
            write_high = fold(packed_left(split(corner[j])), right_low) + fold(
                left[2 * j + 1], right_high
            )
            write_ref[j, :half] = write_low
            write_ref[j, half:] = write_high
            tail = jnp.exp(row[:, count - 1 :] - row)
            trailing = turned_ref[j // 2] * tail
            moved = mul(trailing[:, :half], write_low) + mul(trailing[:, half:], write_high)
            gone = jnp.exp(row[:, count - 1 :])
            trans_ref[j] = keep * (gone * eye - moved)

    return call(
        body, sp, inputs, specs, outs, [pltpu.VMEM((RIM + count, HEAD), F32)], after=after,
    )


def value_phase(gathered, first, number, count, tables, turned, solve, sp, after=()):
    inputs, specs, jobs = gathered
    received = (len(inputs) - 2) // len(jobs) - 2
    at = len(inputs)
    inputs = inputs + tables + [turned, solve]
    specs = specs + [whole(a) for a in inputs[at:]]
    half = count // 2
    outs = [
        jax.ShapeDtypeStruct((number, count, HEAD), F32),
        jax.ShapeDtypeStruct((number, HEAD, HEAD), BF16),
    ]
    total = len(inputs)

    def body(sp_ref, *refs):
        write_ref, trans_ref, scratch = refs[total:]
        sums, beta_col = refs[at][...], refs[at + 2][...]
        turned_ref, solve_ref = refs[at + 3 : at + 5]
        for i, job in enumerate(jobs):
            values = activate(refs, job, received, scratch)
            for j in (2 * i, 2 * i + 1):
                r = first + j
                row, rate = sums[r : r + 1], beta_col[:, r : r + 1]
                right = rate * values[:, (j % 2) * HEAD : (j % 2 + 1) * HEAD]
                low = packed_right(split(right[:half]))
                high = packed_right(split(right[half:]))
                top, bottom, side = [
                    packed_left(split(solve_ref[j, which])) for which in range(3)
                ]
                write_low = fold(top, low)
                write_high = fold(side, low) + fold(bottom, high)
                write_ref[j, :half] = write_low
                write_ref[j, half:] = write_high
                trailing = turned_ref[i] * jnp.exp(row[:, count - 1 :] - row)
                trans_ref[j] = (
                    mul(trailing[:, :half], write_low) + mul(trailing[:, half:], write_high)
                ).astype(BF16)

    return call(
        body, sp, inputs, specs, outs, [pltpu.VMEM((RIM + count, 2 * HEAD), F32)], after=after,
    )


def query_phase(gathered, number, count, tables, parts, sp, after=()):
    inputs, specs, jobs = gathered
    received = (len(inputs) - 2) // len(jobs) - 2
    at = len(inputs)
    inputs = inputs + tables
    for part in parts:
        inputs = inputs + list(part)
    specs = specs + [whole(a) for a in inputs[at:]]
    half = count // 2
    outs = [
        jax.ShapeDtypeStruct((number, count, HEAD), F32),
        jax.ShapeDtypeStruct((number, count, HEAD), F32),
    ]
    total = len(inputs)
    group = parts[0][0].shape[0]

    def body(sp_ref, *refs):
        inner_ref, query_ref, scratch = refs[total:]
        sums, sums_col = refs[at][...], refs[at + 1][...]
        rows, cols = iotas(half)
        low, high = slice(0, half), slice(half, count)
        for i, job in enumerate(jobs):
            place = at + 3 + 3 * (i // group)
            key_ref, write_k_ref, write_v_ref = refs[place : place + 3]
            query = unit_rows(activate(refs, job, received, scratch))
            key = key_ref[i % group]
            left = [packed_left(split(query[span])) for span in (low, high)]
            right = [packed_turned(split(key[span])) for span in (low, high)]
            alike = {
                (0, 0): fold(left[0], right[0], NT),
                (1, 1): fold(left[1], right[1], NT),
                (1, 0): fold(left[1], right[0], NT),
            }
            for j in (2 * i, 2 * i + 1):
                row, col = sums[j : j + 1], sums_col[:, j : j + 1]
                wrote = [
                    split(
                        jnp.concatenate(
                            [part[j % (2 * group), span] for part in (write_v_ref, write_k_ref)],
                            axis=1,
                        )
                    )
                    for span in (low, high)
                ]
                tall = [jnp.concatenate([w[0], w[0]], axis=0) for w in wrote]
                read = [None, None]
                for (t, s), product in alike.items():
                    fade = jnp.exp(
                        jnp.minimum(col[(low, high)[t]] - row[:, (low, high)[s]], 0.0)
                    )
                    attend = fade * product
                    if t == s:
                        attend = jnp.where(cols <= rows, attend, 0.0)
                    attend = split(attend)
                    part = jnp.dot(
                        packed_left(attend), tall[s], preferred_element_type=F32
                    ) + jnp.dot(attend[0], wrote[s][1], preferred_element_type=F32)
                    read[t] = part if read[t] is None else read[t] + part
                for t, span in enumerate((low, high)):
                    inner_ref[j, span] = read[t][:, :HEAD]
                    query_ref[j, span] = jnp.exp(col[span]) * query[span] - read[t][:, HEAD:]

    return call(
        body, sp, inputs, specs, outs, [pltpu.VMEM((RIM + count, HEAD), F32)], after=after,
    )


def join_cores(mine_a, other_a, mine_b, other_b, sp, place, after=()):
    half = mine_a.shape[0] // 2
    inputs = [mine_a, other_a, mine_b, other_b]
    outs = [
        jax.ShapeDtypeStruct((2, half, HEAD, HEAD), BF16),
        jax.ShapeDtypeStruct((half, HEAD, HEAD), BF16),
    ]

    def body(sp_ref, *refs):
        core = sp_ref[place]
        for i in range(half):
            h = core * half + i
            held = [ref[h].astype(F32) for ref in refs[:4]]
            early_a, early_b = [jnp.where(core == 0, held[k], held[k + 1]) for k in (0, 2)]
            late_a, late_b = [jnp.where(core == 0, held[k + 1], held[k]) for k in (0, 2)]
            late = packed_left(split(late_a))
            write = (fold(late, packed_right(split(early_b))) + late_b).astype(BF16)
            refs[4][0, i] = fold(late, packed_right(split(early_a))).astype(BF16)
            refs[4][1, i] = write
            refs[5][i] = write

    return call(body, sp, inputs, [whole(a) for a in inputs], outs, after=after)


def run_chain(parts, sp, after=()):
    half = parts[0].shape[0]
    out = jax.ShapeDtypeStruct((half, HEAD, HEAD), BF16)

    def body(sp_ref, *refs):
        for i in range(half):
            state = refs[0][i].astype(F32)
            for ref in refs[1:-1]:
                left = ref[0, i]
                state = fold(
                    packed_left((left, jnp.zeros_like(left))), packed_right(split(state))
                ) + ref[1, i].astype(F32)
            refs[-1][i] = state.astype(BF16)

    return call(body, sp, parts, [whole(a) for a in parts], [out], after=after)[0]


def shifted(value, steps):
    count = lax.axis_size("ctx")
    return lax.ppermute(value, "ctx", [(i, i + steps) for i in range(count - steps)])


def swapped(value):
    count = lax.axis_size("ctx")
    return lax.ppermute(value, "ctx", [(i, i ^ 1) for i in range(count)])


def enter_far(joined):
    chips = lax.axis_size("ctx") // 2
    joined = shifted(joined, 2)
    step = 1
    while step < chips:
        early = shifted(joined, 2 * step).astype(F32)
        late = joined.astype(F32)
        both = jnp.einsum("hij,xhjk->xhik", late[0], early, precision=lax.Precision.HIGHEST)
        joined = (both + late * jnp.array([0.0, 1.0], F32)[:, None, None, None]).astype(BF16)
        step *= 2
    return joined[1]


def finish(inner, query, groups, gain, sp, place):
    inputs = [inner, query, gain]
    for part in groups:
        inputs += list(part)
    number, count = inner.shape[:2]
    group = groups[0][2].shape[0]
    half = group // 2
    out = jax.ShapeDtypeStruct((count, number * HEAD), BF16)

    def body(sp_ref, inner_ref, query_ref, gain_ref, *refs):
        core = sp_ref[place]
        keep = sp_ref[1].astype(F32)
        for j in range(number):
            at, h = 4 * (j // group), j % group
            mine, other, early_a, early_b = refs[at : at + 4]
            own, far = mine[h % half].astype(F32), other[h % half].astype(F32)
            state = jnp.where((core == 0) == (h < half), own, far)
            stepped = mul(early_a[h], state) + early_b[h].astype(F32)
            state = keep * jnp.where(core == 0, state, stepped)
            read = inner_ref[j] + mul(query_ref[j], state)
            scale = lax.rsqrt(jnp.mean(read * read, axis=-1, keepdims=True) + EPS)
            cols = slice(j * HEAD, (j + 1) * HEAD)
            refs[-1][:, cols] = (read * scale * gain_ref[...]).astype(BF16)

    return call(body, sp, inputs, [whole(a) for a in inputs], [out])[0]


def per_device(
    hidden,
    w_query,
    w_key,
    payload_projection_matrix,
    conv_weight,
    log_decay,
    beta_rate,
    norm_gain,
    head_order,
    block_starts,
):
    count = hidden.shape[0]
    ranks = lax.axis_size("head")
    chips = lax.axis_size("ctx") // 2
    total_heads = head_order.shape[0]
    key_heads = total_heads // ranks
    serve = lax.axis_index("head")
    core = lax.axis_index("ctx") % 2
    keep = 1 - block_starts[0]
    place = 2 + total_heads
    w_value = payload_projection_matrix

    rim = shifted(hidden[count - RIM :], 1) * keep.astype(BF16)
    sp = jnp.concatenate(
        [jnp.stack([serve, keep]), head_order, jnp.stack([core])]
    ).astype(jnp.int32)

    size = max(1, key_heads // 2)
    groups = [list(range(g, g + size)) for g in range(0, key_heads, size)]
    everyone = list(range(key_heads))

    def send(heads, width, weight, after=()):
        return partial_sums(key_heads, ranks, heads, width, hidden, rim, weight, sp, after)

    def gathered(heads, width, weight, base, received):
        return gather_specs(
            key_heads, heads, width, hidden, rim, weight, conv_weight, base, received
        )

    part_k = send(everyone, HEAD, w_key)
    got_k = exchange(part_k)
    tables = list(prepare(log_decay, beta_rate, sp, after=part_k[:1]))
    part_v = [send(groups[0], 2 * HEAD, w_value, after=tables[:1])]
    last = part_v[0][:1]
    keyed = []
    for g, heads in enumerate(groups):
        keyed.append(
            key_phase(
                gathered([(h, h) for h in heads], HEAD, w_key, total_heads, got_k),
                2 * heads[0], 2 * size, count, tables, sp, after=last,
            )
        )
        last = keyed[-1][4:]
        if g + 1 < len(groups):
            part_v.append(send(groups[g + 1], 2 * HEAD, w_value, after=last))
            last = part_v[-1][:1]
    got_v = [exchange(part) for part in part_v]
    other_a = [swapped(group[4]) for group in keyed]

    entered, wrote = [], []
    part_q = None
    for g, heads in enumerate(groups):
        write_v, trans_b = value_phase(
            gathered([(h, i) for i, h in enumerate(heads)], 2 * HEAD, w_value, total_heads, got_v[g]),
            2 * heads[0], 2 * size, count, tables, keyed[g][1], keyed[g][2], sp, after=last,
        )
        wrote.append((keyed[g][0], keyed[g][3], write_v))
        other_b = swapped(trans_b)
        last = [trans_b]
        if part_q is None:
            part_q = send(everyone, HEAD, w_query, after=last)
            got_q = exchange(part_q)
            last = part_q[:1]
        joined, joined_b = join_cores(
            keyed[g][4], other_a[g], trans_b, other_b, sp, place, after=last
        )
        last = [joined_b]
        entered.append([joined, joined_b, other_b])
    inner, query = query_phase(
        gathered([(h, h) for h in everyone], HEAD, w_query, 0, got_q),
        2 * key_heads, count, tables, wrote, sp, after=last,
    )
    last = [query]
    ends = []
    for g, (joined, joined_b, other_b) in enumerate(entered):
        if chips <= 4:
            far = [shifted(joined_b, 2 * (chips - 1))]
            far += [shifted(joined, 2 * d) for d in range(chips - 2, 0, -1)]
            mine = run_chain(far, sp, after=last)
            last = [mine]
        else:
            mine = enter_far(joined)
        ends.append((mine, swapped(mine), other_a[g], other_b))
    return finish(inner, query, ends, norm_gain[None, :], sp, place)


def solution(mesh):
    return jax.shard_map(
        per_device,
        mesh=mesh,
        in_specs=(
            P("ctx", None),
            P("head", None),
            P("head", None),
            P("head", None),
            P(),
            P("head", "ctx"),
            P("head", "ctx"),
            P(),
            P(),
            P("ctx"),
        ),
        out_specs=P("ctx", "head"),
        check_vma=False,
    )
```

time: 98.7 us -> 86.1 us (0.87)
  Pallas kernels: 40 us -> 32.5 us
  waiting for transfers between devices: 8.92 us -> 5.9 us
  local copies, waits for them, and re-layouts: 6.07 us -> 3.69 us
  starting transfers between devices: 40.4 us -> 41.6 us
    pallas_call x16 -> x15, Pallas kernels: 40 us -> 32.5 us  [call(): pl.pallas_call(inner, grid_spec=pltpu.PrefetchScalarGridSpec(num_scalar_p...]
    all_to_all x1 -> x0, starting transfers between devices: 4.07 us -> none  [per_device(): lax.all_to_all(rim_products(plan, rim, w_key, ranks, sp, after=sent), 'he...]
    ppermute x12, starting transfers between devices: 13.5 us -> 16.9 us  [exchange(): lax.ppermute(part, 'head', [(i, i ^ unit + 1) for i in range(ranks)])]
    unnamed x34 -> x20, local copies, waits for them, and re-layouts: 5.36 us -> 2.85 us
    all_to_all x1 -> x0, waiting for transfers between devices: 2.48 us -> none  [per_device(): lax.all_to_all(rim_products(plan, rim, w_key, ranks, sp, after=sent), 'he...]
    ppermute x6 -> x7, waiting for transfers between devices: 2.49 us -> 0.04 us  [shifted(): lax.ppermute(value, 'ctx', [(i, i + steps) for i in range(count - steps)])]
    ppermute x12, waiting for transfers between devices: 3.94 us -> 4.95 us  [exchange(): lax.ppermute(part, 'head', [(i, i ^ unit + 1) for i in range(ranks)])]
    ppermute x4 -> x6, starting transfers between devices: 1.42 us -> 2.39 us  [swapped(): return lax.ppermute(value, 'ctx', [(i, i ^ 1) for i in range(count)])]
  transfers between devices with their start and end apart: 23 -> 25, of which waited for: 4 -> 4; matrix products, arithmetic and copies ran while one was open for 1% -> 1% of each run, Pallas kernels for 38% -> 33%
where the time goes in v3:
time: 86.1 us; the launch traced here: 85.5 us
  starting transfers between devices  41.6 us (48%)
  Pallas kernels  32.5 us (38%)
  waiting for transfers between devices  5.9 us (7%)
  local copies, waits for them, and re-layouts  3.69 us (4%)
  between operations  1.01 us (1%)
    pallas_call x15, Pallas kernels, call(): pl.pallas_call(inner, grid_spec=pltpu.PrefetchScalarGridSpec(num_scalar_p...  32.5 us
    ppermute x7, starting transfers between devices, shifted(): lax.ppermute(value, 'ctx', [(i, i + steps) for i in range(count - steps)])  22.3 us
    ppermute x12, starting transfers between devices, exchange(): lax.ppermute(part, 'head', [(i, i ^ unit + 1) for i in range(ranks)])  16.9 us
    ppermute x12, waiting for transfers between devices, exchange(): lax.ppermute(part, 'head', [(i, i ^ unit + 1) for i in range(ranks)])  4.95 us
    unnamed x20, local copies, waits for them, and re-layouts  2.85 us
    ppermute x6, starting transfers between devices, swapped(): return lax.ppermute(value, 'ctx', [(i, i ^ 1) for i in range(count)])  2.39 us
  transfers between devices with their start and end apart: 25, of which 4 were waited for; matrix products, arithmetic and copies ran while one was open for 1% of the time, Pallas kernels for 33%

profile of v3, /device:TPU:0, one launch (start us, length us, event | category | flops | bytes accessed | tf_op | source)
XLA Modules:
  0.0 85.5 jit_solution(16367580294371224158)
XLA Ops:
  0.0 0.8 slice.3
  0.8 2.3 %collective-permute-start = (bf16[16,2048]{1,0:T(8,128)(2,1)S(1)}, bf16[16,2048]{1,0:T(8,128)(2,1)S(1)}, u32[]{:S(2)}, u32[]{:S(2)}) collective-permute-start(bf16[16,2048]{1,0:T(8,128)(2,1)S(1)} %slice.3), channel_id=1, source_target_pairs={{0,4},{4,8},{8,12},{12,16},{16,20},{20,24},{24,28},{1,5},{5,9},{9,... | collective-permute-start | bytes 196616 | tf_op jit(solution)/shard_map/ppermute | solution.py:468
  3.9 0.7 pad_add_fusion.sp_ref
  4.6 0.0 collective-permute-done
  4.6 0.0 copy-start.1
  4.6 1.6 %copy-done.1 = bf16[512,2048]{1,0:T(8,128)(2,1)S(1)} copy-done((bf16[512,2048]{1,0:T(8,128)(2,1)S(1)}, bf16[512,2048]{1,0:T(8,128)(2,1)}, u32[]{:S(2)}) %copy-start.1) | copy-done | bytes 2097176
  6.2 1.2 %copy-done.4 = bf16[256,2048]{1,0:T(8,128)(2,1)S(1)} copy-done((bf16[256,2048]{1,0:T(8,128)(2,1)S(1)}, bf16[256,2048]{1,0:T(8,128)(2,1)}, u32[]{:S(2)}) %copy-start.4) | copy-done | bytes 1048600
  7.4 2.0 %shard_map.100 = (bf16[272,512]{1,0:T(8,128)(2,1)S(1)}, bf16[272,512]{1,0:T(8,128)(2,1)S(1)}, bf16[272,512]{1,0:T(8,128)(2,1)S(1)}) custom-call(s32[19]{0:T(128)S(1)} %pad_add_fusion.sp_ref, bf16[256,2048]{1,0:T(8,128)(2,1)S(1)} %copy-done.4, bf16[16,2048]{1,0:T(8,128)(2,1)S(1)} %broadcast_multiply_fusion.refs_1_, bf16[512,2048]{1,0:T(8,128)(2,1)S(1)} %copy-done.1, ...), custom_call_target="tpu_custom_call" | custom-call | flops 1000 | bytes 1000 | tf_op jit(solution)/shard_map/pallas_call | solution.py:85
  9.4 2.4 %collective-permute-start.4 = (bf16[272,512]{1,0:T(8,128)(2,1)S(1)}, bf16[272,512]{1,0:T(8,128)(2,1)S(1)}, u32[]{:S(2)}, u32[]{:S(2)}) collective-permute-start(bf16[272,512]{1,0:T(8,128)(2,1)S(1)} %get-tuple-element.40.refs_2_), channel_id=1, source_target_pairs={{0,1},{1,0},{2,3},{3,2},{4,5},{5,4},{6,7},{7,6},{8,9},{9,8},{10,11... | collective-permute-start | bytes 835592 | tf_op jit(solution)/shard_map/ppermute | solution.py:140
  11.8 1.5 %collective-permute-start.5 = (bf16[272,512]{1,0:T(8,128)(2,1)S(1)}, bf16[272,512]{1,0:T(8,128)(2,1)S(1)}, u32[]{:S(2)}, u32[]{:S(2)}) collective-permute-start(bf16[272,512]{1,0:T(8,128)(2,1)S(1)} %get-tuple-element.47), channel_id=1, source_target_pairs={{0,2},{1,3},{2,0},{3,1},{4,6},{5,7},{6,4},{7,5},{8,10},{9,11},{10,... | collective-permute-start | bytes 835592 | tf_op jit(solution)/shard_map/ppermute | solution.py:140
  13.3 0.0 collective-permute-start.6
  13.3 1.2 %shard_map.101 = (f32[8,256]{1,0:T(8,128)S(1)}, f32[256,8]{1,0:T(8,128)S(1)}, f32[256,8]{1,0:T(8,128)S(1)}) custom-call(s32[19]{0:T(128)S(1)} %pad_add_fusion.sp_ref, f32[8,256]{1,0:T(8,128)S(1)} %copy-done.7, f32[8,256]{1,0:T(8,128)S(1)} %copy-done.8, bf16[272,512]{1,0:T(8,128)(2,1)S(1)} %get-tuple-element.40.refs_2_), custom_call_target="tpu_custom_call" | custom-call | flops 1000 | bytes 1000 | tf_op jit(solution)/shard_map/pallas_call | solution.py:85
  14.5 0.0 copy-start.2
  14.6 0.0 copy-start.6
  14.6 1.3 %shard_map.102 = (bf16[272,512]{1,0:T(8,128)(2,1)S(1)}, bf16[272,512]{1,0:T(8,128)(2,1)S(1)}, bf16[272,512]{1,0:T(8,128)(2,1)S(1)}) custom-call(s32[19]{0:T(128)S(1)} %pad_add_fusion.sp_ref, bf16[256,2048]{1,0:T(8,128)(2,1)S(1)} %copy-done.5, bf16[16,2048]{1,0:T(8,128)(2,1)S(1)} %broadcast_multiply_fusion.refs_1_, bf16[512,4096]{1,0:T(8,128)(2,1)S(1)} %copy-done, ...), custom_call_target="tpu_custom_call" | custom-call | flops 1000 | bytes 1000 | tf_op jit(solution)/shard_map/pallas_call | solution.py:85
  15.9 2.0 %collective-permute-start.1 = (bf16[272,512]{1,0:T(8,128)(2,1)S(1)}, bf16[272,512]{1,0:T(8,128)(2,1)S(1)}, u32[]{:S(2)}, u32[]{:S(2)}) collective-permute-start(bf16[272,512]{1,0:T(8,128)(2,1)S(1)} %get-tuple-element.42.refs_15_), channel_id=1, source_target_pairs={{0,1},{1,0},{2,3},{3,2},{4,5},{5,4},{6,7},{7,6},{8,9},{9,8},{10,11... | collective-permute-start | bytes 835592 | tf_op jit(solution)/shard_map/ppermute | solution.py:140
  17.9 1.5 %collective-permute-start.2 = (bf16[272,512]{1,0:T(8,128)(2,1)S(1)}, bf16[272,512]{1,0:T(8,128)(2,1)S(1)}, u32[]{:S(2)}, u32[]{:S(2)}) collective-permute-start(bf16[272,512]{1,0:T(8,128)(2,1)S(1)} %get-tuple-element.43), channel_id=1, source_target_pairs={{0,2},{1,3},{2,0},{3,1},{4,6},{5,7},{6,4},{7,5},{8,10},{9,11},{10,... | collective-permute-start | bytes 835592 | tf_op jit(solution)/shard_map/ppermute | solution.py:140
  19.4 0.0 collective-permute-done.4.refs_4_.refs_9_
  19.4 2.0 %collective-permute-start.3 = (bf16[272,512]{1,0:T(8,128)(2,1)S(1)}, bf16[272,512]{1,0:T(8,128)(2,1)S(1)}, u32[]{:S(2)}, u32[]{:S(2)}) collective-permute-start(bf16[272,512]{1,0:T(8,128)(2,1)S(1)} %get-tuple-element.44), channel_id=1, source_target_pairs={{0,3},{1,2},{2,1},{3,0},{4,7},{5,6},{6,5},{7,4},{8,11},{9,10},{10,... | collective-permute-start | bytes 835592 | tf_op jit(solution)/shard_map/ppermute | solution.py:140
  21.4 3.9 %collective-permute-done.5.refs_5_.refs_10_ = bf16[272,512]{1,0:T(8,128)(2,1)S(1)} collective-permute-done((bf16[272,512]{1,0:T(8,128)(2,1)S(1)}, bf16[272,512]{1,0:T(8,128)(2,1)S(1)}, u32[]{:S(2)}, u32[]{:S(2)}) %collective-permute-start.5) | collective-permute-done | bytes 278560 | tf_op jit(solution)/shard_map/ppermute | solution.py:140
  25.3 0.7 collective-permute-done.6.refs_6_.refs_11_
  26.0 4.9 %shard_map.103 = (f32[2,256,128]{2,1,0:T(8,128)S(1)}, f32[2,128,256]{2,1,0:T(8,128)S(1)}, f32[4,3,128,128]{3,2,1,0:T(8,128)S(1)}, f32[4,256,128]{2,1,0:T(8,128)S(1)}, f32[4,128,128]{2,1,0:T(8,128)S(1)}) custom-call(s32[19]{0:T(128)S(1)} %pad_add_fusion.sp_ref, bf16[256,2048]{1,0:T(8,128)(2,1)S(1)} %copy-done.5, ...), custom_call_target="tpu_custom_call" | custom-call | flops 1000 | bytes 1000 | tf_op jit(solution)/shard_map/pallas_call | solution.py:85
  30.9 1.3 %shard_map.104 = (bf16[272,512]{1,0:T(8,128)(2,1)S(1)}, bf16[272,512]{1,0:T(8,128)(2,1)S(1)}, bf16[272,512]{1,0:T(8,128)(2,1)S(1)}) custom-call(s32[19]{0:T(128)S(1)} %pad_add_fusion.sp_ref, bf16[256,2048]{1,0:T(8,128)(2,1)S(1)} %copy-done.5, bf16[16,2048]{1,0:T(8,128)(2,1)S(1)} %broadcast_multiply_fusion.refs_1_, bf16[512,4096]{1,0:T(8,128)(2,1)S(1)} %copy-done, ...), custom_call_target="tpu_custom_call" | custom-call | flops 1000 | bytes 1000 | tf_op jit(solution)/shard_map/pallas_call | solution.py:85
  32.3 1.5 %collective-permute-start.10 = (bf16[272,512]{1,0:T(8,128)(2,1)S(1)}, bf16[272,512]{1,0:T(8,128)(2,1)S(1)}, u32[]{:S(2)}, u32[]{:S(2)}) collective-permute-start(bf16[272,512]{1,0:T(8,128)(2,1)S(1)} %get-tuple-element.52.refs_15_), channel_id=1, source_target_pairs={{0,1},{1,0},{2,3},{3,2},{4,5},{5,4},{6,7},{7,6},{8,9},{9,8},{10,11... | collective-permute-start | bytes 835592 | tf_op jit(solution)/shard_map/ppermute | solution.py:140
  33.8 0.9 %collective-permute-start.11 = (bf16[272,512]{1,0:T(8,128)(2,1)S(1)}, bf16[272,512]{1,0:T(8,128)(2,1)S(1)}, u32[]{:S(2)}, u32[]{:S(2)}) collective-permute-start(bf16[272,512]{1,0:T(8,128)(2,1)S(1)} %get-tuple-element.63), channel_id=1, source_target_pairs={{0,2},{1,3},{2,0},{3,1},{4,6},{5,7},{6,4},{7,5},{8,10},{9,11},{10,... | collective-permute-start | bytes 835592 | tf_op jit(solution)/shard_map/ppermute | solution.py:140
  34.7 1.1 %collective-permute-start.13 = (f32[4,128,128]{2,1,0:T(8,128)S(1)}, f32[4,128,128]{2,1,0:T(8,128)S(1)}, u32[]{:S(2)}, u32[]{:S(2)}) collective-permute-start(f32[4,128,128]{2,1,0:T(8,128)S(1)} %get-tuple-element.51.refs_8_.refs_0_), channel_id=1, source_target_pairs={{0,4},{4,0},{8,12},{12,8},{16,20},{20,16},{24,28},{28,24},{1,5},{5... | collective-permute-start | bytes 786440 | tf_op jit(solution)/shard_map/ppermute | solution.py:473
  35.8 4.9 %shard_map.105 = (f32[2,256,128]{2,1,0:T(8,128)S(1)}, f32[2,128,256]{2,1,0:T(8,128)S(1)}, f32[4,3,128,128]{3,2,1,0:T(8,128)S(1)}, f32[4,256,128]{2,1,0:T(8,128)S(1)}, f32[4,128,128]{2,1,0:T(8,128)S(1)}) custom-call(s32[19]{0:T(128)S(1)} %pad_add_fusion.sp_ref, bf16[256,2048]{1,0:T(8,128)(2,1)S(1)} %copy-done.5, ...), custom_call_target="tpu_custom_call" | custom-call | flops 1000 | bytes 1000 | tf_op jit(solution)/shard_map/pallas_call | solution.py:85
  40.8 1.5 %collective-permute-start.12 = (bf16[272,512]{1,0:T(8,128)(2,1)S(1)}, bf16[272,512]{1,0:T(8,128)(2,1)S(1)}, u32[]{:S(2)}, u32[]{:S(2)}) collective-permute-start(bf16[272,512]{1,0:T(8,128)(2,1)S(1)} %get-tuple-element.64), channel_id=1, source_target_pairs={{0,3},{1,2},{2,1},{3,0},{4,7},{5,6},{6,5},{7,4},{8,11},{9,10},{10,... | collective-permute-start | bytes 835592 | tf_op jit(solution)/shard_map/ppermute | solution.py:140
  42.3 2.6 %shard_map.106 = (f32[4,256,128]{2,1,0:T(8,128)S(1)}, bf16[4,128,128]{2,1,0:T(8,128)(2,1)S(1)}) custom-call(s32[19]{0:T(128)S(1)} %pad_add_fusion.sp_ref, bf16[256,2048]{1,0:T(8,128)(2,1)S(1)} %copy-done.5, bf16[16,2048]{1,0:T(8,128)(2,1)S(1)} %broadcast_multiply_fusion.refs_1_, bf16[512,4096]{1,0:T(8,128)(2,1)S(1)} %copy-done, ...), custom_call_target="tpu_custom_call" | custom-call | flops 1000 | bytes 1000 | tf_op jit(solution)/shard_map/pallas_call | solution.py:85
  44.9 0.1 collective-permute-start.14
  45.0 2.0 %shard_map.107 = (bf16[272,512]{1,0:T(8,128)(2,1)S(1)}, bf16[272,512]{1,0:T(8,128)(2,1)S(1)}, bf16[272,512]{1,0:T(8,128)(2,1)S(1)}) custom-call(s32[19]{0:T(128)S(1)} %pad_add_fusion.sp_ref, bf16[256,2048]{1,0:T(8,128)(2,1)S(1)} %copy-done.5, bf16[16,2048]{1,0:T(8,128)(2,1)S(1)} %broadcast_multiply_fusion.refs_1_, bf16[512,2048]{1,0:T(8,128)(2,1)S(1)} %copy-done.3, ...), custom_call_target="tpu_custom_call" | custom-call | flops 1000 | bytes 1000 | tf_op jit(solution)/shard_map/pallas_call | solution.py:85
  46.9 1.1 %collective-permute-start.7 = (bf16[272,512]{1,0:T(8,128)(2,1)S(1)}, bf16[272,512]{1,0:T(8,128)(2,1)S(1)}, u32[]{:S(2)}, u32[]{:S(2)}) collective-permute-start(bf16[272,512]{1,0:T(8,128)(2,1)S(1)} %get-tuple-element.55.refs_4_), channel_id=1, source_target_pairs={{0,1},{1,0},{2,3},{3,2},{4,5},{5,4},{6,7},{7,6},{8,9},{9,8},{10,11... | collective-permute-start | bytes 835592 | tf_op jit(solution)/shard_map/ppermute | solution.py:140
  48.0 1.0 %collective-permute-start.8 = (bf16[272,512]{1,0:T(8,128)(2,1)S(1)}, bf16[272,512]{1,0:T(8,128)(2,1)S(1)}, u32[]{:S(2)}, u32[]{:S(2)}) collective-permute-start(bf16[272,512]{1,0:T(8,128)(2,1)S(1)} %get-tuple-element.56), channel_id=1, source_target_pairs={{0,2},{1,3},{2,0},{3,1},{4,6},{5,7},{6,4},{7,5},{8,10},{9,11},{10,... | collective-permute-start | bytes 835592 | tf_op jit(solution)/shard_map/ppermute | solution.py:140
  49.0 0.0 collective-permute-done.10.refs_4_.refs_9_
  49.0 1.5 %collective-permute-start.9 = (bf16[272,512]{1,0:T(8,128)(2,1)S(1)}, bf16[272,512]{1,0:T(8,128)(2,1)S(1)}, u32[]{:S(2)}, u32[]{:S(2)}) collective-permute-start(bf16[272,512]{1,0:T(8,128)(2,1)S(1)} %get-tuple-element.57), channel_id=1, source_target_pairs={{0,3},{1,2},{2,1},{3,0},{4,7},{5,6},{6,5},{7,4},{8,11},{9,10},{10,... | collective-permute-start | bytes 835592 | tf_op jit(solution)/shard_map/ppermute | solution.py:140
  50.5 0.3 collective-permute-done.11.refs_5_.refs_10_
  50.8 0.4 collective-permute-start.15
  51.3 0.8 shard_map.108
  52.1 2.4 %shard_map.109 = (f32[4,256,128]{2,1,0:T(8,128)S(1)}, bf16[4,128,128]{2,1,0:T(8,128)(2,1)S(1)}) custom-call(s32[19]{0:T(128)S(1)} %pad_add_fusion.sp_ref, bf16[256,2048]{1,0:T(8,128)(2,1)S(1)} %copy-done.5, bf16[16,2048]{1,0:T(8,128)(2,1)S(1)} %broadcast_multiply_fusion.refs_1_, bf16[512,4096]{1,0:T(8,128)(2,1)S(1)} %copy-done, ...), custom_call_target="tpu_custom_call" | custom-call | flops 1000 | bytes 1000 | tf_op jit(solution)/shard_map/pallas_call | solution.py:85
  54.5 0.1 collective-permute-start.16
  54.7 0.0 collective-permute-done.15.refs_1_.refs_9_
  54.7 6.2 %collective-permute-start.18 = (bf16[2,2,128,128]{3,2,1,0:T(8,128)(2,1)S(1)}, bf16[2,2,128,128]{3,2,1,0:T(8,128)(2,1)S(1)}, u32[]{:S(2)}, u32[]{:S(2)}) collective-permute-start(bf16[2,2,128,128]{3,2,1,0:T(8,128)(2,1)S(1)} %get-tuple-element.73), channel_id=1, source_target_pairs={{0,16},{4,20},{8,24},{12,28},{1,17},{5,21},{9,25},{13,29},{2,18},{... | collective-permute-start | bytes 393224 | tf_op jit(solution)/shard_map/ppermute | solution.py:468
  60.9 0.0 collective-permute-done.16.refs_3_.refs_10_
  60.9 3.6 %collective-permute-start.19 = (bf16[2,2,128,128]{3,2,1,0:T(8,128)(2,1)S(1)}, bf16[2,2,128,128]{3,2,1,0:T(8,128)(2,1)S(1)}, u32[]{:S(2)}, u32[]{:S(2)}) collective-permute-start(bf16[2,2,128,128]{3,2,1,0:T(8,128)(2,1)S(1)} %get-tuple-element.73), channel_id=1, source_target_pairs={{0,8},{4,12},{8,16},{12,20},{16,24},{20,28},{1,9},{5,13},{9,17},{1... | collective-permute-start | bytes 393224 | tf_op jit(solution)/shard_map/ppermute | solution.py:468
  64.5 0.8 shard_map.110
  65.3 1.3 %collective-permute-start.17 = (bf16[2,128,128]{2,1,0:T(8,128)(2,1)S(1)}, bf16[2,128,128]{2,1,0:T(8,128)(2,1)S(1)}, u32[]{:S(2)}, u32[]{:S(2)}) collective-permute-start(bf16[2,128,128]{2,1,0:T(8,128)(2,1)S(1)} %get-tuple-element.67.refs_17_), channel_id=1, source_target_pairs={{0,24},{4,28},{1,25},{5,29},{2,26},{6,30},{3,27},{7,31}} | collective-permute-start | bytes 196616 | tf_op jit(solution)/shard_map/ppermute | solution.py:468
  66.6 1.3 %collective-permute-start.22 = (bf16[2,2,128,128]{3,2,1,0:T(8,128)(2,1)S(1)}, bf16[2,2,128,128]{3,2,1,0:T(8,128)(2,1)S(1)}, u32[]{:S(2)}, u32[]{:S(2)}) collective-permute-start(bf16[2,2,128,128]{3,2,1,0:T(8,128)(2,1)S(1)} %get-tuple-element.74), channel_id=1, source_target_pairs={{0,16},{4,20},{8,24},{12,28},{1,17},{5,21},{9,25},{13,29},{2,18},{... | collective-permute-start | bytes 393224 | tf_op jit(solution)/shard_map/ppermute | solution.py:468
  67.9 0.0 collective-permute-done.9.refs_6_.refs_11_.refs_16_.refs_21_
  67.9 1.3 %collective-permute-start.23 = (bf16[2,2,128,128]{3,2,1,0:T(8,128)(2,1)S(1)}, bf16[2,2,128,128]{3,2,1,0:T(8,128)(2,1)S(1)}, u32[]{:S(2)}, u32[]{:S(2)}) collective-permute-start(bf16[2,2,128,128]{3,2,1,0:T(8,128)(2,1)S(1)} %get-tuple-element.74), channel_id=1, source_target_pairs={{0,8},{4,12},{8,16},{12,20},{16,24},{20,28},{1,9},{5,13},{9,17},{1... | collective-permute-start | bytes 393224 | tf_op jit(solution)/shard_map/ppermute | solution.py:468
  69.2 0.0 collective-permute-done.17.refs_0_
  69.3 6.2 %collective-permute-start.21 = (bf16[2,128,128]{2,1,0:T(8,128)(2,1)S(1)}, bf16[2,128,128]{2,1,0:T(8,128)(2,1)S(1)}, u32[]{:S(2)}, u32[]{:S(2)}) collective-permute-start(bf16[2,128,128]{2,1,0:T(8,128)(2,1)S(1)} %get-tuple-element.70.refs_31_), channel_id=1, source_target_pairs={{0,24},{4,28},{1,25},{5,29},{2,26},{6,30},{3,27},{7,31}} | collective-permute-start | bytes 196616 | tf_op jit(solution)/shard_map/ppermute | solution.py:468
  75.5 0.0 copy-start.9
  75.5 3.8 %shard_map.111 = (f32[8,256,128]{2,1,0:T(8,128)S(1)}, f32[8,256,128]{2,1,0:T(8,128)S(1)}) custom-call(s32[19]{0:T(128)S(1)} %pad_add_fusion.sp_ref, bf16[256,2048]{1,0:T(8,128)(2,1)S(1)} %copy-done.5, bf16[16,2048]{1,0:T(8,128)(2,1)S(1)} %broadcast_multiply_fusion.refs_1_, bf16[512,2048]{1,0:T(8,128)(2,1)S(1)} %copy-done.3, bf16[4,8192]{1,0:T(4,128)(2,1)S(1)} %copy-done.6, ...), custom_call_target="tpu_custom_call" | custom-call | flops 1000 | bytes 1000 | tf_op jit(solution)/shard_map/pallas_call | solution.py:85
  79.3 0.0 collective-permute-done.18.refs_1_
  79.3 0.0 collective-permute-done.19.refs_2_
  79.3 0.9 %shard_map.112.refs_3_ = bf16[2,128,128]{2,1,0:T(8,128)(2,1)S(1)} custom-call(s32[19]{0:T(128)S(1)} %pad_add_fusion.sp_ref, bf16[2,128,128]{2,1,0:T(8,128)(2,1)S(1)} %collective-permute-done.17.refs_0_, bf16[2,2,128,128]{3,2,1,0:T(8,128)(2,1)S(1)} %collective-permute-done.18.refs_1_, bf16[2,2,128,128]{3,2,1,0:T(8,128)(2,1)S(1)} %collective-permute-done.19.refs_2_, ...), custom_call_target="tpu_custom_call" | custom-call | flops 1000 | bytes 1000 | tf_op jit(solution)/shard_map/pallas_call | solution.py:85
  80.2 0.1 collective-permute-start.20
  80.3 0.0 collective-permute-done.21.refs_0_
  80.3 0.0 collective-permute-done.22.refs_1_
  80.4 0.9 %shard_map.113.refs_7_ = bf16[2,128,128]{2,1,0:T(8,128)(2,1)S(1)} custom-call(s32[19]{0:T(128)S(1)} %pad_add_fusion.sp_ref, bf16[2,128,128]{2,1,0:T(8,128)(2,1)S(1)} %collective-permute-done.21.refs_0_, bf16[2,2,128,128]{3,2,1,0:T(8,128)(2,1)S(1)} %collective-permute-done.22.refs_1_, bf16[2,2,128,128]{3,2,1,0:T(8,128)(2,1)S(1)} %collective-permute-done.23.refs_2_, ...), custom_call_target="tpu_custom_call" | custom-call | flops 1000 | bytes 1000 | tf_op jit(solution)/shard_map/pallas_call | solution.py:85
  81.3 0.5 collective-permute-start.24
  81.8 0.0 collective-permute-done.20.refs_4_
  81.8 0.9 %collective-permute-done.24.refs_8_ = bf16[2,128,128]{2,1,0:T(8,128)(2,1)S(1)} collective-permute-done((bf16[2,128,128]{2,1,0:T(8,128)(2,1)S(1)}, bf16[2,128,128]{2,1,0:T(8,128)(2,1)S(1)}, u32[]{:S(2)}, u32[]{:S(2)}) %collective-permute-start.24) | collective-permute-done | bytes 65568 | tf_op jit(solution)/shard_map/ppermute | solution.py:473
  82.7 2.7 %shard_map.114 = bf16[256,1024]{1,0:T(8,128)(2,1)} custom-call(s32[19]{0:T(128)S(1)} %pad_add_fusion.sp_ref, f32[8,256,128]{2,1,0:T(8,128)S(1)} %get-tuple-element.71.refs_0_, f32[8,256,128]{2,1,0:T(8,128)S(1)} %get-tuple-element.72.refs_3_.refs_1_, f32[1,128]{1,0:T(1,128)S(1)} %bitcast.4, bf16[2,128,128]{2,1,0:T(8,128)(2,1)S(1)} %shard_map.112.refs_3_, ...), custom_call_target="tpu_custom_call" | custom-call | flops 1000 | bytes 1000 | tf_op jit(solution)/shard_map/pallas_call | solution.py:85
  (24 shorter events, 0.1 us)
Async XLA Ops:
  0.8 3.8 %collective-permute-start = (bf16[16,2048]{1,0:T(8,128)(2,1)S(1)}, bf16[16,2048]{1,0:T(8,128)(2,1)S(1)}, u32[]{:S(2)}, u32[]{:S(2)}) collective-permute-start(bf16[16,2048]{1,0:T(8,128)(2,1)S(1)} %slice.3), channel_id=1, source_target_pairs={{0,4},{4,8},{8,12},{12,16},{16,20},{20,24},{24,28},{1,5},{5,9},{9,... | collective-permute-start | bytes 196616 | tf_op jit(solution)/shard_map/ppermute | solution.py:468
  4.6 1.6 %copy-start.1 = (bf16[512,2048]{1,0:T(8,128)(2,1)S(1)}, bf16[512,2048]{1,0:T(8,128)(2,1)}, u32[]{:S(2)}) copy-start(bf16[512,2048]{1,0:T(8,128)(2,1)} %refs_7_.13) | copy-start | bytes 6291460
  6.2 1.2 %copy-start.4 = (bf16[256,2048]{1,0:T(8,128)(2,1)S(1)}, bf16[256,2048]{1,0:T(8,128)(2,1)}, u32[]{:S(2)}) copy-start(bf16[256,2048]{1,0:T(8,128)(2,1)} %refs_0_.19) | copy-start | bytes 3145732
  7.4 5.9 %copy-start.7 = (f32[8,256]{1,0:T(8,128)S(1)}, f32[8,256]{1,0:T(8,128)}, u32[]{:S(2)}) copy-start(f32[8,256]{1,0:T(8,128)} %refs_0_.11) | copy-start | bytes 24580
  7.4 5.9 %copy-start.8 = (f32[8,256]{1,0:T(8,128)S(1)}, f32[8,256]{1,0:T(8,128)}, u32[]{:S(2)}) copy-start(f32[8,256]{1,0:T(8,128)} %refs_1_.1) | copy-start | bytes 24580
  7.4 7.1 %copy-start = (bf16[512,4096]{1,0:T(8,128)(2,1)S(1)}, bf16[512,4096]{1,0:T(8,128)(2,1)}, u32[]{:S(2)}) copy-start(bf16[512,4096]{1,0:T(8,128)(2,1)} %refs_7_.16) | copy-start | bytes 12582916
  7.4 7.1 %copy-start.5 = (bf16[256,2048]{1,0:T(8,128)(2,1)S(1)}, bf16[256,2048]{1,0:T(8,128)(2,1)}, u32[]{:S(2)}) copy-start(bf16[256,2048]{1,0:T(8,128)(2,1)} %refs_0_.19) | copy-start | bytes 3145732
  9.4 10.0 %collective-permute-start.4 = (bf16[272,512]{1,0:T(8,128)(2,1)S(1)}, bf16[272,512]{1,0:T(8,128)(2,1)S(1)}, u32[]{:S(2)}, u32[]{:S(2)}) collective-permute-start(bf16[272,512]{1,0:T(8,128)(2,1)S(1)} %get-tuple-element.40.refs_2_), channel_id=1, source_target_pairs={{0,1},{1,0},{2,3},{3,2},{4,5},{5,4},{6,7},{7,6},{8,9},{9,8},{10,11... | collective-permute-start | bytes 835592 | tf_op jit(solution)/shard_map/ppermute | solution.py:140
  11.8 13.5 %collective-permute-start.5 = (bf16[272,512]{1,0:T(8,128)(2,1)S(1)}, bf16[272,512]{1,0:T(8,128)(2,1)S(1)}, u32[]{:S(2)}, u32[]{:S(2)}) collective-permute-start(bf16[272,512]{1,0:T(8,128)(2,1)S(1)} %get-tuple-element.47), channel_id=1, source_target_pairs={{0,2},{1,3},{2,0},{3,1},{4,6},{5,7},{6,4},{7,5},{8,10},{9,11},{10,... | collective-permute-start | bytes 835592 | tf_op jit(solution)/shard_map/ppermute | solution.py:140
  13.3 12.7 %collective-permute-start.6 = (bf16[272,512]{1,0:T(8,128)(2,1)S(1)}, bf16[272,512]{1,0:T(8,128)(2,1)S(1)}, u32[]{:S(2)}, u32[]{:S(2)}) collective-permute-start(bf16[272,512]{1,0:T(8,128)(2,1)S(1)} %get-tuple-element.48), channel_id=1, source_target_pairs={{0,3},{1,2},{2,1},{3,0},{4,7},{5,6},{6,5},{7,4},{8,11},{9,10},{10,... | collective-permute-start | bytes 835592 | tf_op jit(solution)/shard_map/ppermute | solution.py:140
  14.5 11.4 %copy-start.2 = (bf16[512,2048]{1,0:T(8,128)(2,1)S(1)}, bf16[512,2048]{1,0:T(8,128)(2,1)}, u32[]{:S(2)}) copy-start(bf16[512,2048]{1,0:T(8,128)(2,1)} %refs_7_.13) | copy-start | bytes 6291460
  14.6 11.4 %copy-start.6 = (bf16[4,8192]{1,0:T(4,128)(2,1)S(1)}, bf16[4,8192]{1,0:T(4,128)(2,1)}, u32[]{:S(2)}) copy-start(bf16[4,8192]{1,0:T(4,128)(2,1)} %refs_18_.1) | copy-start | bytes 196612
  15.9 18.8 %collective-permute-start.1 = (bf16[272,512]{1,0:T(8,128)(2,1)S(1)}, bf16[272,512]{1,0:T(8,128)(2,1)S(1)}, u32[]{:S(2)}, u32[]{:S(2)}) collective-permute-start(bf16[272,512]{1,0:T(8,128)(2,1)S(1)} %get-tuple-element.42.refs_15_), channel_id=1, source_target_pairs={{0,1},{1,0},{2,3},{3,2},{4,5},{5,4},{6,7},{7,6},{8,9},{9,8},{10,11... | collective-permute-start | bytes 835592 | tf_op jit(solution)/shard_map/ppermute | solution.py:140
  17.9 22.8 %collective-permute-start.2 = (bf16[272,512]{1,0:T(8,128)(2,1)S(1)}, bf16[272,512]{1,0:T(8,128)(2,1)S(1)}, u32[]{:S(2)}, u32[]{:S(2)}) collective-permute-start(bf16[272,512]{1,0:T(8,128)(2,1)S(1)} %get-tuple-element.43), channel_id=1, source_target_pairs={{0,2},{1,3},{2,0},{3,1},{4,6},{5,7},{6,4},{7,5},{8,10},{9,11},{10,... | collective-permute-start | bytes 835592 | tf_op jit(solution)/shard_map/ppermute | solution.py:140
  19.4 22.8 %collective-permute-start.3 = (bf16[272,512]{1,0:T(8,128)(2,1)S(1)}, bf16[272,512]{1,0:T(8,128)(2,1)S(1)}, u32[]{:S(2)}, u32[]{:S(2)}) collective-permute-start(bf16[272,512]{1,0:T(8,128)(2,1)S(1)} %get-tuple-element.44), channel_id=1, source_target_pairs={{0,3},{1,2},{2,1},{3,0},{4,7},{5,6},{6,5},{7,4},{8,11},{9,10},{10,... | collective-permute-start | bytes 835592 | tf_op jit(solution)/shard_map/ppermute | solution.py:140
  32.3 16.8 %collective-permute-start.10 = (bf16[272,512]{1,0:T(8,128)(2,1)S(1)}, bf16[272,512]{1,0:T(8,128)(2,1)S(1)}, u32[]{:S(2)}, u32[]{:S(2)}) collective-permute-start(bf16[272,512]{1,0:T(8,128)(2,1)S(1)} %get-tuple-element.52.refs_15_), channel_id=1, source_target_pairs={{0,1},{1,0},{2,3},{3,2},{4,5},{5,4},{6,7},{7,6},{8,9},{9,8},{10,11... | collective-permute-start | bytes 835592 | tf_op jit(solution)/shard_map/ppermute | solution.py:140
  33.8 17.0 %collective-permute-start.11 = (bf16[272,512]{1,0:T(8,128)(2,1)S(1)}, bf16[272,512]{1,0:T(8,128)(2,1)S(1)}, u32[]{:S(2)}, u32[]{:S(2)}) collective-permute-start(bf16[272,512]{1,0:T(8,128)(2,1)S(1)} %get-tuple-element.63), channel_id=1, source_target_pairs={{0,2},{1,3},{2,0},{3,1},{4,6},{5,7},{6,4},{7,5},{8,10},{9,11},{10,... | collective-permute-start | bytes 835592 | tf_op jit(solution)/shard_map/ppermute | solution.py:140
  34.7 13.3 %collective-permute-start.13 = (f32[4,128,128]{2,1,0:T(8,128)S(1)}, f32[4,128,128]{2,1,0:T(8,128)S(1)}, u32[]{:S(2)}, u32[]{:S(2)}) collective-permute-start(f32[4,128,128]{2,1,0:T(8,128)S(1)} %get-tuple-element.51.refs_8_.refs_0_), channel_id=1, source_target_pairs={{0,4},{4,0},{8,12},{12,8},{16,20},{20,16},{24,28},{28,24},{1,5},{5... | collective-permute-start | bytes 786440 | tf_op jit(solution)/shard_map/ppermute | solution.py:473
  40.8 11.3 %collective-permute-start.12 = (bf16[272,512]{1,0:T(8,128)(2,1)S(1)}, bf16[272,512]{1,0:T(8,128)(2,1)S(1)}, u32[]{:S(2)}, u32[]{:S(2)}) collective-permute-start(bf16[272,512]{1,0:T(8,128)(2,1)S(1)} %get-tuple-element.64), channel_id=1, source_target_pairs={{0,3},{1,2},{2,1},{3,0},{4,7},{5,6},{6,5},{7,4},{8,11},{9,10},{10,... | collective-permute-start | bytes 835592 | tf_op jit(solution)/shard_map/ppermute | solution.py:140
  42.3 2.7 %copy-start.3 = (bf16[512,2048]{1,0:T(8,128)(2,1)S(1)}, bf16[512,2048]{1,0:T(8,128)(2,1)}, u32[]{:S(2)}) copy-start(bf16[512,2048]{1,0:T(8,128)(2,1)} %refs_17_.1) | copy-start | bytes 6291460
  44.9 2.0 %collective-permute-start.14 = (bf16[4,128,128]{2,1,0:T(8,128)(2,1)S(1)}, bf16[4,128,128]{2,1,0:T(8,128)(2,1)S(1)}, u32[]{:S(2)}, u32[]{:S(2)}) collective-permute-start(bf16[4,128,128]{2,1,0:T(8,128)(2,1)S(1)} %get-tuple-element.54.refs_14_.refs_2_), channel_id=1, source_target_pairs={{0,4},{4,0},{8,12},{12,8},{16,20},{20,16},{24,28},{28,24},{1,5},{5... | collective-permute-start | bytes 393224 | tf_op jit(solution)/shard_map/ppermute | solution.py:473
  46.9 18.4 %collective-permute-start.7 = (bf16[272,512]{1,0:T(8,128)(2,1)S(1)}, bf16[272,512]{1,0:T(8,128)(2,1)S(1)}, u32[]{:S(2)}, u32[]{:S(2)}) collective-permute-start(bf16[272,512]{1,0:T(8,128)(2,1)S(1)} %get-tuple-element.55.refs_4_), channel_id=1, source_target_pairs={{0,1},{1,0},{2,3},{3,2},{4,5},{5,4},{6,7},{7,6},{8,9},{9,8},{10,11... | collective-permute-start | bytes 835592 | tf_op jit(solution)/shard_map/ppermute | solution.py:140
  48.0 18.6 %collective-permute-start.8 = (bf16[272,512]{1,0:T(8,128)(2,1)S(1)}, bf16[272,512]{1,0:T(8,128)(2,1)S(1)}, u32[]{:S(2)}, u32[]{:S(2)}) collective-permute-start(bf16[272,512]{1,0:T(8,128)(2,1)S(1)} %get-tuple-element.56), channel_id=1, source_target_pairs={{0,2},{1,3},{2,0},{3,1},{4,6},{5,7},{6,4},{7,5},{8,10},{9,11},{10,... | collective-permute-start | bytes 835592 | tf_op jit(solution)/shard_map/ppermute | solution.py:140
  49.0 18.9 %collective-permute-start.9 = (bf16[272,512]{1,0:T(8,128)(2,1)S(1)}, bf16[272,512]{1,0:T(8,128)(2,1)S(1)}, u32[]{:S(2)}, u32[]{:S(2)}) collective-permute-start(bf16[272,512]{1,0:T(8,128)(2,1)S(1)} %get-tuple-element.57), channel_id=1, source_target_pairs={{0,3},{1,2},{2,1},{3,0},{4,7},{5,6},{6,5},{7,4},{8,11},{9,10},{10,... | collective-permute-start | bytes 835592 | tf_op jit(solution)/shard_map/ppermute | solution.py:140
  50.8 3.8 %collective-permute-start.15 = (f32[4,128,128]{2,1,0:T(8,128)S(1)}, f32[4,128,128]{2,1,0:T(8,128)S(1)}, u32[]{:S(2)}, u32[]{:S(2)}) collective-permute-start(f32[4,128,128]{2,1,0:T(8,128)S(1)} %get-tuple-element.53.refs_17_.refs_0_), channel_id=1, source_target_pairs={{0,4},{4,0},{8,12},{12,8},{16,20},{20,16},{24,28},{28,24},{1,5},{5... | collective-permute-start | bytes 786440 | tf_op jit(solution)/shard_map/ppermute | solution.py:473
  54.5 6.4 %collective-permute-start.16 = (bf16[4,128,128]{2,1,0:T(8,128)(2,1)S(1)}, bf16[4,128,128]{2,1,0:T(8,128)(2,1)S(1)}, u32[]{:S(2)}, u32[]{:S(2)}) collective-permute-start(bf16[4,128,128]{2,1,0:T(8,128)(2,1)S(1)} %get-tuple-element.69.refs_2_.refs_4_), channel_id=1, source_target_pairs={{0,4},{4,0},{8,12},{12,8},{16,20},{20,16},{24,28},{28,24},{1,5},{5... | collective-permute-start | bytes 393224 | tf_op jit(solution)/shard_map/ppermute | solution.py:473
  54.7 24.6 %collective-permute-start.18 = (bf16[2,2,128,128]{3,2,1,0:T(8,128)(2,1)S(1)}, bf16[2,2,128,128]{3,2,1,0:T(8,128)(2,1)S(1)}, u32[]{:S(2)}, u32[]{:S(2)}) collective-permute-start(bf16[2,2,128,128]{3,2,1,0:T(8,128)(2,1)S(1)} %get-tuple-element.73), channel_id=1, source_target_pairs={{0,16},{4,20},{8,24},{12,28},{1,17},{5,21},{9,25},{13,29},{2,18},{... | collective-permute-start | bytes 393224 | tf_op jit(solution)/shard_map/ppermute | solution.py:468
  60.9 18.4 %collective-permute-start.19 = (bf16[2,2,128,128]{3,2,1,0:T(8,128)(2,1)S(1)}, bf16[2,2,128,128]{3,2,1,0:T(8,128)(2,1)S(1)}, u32[]{:S(2)}, u32[]{:S(2)}) collective-permute-start(bf16[2,2,128,128]{3,2,1,0:T(8,128)(2,1)S(1)} %get-tuple-element.73), channel_id=1, source_target_pairs={{0,8},{4,12},{8,16},{12,20},{16,24},{20,28},{1,9},{5,13},{9,17},{1... | collective-permute-start | bytes 393224 | tf_op jit(solution)/shard_map/ppermute | solution.py:468
  65.3 4.0 %collective-permute-start.17 = (bf16[2,128,128]{2,1,0:T(8,128)(2,1)S(1)}, bf16[2,128,128]{2,1,0:T(8,128)(2,1)S(1)}, u32[]{:S(2)}, u32[]{:S(2)}) collective-permute-start(bf16[2,128,128]{2,1,0:T(8,128)(2,1)S(1)} %get-tuple-element.67.refs_17_), channel_id=1, source_target_pairs={{0,24},{4,28},{1,25},{5,29},{2,26},{6,30},{3,27},{7,31}} | collective-permute-start | bytes 196616 | tf_op jit(solution)/shard_map/ppermute | solution.py:468
  66.6 13.7 %collective-permute-start.22 = (bf16[2,2,128,128]{3,2,1,0:T(8,128)(2,1)S(1)}, bf16[2,2,128,128]{3,2,1,0:T(8,128)(2,1)S(1)}, u32[]{:S(2)}, u32[]{:S(2)}) collective-permute-start(bf16[2,2,128,128]{3,2,1,0:T(8,128)(2,1)S(1)} %get-tuple-element.74), channel_id=1, source_target_pairs={{0,16},{4,20},{8,24},{12,28},{1,17},{5,21},{9,25},{13,29},{2,18},{... | collective-permute-start | bytes 393224 | tf_op jit(solution)/shard_map/ppermute | solution.py:468
  67.9 12.4 %collective-permute-start.23 = (bf16[2,2,128,128]{3,2,1,0:T(8,128)(2,1)S(1)}, bf16[2,2,128,128]{3,2,1,0:T(8,128)(2,1)S(1)}, u32[]{:S(2)}, u32[]{:S(2)}) collective-permute-start(bf16[2,2,128,128]{3,2,1,0:T(8,128)(2,1)S(1)} %get-tuple-element.74), channel_id=1, source_target_pairs={{0,8},{4,12},{8,16},{12,20},{16,24},{20,28},{1,9},{5,13},{9,17},{1... | collective-permute-start | bytes 393224 | tf_op jit(solution)/shard_map/ppermute | solution.py:468
  69.3 11.1 %collective-permute-start.21 = (bf16[2,128,128]{2,1,0:T(8,128)(2,1)S(1)}, bf16[2,128,128]{2,1,0:T(8,128)(2,1)S(1)}, u32[]{:S(2)}, u32[]{:S(2)}) collective-permute-start(bf16[2,128,128]{2,1,0:T(8,128)(2,1)S(1)} %get-tuple-element.70.refs_31_), channel_id=1, source_target_pairs={{0,24},{4,28},{1,25},{5,29},{2,26},{6,30},{3,27},{7,31}} | collective-permute-start | bytes 196616 | tf_op jit(solution)/shard_map/ppermute | solution.py:468
  75.5 7.2 %copy-start.9 = (f32[128]{0:T(128)S(1)}, f32[128]{0:T(128)}, u32[]{:S(2)}) copy-start(f32[128]{0:T(128)} %param.17) | copy-start | bytes 1540
  80.2 1.6 %collective-permute-start.20 = (bf16[2,128,128]{2,1,0:T(8,128)(2,1)S(1)}, bf16[2,128,128]{2,1,0:T(8,128)(2,1)S(1)}, u32[]{:S(2)}, u32[]{:S(2)}) collective-permute-start(bf16[2,128,128]{2,1,0:T(8,128)(2,1)S(1)} %shard_map.112.refs_3_), channel_id=1, source_target_pairs={{0,4},{4,0},{8,12},{12,8},{16,20},{20,16},{24,28},{28,24},{1,5},{5... | collective-permute-start | bytes 196616 | tf_op jit(solution)/shard_map/ppermute | solution.py:473
  81.3 1.4 %collective-permute-start.24 = (bf16[2,128,128]{2,1,0:T(8,128)(2,1)S(1)}, bf16[2,128,128]{2,1,0:T(8,128)(2,1)S(1)}, u32[]{:S(2)}, u32[]{:S(2)}) collective-permute-start(bf16[2,128,128]{2,1,0:T(8,128)(2,1)S(1)} %shard_map.113.refs_7_), channel_id=1, source_target_pairs={{0,4},{4,0},{8,12},{12,8},{16,20},{20,16},{24,28},{28,24},{1,5},{5... | collective-permute-start | bytes 196616 | tf_op jit(solution)/shard_map/ppermute | solution.py:473

commit v4 on v3

v4 whole, which is shorter than its diff:
```python
import functools

import jax
import jax.numpy as jnp
from jax import lax
from jax.experimental import pallas as pl
from jax.experimental.pallas import tpu as pltpu
from jax.sharding import PartitionSpec as P

HEAD = 128
TAPS = 4
RIM = 16
EPS = 1e-06
VMEM_BYTES = 20 * 1024 * 1024
F32 = jnp.float32
BF16 = jnp.bfloat16

NN = (((1,), (0,)), ((), ()))
NT = (((1,), (1,)), ((), ()))


def dot1(a, b, dims=NN):
    return lax.dot_general(
        a.astype(BF16), b.astype(BF16), dims, preferred_element_type=F32
    )


def split(a):
    high = a.astype(BF16)
    return high, (a - high.astype(F32)).astype(BF16)


def dot3s(a, b, dims=NN):
    (ah, al), (bh, bl) = a, b
    one = functools.partial(lax.dot_general, dimension_numbers=dims, preferred_element_type=F32)
    return one(ah, bh) + (one(ah, bl) + one(al, bh))


def dot3(a, b, dims=NN):
    return dot3s(split(a), split(b), dims)


def packed_left(parts):
    return jnp.concatenate(parts, axis=1)


def packed_right(parts):
    wide = jnp.concatenate(parts, axis=1)
    return jnp.concatenate([wide, wide], axis=0)


def packed_turned(parts):
    tall = jnp.concatenate(parts, axis=0)
    return jnp.concatenate([tall, tall], axis=1)


def fold(left, right, dims=NN):
    both = lax.dot_general(left, right, dims, preferred_element_type=F32)
    width = both.shape[1] // 2
    return both[:, :width] + both[:, width:]


def mul(a, b):
    return fold(packed_left(split(a)), packed_right(split(b)))


def dot_full(a, b, dims=NN):
    return lax.dot_general(
        a, b, dims, precision=lax.Precision.HIGHEST, preferred_element_type=F32
    )


def whole(array):
    zeros = (0,) * array.ndim
    return pl.BlockSpec(array.shape, lambda i, sp: zeros)


def call(
    body, sp, inputs, specs, outs, micros, scratch=(), after=()
):
    number = len(inputs)
    specs = list(specs) + [pl.BlockSpec(memory_space=pl.ANY) for _ in after]

    def inner(sp_ref, *refs):
        body(sp_ref, *refs[:number], *refs[number + len(after) :])

    return pl.pallas_call(
        inner,
        grid_spec=pltpu.PrefetchScalarGridSpec(
            num_scalar_prefetch=1,
            grid=(1,),
            in_specs=specs,
            out_specs=[whole(out) for out in outs],
            scratch_shapes=list(scratch),
        ),
        out_shape=[jax.ShapeDtypeStruct(out.shape, out.dtype) for out in outs],
        compiler_params=pltpu.CompilerParams(vmem_limit_bytes=VMEM_BYTES),
        cost_estimate=pl.CostEstimate(
            flops=int(micros * 10**9), bytes_accessed=1000, transcendentals=0
        ),
    )(sp, *inputs, *after)


def weight_spec(key_heads, rows, width, unit, head):
    return pl.BlockSpec(
        (rows, width), lambda i, sp: (0, sp[2 + (sp[0] ^ unit) * key_heads + head])
    )


def tap_spec(key_heads, width, base, head):
    return pl.BlockSpec(
        (TAPS, width), lambda i, sp: (0, base + sp[2 + sp[0] * key_heads + head])
    )


def hidden_spec(hidden, rows):
    return pl.BlockSpec((hidden.shape[0], rows), lambda i, sp: (0, sp[0]))


def partial_sums(key_heads, ranks, heads, width, hidden, rim, weight, sp, after=()):
    rows, count = weight.shape[0], hidden.shape[0]
    inputs, specs = [hidden, rim], [hidden_spec(hidden, rows), hidden_spec(rim, rows)]
    for unit in range(1, ranks):
        for head in heads:
            inputs.append(weight)
            specs.append(weight_spec(key_heads, rows, width, unit, head))
    outs = [jax.ShapeDtypeStruct((RIM + count, width * len(heads)), BF16)] * (ranks - 1)
    step = 2 if width == HEAD and len(heads) % 2 == 0 else 1

    def body(sp_ref, hidden_ref, rim_ref, *refs):
        for unit in range(ranks - 1):
            out = refs[(ranks - 1) * len(heads) + unit]
            for at in range(0, len(heads), step):
                place = unit * len(heads) + at
                held = [refs[place + i][...] for i in range(step)]
                held = held[0] if step == 1 else jnp.concatenate(held, axis=1)
                cols = slice(at * width, (at + step) * width)
                out[RIM:, cols] = plain(hidden_ref[...], held).astype(BF16)
                out[:RIM, cols] = plain(rim_ref[...], held).astype(BF16)

    return call(body, sp, inputs, specs, outs, 1.3, after=after)


def exchange(parts):
    ranks = len(parts) + 1
    return [
        lax.ppermute(part, "head", [(i, i ^ (unit + 1)) for i in range(ranks)])
        for unit, part in enumerate(parts)
    ]


class Halving:
    def __init__(self, ranks, heads):
        bits = [1 << i for i in range(ranks.bit_length() - 1)]
        cut = (len(heads) + 1) // 2
        self.ranks, self.stages = ranks, len(bits)
        self.routes = [
            (order, part) for order, part in ((bits, heads[:cut]), (bits[::-1], heads[cut:])) if part
        ]

    def offsets(self, route, stage):
        out = [0]
        for bit in self.routes[route][0][stage + 1 :]:
            out = out + [o ^ bit for o in out]
        return out

    def send(self, stage, key_heads, width, hidden, rim, weight, received, sp, after=()):
        rows, count = weight.shape[0], hidden.shape[0]
        inputs, specs = [hidden, rim], [hidden_spec(hidden, rows), hidden_spec(rim, rows)]
        jobs, outs = [], []
        for route, (order, heads) in enumerate(self.routes):
            first = len(inputs)
            inputs += received[route]
            specs += [whole(part) for part in received[route]]
            offsets = self.offsets(route, stage)
            for slot, offset in enumerate(offsets):
                unit = offset ^ order[stage]
                sources = [
                    (first + before, self.offsets(route, before).index(unit))
                    for before in range(stage)
                ]
                for at, head in enumerate(heads):
                    jobs.append((len(inputs), sources, route, slot, at))
                    inputs.append(weight)
                    specs.append(weight_spec(key_heads, rows, width, unit, head))
            shape = (len(offsets), RIM + count, width * len(heads))
            outs.append(jax.ShapeDtypeStruct(shape, BF16))
        total = len(inputs)

        def body(sp_ref, *refs):
            for place, sources, route, slot, at in jobs:
                held = refs[place][...]
                cols = slice(at * width, (at + 1) * width)
                for left, span in ((refs[0], slice(RIM, RIM + count)), (refs[1], slice(0, RIM))):
                    part = plain(left[...], held)
                    for source, index in sources:
                        part = part + refs[source][index, span, cols].astype(F32)
                    refs[total + route][slot, span, cols] = part.astype(BF16)

        return call(body, sp, inputs, specs, outs, 1.3, after=after)

    def exchange(self, stage, sent, received):
        for route, part in enumerate(sent):
            bit = self.routes[route][0][stage]
            pairs = [(i, i ^ bit) for i in range(self.ranks)]
            received[route].append(lax.ppermute(part, "head", pairs))

    def parts(self, head, width, received):
        route = [head in heads for _, heads in self.routes].index(True)
        at = self.routes[route][1].index(head)
        return [
            (part, pl.BlockSpec((None, part.shape[1], width), lambda i, sp: (0, 0, at)))
            for part in received[route]
        ]


def direct_parts(head, width, received):
    return [
        (part, pl.BlockSpec((part.shape[0], width), lambda i, sp: (0, head))) for part in received
    ]


def gather_specs(key_heads, width, hidden, rim, weight, taps, base, parts):
    rows = weight.shape[0]
    inputs = [hidden, rim]
    specs = [hidden_spec(hidden, rows), hidden_spec(rim, rows)]
    jobs = []
    for head, received in enumerate(parts):
        jobs.append(len(inputs))
        inputs += [weight, taps]
        specs += [
            weight_spec(key_heads, rows, width, 0, head), tap_spec(key_heads, width, base, head)
        ]
        for part, spec in received:
            inputs.append(part)
            specs.append(spec)
    return inputs, specs, jobs


def activate(refs, job, number, scratch):
    held, taps = refs[job][...], refs[job + 1][...].astype(F32)
    count = refs[0].shape[0]
    for left, span in ((refs[0], slice(RIM, RIM + count)), (refs[1], slice(0, RIM))):
        part = plain(left[...], held)
        for source in range(job + 2, job + 2 + number):
            part = part + refs[source][span, :].astype(F32)
        scratch[span, :] = part
    total = None
    for tap in range(TAPS):
        first = RIM - (TAPS - 1) + tap
        term = taps[tap : tap + 1] * scratch[first : first + count, :]
        total = term if total is None else total + term
    return total / (1.0 + jnp.exp(-total))


def plain(a, b):
    return jnp.dot(a, b, preferred_element_type=F32)


def unit_rows(values):
    return values * lax.rsqrt(jnp.sum(values * values, axis=-1, keepdims=True) + EPS)


def iotas(size):
    return (
        lax.broadcasted_iota(jnp.int32, (size, size), 0),
        lax.broadcasted_iota(jnp.int32, (size, size), 1),
    )


def prepare(decay, beta, sp, after=()):
    heads, count = decay.shape
    outs = [
        jax.ShapeDtypeStruct((heads, count), F32),
        jax.ShapeDtypeStruct((count, heads), F32),
        jax.ShapeDtypeStruct((count, heads), F32),
    ]

    def body(sp_ref, decay_ref, beta_ref, row_ref, col_ref, rate_ref):
        rows, cols = iotas(count)
        row_ref[...] = dot_full(decay_ref[...], (rows <= cols).astype(F32))
        col_ref[...] = dot_full((cols <= rows).astype(F32), decay_ref[...], NT)
        rate_ref[...] = dot_full((rows == cols).astype(F32), beta_ref[...], NT)

    return call(body, sp, [decay, beta], [whole(decay), whole(beta)], outs, 1.2, after=after)


def inverses(systems):
    size = systems[0].shape[0]
    rows, cols = iotas(size)
    eye = (rows == cols).astype(F32)
    cut = [split(low) for low in systems]
    mask = ((rows >> 2) == (cols >> 2)).astype(F32).astype(BF16)
    near = [c[0] * mask for c in cut]
    square = [plain(n, n) for n in near]
    cube = [plain(n, s.astype(BF16)) for n, s in zip(near, square)]
    inv = [
        (eye - n.astype(F32) + s - c).astype(BF16) for n, s, c in zip(near, square, cube)
    ]
    shift = 2
    while (1 << shift) < size:
        inside = ((rows >> (shift + 1)) == (cols >> (shift + 1))) & (
            (rows >> shift) != (cols >> shift)
        )
        mask = inside.astype(F32).astype(BF16)
        middle = [plain(c[0] * mask, x).astype(BF16) for c, x in zip(cut, inv)]
        inv = [x - plain(x, m).astype(BF16) for x, m in zip(inv, middle)]
        shift += 1
    rest = [
        eye - x.astype(F32) - plain(packed_left(c), jnp.concatenate([x, x], axis=0))
        for c, x in zip(cut, inv)
    ]
    return [x.astype(F32) + plain(x, r.astype(BF16)) for x, r in zip(inv, rest)]


def key_phase(gathered, number, count, tables, sp, after=()):
    inputs, specs, jobs = gathered
    received = (len(inputs) - 2) // len(jobs) - 2
    at = len(inputs)
    inputs = inputs + tables
    specs = specs + [whole(table) for table in tables]
    half = count // 2
    heads = range(number // 2)
    outs = [
        jax.ShapeDtypeStruct((len(heads), count, HEAD), F32),
        jax.ShapeDtypeStruct((number, 3, half, 2 * half), BF16),
        jax.ShapeDtypeStruct((number, 2, HEAD, 2 * half), BF16),
        jax.ShapeDtypeStruct((number, HEAD, HEAD), F32),
    ]
    total = len(inputs)

    def body(sp_ref, *refs):
        key_ref, solve_ref, gather_ref, trans_ref, scratch = refs[total:]
        sums, sums_col, beta_col = (ref[...] for ref in refs[at : at + 3])
        rows, cols = iotas(half)
        keys, turned, systems, crosses = [], [], [], []
        for i, job in enumerate(jobs):
            key = unit_rows(activate(refs, job, received, scratch))
            keys.append(key)
            key_ref[i] = key
            turned.append(key.T)
            low, high = split(key[:half]), split(key[half:])
            low_left, high_left = packed_left(low), packed_left(high)
            low_right, high_right = packed_turned(low), packed_turned(high)
            alike = (
                fold(low_left, low_right, NT),
                fold(high_left, high_right, NT),
                fold(high_left, low_right, NT),
            )
            for r in (2 * i, 2 * i + 1):
                row, col, rate = sums[r : r + 1], sums_col[:, r : r + 1], beta_col[:, r : r + 1]
                for b, span in enumerate((slice(0, half), slice(half, count))):
                    fade = jnp.exp(jnp.minimum(col[span] - row[:, span], 0.0))
                    systems.append(jnp.where(cols < rows, rate[span] * fade * alike[b], 0.0))
                fade = jnp.exp(jnp.minimum(col[half:] - row[:, :half], 0.0))
                crosses.append(rate[half:] * fade * alike[2])
        solved = inverses(systems)
        left = [packed_left(split(x)) for x in solved]
        middle = [
            mul(cross, solved[2 * j]) for j, cross in enumerate(crosses)
        ]
        corner = [
            -fold(left[2 * j + 1], packed_right(split(m))) for j, m in enumerate(middle)
        ]
        keep = sp_ref[1].astype(F32)
        eye = (lax.broadcasted_iota(jnp.int32, (HEAD, HEAD), 0)
               == lax.broadcasted_iota(jnp.int32, (HEAD, HEAD), 1)).astype(F32)
        for j in range(number):
            key = keys[j // 2]
            row, col, rate = sums[j : j + 1], sums_col[:, j : j + 1], beta_col[:, j : j + 1]
            side = split(corner[j])
            for which, part in enumerate((left[2 * j], left[2 * j + 1], packed_left(side))):
                solve_ref[j, which] = part
            trailing = turned[j // 2] * jnp.exp(row[:, count - 1 :] - row)
            low, high = [packed_left(split(t)) for t in (trailing[:, :half], trailing[:, half:])]
            taken = (
                fold(low, packed_right(split(solved[2 * j]))) + fold(high, packed_right(side)),
                fold(high, packed_right(split(solved[2 * j + 1]))),
            )
            right = (rate * jnp.exp(col)) * key
            moved = None
            for part, span in zip(taken, (slice(0, half), slice(half, count))):
                part = packed_left(split(part))
                gather_ref[j, 0 if span.start == 0 else 1] = part
                term = fold(part, packed_right(split(right[span])))
                moved = term if moved is None else moved + term
            gone = jnp.exp(row[:, count - 1 :])
            trans_ref[j] = keep * (gone * eye - moved)

    return call(
        body, sp, inputs, specs, outs, 5.0, [pltpu.VMEM((RIM + count, HEAD), F32)], after=after,
    )


def value_phase(gathered, number, count, tables, gathers, trans, sp, place, after=()):
    inputs, specs, jobs = gathered
    received = (len(inputs) - 2) // len(jobs) - 2
    at = len(inputs)
    inputs = inputs + tables + [gathers, trans]
    specs = specs + [whole(a) for a in inputs[at:]]
    half = count // 2
    outs = [
        jax.ShapeDtypeStruct((number, count, HEAD), F32),
        jax.ShapeDtypeStruct((2, number // 2, HEAD, HEAD), BF16),
        jax.ShapeDtypeStruct((2, number // 2, HEAD, HEAD), BF16),
    ]
    total = len(inputs)

    def body(sp_ref, *refs):
        write_ref, keep_ref, give_ref, scratch = refs[total:]
        beta_col = refs[at + 2][...]
        gather_ref, moved_ref = refs[at + 3 : at + 5]
        made = []
        for i, job in enumerate(jobs):
            values = activate(refs, job, received, scratch)
            for j in (2 * i, 2 * i + 1):
                right = beta_col[:, j : j + 1] * values[:, (j % 2) * HEAD : (j % 2 + 1) * HEAD]
                write_ref[j] = right
                made.append(
                    fold(gather_ref[j, 0], packed_right(split(right[:half])))
                    + fold(gather_ref[j, 1], packed_right(split(right[half:])))
                )
        first = sp_ref[place] == 0
        for i in range(number // 2):
            k = i + number // 2
            for ref, mine in ((keep_ref, first), (give_ref, jnp.logical_not(first))):
                ref[0, i] = jnp.where(mine, moved_ref[i], moved_ref[k]).astype(BF16)
                ref[1, i] = jnp.where(mine, made[i], made[k]).astype(BF16)

    return call(
        body, sp, inputs, specs, outs, 0.05, [pltpu.VMEM((RIM + count, 2 * HEAD), F32)], after=after,
    )


def write_phase(right, keys, tables, solve, sp, after=()):
    number, count = right.shape[:2]
    half = count // 2
    inputs = [right, keys, *tables, solve]
    out = jax.ShapeDtypeStruct((number, count, 2 * HEAD), F32)

    def body(sp_ref, right_ref, key_ref, _, col_ref, rate_ref, solve_ref, out_ref):
        for j in range(number):
            col, rate = col_ref[:, j : j + 1], rate_ref[:, j : j + 1]
            both = jnp.concatenate([right_ref[j], (rate * jnp.exp(col)) * key_ref[j // 2]], axis=1)
            parts = []
            for span in (slice(0, half), slice(half, count)):
                high, low = split(both[span])
                parts.append((jnp.concatenate([high, high], axis=0), low))

            def solved(which, part):
                left = solve_ref[j, which]
                return plain(left, part[0]) + plain(left[:, :half], part[1])

            out_ref[j, :half] = solved(0, parts[0])
            out_ref[j, half:] = solved(2, parts[0]) + solved(1, parts[1])

    return call(body, sp, inputs, [whole(a) for a in inputs], [out], 0.05, after=after)[0]


def query_phase(gathered, number, count, tables, keys, writes, sp, after=()):
    inputs, specs, jobs = gathered
    received = (len(inputs) - 2) // len(jobs) - 2
    at = len(inputs)
    inputs = inputs + tables + [keys, writes]
    specs = specs + [whole(a) for a in inputs[at:]]
    half = count // 2
    outs = [
        jax.ShapeDtypeStruct((number, count, HEAD), F32),
        jax.ShapeDtypeStruct((number, count, HEAD), BF16),
    ]
    total = len(inputs)

    def body(sp_ref, *refs):
        inner_ref, query_ref, scratch = refs[total:]
        sums, sums_col = refs[at][...], refs[at + 1][...]
        rows, cols = iotas(half)
        low, high = slice(0, half), slice(half, count)
        for i, job in enumerate(jobs):
            key_ref, write_ref = refs[at + 3 : at + 5]
            query = unit_rows(activate(refs, job, received, scratch))
            key = key_ref[i]
            left = [packed_left(split(query[span])) for span in (low, high)]
            right = [packed_turned(split(key[span])) for span in (low, high)]
            alike = {
                (0, 0): fold(left[0], right[0], NT),
                (1, 1): fold(left[1], right[1], NT),
                (1, 0): fold(left[1], right[0], NT),
            }
            for j in (2 * i, 2 * i + 1):
                row, col = sums[j : j + 1], sums_col[:, j : j + 1]
                wrote = [split(write_ref[j, span]) for span in (low, high)]
                tall = [jnp.concatenate([w[0], w[0]], axis=0) for w in wrote]
                read = [None, None]
                for (t, s), product in alike.items():
                    fade = jnp.exp(
                        jnp.minimum(col[(low, high)[t]] - row[:, (low, high)[s]], 0.0)
                    )
                    attend = fade * product
                    if t == s:
                        attend = jnp.where(cols <= rows, attend, 0.0)
                    attend = split(attend)
                    part = jnp.dot(
                        packed_left(attend), tall[s], preferred_element_type=F32
                    ) + jnp.dot(attend[0], wrote[s][1], preferred_element_type=F32)
                    read[t] = part if read[t] is None else read[t] + part
                for t, span in enumerate((low, high)):
                    inner_ref[j, span] = read[t][:, :HEAD]
                    read_in = jnp.exp(col[span]) * query[span] - read[t][:, HEAD:]
                    query_ref[j, span] = read_in.astype(BF16)

    return call(
        body, sp, inputs, specs, outs, 3.7, [pltpu.VMEM((RIM + count, HEAD), F32)], after=after,
    )


def join_cores(mine, other, sp, place, after=()):
    half = mine.shape[1]
    outs = [
        jax.ShapeDtypeStruct((2, half, HEAD, HEAD), BF16),
        jax.ShapeDtypeStruct((half, HEAD, HEAD), BF16),
    ]

    def body(sp_ref, mine_ref, other_ref, both_ref, write_ref):
        first = sp_ref[place] == 0
        for i in range(half):
            held = [(mine_ref[k, i].astype(F32), other_ref[k, i].astype(F32)) for k in (0, 1)]
            early = [jnp.where(first, pair[0], pair[1]) for pair in held]
            late = [jnp.where(first, pair[1], pair[0]) for pair in held]
            left = late[0].astype(BF16)
            write = plain(left, early[1].astype(BF16)) + late[1]
            both_ref[0, i] = plain(left, early[0].astype(BF16)).astype(BF16)
            both_ref[1, i] = write.astype(BF16)
            write_ref[i] = write.astype(BF16)

    inputs = [mine, other]
    return call(body, sp, inputs, [whole(a) for a in inputs], outs, 0.05, after=after)


def pass_chip(joined, states, sp, after=()):
    half = states[0].shape[0]
    outs = [jax.ShapeDtypeStruct((half, HEAD, HEAD), BF16)] * 2
    inputs = [joined, *states]

    def body(sp_ref, joined_ref, *refs):
        for i in range(half):
            state = sum(ref[i].astype(F32) for ref in refs[:-2]).astype(BF16)
            stepped = plain(joined_ref[0, i], state)
            refs[-2][i] = (stepped + joined_ref[1, i].astype(F32)).astype(BF16)
            refs[-1][i] = state

    return call(body, sp, inputs, [whole(a) for a in inputs], outs, 0.05, after=after)


def shifted(value, steps):
    count = lax.axis_size("ctx")
    return lax.ppermute(value, "ctx", [(i, i + steps) for i in range(count - steps)])


def swapped(value):
    count = lax.axis_size("ctx")
    return lax.ppermute(value, "ctx", [(i, i ^ 1) for i in range(count)])


def enter_far(joined):
    chips = lax.axis_size("ctx") // 2
    joined = shifted(joined, 2)
    step = 1
    while step < chips:
        early = shifted(joined, 2 * step).astype(F32)
        late = joined.astype(F32)
        both = jnp.einsum("hij,xhjk->xhik", late[0], early, precision=lax.Precision.HIGHEST)
        joined = (both + late * jnp.array([0.0, 1.0], F32)[:, None, None, None]).astype(BF16)
        step *= 2
    return joined[1]


def finish(inner, query, mine, others, early, gain, sp, place):
    inputs = [inner, query, *early, gain, *mine, *others]
    number, count = inner.shape[:2]
    half = number // 2
    out = jax.ShapeDtypeStruct((count, number * HEAD), BF16)

    def body(sp_ref, inner_ref, query_ref, low_ref, high_ref, gain_ref, *refs):
        core = sp_ref[place]
        keep = sp_ref[1].astype(F32)
        for j in range(number):
            i, early_ref = j % half, (low_ref, high_ref)[j // half]
            own, far = [
                sum(ref[i].astype(F32) for ref in part)
                for part in (refs[: len(mine)], refs[len(mine) : 2 * len(mine)])
            ]
            state = jnp.where((core == 0) == (j < half), own, far)
            stepped = plain(early_ref[0, i], state.astype(BF16)) + early_ref[1, i].astype(F32)
            state = keep * jnp.where(core == 0, state, stepped)
            read = inner_ref[j] + plain(query_ref[j], state.astype(BF16))
            scale = lax.rsqrt(jnp.mean(read * read, axis=-1, keepdims=True) + EPS)
            cols = slice(j * HEAD, (j + 1) * HEAD)
            refs[-1][:, cols] = (read * scale * gain_ref[...]).astype(BF16)

    return call(body, sp, inputs, [whole(a) for a in inputs], [out], 2.7)[0]


def per_device(
    hidden,
    w_query,
    w_key,
    payload_projection_matrix,
    conv_weight,
    log_decay,
    beta_rate,
    norm_gain,
    head_order,
    block_starts,
):
    count = hidden.shape[0]
    ranks = lax.axis_size("head")
    chips = lax.axis_size("ctx") // 2
    total_heads = head_order.shape[0]
    key_heads = total_heads // ranks
    number = 2 * key_heads
    serve, spot = lax.axis_index("head"), lax.axis_index("ctx")
    keep = 1 - block_starts[0]
    place = 2 + total_heads
    w_value = payload_projection_matrix

    rim = shifted(hidden[count - RIM :], 1) * keep.astype(BF16)
    sp = jnp.concatenate(
        [jnp.stack([serve, keep]), head_order, jnp.stack([spot % 2])]
    ).astype(jnp.int32)

    everyone = list(range(key_heads))
    halving = Halving(ranks, everyone)

    def gathered(width, weight, base, parts):
        return gather_specs(key_heads, width, hidden, rim, weight, conv_weight, base, parts)

    part_k = partial_sums(key_heads, ranks, everyone, HEAD, hidden, rim, w_key, sp)
    got_k = exchange(part_k)
    tables = list(prepare(log_decay, beta_rate, sp, after=part_k[:1]))
    got_v = [[] for _ in halving.routes]
    part_v = halving.send(
        0, key_heads, 2 * HEAD, hidden, rim, w_value, got_v, sp, after=tables[:1]
    )
    halving.exchange(0, part_v, got_v)
    part_q = partial_sums(
        key_heads, ranks, everyone, HEAD, hidden, rim, w_query, sp, after=part_v[:1]
    )
    keys, solve, gathers, trans_a = key_phase(
        gathered(HEAD, w_key, total_heads, [direct_parts(h, HEAD, got_k) for h in everyone]),
        number, count, tables, sp, after=part_q[:1],
    )
    ordered = [trans_a]
    for stage in range(1, halving.stages):
        part_v = halving.send(
            stage, key_heads, 2 * HEAD, hidden, rim, w_value, got_v, sp, after=ordered
        )
        halving.exchange(stage, part_v, got_v)
        ordered = part_v[:1]
    part_q, _ = lax.optimization_barrier((part_q, ordered[0]))
    got_q = exchange(part_q)
    right, own, given = value_phase(
        gathered(
            2 * HEAD, w_value, total_heads,
            [halving.parts(h, 2 * HEAD, got_v) for h in everyone],
        ),
        number, count, tables, gathers, trans_a, sp, place, after=ordered,
    )
    taken = swapped(given)
    joined, joined_b = join_cores(own, taken, sp, place)
    early = swapped(own)
    states, last, writes = [], joined_b, None
    if chips <= 4:
        for chip in range(chips - 1):
            if chip:
                after = [] if writes is None else [writes, early]
                last, so_far = pass_chip(joined, states, sp, after)
                states = [so_far]
            hop = [(2 * chip + c, 2 * chip + 2 + c) for c in range(2)]
            states.append(lax.ppermute(last, "ctx", hop))
            if writes is None and chip + 1 >= min(2, chips - 1):
                writes = write_phase(right, keys, tables, solve, sp, after=[last])
    else:
        states = [enter_far(joined)]
    if writes is None:
        writes = write_phase(right, keys, tables, solve, sp, after=[last])
    inner, query = query_phase(
        gathered(HEAD, w_query, 0, [direct_parts(h, HEAD, got_q) for h in everyone]),
        number, count, tables, keys, writes, sp, after=[last],
    )
    others = [swapped(state) for state in states[:-1]]
    final, _ = lax.optimization_barrier((states[-1], inner))
    return finish(
        inner, query, [*states[:-1], final], [*others, swapped(final)], (early, taken),
        norm_gain[None, :], sp, place,
    )


def solution(mesh):
    return jax.shard_map(
        per_device,
        mesh=mesh,
        in_specs=(
            P("ctx", None),
            P("head", None),
            P("head", None),
            P("head", None),
            P(),
            P("head", "ctx"),
            P("head", "ctx"),
            P(),
            P(),
            P("ctx"),
        ),
        out_specs=P("ctx", "head"),
        check_vma=False,
    )
```

time: 86.1 us -> 77.4 us (0.90)
  starting transfers between devices: 41.6 us -> 20.6 us
  waiting for transfers between devices: 5.9 us -> 22.5 us
  Pallas kernels: 32.5 us -> 26.7 us
  local copies, waits for them, and re-layouts: 3.69 us -> 4.56 us
    ppermute x7 -> x1, starting transfers between devices: 22.3 us -> 2.35 us  [shifted(): lax.ppermute(value, 'ctx', [(i, i + steps) for i in range(count - steps)])]
    ppermute x0 -> x7, waiting for transfers between devices: none -> 14.4 us  [the longest x4 11.9 us: exchange(): received[route].append(lax.ppermute(part, 'head', pairs))]
    ppermute x0 -> x7, starting transfers between devices: none -> 10.5 us  [the longest x4 6.61 us: exchange(): received[route].append(lax.ppermute(part, 'head', pairs))]
    ppermute x12 -> x6, starting transfers between devices: 16.9 us -> 7.52 us  [exchange(): lax.ppermute(part, 'head', [(i, i ^ unit + 1) for i in range(ranks)])]
    pallas_call x15 -> x13, Pallas kernels: 32.5 us -> 26.7 us  [call(): pl.pallas_call(inner, grid_spec=pltpu.PrefetchScalarGridSpec(num_scalar_p...]
    ppermute x6 -> x4, starting transfers between devices: 2.39 us -> 0.28 us  [swapped(): return lax.ppermute(value, 'ctx', [(i, i ^ 1) for i in range(count)])]
    ppermute x12 -> x6, waiting for transfers between devices: 4.95 us -> 6.78 us  [exchange(): lax.ppermute(part, 'head', [(i, i ^ unit + 1) for i in range(ranks)])]
    unnamed x20, local copies, waits for them, and re-layouts: 2.85 us -> 3.71 us
  transfers between devices with their start and end apart: 25 -> 18, of which waited for: 4 -> 10; matrix products, arithmetic and copies ran while one was open for 1% -> 1% of each run, Pallas kernels for 33% -> 25%
where the time goes in v4:
time: 77.4 us; the launch traced here: 76 us
  Pallas kernels  26.7 us (34%)
  waiting for transfers between devices  22.5 us (29%)
  starting transfers between devices  20.6 us (27%)
  local copies, waits for them, and re-layouts  4.56 us (6%)
  between operations  0.9 us (1%)
    pallas_call x13, Pallas kernels, call(): pl.pallas_call(inner, grid_spec=pltpu.PrefetchScalarGridSpec(num_scalar_p...  26.7 us
    ppermute x4, waiting for transfers between devices, exchange(): received[route].append(lax.ppermute(part, 'head', pairs))  11.9 us
    ppermute x6, starting transfers between devices, exchange(): lax.ppermute(part, 'head', [(i, i ^ unit + 1) for i in range(ranks)])  7.52 us
    ppermute x6, waiting for transfers between devices, exchange(): lax.ppermute(part, 'head', [(i, i ^ unit + 1) for i in range(ranks)])  6.78 us
    ppermute x4, starting transfers between devices, exchange(): received[route].append(lax.ppermute(part, 'head', pairs))  6.61 us
    ppermute x3, starting transfers between devices, per_device(): states.append(lax.ppermute(last, 'ctx', hop))  3.88 us
    unnamed x20, local copies, waits for them, and re-layouts  3.71 us
    ppermute x3, waiting for transfers between devices, per_device(): states.append(lax.ppermute(last, 'ctx', hop))  2.43 us
  transfers between devices with their start and end apart: 18, of which 10 were waited for; matrix products, arithmetic and copies ran while one was open for 1% of the time, Pallas kernels for 25%

profile of v4, /device:TPU:0, one launch (start us, length us, event | category | flops | bytes accessed | tf_op | source)
XLA Modules:
  0.0 76.0 jit_solution(16966625700458619911)
XLA Ops:
  0.0 0.8 %slice.3 = bf16[16,2048]{1,0:T(8,128)(2,1)S(1)} slice(bf16[256,2048]{1,0:T(8,128)(2,1)} %refs_0_.15), slice={[240:256], [0:2048]} | slice | bytes 131072 | tf_op jit(solution)/shard_map/slice | solution.py:626
  0.8 2.3 %collective-permute-start = (bf16[16,2048]{1,0:T(8,128)(2,1)S(1)}, bf16[16,2048]{1,0:T(8,128)(2,1)S(1)}, u32[]{:S(2)}, u32[]{:S(2)}) collective-permute-start(bf16[16,2048]{1,0:T(8,128)(2,1)S(1)} %slice.3), channel_id=1, source_target_pairs={{0,4},{4,8},{8,12},{12,16},{16,20},{20,24},{24,28},{1,5},{5,9},{9,... | collective-permute-start | bytes 196616 | tf_op jit(solution)/shard_map/ppermute | solution.py:556
  3.9 0.7 pad_add_fusion.sp_ref
  4.6 0.0 collective-permute-done
  4.6 0.0 copy-start.2
  4.6 1.6 %copy-done.2 = bf16[512,2048]{1,0:T(8,128)(2,1)S(1)} copy-done((bf16[512,2048]{1,0:T(8,128)(2,1)S(1)}, bf16[512,2048]{1,0:T(8,128)(2,1)}, u32[]{:S(2)}) %copy-start.2) | copy-done | bytes 2097176
  6.2 0.0 copy-start.4
  6.2 1.2 %copy-done.4 = bf16[256,2048]{1,0:T(8,128)(2,1)S(1)} copy-done((bf16[256,2048]{1,0:T(8,128)(2,1)S(1)}, bf16[256,2048]{1,0:T(8,128)(2,1)}, u32[]{:S(2)}) %copy-start.4) | copy-done | bytes 1048600
  7.4 1.4 %shard_map.100 = (bf16[272,512]{1,0:T(8,128)(2,1)S(1)}, bf16[272,512]{1,0:T(8,128)(2,1)S(1)}, bf16[272,512]{1,0:T(8,128)(2,1)S(1)}) custom-call(s32[19]{0:T(128)S(1)} %pad_add_fusion.sp_ref, bf16[256,2048]{1,0:T(8,128)(2,1)S(1)} %copy-done.4, bf16[16,2048]{1,0:T(8,128)(2,1)S(1)} %broadcast_multiply_fusion.refs_1_, bf16[512,2048]{1,0:T(8,128)(2,1)S(1)} %copy-done.2, ...), custom_call_target="tpu_custom_call" | custom-call | flops 1300000000 | bytes 1000 | tf_op jit(solution)/shard_map/pallas_call | solution.py:87
  8.9 2.4 %collective-permute-start.4 = (bf16[272,512]{1,0:T(8,128)(2,1)S(1)}, bf16[272,512]{1,0:T(8,128)(2,1)S(1)}, u32[]{:S(2)}, u32[]{:S(2)}) collective-permute-start(bf16[272,512]{1,0:T(8,128)(2,1)S(1)} %get-tuple-element.44), channel_id=1, source_target_pairs={{0,2},{1,3},{2,0},{3,1},{4,6},{5,7},{6,4},{7,5},{8,10},{9,11},{10,... | collective-permute-start | bytes 835592 | tf_op jit(solution)/shard_map/ppermute | solution.py:147
  11.3 1.4 %collective-permute-start.5 = (bf16[272,512]{1,0:T(8,128)(2,1)S(1)}, bf16[272,512]{1,0:T(8,128)(2,1)S(1)}, u32[]{:S(2)}, u32[]{:S(2)}) collective-permute-start(bf16[272,512]{1,0:T(8,128)(2,1)S(1)} %get-tuple-element.45), channel_id=1, source_target_pairs={{0,3},{1,2},{2,1},{3,0},{4,7},{5,6},{6,5},{7,4},{8,11},{9,10},{10,... | collective-permute-start | bytes 835592 | tf_op jit(solution)/shard_map/ppermute | solution.py:147
  12.7 0.1 collective-permute-start.3
  12.8 0.0 copy-done.7
  12.8 0.0 copy-done.8
  12.8 1.2 %shard_map.101 = (f32[8,256]{1,0:T(8,128)S(1)}, f32[256,8]{1,0:T(8,128)S(1)}, f32[256,8]{1,0:T(8,128)S(1)}) custom-call(s32[19]{0:T(128)S(1)} %pad_add_fusion.sp_ref, f32[8,256]{1,0:T(8,128)S(1)} %copy-done.7, f32[8,256]{1,0:T(8,128)S(1)} %copy-done.8, bf16[272,512]{1,0:T(8,128)(2,1)S(1)} %get-tuple-element.37.refs_2_), custom_call_target="tpu_custom_call" | custom-call | flops 1200000000 | bytes 1000 | tf_op jit(solution)/shard_map/pallas_call | solution.py:87
  14.0 0.0 copy-done.5
  14.0 0.9 %copy-done = bf16[512,4096]{1,0:T(8,128)(2,1)S(1)} copy-done((bf16[512,4096]{1,0:T(8,128)(2,1)S(1)}, bf16[512,4096]{1,0:T(8,128)(2,1)}, u32[]{:S(2)}) %copy-start) | copy-done | bytes 4194328
  14.9 1.5 %shard_map.102 = (bf16[2,272,512]{2,1,0:T(8,128)(2,1)S(1)}, bf16[2,272,512]{2,1,0:T(8,128)(2,1)S(1)}) custom-call(s32[19]{0:T(128)S(1)} %pad_add_fusion.sp_ref, bf16[256,2048]{1,0:T(8,128)(2,1)S(1)} %copy-done.5, bf16[16,2048]{1,0:T(8,128)(2,1)S(1)} %broadcast_multiply_fusion.refs_1_, bf16[512,4096]{1,0:T(8,128)(2,1)S(1)} %copy-done, ...), custom_call_target="tpu_custom_call" | custom-call | flops 1300000000 | bytes 1000 | tf_op jit(solution)/shard_map/pallas_call | solution.py:87
  16.5 1.6 %collective-permute-start.2 = (bf16[2,272,512]{2,1,0:T(8,128)(2,1)S(1)}, bf16[2,272,512]{2,1,0:T(8,128)(2,1)S(1)}, u32[]{:S(2)}, u32[]{:S(2)}) collective-permute-start(bf16[2,272,512]{2,1,0:T(8,128)(2,1)S(1)} %get-tuple-element.43), channel_id=1, source_target_pairs={{0,2},{1,3},{2,0},{3,1},{4,6},{5,7},{6,4},{7,5},{8,10},{9,11},{10,... | collective-permute-start | bytes 1671176 | tf_op jit(solution)/shard_map/ppermute | solution.py:206
  18.1 1.1 %collective-permute-start.1 = (bf16[2,272,512]{2,1,0:T(8,128)(2,1)S(1)}, bf16[2,272,512]{2,1,0:T(8,128)(2,1)S(1)}, u32[]{:S(2)}, u32[]{:S(2)}) collective-permute-start(bf16[2,272,512]{2,1,0:T(8,128)(2,1)S(1)} %get-tuple-element.39.refs_14_), channel_id=1, source_target_pairs={{0,1},{1,0},{2,3},{3,2},{4,5},{5,4},{6,7},{7,6},{8,9},{9,8},{10,11... | collective-permute-start | bytes 1671176 | tf_op jit(solution)/shard_map/ppermute | solution.py:206
  19.1 0.0 copy-done.1
  19.1 1.4 %shard_map.103 = (bf16[272,512]{1,0:T(8,128)(2,1)S(1)}, bf16[272,512]{1,0:T(8,128)(2,1)S(1)}, bf16[272,512]{1,0:T(8,128)(2,1)S(1)}) custom-call(s32[19]{0:T(128)S(1)} %pad_add_fusion.sp_ref, bf16[256,2048]{1,0:T(8,128)(2,1)S(1)} %copy-done.5, bf16[16,2048]{1,0:T(8,128)(2,1)S(1)} %broadcast_multiply_fusion.refs_1_, bf16[512,2048]{1,0:T(8,128)(2,1)S(1)} %copy-done.1, ...), custom_call_target="tpu_custom_call" | custom-call | flops 1300000000 | bytes 1000 | tf_op jit(solution)/shard_map/pallas_call | solution.py:87
  20.6 2.9 %collective-permute-done.4.refs_5_.refs_10_.refs_15_.refs_20_ = bf16[272,512]{1,0:T(8,128)(2,1)S(1)} collective-permute-done((bf16[272,512]{1,0:T(8,128)(2,1)S(1)}, bf16[272,512]{1,0:T(8,128)(2,1)S(1)}, u32[]{:S(2)}, u32[]{:S(2)}) %collective-permute-start.4) | collective-permute-done | bytes 278560 | tf_op jit(solution)/shard_map/ppermute | solution.py:147
  23.4 0.0 collective-permute-done.5.refs_6_.refs_11_.refs_16_.refs_21_
  23.5 1.9 %collective-permute-done.3.refs_4_.refs_9_.refs_14_.refs_19_ = bf16[272,512]{1,0:T(8,128)(2,1)S(1)} collective-permute-done((bf16[272,512]{1,0:T(8,128)(2,1)S(1)}, bf16[272,512]{1,0:T(8,128)(2,1)S(1)}, u32[]{:S(2)}, u32[]{:S(2)}) %collective-permute-start.3) | collective-permute-done | bytes 278560 | tf_op jit(solution)/shard_map/ppermute | solution.py:147
  25.4 0.0 copy-done.3
  25.4 0.0 copy-done.6
  25.4 7.1 %shard_map.104 = (f32[4,256,128]{2,1,0:T(8,128)S(1)}, bf16[8,3,128,256]{3,2,1,0:T(8,128)(2,1)S(1)}, bf16[8,2,128,256]{3,2,1,0:T(8,128)(2,1)S(1)}, f32[8,128,128]{2,1,0:T(8,128)S(1)}) custom-call(s32[19]{0:T(128)S(1)} %pad_add_fusion.sp_ref, bf16[256,2048]{1,0:T(8,128)(2,1)S(1)} %copy-done.5, bf16[16,2048]{1,0:T(8,128)(2,1)S(1)} %broadcast_multiply_fusion.refs_1_, ...), custom_call_target="tpu_custom_call" | custom-call | flops 5000000000 | bytes 1000 | tf_op jit(solution)/shard_map/pallas_call | solution.py:87
  32.5 2.9 %collective-permute-done.2.refs_5_.refs_12_.refs_16_ = bf16[2,272,512]{2,1,0:T(8,128)(2,1)S(1)} collective-permute-done((bf16[2,272,512]{2,1,0:T(8,128)(2,1)S(1)}, bf16[2,272,512]{2,1,0:T(8,128)(2,1)S(1)}, u32[]{:S(2)}, u32[]{:S(2)}) %collective-permute-start.2) | collective-permute-done | bytes 557088 | tf_op jit(solution)/shard_map/ppermute | solution.py:206
  35.4 1.9 %collective-permute-done.1.refs_2_.refs_4_.refs_8_ = bf16[2,272,512]{2,1,0:T(8,128)(2,1)S(1)} collective-permute-done((bf16[2,272,512]{2,1,0:T(8,128)(2,1)S(1)}, bf16[2,272,512]{2,1,0:T(8,128)(2,1)S(1)}, u32[]{:S(2)}, u32[]{:S(2)}) %collective-permute-start.1) | collective-permute-done | bytes 557088 | tf_op jit(solution)/shard_map/ppermute | solution.py:206
  37.3 1.1 %shard_map.105 = (bf16[1,272,512]{2,1,0:T(8,128)(2,1)S(1)}, bf16[1,272,512]{2,1,0:T(8,128)(2,1)S(1)}) custom-call(s32[19]{0:T(128)S(1)} %pad_add_fusion.sp_ref, bf16[256,2048]{1,0:T(8,128)(2,1)S(1)} %copy-done.5, bf16[16,2048]{1,0:T(8,128)(2,1)S(1)} %broadcast_multiply_fusion.refs_1_, ...), custom_call_target="tpu_custom_call" | custom-call | flops 1300000000 | bytes 1000 | tf_op jit(solution)/shard_map/pallas_call | solution.py:87
  38.4 2.4 %collective-permute-start.10 = (bf16[1,272,512]{2,1,0:T(8,128)(2,1)S(1)}, bf16[1,272,512]{2,1,0:T(8,128)(2,1)S(1)}, u32[]{:S(2)}, u32[]{:S(2)}) collective-permute-start(bf16[1,272,512]{2,1,0:T(8,128)(2,1)S(1)} %get-tuple-element.54), channel_id=1, source_target_pairs={{0,1},{1,0},{2,3},{3,2},{4,5},{5,4},{6,7},{7,6},{8,9},{9,8},{10,11... | collective-permute-start | bytes 835592 | tf_op jit(solution)/shard_map/ppermute | solution.py:206
  40.9 1.5 %collective-permute-start.9 = (bf16[1,272,512]{2,1,0:T(8,128)(2,1)S(1)}, bf16[1,272,512]{2,1,0:T(8,128)(2,1)S(1)}, u32[]{:S(2)}, u32[]{:S(2)}) collective-permute-start(bf16[1,272,512]{2,1,0:T(8,128)(2,1)S(1)} %get-tuple-element.49.refs_23_), channel_id=1, source_target_pairs={{0,2},{1,3},{2,0},{3,1},{4,6},{5,7},{6,4},{7,5},{8,10},{9,11},{10,... | collective-permute-start | bytes 835592 | tf_op jit(solution)/shard_map/ppermute | solution.py:206
  42.4 5.7 %collective-permute-done.10.refs_13_.refs_17_ = bf16[1,272,512]{2,1,0:T(8,128)(2,1)S(1)} collective-permute-done((bf16[1,272,512]{2,1,0:T(8,128)(2,1)S(1)}, bf16[1,272,512]{2,1,0:T(8,128)(2,1)S(1)}, u32[]{:S(2)}, u32[]{:S(2)}) %collective-permute-start.10) | collective-permute-done | bytes 278560 | tf_op jit(solution)/shard_map/ppermute | solution.py:206
  48.1 1.5 %collective-permute-done.9.refs_5_.refs_9_ = bf16[1,272,512]{2,1,0:T(8,128)(2,1)S(1)} collective-permute-done((bf16[1,272,512]{2,1,0:T(8,128)(2,1)S(1)}, bf16[1,272,512]{2,1,0:T(8,128)(2,1)S(1)}, u32[]{:S(2)}, u32[]{:S(2)}) %collective-permute-start.9) | collective-permute-done | bytes 278560 | tf_op jit(solution)/shard_map/ppermute | solution.py:206
  49.5 2.9 %shard_map.106 = (f32[8,256,128]{2,1,0:T(8,128)S(1)}, bf16[2,4,128,128]{3,2,1,0:T(8,128)(2,1)S(1)}, bf16[2,4,128,128]{3,2,1,0:T(8,128)(2,1)S(1)}) custom-call(s32[19]{0:T(128)S(1)} %pad_add_fusion.sp_ref, bf16[256,2048]{1,0:T(8,128)(2,1)S(1)} %copy-done.5, bf16[16,2048]{1,0:T(8,128)(2,1)S(1)} %broadcast_multiply_fusion.refs_1_, ...), custom_call_target="tpu_custom_call" | custom-call | flops 50000000 | bytes 1000 | tf_op jit(solution)/shard_map/pallas_call | solution.py:87
  52.4 0.1 collective-permute-start.11
  52.5 0.4 collective-permute-start.6
  52.9 1.7 %collective-permute-start.7 = (bf16[272,512]{1,0:T(8,128)(2,1)S(1)}, bf16[272,512]{1,0:T(8,128)(2,1)S(1)}, u32[]{:S(2)}, u32[]{:S(2)}) collective-permute-start(bf16[272,512]{1,0:T(8,128)(2,1)S(1)} %get-tuple-element.51), channel_id=1, source_target_pairs={{0,2},{1,3},{2,0},{3,1},{4,6},{5,7},{6,4},{7,5},{8,10},{9,11},{10,... | collective-permute-start | bytes 835592 | tf_op jit(solution)/shard_map/ppermute | solution.py:147
  54.6 1.4 %collective-permute-start.8 = (bf16[272,512]{1,0:T(8,128)(2,1)S(1)}, bf16[272,512]{1,0:T(8,128)(2,1)S(1)}, u32[]{:S(2)}, u32[]{:S(2)}) collective-permute-start(bf16[272,512]{1,0:T(8,128)(2,1)S(1)} %get-tuple-element.52), channel_id=1, source_target_pairs={{0,3},{1,2},{2,1},{3,0},{4,7},{5,6},{6,5},{7,4},{8,11},{9,10},{10,... | collective-permute-start | bytes 835592 | tf_op jit(solution)/shard_map/ppermute | solution.py:147
  56.0 0.0 collective-permute-done.11.refs_1_.refs_3_
  56.0 0.8 %shard_map.107 = (bf16[2,4,128,128]{3,2,1,0:T(8,128)(2,1)S(1)}, bf16[4,128,128]{2,1,0:T(8,128)(2,1)S(1)}) custom-call(s32[19]{0:T(128)S(1)} %pad_add_fusion.sp_ref, bf16[2,4,128,128]{3,2,1,0:T(8,128)(2,1)S(1)} %get-tuple-element.58.refs_0_, bf16[2,4,128,128]{3,2,1,0:T(8,128)(2,1)S(1)} %collective-permute-done.11.refs_1_.refs_3_), custom_call_target="tpu_custom_call" | custom-call | flops 50000000 | bytes 1000 | tf_op jit(solution)/shard_map/pallas_call | solution.py:87
  56.8 2.5 %collective-permute-start.12 = (bf16[4,128,128]{2,1,0:T(8,128)(2,1)S(1)}, bf16[4,128,128]{2,1,0:T(8,128)(2,1)S(1)}, u32[]{:S(2)}, u32[]{:S(2)}) collective-permute-start(bf16[4,128,128]{2,1,0:T(8,128)(2,1)S(1)} %get-tuple-element.61), channel_id=1, source_target_pairs={{0,8},{4,12},{1,9},{5,13},{2,10},{6,14},{3,11},{7,15}} | collective-permute-start | bytes 393224 | tf_op jit(solution)/shard_map/ppermute | solution.py:679
  59.4 0.1 collective-permute-start.14
  59.4 2.4 %collective-permute-done.12.refs_1_ = bf16[4,128,128]{2,1,0:T(8,128)(2,1)S(1)} collective-permute-done((bf16[4,128,128]{2,1,0:T(8,128)(2,1)S(1)}, bf16[4,128,128]{2,1,0:T(8,128)(2,1)S(1)}, u32[]{:S(2)}, u32[]{:S(2)}) %collective-permute-start.12) | collective-permute-done | bytes 131104 | tf_op jit(solution)/shard_map/ppermute | solution.py:679
  61.9 0.7 shard_map.108
  62.6 0.7 collective-permute-start.13
  63.3 1.7 %shard_map.109.refs_3_.refs_26_ = f32[8,256,256]{2,1,0:T(8,128)S(1)} custom-call(s32[19]{0:T(128)S(1)} %pad_add_fusion.sp_ref, f32[8,256,128]{2,1,0:T(8,128)S(1)} %get-tuple-element.56.refs_0_, f32[4,256,128]{2,1,0:T(8,128)S(1)} %get-tuple-element.53.refs_1_.refs_25_, f32[8,256]{1,0:T(8,128)S(1)} %get-tuple-element.38.refs_10_.refs_22_.refs_18_.refs_2_, ...), custom_call_target="tpu_custom_call" | custom-call | flops 50000000 | bytes 1000 | tf_op jit(solution)/shard_map/pallas_call | solution.py:87
  65.0 0.0 collective-permute-done.14.refs_4_.refs_2_
  65.0 0.0 collective-permute-done.13.refs_2_
  65.0 0.7 shard_map.110
  65.7 0.7 collective-permute-start.15
  66.4 0.0 copy-start.9
  66.4 0.1 collective-permute-start.16
  66.5 0.0 collective-permute-done.6.refs_4_.refs_9_.refs_14_.refs_19_
  66.5 0.3 collective-permute-done.7.refs_5_.refs_10_.refs_15_.refs_20_
  66.8 1.6 %collective-permute-done.8.refs_6_.refs_11_.refs_16_.refs_21_ = bf16[272,512]{1,0:T(8,128)(2,1)S(1)} collective-permute-done((bf16[272,512]{1,0:T(8,128)(2,1)S(1)}, bf16[272,512]{1,0:T(8,128)(2,1)S(1)}, u32[]{:S(2)}, u32[]{:S(2)}) %collective-permute-start.8) | collective-permute-done | bytes 278560 | tf_op jit(solution)/shard_map/ppermute | solution.py:147
  68.5 3.7 %shard_map.111 = (f32[8,256,128]{2,1,0:T(8,128)S(1)}, bf16[8,256,128]{2,1,0:T(8,128)(2,1)S(1)}) custom-call(s32[19]{0:T(128)S(1)} %pad_add_fusion.sp_ref, bf16[256,2048]{1,0:T(8,128)(2,1)S(1)} %copy-done.5, bf16[16,2048]{1,0:T(8,128)(2,1)S(1)} %broadcast_multiply_fusion.refs_1_, bf16[512,2048]{1,0:T(8,128)(2,1)S(1)} %copy-done.1, ...), custom_call_target="tpu_custom_call" | custom-call | flops 3700000000 | bytes 1000 | tf_op jit(solution)/shard_map/pallas_call | solution.py:87
  72.2 0.0 collective-permute-done.15.refs_6_
  72.2 0.1 collective-permute-start.17
  72.3 0.0 collective-permute-done.16.refs_7_
  72.3 1.3 %collective-permute-done.17.refs_8_ = bf16[4,128,128]{2,1,0:T(8,128)(2,1)S(1)} collective-permute-done((bf16[4,128,128]{2,1,0:T(8,128)(2,1)S(1)}, bf16[4,128,128]{2,1,0:T(8,128)(2,1)S(1)}, u32[]{:S(2)}, u32[]{:S(2)}) %collective-permute-start.17) | collective-permute-done | bytes 131104 | tf_op jit(solution)/shard_map/ppermute | solution.py:561
  73.6 0.0 copy-done.9
  73.6 2.4 %shard_map.112 = bf16[256,1024]{1,0:T(8,128)(2,1)} custom-call(s32[19]{0:T(128)S(1)} %pad_add_fusion.sp_ref, f32[8,256,128]{2,1,0:T(8,128)S(1)} %get-tuple-element.65.refs_0_, bf16[8,256,128]{2,1,0:T(8,128)(2,1)S(1)} %get-tuple-element.66.refs_1_, bf16[2,4,128,128]{3,2,1,0:T(8,128)(2,1)S(1)} %collective-permute-done.14.refs_4_.refs_2_, ...), custom_call_target="tpu_custom_call" | custom-call | flops 2700000000 | bytes 1000 | tf_op jit(solution)/shard_map/pallas_call | solution.py:87
  (8 shorter events, 0.0 us)
Async XLA Ops:
  0.8 3.8 %collective-permute-start = (bf16[16,2048]{1,0:T(8,128)(2,1)S(1)}, bf16[16,2048]{1,0:T(8,128)(2,1)S(1)}, u32[]{:S(2)}, u32[]{:S(2)}) collective-permute-start(bf16[16,2048]{1,0:T(8,128)(2,1)S(1)} %slice.3), channel_id=1, source_target_pairs={{0,4},{4,8},{8,12},{12,16},{16,20},{20,24},{24,28},{1,5},{5,9},{9,... | collective-permute-start | bytes 196616 | tf_op jit(solution)/shard_map/ppermute | solution.py:556
  4.6 1.6 %copy-start.2 = (bf16[512,2048]{1,0:T(8,128)(2,1)S(1)}, bf16[512,2048]{1,0:T(8,128)(2,1)}, u32[]{:S(2)}) copy-start(bf16[512,2048]{1,0:T(8,128)(2,1)} %refs_17_.2) | copy-start | bytes 6291460
  6.2 1.2 %copy-start.4 = (bf16[256,2048]{1,0:T(8,128)(2,1)S(1)}, bf16[256,2048]{1,0:T(8,128)(2,1)}, u32[]{:S(2)}) copy-start(bf16[256,2048]{1,0:T(8,128)(2,1)} %refs_0_.15) | copy-start | bytes 3145732
  7.4 5.4 %copy-start.7 = (f32[8,256]{1,0:T(8,128)S(1)}, f32[8,256]{1,0:T(8,128)}, u32[]{:S(2)}) copy-start(f32[8,256]{1,0:T(8,128)} %refs_0_.9) | copy-start | bytes 24580
  7.4 5.4 %copy-start.8 = (f32[8,256]{1,0:T(8,128)S(1)}, f32[8,256]{1,0:T(8,128)}, u32[]{:S(2)}) copy-start(f32[8,256]{1,0:T(8,128)} %refs_1_.1) | copy-start | bytes 24580
  7.4 6.6 %copy-start.5 = (bf16[256,2048]{1,0:T(8,128)(2,1)S(1)}, bf16[256,2048]{1,0:T(8,128)(2,1)}, u32[]{:S(2)}) copy-start(bf16[256,2048]{1,0:T(8,128)(2,1)} %refs_0_.15) | copy-start | bytes 3145732
  8.9 14.6 %collective-permute-start.4 = (bf16[272,512]{1,0:T(8,128)(2,1)S(1)}, bf16[272,512]{1,0:T(8,128)(2,1)S(1)}, u32[]{:S(2)}, u32[]{:S(2)}) collective-permute-start(bf16[272,512]{1,0:T(8,128)(2,1)S(1)} %get-tuple-element.44), channel_id=1, source_target_pairs={{0,2},{1,3},{2,0},{3,1},{4,6},{5,7},{6,4},{7,5},{8,10},{9,11},{10,... | collective-permute-start | bytes 835592 | tf_op jit(solution)/shard_map/ppermute | solution.py:147
  11.3 12.2 %collective-permute-start.5 = (bf16[272,512]{1,0:T(8,128)(2,1)S(1)}, bf16[272,512]{1,0:T(8,128)(2,1)S(1)}, u32[]{:S(2)}, u32[]{:S(2)}) collective-permute-start(bf16[272,512]{1,0:T(8,128)(2,1)S(1)} %get-tuple-element.45), channel_id=1, source_target_pairs={{0,3},{1,2},{2,1},{3,0},{4,7},{5,6},{6,5},{7,4},{8,11},{9,10},{10,... | collective-permute-start | bytes 835592 | tf_op jit(solution)/shard_map/ppermute | solution.py:147
  12.7 2.2 %copy-start = (bf16[512,4096]{1,0:T(8,128)(2,1)S(1)}, bf16[512,4096]{1,0:T(8,128)(2,1)}, u32[]{:S(2)}) copy-start(bf16[512,4096]{1,0:T(8,128)(2,1)} %refs_14_.1) | copy-start | bytes 12582916
  12.7 12.6 %collective-permute-start.3 = (bf16[272,512]{1,0:T(8,128)(2,1)S(1)}, bf16[272,512]{1,0:T(8,128)(2,1)S(1)}, u32[]{:S(2)}, u32[]{:S(2)}) collective-permute-start(bf16[272,512]{1,0:T(8,128)(2,1)S(1)} %get-tuple-element.37.refs_2_), channel_id=1, source_target_pairs={{0,1},{1,0},{2,3},{3,2},{4,5},{5,4},{6,7},{7,6},{8,9},{9,8},{10,11... | collective-permute-start | bytes 835592 | tf_op jit(solution)/shard_map/ppermute | solution.py:147
  14.9 4.2 %copy-start.1 = (bf16[512,2048]{1,0:T(8,128)(2,1)S(1)}, bf16[512,2048]{1,0:T(8,128)(2,1)}, u32[]{:S(2)}) copy-start(bf16[512,2048]{1,0:T(8,128)(2,1)} %refs_17_.3) | copy-start | bytes 6291460
  16.5 18.9 %collective-permute-start.2 = (bf16[2,272,512]{2,1,0:T(8,128)(2,1)S(1)}, bf16[2,272,512]{2,1,0:T(8,128)(2,1)S(1)}, u32[]{:S(2)}, u32[]{:S(2)}) collective-permute-start(bf16[2,272,512]{2,1,0:T(8,128)(2,1)S(1)} %get-tuple-element.43), channel_id=1, source_target_pairs={{0,2},{1,3},{2,0},{3,1},{4,6},{5,7},{6,4},{7,5},{8,10},{9,11},{10,... | collective-permute-start | bytes 1671176 | tf_op jit(solution)/shard_map/ppermute | solution.py:206
  18.0 7.3 %copy-start.3 = (bf16[512,2048]{1,0:T(8,128)(2,1)S(1)}, bf16[512,2048]{1,0:T(8,128)(2,1)}, u32[]{:S(2)}) copy-start(bf16[512,2048]{1,0:T(8,128)(2,1)} %refs_17_.2) | copy-start | bytes 6291460
  18.1 7.3 %copy-start.6 = (bf16[4,8192]{1,0:T(4,128)(2,1)S(1)}, bf16[4,8192]{1,0:T(4,128)(2,1)}, u32[]{:S(2)}) copy-start(bf16[4,8192]{1,0:T(4,128)(2,1)} %refs_18_.3) | copy-start | bytes 196612
  18.1 19.3 %collective-permute-start.1 = (bf16[2,272,512]{2,1,0:T(8,128)(2,1)S(1)}, bf16[2,272,512]{2,1,0:T(8,128)(2,1)S(1)}, u32[]{:S(2)}, u32[]{:S(2)}) collective-permute-start(bf16[2,272,512]{2,1,0:T(8,128)(2,1)S(1)} %get-tuple-element.39.refs_14_), channel_id=1, source_target_pairs={{0,1},{1,0},{2,3},{3,2},{4,5},{5,4},{6,7},{7,6},{8,9},{9,8},{10,11... | collective-permute-start | bytes 1671176 | tf_op jit(solution)/shard_map/ppermute | solution.py:206
  38.4 9.6 %collective-permute-start.10 = (bf16[1,272,512]{2,1,0:T(8,128)(2,1)S(1)}, bf16[1,272,512]{2,1,0:T(8,128)(2,1)S(1)}, u32[]{:S(2)}, u32[]{:S(2)}) collective-permute-start(bf16[1,272,512]{2,1,0:T(8,128)(2,1)S(1)} %get-tuple-element.54), channel_id=1, source_target_pairs={{0,1},{1,0},{2,3},{3,2},{4,5},{5,4},{6,7},{7,6},{8,9},{9,8},{10,11... | collective-permute-start | bytes 835592 | tf_op jit(solution)/shard_map/ppermute | solution.py:206
  40.9 8.6 %collective-permute-start.9 = (bf16[1,272,512]{2,1,0:T(8,128)(2,1)S(1)}, bf16[1,272,512]{2,1,0:T(8,128)(2,1)S(1)}, u32[]{:S(2)}, u32[]{:S(2)}) collective-permute-start(bf16[1,272,512]{2,1,0:T(8,128)(2,1)S(1)} %get-tuple-element.49.refs_23_), channel_id=1, source_target_pairs={{0,2},{1,3},{2,0},{3,1},{4,6},{5,7},{6,4},{7,5},{8,10},{9,11},{10,... | collective-permute-start | bytes 835592 | tf_op jit(solution)/shard_map/ppermute | solution.py:206
  52.4 3.6 %collective-permute-start.11 = (bf16[2,4,128,128]{3,2,1,0:T(8,128)(2,1)S(1)}, bf16[2,4,128,128]{3,2,1,0:T(8,128)(2,1)S(1)}, u32[]{:S(2)}, u32[]{:S(2)}) collective-permute-start(bf16[2,4,128,128]{3,2,1,0:T(8,128)(2,1)S(1)} %get-tuple-element.59), channel_id=1, source_target_pairs={{0,4},{4,0},{8,12},{12,8},{16,20},{20,16},{24,28},{28,24},{1,5},{5... | collective-permute-start | bytes 786440 | tf_op jit(solution)/shard_map/ppermute | solution.py:561
  52.5 14.0 %collective-permute-start.6 = (bf16[272,512]{1,0:T(8,128)(2,1)S(1)}, bf16[272,512]{1,0:T(8,128)(2,1)S(1)}, u32[]{:S(2)}, u32[]{:S(2)}) collective-permute-start(bf16[272,512]{1,0:T(8,128)(2,1)S(1)} %get-tuple-element.50.refs_25_), channel_id=1, source_target_pairs={{0,1},{1,0},{2,3},{3,2},{4,5},{5,4},{6,7},{7,6},{8,9},{9,8},{10,11... | collective-permute-start | bytes 835592 | tf_op jit(solution)/shard_map/ppermute | solution.py:147
  52.9 13.9 %collective-permute-start.7 = (bf16[272,512]{1,0:T(8,128)(2,1)S(1)}, bf16[272,512]{1,0:T(8,128)(2,1)S(1)}, u32[]{:S(2)}, u32[]{:S(2)}) collective-permute-start(bf16[272,512]{1,0:T(8,128)(2,1)S(1)} %get-tuple-element.51), channel_id=1, source_target_pairs={{0,2},{1,3},{2,0},{3,1},{4,6},{5,7},{6,4},{7,5},{8,10},{9,11},{10,... | collective-permute-start | bytes 835592 | tf_op jit(solution)/shard_map/ppermute | solution.py:147
  54.6 13.9 %collective-permute-start.8 = (bf16[272,512]{1,0:T(8,128)(2,1)S(1)}, bf16[272,512]{1,0:T(8,128)(2,1)S(1)}, u32[]{:S(2)}, u32[]{:S(2)}) collective-permute-start(bf16[272,512]{1,0:T(8,128)(2,1)S(1)} %get-tuple-element.52), channel_id=1, source_target_pairs={{0,3},{1,2},{2,1},{3,0},{4,7},{5,6},{6,5},{7,4},{8,11},{9,10},{10,... | collective-permute-start | bytes 835592 | tf_op jit(solution)/shard_map/ppermute | solution.py:147
  56.8 5.1 %collective-permute-start.12 = (bf16[4,128,128]{2,1,0:T(8,128)(2,1)S(1)}, bf16[4,128,128]{2,1,0:T(8,128)(2,1)S(1)}, u32[]{:S(2)}, u32[]{:S(2)}) collective-permute-start(bf16[4,128,128]{2,1,0:T(8,128)(2,1)S(1)} %get-tuple-element.61), channel_id=1, source_target_pairs={{0,8},{4,12},{1,9},{5,13},{2,10},{6,14},{3,11},{7,15}} | collective-permute-start | bytes 393224 | tf_op jit(solution)/shard_map/ppermute | solution.py:679
  59.4 5.6 %collective-permute-start.14 = (bf16[2,4,128,128]{3,2,1,0:T(8,128)(2,1)S(1)}, bf16[2,4,128,128]{3,2,1,0:T(8,128)(2,1)S(1)}, u32[]{:S(2)}, u32[]{:S(2)}) collective-permute-start(bf16[2,4,128,128]{3,2,1,0:T(8,128)(2,1)S(1)} %get-tuple-element.58.refs_0_), channel_id=1, source_target_pairs={{0,4},{4,0},{8,12},{12,8},{16,20},{20,16},{24,28},{28,24},{1,5},{5... | collective-permute-start | bytes 786440 | tf_op jit(solution)/shard_map/ppermute | solution.py:561
  62.6 2.4 %collective-permute-start.13 = (bf16[4,128,128]{2,1,0:T(8,128)(2,1)S(1)}, bf16[4,128,128]{2,1,0:T(8,128)(2,1)S(1)}, u32[]{:S(2)}, u32[]{:S(2)}) collective-permute-start(bf16[4,128,128]{2,1,0:T(8,128)(2,1)S(1)} %get-tuple-element.62.refs_6_), channel_id=1, source_target_pairs={{8,16},{12,20},{9,17},{13,21},{10,18},{14,22},{11,19},{15,23}} | collective-permute-start | bytes 393224 | tf_op jit(solution)/shard_map/ppermute | solution.py:679
  65.7 6.5 %collective-permute-start.15 = (bf16[4,128,128]{2,1,0:T(8,128)(2,1)S(1)}, bf16[4,128,128]{2,1,0:T(8,128)(2,1)S(1)}, u32[]{:S(2)}, u32[]{:S(2)}) collective-permute-start(bf16[4,128,128]{2,1,0:T(8,128)(2,1)S(1)} %get-tuple-element.64.refs_27_), channel_id=1, source_target_pairs={{16,24},{20,28},{17,25},{21,29},{18,26},{22,30},{19,27},{23,31}} | collective-permute-start | bytes 393224 | tf_op jit(solution)/shard_map/ppermute | solution.py:679
  66.4 7.2 %copy-start.9 = (f32[128]{0:T(128)S(1)}, f32[128]{0:T(128)}, u32[]{:S(2)}) copy-start(f32[128]{0:T(128)} %param.17) | copy-start | bytes 1540
  66.4 5.9 %collective-permute-start.16 = (bf16[4,128,128]{2,1,0:T(8,128)(2,1)S(1)}, bf16[4,128,128]{2,1,0:T(8,128)(2,1)S(1)}, u32[]{:S(2)}, u32[]{:S(2)}) collective-permute-start(bf16[4,128,128]{2,1,0:T(8,128)(2,1)S(1)} %get-tuple-element.67.refs_5_), channel_id=1, source_target_pairs={{0,4},{4,0},{8,12},{12,8},{16,20},{20,16},{24,28},{28,24},{1,5},{5... | collective-permute-start | bytes 393224 | tf_op jit(solution)/shard_map/ppermute | solution.py:561
  72.2 1.4 %collective-permute-start.17 = (bf16[4,128,128]{2,1,0:T(8,128)(2,1)S(1)}, bf16[4,128,128]{2,1,0:T(8,128)(2,1)S(1)}, u32[]{:S(2)}, u32[]{:S(2)}) collective-permute-start(bf16[4,128,128]{2,1,0:T(8,128)(2,1)S(1)} %collective-permute-done.15.refs_6_), channel_id=1, source_target_pairs={{0,4},{4,0},{8,12},{12,8},{16,20},{20,16},{24,28},{28,24},{1,5},{5... | collective-permute-start | bytes 393224 | tf_op jit(solution)/shard_map/ppermute | solution.py:561

commit v5 on v4

--- a/solution.py
+++ b/solution.py
@@ -114,7 +114,7 @@
 
 
 def hidden_spec(hidden, rows):
-    return pl.BlockSpec((hidden.shape[0], rows), lambda i, sp: (0, sp[0]))
+    return whole(hidden)
 
 
 def partial_sums(key_heads, ranks, heads, width, hidden, rim, weight, sp, after=()):
@@ -623,7 +623,10 @@
     place = 2 + total_heads
     w_value = payload_projection_matrix
 
-    rim = shifted(hidden[count - RIM :], 1) * keep.astype(BF16)
+    rows = w_key.shape[0]
+    edge = lax.dynamic_slice(hidden, (count - RIM, serve * rows), (RIM, rows))
+    rim = shifted(edge, 1) * keep.astype(BF16)
+    hidden = lax.dynamic_slice(hidden, (0, serve * rows), (count, rows))
     sp = jnp.concatenate(
         [jnp.stack([serve, keep]), head_order, jnp.stack([spot % 2])]
     ).astype(jnp.int32)
@@ -634,8 +637,9 @@
     def gathered(width, weight, base, parts):
         return gather_specs(key_heads, width, hidden, rim, weight, conv_weight, base, parts)
 
-    part_k = partial_sums(key_heads, ranks, everyone, HEAD, hidden, rim, w_key, sp)
-    got_k = exchange(part_k)
+    got_k = [[] for _ in halving.routes]
+    part_k = halving.send(0, key_heads, HEAD, hidden, rim, w_key, got_k, sp)
+    halving.exchange(0, part_k, got_k)
     tables = list(prepare(log_decay, beta_rate, sp, after=part_k[:1]))
     got_v = [[] for _ in halving.routes]
     part_v = halving.send(
@@ -645,9 +649,14 @@
     part_q = partial_sums(
         key_heads, ranks, everyone, HEAD, hidden, rim, w_query, sp, after=part_v[:1]
     )
+    for stage in range(1, halving.stages):
+        part_k = halving.send(
+            stage, key_heads, HEAD, hidden, rim, w_key, got_k, sp, after=part_q[:1]
+        )
+        halving.exchange(stage, part_k, got_k)
     keys, solve, gathers, trans_a = key_phase(
-        gathered(HEAD, w_key, total_heads, [direct_parts(h, HEAD, got_k) for h in everyone]),
-        number, count, tables, sp, after=part_q[:1],
+        gathered(HEAD, w_key, total_heads, [halving.parts(h, HEAD, got_k) for h in everyone]),
+        number, count, tables, sp, after=part_k[:1],
     )
     ordered = [trans_a]
     for stage in range(1, halving.stages):
@@ -667,12 +676,11 @@
     )
     taken = swapped(given)
     joined, joined_b = join_cores(own, taken, sp, place)
-    early = swapped(own)
     states, last, writes = [], joined_b, None
     if chips <= 4:
         for chip in range(chips - 1):
             if chip:
-                after = [] if writes is None else [writes, early]
+                after = [] if writes is None else [writes]
                 last, so_far = pass_chip(joined, states, sp, after)
                 states = [so_far]
             hop = [(2 * chip + c, 2 * chip + 2 + c) for c in range(2)]
@@ -687,6 +695,8 @@
         gathered(HEAD, w_query, 0, [direct_parts(h, HEAD, got_q) for h in everyone]),
         number, count, tables, keys, writes, sp, after=[last],
     )
+    own, _ = lax.optimization_barrier((own, writes))
+    early = swapped(own)
     others = [swapped(state) for state in states[:-1]]
     final, _ = lax.optimization_barrier((states[-1], inner))
     return finish(

time: 77.4 us -> 76.6 us (0.990)
  waiting for transfers between devices: 22.5 us -> 24.4 us
  local copies, waits for them, and re-layouts: 4.56 us -> 2.91 us
  starting transfers between devices: 20.6 us -> 19 us
  Pallas kernels: 26.7 us -> 28 us
    ppermute x4 -> x8, waiting for transfers between devices: 11.9 us -> 18.4 us  [exchange(): received[route].append(lax.ppermute(part, 'head', pairs))]
    ppermute x6 -> x3, waiting for transfers between devices: 6.78 us -> 2.12 us  [exchange(): lax.ppermute(part, 'head', [(i, i ^ unit + 1) for i in range(ranks)])]
    ppermute x6 -> x3, starting transfers between devices: 7.52 us -> 3.55 us  [exchange(): lax.ppermute(part, 'head', [(i, i ^ unit + 1) for i in range(ranks)])]
    ppermute x4 -> x8, starting transfers between devices: 6.61 us -> 8.96 us  [exchange(): received[route].append(lax.ppermute(part, 'head', pairs))]
    pallas_call x13 -> x14, Pallas kernels: 26.7 us -> 28 us  [call(): pl.pallas_call(inner, grid_spec=pltpu.PrefetchScalarGridSpec(num_scalar_p...]
    slice x1 -> x0, local copies, waits for them, and re-layouts: 0.84 us -> none  [per_device(): rim = shifted(hidden[count - RIM:], 1) * keep.astype(BF16)]
    unnamed x20 -> x18, local copies, waits for them, and re-layouts: 3.71 us -> 2.88 us
  transfers between devices with their start and end apart: 18 -> 19, of which waited for: 10 -> 10; matrix products, arithmetic and copies ran while one was open for 1% -> 1% of each run, Pallas kernels for 25% -> 25%
where the time goes in v5:
time: 76.6 us; the launch traced here: 75.9 us
  Pallas kernels  28 us (37%)
  waiting for transfers between devices  24.4 us (32%)
  starting transfers between devices  19 us (25%)
  local copies, waits for them, and re-layouts  2.91 us (4%)
  between operations  0.91 us (1%)
    pallas_call x14, Pallas kernels, call(): pl.pallas_call(inner, grid_spec=pltpu.PrefetchScalarGridSpec(num_scalar_p...  28 us
    ppermute x8, waiting for transfers between devices, exchange(): received[route].append(lax.ppermute(part, 'head', pairs))  18.4 us
    ppermute x8, starting transfers between devices, exchange(): received[route].append(lax.ppermute(part, 'head', pairs))  8.96 us
    ppermute x3, starting transfers between devices, exchange(): lax.ppermute(part, 'head', [(i, i ^ unit + 1) for i in range(ranks)])  3.55 us
    ppermute x3, starting transfers between devices, per_device(): states.append(lax.ppermute(last, 'ctx', hop))  3.39 us
    unnamed x18, local copies, waits for them, and re-layouts  2.88 us
    ppermute x3, waiting for transfers between devices, per_device(): states.append(lax.ppermute(last, 'ctx', hop))  2.51 us
    ppermute x1, starting transfers between devices, shifted(): lax.ppermute(value, 'ctx', [(i, i + steps) for i in range(count - steps)])  2.35 us
  transfers between devices with their start and end apart: 19, of which 10 were waited for; matrix products, arithmetic and copies ran while one was open for 1% of the time, Pallas kernels for 25%

profile of v5, /device:TPU:0, one launch (start us, length us, event | category | flops | bytes accessed | tf_op | source)
XLA Modules:
  0.0 75.9 jit_solution(5199557909442734450)
XLA Ops:
  0.0 0.0 copy-start
  0.0 1.2 %copy-done = bf16[256,2048]{1,0:T(8,128)(2,1)S(1)} copy-done((bf16[256,2048]{1,0:T(8,128)(2,1)S(1)}, bf16[256,2048]{1,0:T(8,128)(2,1)}, u32[]{:S(2)}) %copy-start) | copy-done | bytes 1048600
  1.2 2.3 %collective-permute-start = (bf16[16,512]{1,0:T(8,128)(2,1)S(1)}, bf16[16,512]{1,0:T(8,128)(2,1)S(1)}, u32[]{:S(2)}, u32[]{:S(2)}) collective-permute-start(bf16[16,512]{1,0:T(8,128)(2,1)S(1)} %constant_dynamic-slice_fusion), channel_id=1, source_target_pairs={{0,4},{4,8},{8,12},{12,16},{16,20},{20,24},{24,28},{1,5},{5,9},{9,... | collective-permute-start | bytes 49160 | tf_op jit(solution)/shard_map/ppermute | solution.py:556
  4.3 0.7 pad_add_fusion.sp_ref
  5.0 0.0 collective-permute-done
  5.0 0.0 copy-start.3
  5.0 1.6 %copy-done.3 = bf16[512,2048]{1,0:T(8,128)(2,1)S(1)} copy-done((bf16[512,2048]{1,0:T(8,128)(2,1)S(1)}, bf16[512,2048]{1,0:T(8,128)(2,1)}, u32[]{:S(2)}) %copy-start.3) | copy-done | bytes 2097176
  6.6 1.6 %shard_map.100 = (bf16[2,272,256]{2,1,0:T(8,128)(2,1)S(1)}, bf16[2,272,256]{2,1,0:T(8,128)(2,1)S(1)}) custom-call(s32[19]{0:T(128)S(1)} %pad_add_fusion.sp_ref, bf16[256,512]{1,0:T(8,128)(2,1)S(1)} %constant_dynamic-slice_fusion.1.refs_0_, bf16[16,512]{1,0:T(8,128)(2,1)S(1)} %broadcast_multiply_fusion.refs_1_, bf16[512,2048]{1,0:T(8,128)(2,1)S(1)} %copy-done.3, ...), custom_call_target="tpu_custom_call" | custom-call | flops 1300000000 | bytes 1000 | tf_op jit(solution)/shard_map/pallas_call | solution.py:87
  8.2 2.4 %collective-permute-start.4 = (bf16[2,272,256]{2,1,0:T(8,128)(2,1)S(1)}, bf16[2,272,256]{2,1,0:T(8,128)(2,1)S(1)}, u32[]{:S(2)}, u32[]{:S(2)}) collective-permute-start(bf16[2,272,256]{2,1,0:T(8,128)(2,1)S(1)} %get-tuple-element.46), channel_id=1, source_target_pairs={{0,2},{1,3},{2,0},{3,1},{4,6},{5,7},{6,4},{7,5},{8,10},{9,11},{10,... | collective-permute-start | bytes 835592 | tf_op jit(solution)/shard_map/ppermute | solution.py:206
  10.6 1.5 %collective-permute-start.3 = (bf16[2,272,256]{2,1,0:T(8,128)(2,1)S(1)}, bf16[2,272,256]{2,1,0:T(8,128)(2,1)S(1)}, u32[]{:S(2)}, u32[]{:S(2)}) collective-permute-start(bf16[2,272,256]{2,1,0:T(8,128)(2,1)S(1)} %get-tuple-element.39.refs_2_), channel_id=1, source_target_pairs={{0,1},{1,0},{2,3},{3,2},{4,5},{5,4},{6,7},{7,6},{8,9},{9,8},{10,11... | collective-permute-start | bytes 835592 | tf_op jit(solution)/shard_map/ppermute | solution.py:206
  12.1 0.0 copy-done.6
  12.1 0.0 copy-done.7
  12.1 1.2 %shard_map.101 = (f32[8,256]{1,0:T(8,128)S(1)}, f32[256,8]{1,0:T(8,128)S(1)}, f32[256,8]{1,0:T(8,128)S(1)}) custom-call(s32[19]{0:T(128)S(1)} %pad_add_fusion.sp_ref, f32[8,256]{1,0:T(8,128)S(1)} %copy-done.6, f32[8,256]{1,0:T(8,128)S(1)} %copy-done.7, bf16[2,272,256]{2,1,0:T(8,128)(2,1)S(1)} %get-tuple-element.39.refs_2_), custom_call_target="tpu_custom_call" | custom-call | flops 1200000000 | bytes 1000 | tf_op jit(solution)/shard_map/pallas_call | solution.py:87
  13.3 0.0 copy-done.1
  13.3 0.0 copy-start.2
  13.3 1.5 %shard_map.102 = (bf16[2,272,512]{2,1,0:T(8,128)(2,1)S(1)}, bf16[2,272,512]{2,1,0:T(8,128)(2,1)S(1)}) custom-call(s32[19]{0:T(128)S(1)} %pad_add_fusion.sp_ref, bf16[256,512]{1,0:T(8,128)(2,1)S(1)} %constant_dynamic-slice_fusion.1.refs_0_, bf16[16,512]{1,0:T(8,128)(2,1)S(1)} %broadcast_multiply_fusion.refs_1_, bf16[512,4096]{1,0:T(8,128)(2,1)S(1)} %copy-done.1, ...), custom_call_target="tpu_custom_call" | custom-call | flops 1300000000 | bytes 1000 | tf_op jit(solution)/shard_map/pallas_call | solution.py:87
  14.9 0.0 copy-done.2
  14.9 1.5 %shard_map.103 = (bf16[272,512]{1,0:T(8,128)(2,1)S(1)}, bf16[272,512]{1,0:T(8,128)(2,1)S(1)}, bf16[272,512]{1,0:T(8,128)(2,1)S(1)}) custom-call(s32[19]{0:T(128)S(1)} %pad_add_fusion.sp_ref, bf16[256,512]{1,0:T(8,128)(2,1)S(1)} %constant_dynamic-slice_fusion.1.refs_0_, bf16[16,512]{1,0:T(8,128)(2,1)S(1)} %broadcast_multiply_fusion.refs_1_, ...), custom_call_target="tpu_custom_call" | custom-call | flops 1300000000 | bytes 1000 | tf_op jit(solution)/shard_map/pallas_call | solution.py:87
  16.4 0.4 collective-permute-done.4.refs_5_.refs_12_.refs_16_
  16.8 2.8 %collective-permute-done.3.refs_2_.refs_4_.refs_8_ = bf16[2,272,256]{2,1,0:T(8,128)(2,1)S(1)} collective-permute-done((bf16[2,272,256]{2,1,0:T(8,128)(2,1)S(1)}, bf16[2,272,256]{2,1,0:T(8,128)(2,1)S(1)}, u32[]{:S(2)}, u32[]{:S(2)}) %collective-permute-start.3) | collective-permute-done | bytes 278560 | tf_op jit(solution)/shard_map/ppermute | solution.py:206
  19.6 1.1 %shard_map.104 = (bf16[1,272,256]{2,1,0:T(8,128)(2,1)S(1)}, bf16[1,272,256]{2,1,0:T(8,128)(2,1)S(1)}) custom-call(s32[19]{0:T(128)S(1)} %pad_add_fusion.sp_ref, bf16[256,512]{1,0:T(8,128)(2,1)S(1)} %constant_dynamic-slice_fusion.1.refs_0_, bf16[16,512]{1,0:T(8,128)(2,1)S(1)} %broadcast_multiply_fusion.refs_1_, ...), custom_call_target="tpu_custom_call" | custom-call | flops 1300000000 | bytes 1000 | tf_op jit(solution)/shard_map/pallas_call | solution.py:87
  20.7 1.6 %collective-permute-start.6 = (bf16[1,272,256]{2,1,0:T(8,128)(2,1)S(1)}, bf16[1,272,256]{2,1,0:T(8,128)(2,1)S(1)}, u32[]{:S(2)}, u32[]{:S(2)}) collective-permute-start(bf16[1,272,256]{2,1,0:T(8,128)(2,1)S(1)} %get-tuple-element.48), channel_id=1, source_target_pairs={{0,1},{1,0},{2,3},{3,2},{4,5},{5,4},{6,7},{7,6},{8,9},{9,8},{10,11... | collective-permute-start | bytes 417800 | tf_op jit(solution)/shard_map/ppermute | solution.py:206
  22.3 0.5 collective-permute-start.5
  22.8 1.5 %collective-permute-start.2 = (bf16[2,272,512]{2,1,0:T(8,128)(2,1)S(1)}, bf16[2,272,512]{2,1,0:T(8,128)(2,1)S(1)}, u32[]{:S(2)}, u32[]{:S(2)}) collective-permute-start(bf16[2,272,512]{2,1,0:T(8,128)(2,1)S(1)} %get-tuple-element.45), channel_id=1, source_target_pairs={{0,2},{1,3},{2,0},{3,1},{4,6},{5,7},{6,4},{7,5},{8,10},{9,11},{10,... | collective-permute-start | bytes 1671176 | tf_op jit(solution)/shard_map/ppermute | solution.py:206
  24.3 0.5 collective-permute-start.1
  24.9 2.1 %collective-permute-done.6.refs_13_.refs_17_ = bf16[1,272,256]{2,1,0:T(8,128)(2,1)S(1)} collective-permute-done((bf16[1,272,256]{2,1,0:T(8,128)(2,1)S(1)}, bf16[1,272,256]{2,1,0:T(8,128)(2,1)S(1)}, u32[]{:S(2)}, u32[]{:S(2)}) %collective-permute-start.6) | collective-permute-done | bytes 139296 | tf_op jit(solution)/shard_map/ppermute | solution.py:206
  27.0 1.9 %collective-permute-done.5.refs_5_.refs_9_ = bf16[1,272,256]{2,1,0:T(8,128)(2,1)S(1)} collective-permute-done((bf16[1,272,256]{2,1,0:T(8,128)(2,1)S(1)}, bf16[1,272,256]{2,1,0:T(8,128)(2,1)S(1)}, u32[]{:S(2)}, u32[]{:S(2)}) %collective-permute-start.5) | collective-permute-done | bytes 139296 | tf_op jit(solution)/shard_map/ppermute | solution.py:206
  28.8 7.1 %shard_map.105 = (f32[4,256,128]{2,1,0:T(8,128)S(1)}, bf16[8,3,128,256]{3,2,1,0:T(8,128)(2,1)S(1)}, bf16[8,2,128,256]{3,2,1,0:T(8,128)(2,1)S(1)}, f32[8,128,128]{2,1,0:T(8,128)S(1)}) custom-call(s32[19]{0:T(128)S(1)} %pad_add_fusion.sp_ref, bf16[256,512]{1,0:T(8,128)(2,1)S(1)} %constant_dynamic-slice_fusion.1.refs_0_, ...), custom_call_target="tpu_custom_call" | custom-call | flops 5000000000 | bytes 1000 | tf_op jit(solution)/shard_map/pallas_call | solution.py:87
  35.9 4.0 %collective-permute-done.2.refs_5_.refs_12_.refs_16_ = bf16[2,272,512]{2,1,0:T(8,128)(2,1)S(1)} collective-permute-done((bf16[2,272,512]{2,1,0:T(8,128)(2,1)S(1)}, bf16[2,272,512]{2,1,0:T(8,128)(2,1)S(1)}, u32[]{:S(2)}, u32[]{:S(2)}) %collective-permute-start.2) | collective-permute-done | bytes 557088 | tf_op jit(solution)/shard_map/ppermute | solution.py:206
  39.9 0.0 collective-permute-done.1.refs_2_.refs_4_.refs_8_
  39.9 1.1 %shard_map.106 = (bf16[1,272,512]{2,1,0:T(8,128)(2,1)S(1)}, bf16[1,272,512]{2,1,0:T(8,128)(2,1)S(1)}) custom-call(s32[19]{0:T(128)S(1)} %pad_add_fusion.sp_ref, bf16[256,512]{1,0:T(8,128)(2,1)S(1)} %constant_dynamic-slice_fusion.1.refs_0_, bf16[16,512]{1,0:T(8,128)(2,1)S(1)} %broadcast_multiply_fusion.refs_1_, ...), custom_call_target="tpu_custom_call" | custom-call | flops 1300000000 | bytes 1000 | tf_op jit(solution)/shard_map/pallas_call | solution.py:87
  41.0 0.6 collective-permute-start.11
  41.6 0.3 collective-permute-start.10
  41.9 7.0 %collective-permute-done.11.refs_13_.refs_17_ = bf16[1,272,512]{2,1,0:T(8,128)(2,1)S(1)} collective-permute-done((bf16[1,272,512]{2,1,0:T(8,128)(2,1)S(1)}, bf16[1,272,512]{2,1,0:T(8,128)(2,1)S(1)}, u32[]{:S(2)}, u32[]{:S(2)}) %collective-permute-start.11) | collective-permute-done | bytes 278560 | tf_op jit(solution)/shard_map/ppermute | solution.py:206
  48.9 0.3 collective-permute-done.10.refs_5_.refs_9_
  49.2 2.9 %shard_map.107 = (f32[8,256,128]{2,1,0:T(8,128)S(1)}, bf16[2,4,128,128]{3,2,1,0:T(8,128)(2,1)S(1)}, bf16[2,4,128,128]{3,2,1,0:T(8,128)(2,1)S(1)}) custom-call(s32[19]{0:T(128)S(1)} %pad_add_fusion.sp_ref, bf16[256,512]{1,0:T(8,128)(2,1)S(1)} %constant_dynamic-slice_fusion.1.refs_0_, bf16[16,512]{1,0:T(8,128)(2,1)S(1)} %broadcast_multiply_fusion.refs_1_, ...), custom_call_target="tpu_custom_call" | custom-call | flops 50000000 | bytes 1000 | tf_op jit(solution)/shard_map/pallas_call | solution.py:87
  52.1 0.1 collective-permute-start.12
  52.2 1.5 %collective-permute-start.7 = (bf16[272,512]{1,0:T(8,128)(2,1)S(1)}, bf16[272,512]{1,0:T(8,128)(2,1)S(1)}, u32[]{:S(2)}, u32[]{:S(2)}) collective-permute-start(bf16[272,512]{1,0:T(8,128)(2,1)S(1)} %get-tuple-element.53.refs_8_), channel_id=1, source_target_pairs={{0,1},{1,0},{2,3},{3,2},{4,5},{5,4},{6,7},{7,6},{8,9},{9,8},{10,11... | collective-permute-start | bytes 835592 | tf_op jit(solution)/shard_map/ppermute | solution.py:147
  53.7 0.5 collective-permute-start.8
  54.1 1.6 %collective-permute-start.9 = (bf16[272,512]{1,0:T(8,128)(2,1)S(1)}, bf16[272,512]{1,0:T(8,128)(2,1)S(1)}, u32[]{:S(2)}, u32[]{:S(2)}) collective-permute-start(bf16[272,512]{1,0:T(8,128)(2,1)S(1)} %get-tuple-element.55), channel_id=1, source_target_pairs={{0,3},{1,2},{2,1},{3,0},{4,7},{5,6},{6,5},{7,4},{8,11},{9,10},{10,... | collective-permute-start | bytes 835592 | tf_op jit(solution)/shard_map/ppermute | solution.py:147
  55.7 0.0 collective-permute-done.12.refs_1_.refs_3_
  55.7 0.8 %shard_map.108 = (bf16[2,4,128,128]{3,2,1,0:T(8,128)(2,1)S(1)}, bf16[4,128,128]{2,1,0:T(8,128)(2,1)S(1)}) custom-call(s32[19]{0:T(128)S(1)} %pad_add_fusion.sp_ref, bf16[2,4,128,128]{3,2,1,0:T(8,128)(2,1)S(1)} %get-tuple-element.70.refs_0_, bf16[2,4,128,128]{3,2,1,0:T(8,128)(2,1)S(1)} %collective-permute-done.12.refs_1_.refs_3_), custom_call_target="tpu_custom_call" | custom-call | flops 50000000 | bytes 1000 | tf_op jit(solution)/shard_map/pallas_call | solution.py:87
  56.5 2.1 %collective-permute-start.13 = (bf16[4,128,128]{2,1,0:T(8,128)(2,1)S(1)}, bf16[4,128,128]{2,1,0:T(8,128)(2,1)S(1)}, u32[]{:S(2)}, u32[]{:S(2)}) collective-permute-start(bf16[4,128,128]{2,1,0:T(8,128)(2,1)S(1)} %get-tuple-element.64), channel_id=1, source_target_pairs={{0,8},{4,12},{1,9},{5,13},{2,10},{6,14},{3,11},{7,15}} | collective-permute-start | bytes 393224 | tf_op jit(solution)/shard_map/ppermute | solution.py:687
  58.6 2.5 %collective-permute-done.13.refs_1_ = bf16[4,128,128]{2,1,0:T(8,128)(2,1)S(1)} collective-permute-done((bf16[4,128,128]{2,1,0:T(8,128)(2,1)S(1)}, bf16[4,128,128]{2,1,0:T(8,128)(2,1)S(1)}, u32[]{:S(2)}, u32[]{:S(2)}) %collective-permute-start.13) | collective-permute-done | bytes 131104 | tf_op jit(solution)/shard_map/ppermute | solution.py:687
  61.1 0.7 shard_map.109
  61.8 0.7 collective-permute-start.14
  62.5 1.7 %shard_map.110.refs_3_.refs_26_ = f32[8,256,256]{2,1,0:T(8,128)S(1)} custom-call(s32[19]{0:T(128)S(1)} %pad_add_fusion.sp_ref, f32[8,256,128]{2,1,0:T(8,128)S(1)} %get-tuple-element.59.refs_0_, f32[4,256,128]{2,1,0:T(8,128)S(1)} %get-tuple-element.56.refs_1_.refs_25_, f32[8,256]{1,0:T(8,128)S(1)} %get-tuple-element.40.refs_10_.refs_18_.refs_2_.refs_22_, ...), custom_call_target="tpu_custom_call" | custom-call | flops 50000000 | bytes 1000 | tf_op jit(solution)/shard_map/pallas_call | solution.py:87
  64.2 0.1 collective-permute-start.15
  64.3 0.0 collective-permute-done.14.refs_2_
  64.3 0.7 shard_map.111
  65.0 0.7 collective-permute-start.16
  65.7 0.0 collective-permute-done.7.refs_4_.refs_9_.refs_14_.refs_19_
  65.7 0.0 copy-start.8
  65.7 0.6 collective-permute-start.17
  66.3 2.1 %collective-permute-done.8.refs_5_.refs_10_.refs_15_.refs_20_ = bf16[272,512]{1,0:T(8,128)(2,1)S(1)} collective-permute-done((bf16[272,512]{1,0:T(8,128)(2,1)S(1)}, bf16[272,512]{1,0:T(8,128)(2,1)S(1)}, u32[]{:S(2)}, u32[]{:S(2)}) %collective-permute-start.8) | collective-permute-done | bytes 278560 | tf_op jit(solution)/shard_map/ppermute | solution.py:147
  68.4 0.0 collective-permute-done.9.refs_6_.refs_11_.refs_16_.refs_21_
  68.4 3.7 %shard_map.112 = (f32[8,256,128]{2,1,0:T(8,128)S(1)}, bf16[8,256,128]{2,1,0:T(8,128)(2,1)S(1)}) custom-call(s32[19]{0:T(128)S(1)} %pad_add_fusion.sp_ref, bf16[256,512]{1,0:T(8,128)(2,1)S(1)} %constant_dynamic-slice_fusion.1.refs_0_, bf16[16,512]{1,0:T(8,128)(2,1)S(1)} %broadcast_multiply_fusion.refs_1_, bf16[512,2048]{1,0:T(8,128)(2,1)S(1)} %copy-done.2, ...), custom_call_target="tpu_custom_call" | custom-call | flops 3700000000 | bytes 1000 | tf_op jit(solution)/shard_map/pallas_call | solution.py:87
  72.1 0.0 collective-permute-done.16.refs_6_
  72.1 0.1 collective-permute-start.18
  72.2 0.0 collective-permute-done.17.refs_7_
  72.2 0.0 collective-permute-done.15.refs_2_
  72.2 1.3 %collective-permute-done.18.refs_8_ = bf16[4,128,128]{2,1,0:T(8,128)(2,1)S(1)} collective-permute-done((bf16[4,128,128]{2,1,0:T(8,128)(2,1)S(1)}, bf16[4,128,128]{2,1,0:T(8,128)(2,1)S(1)}, u32[]{:S(2)}, u32[]{:S(2)}) %collective-permute-start.18) | collective-permute-done | bytes 131104 | tf_op jit(solution)/shard_map/ppermute | solution.py:561
  73.5 0.0 copy-done.8
  73.5 2.4 %shard_map.113 = bf16[256,1024]{1,0:T(8,128)(2,1)} custom-call(s32[19]{0:T(128)S(1)} %pad_add_fusion.sp_ref, f32[8,256,128]{2,1,0:T(8,128)S(1)} %get-tuple-element.68.refs_0_, bf16[8,256,128]{2,1,0:T(8,128)(2,1)S(1)} %get-tuple-element.69.refs_1_, bf16[2,4,128,128]{3,2,1,0:T(8,128)(2,1)S(1)} %collective-permute-done.15.refs_2_, ...), custom_call_target="tpu_custom_call" | custom-call | flops 2700000000 | bytes 1000 | tf_op jit(solution)/shard_map/pallas_call | solution.py:87
  (10 shorter events, 0.0 us)
Async XLA Ops:
  0.0 1.2 %copy-start = (bf16[256,2048]{1,0:T(8,128)(2,1)S(1)}, bf16[256,2048]{1,0:T(8,128)(2,1)}, u32[]{:S(2)}) copy-start(bf16[256,2048]{1,0:T(8,128)(2,1)} %param.10) | copy-start | bytes 3145732
  1.2 3.8 %collective-permute-start = (bf16[16,512]{1,0:T(8,128)(2,1)S(1)}, bf16[16,512]{1,0:T(8,128)(2,1)S(1)}, u32[]{:S(2)}, u32[]{:S(2)}) collective-permute-start(bf16[16,512]{1,0:T(8,128)(2,1)S(1)} %constant_dynamic-slice_fusion), channel_id=1, source_target_pairs={{0,4},{4,8},{8,12},{12,16},{16,20},{20,24},{24,28},{1,5},{5,9},{9,... | collective-permute-start | bytes 49160 | tf_op jit(solution)/shard_map/ppermute | solution.py:556
  5.0 1.6 %copy-start.3 = (bf16[512,2048]{1,0:T(8,128)(2,1)S(1)}, bf16[512,2048]{1,0:T(8,128)(2,1)}, u32[]{:S(2)}) copy-start(bf16[512,2048]{1,0:T(8,128)(2,1)} %refs_14_.2) | copy-start | bytes 6291460
  6.6 5.5 %copy-start.6 = (f32[8,256]{1,0:T(8,128)S(1)}, f32[8,256]{1,0:T(8,128)}, u32[]{:S(2)}) copy-start(f32[8,256]{1,0:T(8,128)} %refs_0_.1) | copy-start | bytes 24580
  6.6 5.5 %copy-start.7 = (f32[8,256]{1,0:T(8,128)S(1)}, f32[8,256]{1,0:T(8,128)}, u32[]{:S(2)}) copy-start(f32[8,256]{1,0:T(8,128)} %refs_1_.1) | copy-start | bytes 24580
  8.2 8.6 %collective-permute-start.4 = (bf16[2,272,256]{2,1,0:T(8,128)(2,1)S(1)}, bf16[2,272,256]{2,1,0:T(8,128)(2,1)S(1)}, u32[]{:S(2)}, u32[]{:S(2)}) collective-permute-start(bf16[2,272,256]{2,1,0:T(8,128)(2,1)S(1)} %get-tuple-element.46), channel_id=1, source_target_pairs={{0,2},{1,3},{2,0},{3,1},{4,6},{5,7},{6,4},{7,5},{8,10},{9,11},{10,... | collective-permute-start | bytes 835592 | tf_op jit(solution)/shard_map/ppermute | solution.py:206
  10.6 2.7 %copy-start.1 = (bf16[512,4096]{1,0:T(8,128)(2,1)S(1)}, bf16[512,4096]{1,0:T(8,128)(2,1)}, u32[]{:S(2)}) copy-start(bf16[512,4096]{1,0:T(8,128)(2,1)} %refs_14_.3) | copy-start | bytes 12582916
  10.6 9.0 %collective-permute-start.3 = (bf16[2,272,256]{2,1,0:T(8,128)(2,1)S(1)}, bf16[2,272,256]{2,1,0:T(8,128)(2,1)S(1)}, u32[]{:S(2)}, u32[]{:S(2)}) collective-permute-start(bf16[2,272,256]{2,1,0:T(8,128)(2,1)S(1)} %get-tuple-element.39.refs_2_), channel_id=1, source_target_pairs={{0,1},{1,0},{2,3},{3,2},{4,5},{5,4},{6,7},{7,6},{8,9},{9,8},{10,11... | collective-permute-start | bytes 835592 | tf_op jit(solution)/shard_map/ppermute | solution.py:206
  13.3 1.6 %copy-start.2 = (bf16[512,2048]{1,0:T(8,128)(2,1)S(1)}, bf16[512,2048]{1,0:T(8,128)(2,1)}, u32[]{:S(2)}) copy-start(bf16[512,2048]{1,0:T(8,128)(2,1)} %refs_17_.1) | copy-start | bytes 6291460
  14.9 4.7 %copy-start.4 = (bf16[512,2048]{1,0:T(8,128)(2,1)S(1)}, bf16[512,2048]{1,0:T(8,128)(2,1)}, u32[]{:S(2)}) copy-start(bf16[512,2048]{1,0:T(8,128)(2,1)} %refs_14_.2) | copy-start | bytes 6291460
  19.6 9.2 %copy-start.5 = (bf16[4,8192]{1,0:T(4,128)(2,1)S(1)}, bf16[4,8192]{1,0:T(4,128)(2,1)}, u32[]{:S(2)}) copy-start(bf16[4,8192]{1,0:T(4,128)(2,1)} %refs_18_.1) | copy-start | bytes 196612
  20.7 6.2 %collective-permute-start.6 = (bf16[1,272,256]{2,1,0:T(8,128)(2,1)S(1)}, bf16[1,272,256]{2,1,0:T(8,128)(2,1)S(1)}, u32[]{:S(2)}, u32[]{:S(2)}) collective-permute-start(bf16[1,272,256]{2,1,0:T(8,128)(2,1)S(1)} %get-tuple-element.48), channel_id=1, source_target_pairs={{0,1},{1,0},{2,3},{3,2},{4,5},{5,4},{6,7},{7,6},{8,9},{9,8},{10,11... | collective-permute-start | bytes 417800 | tf_op jit(solution)/shard_map/ppermute | solution.py:206
  22.3 6.5 %collective-permute-start.5 = (bf16[1,272,256]{2,1,0:T(8,128)(2,1)S(1)}, bf16[1,272,256]{2,1,0:T(8,128)(2,1)S(1)}, u32[]{:S(2)}, u32[]{:S(2)}) collective-permute-start(bf16[1,272,256]{2,1,0:T(8,128)(2,1)S(1)} %get-tuple-element.47.refs_21_), channel_id=1, source_target_pairs={{0,2},{1,3},{2,0},{3,1},{4,6},{5,7},{6,4},{7,5},{8,10},{9,11},{10,... | collective-permute-start | bytes 417800 | tf_op jit(solution)/shard_map/ppermute | solution.py:206
  22.8 17.1 %collective-permute-start.2 = (bf16[2,272,512]{2,1,0:T(8,128)(2,1)S(1)}, bf16[2,272,512]{2,1,0:T(8,128)(2,1)S(1)}, u32[]{:S(2)}, u32[]{:S(2)}) collective-permute-start(bf16[2,272,512]{2,1,0:T(8,128)(2,1)S(1)} %get-tuple-element.45), channel_id=1, source_target_pairs={{0,2},{1,3},{2,0},{3,1},{4,6},{5,7},{6,4},{7,5},{8,10},{9,11},{10,... | collective-permute-start | bytes 1671176 | tf_op jit(solution)/shard_map/ppermute | solution.py:206
  24.3 15.6 %collective-permute-start.1 = (bf16[2,272,512]{2,1,0:T(8,128)(2,1)S(1)}, bf16[2,272,512]{2,1,0:T(8,128)(2,1)S(1)}, u32[]{:S(2)}, u32[]{:S(2)}) collective-permute-start(bf16[2,272,512]{2,1,0:T(8,128)(2,1)S(1)} %get-tuple-element.41.refs_14_), channel_id=1, source_target_pairs={{0,1},{1,0},{2,3},{3,2},{4,5},{5,4},{6,7},{7,6},{8,9},{9,8},{10,11... | collective-permute-start | bytes 1671176 | tf_op jit(solution)/shard_map/ppermute | solution.py:206
  41.0 7.9 %collective-permute-start.11 = (bf16[1,272,512]{2,1,0:T(8,128)(2,1)S(1)}, bf16[1,272,512]{2,1,0:T(8,128)(2,1)S(1)}, u32[]{:S(2)}, u32[]{:S(2)}) collective-permute-start(bf16[1,272,512]{2,1,0:T(8,128)(2,1)S(1)} %get-tuple-element.57), channel_id=1, source_target_pairs={{0,1},{1,0},{2,3},{3,2},{4,5},{5,4},{6,7},{7,6},{8,9},{9,8},{10,11... | collective-permute-start | bytes 835592 | tf_op jit(solution)/shard_map/ppermute | solution.py:206
  41.6 7.6 %collective-permute-start.10 = (bf16[1,272,512]{2,1,0:T(8,128)(2,1)S(1)}, bf16[1,272,512]{2,1,0:T(8,128)(2,1)S(1)}, u32[]{:S(2)}, u32[]{:S(2)}) collective-permute-start(bf16[1,272,512]{2,1,0:T(8,128)(2,1)S(1)} %get-tuple-element.52.refs_23_), channel_id=1, source_target_pairs={{0,2},{1,3},{2,0},{3,1},{4,6},{5,7},{6,4},{7,5},{8,10},{9,11},{10,... | collective-permute-start | bytes 835592 | tf_op jit(solution)/shard_map/ppermute | solution.py:206
  52.1 3.6 %collective-permute-start.12 = (bf16[2,4,128,128]{3,2,1,0:T(8,128)(2,1)S(1)}, bf16[2,4,128,128]{3,2,1,0:T(8,128)(2,1)S(1)}, u32[]{:S(2)}, u32[]{:S(2)}) collective-permute-start(bf16[2,4,128,128]{3,2,1,0:T(8,128)(2,1)S(1)} %get-tuple-element.62), channel_id=1, source_target_pairs={{0,4},{4,0},{8,12},{12,8},{16,20},{20,16},{24,28},{28,24},{1,5},{5... | collective-permute-start | bytes 786440 | tf_op jit(solution)/shard_map/ppermute | solution.py:561
  52.2 13.5 %collective-permute-start.7 = (bf16[272,512]{1,0:T(8,128)(2,1)S(1)}, bf16[272,512]{1,0:T(8,128)(2,1)S(1)}, u32[]{:S(2)}, u32[]{:S(2)}) collective-permute-start(bf16[272,512]{1,0:T(8,128)(2,1)S(1)} %get-tuple-element.53.refs_8_), channel_id=1, source_target_pairs={{0,1},{1,0},{2,3},{3,2},{4,5},{5,4},{6,7},{7,6},{8,9},{9,8},{10,11... | collective-permute-start | bytes 835592 | tf_op jit(solution)/shard_map/ppermute | solution.py:147
  53.7 14.7 %collective-permute-start.8 = (bf16[272,512]{1,0:T(8,128)(2,1)S(1)}, bf16[272,512]{1,0:T(8,128)(2,1)S(1)}, u32[]{:S(2)}, u32[]{:S(2)}) collective-permute-start(bf16[272,512]{1,0:T(8,128)(2,1)S(1)} %get-tuple-element.54), channel_id=1, source_target_pairs={{0,2},{1,3},{2,0},{3,1},{4,6},{5,7},{6,4},{7,5},{8,10},{9,11},{10,... | collective-permute-start | bytes 835592 | tf_op jit(solution)/shard_map/ppermute | solution.py:147
  54.1 14.2 %collective-permute-start.9 = (bf16[272,512]{1,0:T(8,128)(2,1)S(1)}, bf16[272,512]{1,0:T(8,128)(2,1)S(1)}, u32[]{:S(2)}, u32[]{:S(2)}) collective-permute-start(bf16[272,512]{1,0:T(8,128)(2,1)S(1)} %get-tuple-element.55), channel_id=1, source_target_pairs={{0,3},{1,2},{2,1},{3,0},{4,7},{5,6},{6,5},{7,4},{8,11},{9,10},{10,... | collective-permute-start | bytes 835592 | tf_op jit(solution)/shard_map/ppermute | solution.py:147
  56.5 4.6 %collective-permute-start.13 = (bf16[4,128,128]{2,1,0:T(8,128)(2,1)S(1)}, bf16[4,128,128]{2,1,0:T(8,128)(2,1)S(1)}, u32[]{:S(2)}, u32[]{:S(2)}) collective-permute-start(bf16[4,128,128]{2,1,0:T(8,128)(2,1)S(1)} %get-tuple-element.64), channel_id=1, source_target_pairs={{0,8},{4,12},{1,9},{5,13},{2,10},{6,14},{3,11},{7,15}} | collective-permute-start | bytes 393224 | tf_op jit(solution)/shard_map/ppermute | solution.py:687
  61.8 2.5 %collective-permute-start.14 = (bf16[4,128,128]{2,1,0:T(8,128)(2,1)S(1)}, bf16[4,128,128]{2,1,0:T(8,128)(2,1)S(1)}, u32[]{:S(2)}, u32[]{:S(2)}) collective-permute-start(bf16[4,128,128]{2,1,0:T(8,128)(2,1)S(1)} %get-tuple-element.65.refs_6_), channel_id=1, source_target_pairs={{8,16},{12,20},{9,17},{13,21},{10,18},{14,22},{11,19},{15,23}} | collective-permute-start | bytes 393224 | tf_op jit(solution)/shard_map/ppermute | solution.py:687
  64.2 8.0 %collective-permute-start.15 = (bf16[2,4,128,128]{3,2,1,0:T(8,128)(2,1)S(1)}, bf16[2,4,128,128]{3,2,1,0:T(8,128)(2,1)S(1)}, u32[]{:S(2)}, u32[]{:S(2)}) collective-permute-start(bf16[2,4,128,128]{3,2,1,0:T(8,128)(2,1)S(1)} %get-tuple-element.70.refs_0_), channel_id=1, source_target_pairs={{0,4},{4,0},{8,12},{12,8},{16,20},{20,16},{24,28},{28,24},{1,5},{5... | collective-permute-start | bytes 786440 | tf_op jit(solution)/shard_map/ppermute | solution.py:561
  65.0 7.1 %collective-permute-start.16 = (bf16[4,128,128]{2,1,0:T(8,128)(2,1)S(1)}, bf16[4,128,128]{2,1,0:T(8,128)(2,1)S(1)}, u32[]{:S(2)}, u32[]{:S(2)}) collective-permute-start(bf16[4,128,128]{2,1,0:T(8,128)(2,1)S(1)} %get-tuple-element.67.refs_27_), channel_id=1, source_target_pairs={{16,24},{20,28},{17,25},{21,29},{18,26},{22,30},{19,27},{23,31}} | collective-permute-start | bytes 393224 | tf_op jit(solution)/shard_map/ppermute | solution.py:687
  65.7 7.9 %copy-start.8 = (f32[128]{0:T(128)S(1)}, f32[128]{0:T(128)}, u32[]{:S(2)}) copy-start(f32[128]{0:T(128)} %param.17) | copy-start | bytes 1540
  65.7 6.5 %collective-permute-start.17 = (bf16[4,128,128]{2,1,0:T(8,128)(2,1)S(1)}, bf16[4,128,128]{2,1,0:T(8,128)(2,1)S(1)}, u32[]{:S(2)}, u32[]{:S(2)}) collective-permute-start(bf16[4,128,128]{2,1,0:T(8,128)(2,1)S(1)} %get-tuple-element.71.refs_5_), channel_id=1, source_target_pairs={{0,4},{4,0},{8,12},{12,8},{16,20},{20,16},{24,28},{28,24},{1,5},{5... | collective-permute-start | bytes 393224 | tf_op jit(solution)/shard_map/ppermute | solution.py:561
  72.1 1.4 %collective-permute-start.18 = (bf16[4,128,128]{2,1,0:T(8,128)(2,1)S(1)}, bf16[4,128,128]{2,1,0:T(8,128)(2,1)S(1)}, u32[]{:S(2)}, u32[]{:S(2)}) collective-permute-start(bf16[4,128,128]{2,1,0:T(8,128)(2,1)S(1)} %collective-permute-done.16.refs_6_), channel_id=1, source_target_pairs={{0,4},{4,0},{8,12},{12,8},{16,20},{20,16},{24,28},{28,24},{1,5},{5... | collective-permute-start | bytes 393224 | tf_op jit(solution)/shard_map/ppermute | solution.py:561

commit v6 on v5

--- a/solution.py
+++ b/solution.py
@@ -416,9 +416,10 @@
             for j in (2 * i, 2 * i + 1):
                 right = beta_col[:, j : j + 1] * values[:, (j % 2) * HEAD : (j % 2 + 1) * HEAD]
                 write_ref[j] = right
+                low, high = [right[span].astype(BF16) for span in (slice(0, half), slice(half, count))]
                 made.append(
-                    fold(gather_ref[j, 0], packed_right(split(right[:half])))
-                    + fold(gather_ref[j, 1], packed_right(split(right[half:])))
+                    plain(gather_ref[j, 0], jnp.concatenate([low, low], axis=0))
+                    + plain(gather_ref[j, 1], jnp.concatenate([high, high], axis=0))
                 )
         first = sp_ref[place] == 0
         for i in range(number // 2):
@@ -695,7 +696,7 @@
         gathered(HEAD, w_query, 0, [direct_parts(h, HEAD, got_q) for h in everyone]),
         number, count, tables, keys, writes, sp, after=[last],
     )
-    own, _ = lax.optimization_barrier((own, writes))
+    own, _ = lax.optimization_barrier((own, joined))
     early = swapped(own)
     others = [swapped(state) for state in states[:-1]]
     final, _ = lax.optimization_barrier((states[-1], inner))

time: 76.6 us -> 76.6 us (level)
  no operation moved by 1% of the time
where the time goes in v6:
time: 76.6 us; the launch traced here: 75.9 us
  Pallas kernels  27.9 us (36%)
  waiting for transfers between devices  24.4 us (32%)
  starting transfers between devices  19 us (25%)
  local copies, waits for them, and re-layouts  2.91 us (4%)
  between operations  0.91 us (1%)
    pallas_call x14, Pallas kernels, call(): pl.pallas_call(inner, grid_spec=pltpu.PrefetchScalarGridSpec(num_scalar_p...  27.9 us
    ppermute x8, waiting for transfers between devices, exchange(): received[route].append(lax.ppermute(part, 'head', pairs))  18.4 us
    ppermute x8, starting transfers between devices, exchange(): received[route].append(lax.ppermute(part, 'head', pairs))  8.95 us
    ppermute x3, starting transfers between devices, exchange(): lax.ppermute(part, 'head', [(i, i ^ unit + 1) for i in range(ranks)])  3.55 us
    ppermute x3, starting transfers between devices, per_device(): states.append(lax.ppermute(last, 'ctx', hop))  3.4 us
    unnamed x18, local copies, waits for them, and re-layouts  2.88 us
    ppermute x3, waiting for transfers between devices, per_device(): states.append(lax.ppermute(last, 'ctx', hop))  2.51 us
    ppermute x1, starting transfers between devices, shifted(): lax.ppermute(value, 'ctx', [(i, i + steps) for i in range(count - steps)])  2.35 us
  transfers between devices with their start and end apart: 19, of which 10 were waited for; matrix products, arithmetic and copies ran while one was open for 1% of the time, Pallas kernels for 25%

profile of v6, /device:TPU:0, one launch (start us, length us, event | category | flops | bytes accessed | tf_op | source)
XLA Modules:
  0.0 75.9 jit_solution(8711841567360164284)
XLA Ops:
  0.0 0.0 copy-start
  0.0 1.2 %copy-done = bf16[256,2048]{1,0:T(8,128)(2,1)S(1)} copy-done((bf16[256,2048]{1,0:T(8,128)(2,1)S(1)}, bf16[256,2048]{1,0:T(8,128)(2,1)}, u32[]{:S(2)}) %copy-start) | copy-done | bytes 1048600
  1.2 2.3 %collective-permute-start = (bf16[16,512]{1,0:T(8,128)(2,1)S(1)}, bf16[16,512]{1,0:T(8,128)(2,1)S(1)}, u32[]{:S(2)}, u32[]{:S(2)}) collective-permute-start(bf16[16,512]{1,0:T(8,128)(2,1)S(1)} %constant_dynamic-slice_fusion), channel_id=1, source_target_pairs={{0,4},{4,8},{8,12},{12,16},{16,20},{20,24},{24,28},{1,5},{5,9},{9,... | collective-permute-start | bytes 49160 | tf_op jit(solution)/shard_map/ppermute | solution.py:557
  4.3 0.7 pad_add_fusion.sp_ref
  5.0 0.0 collective-permute-done
  5.0 0.0 copy-start.3
  5.0 1.6 %copy-done.3 = bf16[512,2048]{1,0:T(8,128)(2,1)S(1)} copy-done((bf16[512,2048]{1,0:T(8,128)(2,1)S(1)}, bf16[512,2048]{1,0:T(8,128)(2,1)}, u32[]{:S(2)}) %copy-start.3) | copy-done | bytes 2097176
  6.6 1.6 %shard_map.100 = (bf16[2,272,256]{2,1,0:T(8,128)(2,1)S(1)}, bf16[2,272,256]{2,1,0:T(8,128)(2,1)S(1)}) custom-call(s32[19]{0:T(128)S(1)} %pad_add_fusion.sp_ref, bf16[256,512]{1,0:T(8,128)(2,1)S(1)} %constant_dynamic-slice_fusion.1.refs_0_, bf16[16,512]{1,0:T(8,128)(2,1)S(1)} %broadcast_multiply_fusion.refs_1_, bf16[512,2048]{1,0:T(8,128)(2,1)S(1)} %copy-done.3, ...), custom_call_target="tpu_custom_call" | custom-call | flops 1300000000 | bytes 1000 | tf_op jit(solution)/shard_map/pallas_call | solution.py:87
  8.2 2.4 %collective-permute-start.4 = (bf16[2,272,256]{2,1,0:T(8,128)(2,1)S(1)}, bf16[2,272,256]{2,1,0:T(8,128)(2,1)S(1)}, u32[]{:S(2)}, u32[]{:S(2)}) collective-permute-start(bf16[2,272,256]{2,1,0:T(8,128)(2,1)S(1)} %get-tuple-element.46), channel_id=1, source_target_pairs={{0,2},{1,3},{2,0},{3,1},{4,6},{5,7},{6,4},{7,5},{8,10},{9,11},{10,... | collective-permute-start | bytes 835592 | tf_op jit(solution)/shard_map/ppermute | solution.py:206
  10.6 1.5 %collective-permute-start.3 = (bf16[2,272,256]{2,1,0:T(8,128)(2,1)S(1)}, bf16[2,272,256]{2,1,0:T(8,128)(2,1)S(1)}, u32[]{:S(2)}, u32[]{:S(2)}) collective-permute-start(bf16[2,272,256]{2,1,0:T(8,128)(2,1)S(1)} %get-tuple-element.39.refs_2_), channel_id=1, source_target_pairs={{0,1},{1,0},{2,3},{3,2},{4,5},{5,4},{6,7},{7,6},{8,9},{9,8},{10,11... | collective-permute-start | bytes 835592 | tf_op jit(solution)/shard_map/ppermute | solution.py:206
  12.1 0.0 copy-done.6
  12.1 0.0 copy-done.7
  12.1 1.2 %shard_map.101 = (f32[8,256]{1,0:T(8,128)S(1)}, f32[256,8]{1,0:T(8,128)S(1)}, f32[256,8]{1,0:T(8,128)S(1)}) custom-call(s32[19]{0:T(128)S(1)} %pad_add_fusion.sp_ref, f32[8,256]{1,0:T(8,128)S(1)} %copy-done.6, f32[8,256]{1,0:T(8,128)S(1)} %copy-done.7, bf16[2,272,256]{2,1,0:T(8,128)(2,1)S(1)} %get-tuple-element.39.refs_2_), custom_call_target="tpu_custom_call" | custom-call | flops 1200000000 | bytes 1000 | tf_op jit(solution)/shard_map/pallas_call | solution.py:87
  13.3 0.0 copy-done.1
  13.3 0.0 copy-start.2
  13.3 1.5 %shard_map.102 = (bf16[2,272,512]{2,1,0:T(8,128)(2,1)S(1)}, bf16[2,272,512]{2,1,0:T(8,128)(2,1)S(1)}) custom-call(s32[19]{0:T(128)S(1)} %pad_add_fusion.sp_ref, bf16[256,512]{1,0:T(8,128)(2,1)S(1)} %constant_dynamic-slice_fusion.1.refs_0_, bf16[16,512]{1,0:T(8,128)(2,1)S(1)} %broadcast_multiply_fusion.refs_1_, bf16[512,4096]{1,0:T(8,128)(2,1)S(1)} %copy-done.1, ...), custom_call_target="tpu_custom_call" | custom-call | flops 1300000000 | bytes 1000 | tf_op jit(solution)/shard_map/pallas_call | solution.py:87
  14.8 0.0 copy-done.2
  14.9 1.5 %shard_map.103 = (bf16[272,512]{1,0:T(8,128)(2,1)S(1)}, bf16[272,512]{1,0:T(8,128)(2,1)S(1)}, bf16[272,512]{1,0:T(8,128)(2,1)S(1)}) custom-call(s32[19]{0:T(128)S(1)} %pad_add_fusion.sp_ref, bf16[256,512]{1,0:T(8,128)(2,1)S(1)} %constant_dynamic-slice_fusion.1.refs_0_, bf16[16,512]{1,0:T(8,128)(2,1)S(1)} %broadcast_multiply_fusion.refs_1_, ...), custom_call_target="tpu_custom_call" | custom-call | flops 1300000000 | bytes 1000 | tf_op jit(solution)/shard_map/pallas_call | solution.py:87
  16.4 0.4 collective-permute-done.4.refs_5_.refs_12_.refs_16_
  16.8 2.8 %collective-permute-done.3.refs_2_.refs_4_.refs_8_ = bf16[2,272,256]{2,1,0:T(8,128)(2,1)S(1)} collective-permute-done((bf16[2,272,256]{2,1,0:T(8,128)(2,1)S(1)}, bf16[2,272,256]{2,1,0:T(8,128)(2,1)S(1)}, u32[]{:S(2)}, u32[]{:S(2)}) %collective-permute-start.3) | collective-permute-done | bytes 278560 | tf_op jit(solution)/shard_map/ppermute | solution.py:206
  19.6 0.0 copy-done.4
  19.6 1.1 %shard_map.104 = (bf16[1,272,256]{2,1,0:T(8,128)(2,1)S(1)}, bf16[1,272,256]{2,1,0:T(8,128)(2,1)S(1)}) custom-call(s32[19]{0:T(128)S(1)} %pad_add_fusion.sp_ref, bf16[256,512]{1,0:T(8,128)(2,1)S(1)} %constant_dynamic-slice_fusion.1.refs_0_, bf16[16,512]{1,0:T(8,128)(2,1)S(1)} %broadcast_multiply_fusion.refs_1_, ...), custom_call_target="tpu_custom_call" | custom-call | flops 1300000000 | bytes 1000 | tf_op jit(solution)/shard_map/pallas_call | solution.py:87
  20.7 1.6 %collective-permute-start.6 = (bf16[1,272,256]{2,1,0:T(8,128)(2,1)S(1)}, bf16[1,272,256]{2,1,0:T(8,128)(2,1)S(1)}, u32[]{:S(2)}, u32[]{:S(2)}) collective-permute-start(bf16[1,272,256]{2,1,0:T(8,128)(2,1)S(1)} %get-tuple-element.48), channel_id=1, source_target_pairs={{0,1},{1,0},{2,3},{3,2},{4,5},{5,4},{6,7},{7,6},{8,9},{9,8},{10,11... | collective-permute-start | bytes 417800 | tf_op jit(solution)/shard_map/ppermute | solution.py:206
  22.3 0.5 collective-permute-start.5
  22.8 1.5 %collective-permute-start.2 = (bf16[2,272,512]{2,1,0:T(8,128)(2,1)S(1)}, bf16[2,272,512]{2,1,0:T(8,128)(2,1)S(1)}, u32[]{:S(2)}, u32[]{:S(2)}) collective-permute-start(bf16[2,272,512]{2,1,0:T(8,128)(2,1)S(1)} %get-tuple-element.45), channel_id=1, source_target_pairs={{0,2},{1,3},{2,0},{3,1},{4,6},{5,7},{6,4},{7,5},{8,10},{9,11},{10,... | collective-permute-start | bytes 1671176 | tf_op jit(solution)/shard_map/ppermute | solution.py:206
  24.3 0.5 collective-permute-start.1
  24.9 2.1 %collective-permute-done.6.refs_13_.refs_17_ = bf16[1,272,256]{2,1,0:T(8,128)(2,1)S(1)} collective-permute-done((bf16[1,272,256]{2,1,0:T(8,128)(2,1)S(1)}, bf16[1,272,256]{2,1,0:T(8,128)(2,1)S(1)}, u32[]{:S(2)}, u32[]{:S(2)}) %collective-permute-start.6) | collective-permute-done | bytes 139296 | tf_op jit(solution)/shard_map/ppermute | solution.py:206
  27.0 1.8 %collective-permute-done.5.refs_5_.refs_9_ = bf16[1,272,256]{2,1,0:T(8,128)(2,1)S(1)} collective-permute-done((bf16[1,272,256]{2,1,0:T(8,128)(2,1)S(1)}, bf16[1,272,256]{2,1,0:T(8,128)(2,1)S(1)}, u32[]{:S(2)}, u32[]{:S(2)}) %collective-permute-start.5) | collective-permute-done | bytes 139296 | tf_op jit(solution)/shard_map/ppermute | solution.py:206
  28.8 7.1 %shard_map.105 = (f32[4,256,128]{2,1,0:T(8,128)S(1)}, bf16[8,3,128,256]{3,2,1,0:T(8,128)(2,1)S(1)}, bf16[8,2,128,256]{3,2,1,0:T(8,128)(2,1)S(1)}, f32[8,128,128]{2,1,0:T(8,128)S(1)}) custom-call(s32[19]{0:T(128)S(1)} %pad_add_fusion.sp_ref, bf16[256,512]{1,0:T(8,128)(2,1)S(1)} %constant_dynamic-slice_fusion.1.refs_0_, ...), custom_call_target="tpu_custom_call" | custom-call | flops 5000000000 | bytes 1000 | tf_op jit(solution)/shard_map/pallas_call | solution.py:87
  35.9 4.0 %collective-permute-done.2.refs_5_.refs_12_.refs_16_ = bf16[2,272,512]{2,1,0:T(8,128)(2,1)S(1)} collective-permute-done((bf16[2,272,512]{2,1,0:T(8,128)(2,1)S(1)}, bf16[2,272,512]{2,1,0:T(8,128)(2,1)S(1)}, u32[]{:S(2)}, u32[]{:S(2)}) %collective-permute-start.2) | collective-permute-done | bytes 557088 | tf_op jit(solution)/shard_map/ppermute | solution.py:206
  39.9 0.0 collective-permute-done.1.refs_2_.refs_4_.refs_8_
  39.9 1.1 %shard_map.106 = (bf16[1,272,512]{2,1,0:T(8,128)(2,1)S(1)}, bf16[1,272,512]{2,1,0:T(8,128)(2,1)S(1)}) custom-call(s32[19]{0:T(128)S(1)} %pad_add_fusion.sp_ref, bf16[256,512]{1,0:T(8,128)(2,1)S(1)} %constant_dynamic-slice_fusion.1.refs_0_, bf16[16,512]{1,0:T(8,128)(2,1)S(1)} %broadcast_multiply_fusion.refs_1_, ...), custom_call_target="tpu_custom_call" | custom-call | flops 1300000000 | bytes 1000 | tf_op jit(solution)/shard_map/pallas_call | solution.py:87
  41.0 0.6 collective-permute-start.11
  41.6 0.3 collective-permute-start.10
  41.9 6.9 %collective-permute-done.11.refs_13_.refs_17_ = bf16[1,272,512]{2,1,0:T(8,128)(2,1)S(1)} collective-permute-done((bf16[1,272,512]{2,1,0:T(8,128)(2,1)S(1)}, bf16[1,272,512]{2,1,0:T(8,128)(2,1)S(1)}, u32[]{:S(2)}, u32[]{:S(2)}) %collective-permute-start.11) | collective-permute-done | bytes 278560 | tf_op jit(solution)/shard_map/ppermute | solution.py:206
  48.9 0.3 collective-permute-done.10.refs_5_.refs_9_
  49.2 2.8 %shard_map.107 = (f32[8,256,128]{2,1,0:T(8,128)S(1)}, bf16[2,4,128,128]{3,2,1,0:T(8,128)(2,1)S(1)}, bf16[2,4,128,128]{3,2,1,0:T(8,128)(2,1)S(1)}) custom-call(s32[19]{0:T(128)S(1)} %pad_add_fusion.sp_ref, bf16[256,512]{1,0:T(8,128)(2,1)S(1)} %constant_dynamic-slice_fusion.1.refs_0_, bf16[16,512]{1,0:T(8,128)(2,1)S(1)} %broadcast_multiply_fusion.refs_1_, ...), custom_call_target="tpu_custom_call" | custom-call | flops 50000000 | bytes 1000 | tf_op jit(solution)/shard_map/pallas_call | solution.py:87
  52.0 0.1 collective-permute-start.12
  52.1 1.5 %collective-permute-start.7 = (bf16[272,512]{1,0:T(8,128)(2,1)S(1)}, bf16[272,512]{1,0:T(8,128)(2,1)S(1)}, u32[]{:S(2)}, u32[]{:S(2)}) collective-permute-start(bf16[272,512]{1,0:T(8,128)(2,1)S(1)} %get-tuple-element.53.refs_8_), channel_id=1, source_target_pairs={{0,1},{1,0},{2,3},{3,2},{4,5},{5,4},{6,7},{7,6},{8,9},{9,8},{10,11... | collective-permute-start | bytes 835592 | tf_op jit(solution)/shard_map/ppermute | solution.py:147
  53.6 0.5 collective-permute-start.8
  54.1 1.5 %collective-permute-start.9 = (bf16[272,512]{1,0:T(8,128)(2,1)S(1)}, bf16[272,512]{1,0:T(8,128)(2,1)S(1)}, u32[]{:S(2)}, u32[]{:S(2)}) collective-permute-start(bf16[272,512]{1,0:T(8,128)(2,1)S(1)} %get-tuple-element.55), channel_id=1, source_target_pairs={{0,3},{1,2},{2,1},{3,0},{4,7},{5,6},{6,5},{7,4},{8,11},{9,10},{10,... | collective-permute-start | bytes 835592 | tf_op jit(solution)/shard_map/ppermute | solution.py:147
  55.7 0.0 collective-permute-done.12.refs_1_.refs_3_
  55.7 0.8 %shard_map.108 = (bf16[2,4,128,128]{3,2,1,0:T(8,128)(2,1)S(1)}, bf16[4,128,128]{2,1,0:T(8,128)(2,1)S(1)}) custom-call(s32[19]{0:T(128)S(1)} %pad_add_fusion.sp_ref, bf16[2,4,128,128]{3,2,1,0:T(8,128)(2,1)S(1)} %get-tuple-element.70.refs_0_, bf16[2,4,128,128]{3,2,1,0:T(8,128)(2,1)S(1)} %collective-permute-done.12.refs_1_.refs_3_), custom_call_target="tpu_custom_call" | custom-call | flops 50000000 | bytes 1000 | tf_op jit(solution)/shard_map/pallas_call | solution.py:87
  56.4 2.1 %collective-permute-start.13 = (bf16[4,128,128]{2,1,0:T(8,128)(2,1)S(1)}, bf16[4,128,128]{2,1,0:T(8,128)(2,1)S(1)}, u32[]{:S(2)}, u32[]{:S(2)}) collective-permute-start(bf16[4,128,128]{2,1,0:T(8,128)(2,1)S(1)} %get-tuple-element.64), channel_id=1, source_target_pairs={{0,8},{4,12},{1,9},{5,13},{2,10},{6,14},{3,11},{7,15}} | collective-permute-start | bytes 393224 | tf_op jit(solution)/shard_map/ppermute | solution.py:688
  58.5 2.5 %collective-permute-done.13.refs_1_ = bf16[4,128,128]{2,1,0:T(8,128)(2,1)S(1)} collective-permute-done((bf16[4,128,128]{2,1,0:T(8,128)(2,1)S(1)}, bf16[4,128,128]{2,1,0:T(8,128)(2,1)S(1)}, u32[]{:S(2)}, u32[]{:S(2)}) %collective-permute-start.13) | collective-permute-done | bytes 131104 | tf_op jit(solution)/shard_map/ppermute | solution.py:688
  61.0 0.7 shard_map.109
  61.7 0.7 collective-permute-start.14
  62.4 0.1 collective-permute-start.15
  62.5 1.7 %shard_map.110.refs_3_.refs_26_ = f32[8,256,256]{2,1,0:T(8,128)S(1)} custom-call(s32[19]{0:T(128)S(1)} %pad_add_fusion.sp_ref, f32[8,256,128]{2,1,0:T(8,128)S(1)} %get-tuple-element.59.refs_0_, f32[4,256,128]{2,1,0:T(8,128)S(1)} %get-tuple-element.56.refs_1_.refs_25_, f32[8,256]{1,0:T(8,128)S(1)} %get-tuple-element.40.refs_10_.refs_18_.refs_2_.refs_22_, ...), custom_call_target="tpu_custom_call" | custom-call | flops 50000000 | bytes 1000 | tf_op jit(solution)/shard_map/pallas_call | solution.py:87
  64.2 0.0 collective-permute-done.14.refs_2_
  64.2 0.7 shard_map.111
  64.9 0.7 collective-permute-start.16
  65.6 0.0 collective-permute-done.7.refs_4_.refs_9_.refs_14_.refs_19_
  65.6 0.0 copy-start.8
  65.6 0.6 collective-permute-start.17
  66.2 2.1 %collective-permute-done.8.refs_5_.refs_10_.refs_15_.refs_20_ = bf16[272,512]{1,0:T(8,128)(2,1)S(1)} collective-permute-done((bf16[272,512]{1,0:T(8,128)(2,1)S(1)}, bf16[272,512]{1,0:T(8,128)(2,1)S(1)}, u32[]{:S(2)}, u32[]{:S(2)}) %collective-permute-start.8) | collective-permute-done | bytes 278560 | tf_op jit(solution)/shard_map/ppermute | solution.py:147
  68.3 0.0 collective-permute-done.9.refs_6_.refs_11_.refs_16_.refs_21_
  68.3 3.7 %shard_map.112 = (f32[8,256,128]{2,1,0:T(8,128)S(1)}, bf16[8,256,128]{2,1,0:T(8,128)(2,1)S(1)}) custom-call(s32[19]{0:T(128)S(1)} %pad_add_fusion.sp_ref, bf16[256,512]{1,0:T(8,128)(2,1)S(1)} %constant_dynamic-slice_fusion.1.refs_0_, bf16[16,512]{1,0:T(8,128)(2,1)S(1)} %broadcast_multiply_fusion.refs_1_, bf16[512,2048]{1,0:T(8,128)(2,1)S(1)} %copy-done.2, ...), custom_call_target="tpu_custom_call" | custom-call | flops 3700000000 | bytes 1000 | tf_op jit(solution)/shard_map/pallas_call | solution.py:87
  72.1 0.0 collective-permute-done.16.refs_6_
  72.1 0.1 collective-permute-start.18
  72.1 0.0 collective-permute-done.15.refs_2_
  72.2 0.0 collective-permute-done.17.refs_7_
  72.2 1.3 %collective-permute-done.18.refs_8_ = bf16[4,128,128]{2,1,0:T(8,128)(2,1)S(1)} collective-permute-done((bf16[4,128,128]{2,1,0:T(8,128)(2,1)S(1)}, bf16[4,128,128]{2,1,0:T(8,128)(2,1)S(1)}, u32[]{:S(2)}, u32[]{:S(2)}) %collective-permute-start.18) | collective-permute-done | bytes 131104 | tf_op jit(solution)/shard_map/ppermute | solution.py:562
  73.5 2.4 %shard_map.113 = bf16[256,1024]{1,0:T(8,128)(2,1)} custom-call(s32[19]{0:T(128)S(1)} %pad_add_fusion.sp_ref, f32[8,256,128]{2,1,0:T(8,128)S(1)} %get-tuple-element.68.refs_0_, bf16[8,256,128]{2,1,0:T(8,128)(2,1)S(1)} %get-tuple-element.69.refs_1_, bf16[2,4,128,128]{3,2,1,0:T(8,128)(2,1)S(1)} %collective-permute-done.15.refs_2_, ...), custom_call_target="tpu_custom_call" | custom-call | flops 2700000000 | bytes 1000 | tf_op jit(solution)/shard_map/pallas_call | solution.py:87
  (10 shorter events, 0.0 us)
Async XLA Ops:
  0.0 1.2 %copy-start = (bf16[256,2048]{1,0:T(8,128)(2,1)S(1)}, bf16[256,2048]{1,0:T(8,128)(2,1)}, u32[]{:S(2)}) copy-start(bf16[256,2048]{1,0:T(8,128)(2,1)} %param.10) | copy-start | bytes 3145732
  1.2 3.8 %collective-permute-start = (bf16[16,512]{1,0:T(8,128)(2,1)S(1)}, bf16[16,512]{1,0:T(8,128)(2,1)S(1)}, u32[]{:S(2)}, u32[]{:S(2)}) collective-permute-start(bf16[16,512]{1,0:T(8,128)(2,1)S(1)} %constant_dynamic-slice_fusion), channel_id=1, source_target_pairs={{0,4},{4,8},{8,12},{12,16},{16,20},{20,24},{24,28},{1,5},{5,9},{9,... | collective-permute-start | bytes 49160 | tf_op jit(solution)/shard_map/ppermute | solution.py:557
  5.0 1.6 %copy-start.3 = (bf16[512,2048]{1,0:T(8,128)(2,1)S(1)}, bf16[512,2048]{1,0:T(8,128)(2,1)}, u32[]{:S(2)}) copy-start(bf16[512,2048]{1,0:T(8,128)(2,1)} %refs_14_.2) | copy-start | bytes 6291460
  6.6 5.5 %copy-start.6 = (f32[8,256]{1,0:T(8,128)S(1)}, f32[8,256]{1,0:T(8,128)}, u32[]{:S(2)}) copy-start(f32[8,256]{1,0:T(8,128)} %refs_0_.1) | copy-start | bytes 24580
  6.6 5.5 %copy-start.7 = (f32[8,256]{1,0:T(8,128)S(1)}, f32[8,256]{1,0:T(8,128)}, u32[]{:S(2)}) copy-start(f32[8,256]{1,0:T(8,128)} %refs_1_.1) | copy-start | bytes 24580
  8.2 8.6 %collective-permute-start.4 = (bf16[2,272,256]{2,1,0:T(8,128)(2,1)S(1)}, bf16[2,272,256]{2,1,0:T(8,128)(2,1)S(1)}, u32[]{:S(2)}, u32[]{:S(2)}) collective-permute-start(bf16[2,272,256]{2,1,0:T(8,128)(2,1)S(1)} %get-tuple-element.46), channel_id=1, source_target_pairs={{0,2},{1,3},{2,0},{3,1},{4,6},{5,7},{6,4},{7,5},{8,10},{9,11},{10,... | collective-permute-start | bytes 835592 | tf_op jit(solution)/shard_map/ppermute | solution.py:206
  10.6 2.7 %copy-start.1 = (bf16[512,4096]{1,0:T(8,128)(2,1)S(1)}, bf16[512,4096]{1,0:T(8,128)(2,1)}, u32[]{:S(2)}) copy-start(bf16[512,4096]{1,0:T(8,128)(2,1)} %refs_14_.3) | copy-start | bytes 12582916
  10.6 9.0 %collective-permute-start.3 = (bf16[2,272,256]{2,1,0:T(8,128)(2,1)S(1)}, bf16[2,272,256]{2,1,0:T(8,128)(2,1)S(1)}, u32[]{:S(2)}, u32[]{:S(2)}) collective-permute-start(bf16[2,272,256]{2,1,0:T(8,128)(2,1)S(1)} %get-tuple-element.39.refs_2_), channel_id=1, source_target_pairs={{0,1},{1,0},{2,3},{3,2},{4,5},{5,4},{6,7},{7,6},{8,9},{9,8},{10,11... | collective-permute-start | bytes 835592 | tf_op jit(solution)/shard_map/ppermute | solution.py:206
  13.3 1.6 %copy-start.2 = (bf16[512,2048]{1,0:T(8,128)(2,1)S(1)}, bf16[512,2048]{1,0:T(8,128)(2,1)}, u32[]{:S(2)}) copy-start(bf16[512,2048]{1,0:T(8,128)(2,1)} %refs_17_.1) | copy-start | bytes 6291460
  14.9 4.7 %copy-start.4 = (bf16[512,2048]{1,0:T(8,128)(2,1)S(1)}, bf16[512,2048]{1,0:T(8,128)(2,1)}, u32[]{:S(2)}) copy-start(bf16[512,2048]{1,0:T(8,128)(2,1)} %refs_14_.2) | copy-start | bytes 6291460
  19.6 9.2 %copy-start.5 = (bf16[4,8192]{1,0:T(4,128)(2,1)S(1)}, bf16[4,8192]{1,0:T(4,128)(2,1)}, u32[]{:S(2)}) copy-start(bf16[4,8192]{1,0:T(4,128)(2,1)} %refs_18_.1) | copy-start | bytes 196612
  20.7 6.3 %collective-permute-start.6 = (bf16[1,272,256]{2,1,0:T(8,128)(2,1)S(1)}, bf16[1,272,256]{2,1,0:T(8,128)(2,1)S(1)}, u32[]{:S(2)}, u32[]{:S(2)}) collective-permute-start(bf16[1,272,256]{2,1,0:T(8,128)(2,1)S(1)} %get-tuple-element.48), channel_id=1, source_target_pairs={{0,1},{1,0},{2,3},{3,2},{4,5},{5,4},{6,7},{7,6},{8,9},{9,8},{10,11... | collective-permute-start | bytes 417800 | tf_op jit(solution)/shard_map/ppermute | solution.py:206
  22.3 6.5 %collective-permute-start.5 = (bf16[1,272,256]{2,1,0:T(8,128)(2,1)S(1)}, bf16[1,272,256]{2,1,0:T(8,128)(2,1)S(1)}, u32[]{:S(2)}, u32[]{:S(2)}) collective-permute-start(bf16[1,272,256]{2,1,0:T(8,128)(2,1)S(1)} %get-tuple-element.47.refs_21_), channel_id=1, source_target_pairs={{0,2},{1,3},{2,0},{3,1},{4,6},{5,7},{6,4},{7,5},{8,10},{9,11},{10,... | collective-permute-start | bytes 417800 | tf_op jit(solution)/shard_map/ppermute | solution.py:206
  22.8 17.1 %collective-permute-start.2 = (bf16[2,272,512]{2,1,0:T(8,128)(2,1)S(1)}, bf16[2,272,512]{2,1,0:T(8,128)(2,1)S(1)}, u32[]{:S(2)}, u32[]{:S(2)}) collective-permute-start(bf16[2,272,512]{2,1,0:T(8,128)(2,1)S(1)} %get-tuple-element.45), channel_id=1, source_target_pairs={{0,2},{1,3},{2,0},{3,1},{4,6},{5,7},{6,4},{7,5},{8,10},{9,11},{10,... | collective-permute-start | bytes 1671176 | tf_op jit(solution)/shard_map/ppermute | solution.py:206
  24.3 15.6 %collective-permute-start.1 = (bf16[2,272,512]{2,1,0:T(8,128)(2,1)S(1)}, bf16[2,272,512]{2,1,0:T(8,128)(2,1)S(1)}, u32[]{:S(2)}, u32[]{:S(2)}) collective-permute-start(bf16[2,272,512]{2,1,0:T(8,128)(2,1)S(1)} %get-tuple-element.41.refs_14_), channel_id=1, source_target_pairs={{0,1},{1,0},{2,3},{3,2},{4,5},{5,4},{6,7},{7,6},{8,9},{9,8},{10,11... | collective-permute-start | bytes 1671176 | tf_op jit(solution)/shard_map/ppermute | solution.py:206
  41.0 7.9 %collective-permute-start.11 = (bf16[1,272,512]{2,1,0:T(8,128)(2,1)S(1)}, bf16[1,272,512]{2,1,0:T(8,128)(2,1)S(1)}, u32[]{:S(2)}, u32[]{:S(2)}) collective-permute-start(bf16[1,272,512]{2,1,0:T(8,128)(2,1)S(1)} %get-tuple-element.57), channel_id=1, source_target_pairs={{0,1},{1,0},{2,3},{3,2},{4,5},{5,4},{6,7},{7,6},{8,9},{9,8},{10,11... | collective-permute-start | bytes 835592 | tf_op jit(solution)/shard_map/ppermute | solution.py:206
  41.6 7.6 %collective-permute-start.10 = (bf16[1,272,512]{2,1,0:T(8,128)(2,1)S(1)}, bf16[1,272,512]{2,1,0:T(8,128)(2,1)S(1)}, u32[]{:S(2)}, u32[]{:S(2)}) collective-permute-start(bf16[1,272,512]{2,1,0:T(8,128)(2,1)S(1)} %get-tuple-element.52.refs_23_), channel_id=1, source_target_pairs={{0,2},{1,3},{2,0},{3,1},{4,6},{5,7},{6,4},{7,5},{8,10},{9,11},{10,... | collective-permute-start | bytes 835592 | tf_op jit(solution)/shard_map/ppermute | solution.py:206
  52.0 3.6 %collective-permute-start.12 = (bf16[2,4,128,128]{3,2,1,0:T(8,128)(2,1)S(1)}, bf16[2,4,128,128]{3,2,1,0:T(8,128)(2,1)S(1)}, u32[]{:S(2)}, u32[]{:S(2)}) collective-permute-start(bf16[2,4,128,128]{3,2,1,0:T(8,128)(2,1)S(1)} %get-tuple-element.62), channel_id=1, source_target_pairs={{0,4},{4,0},{8,12},{12,8},{16,20},{20,16},{24,28},{28,24},{1,5},{5... | collective-permute-start | bytes 786440 | tf_op jit(solution)/shard_map/ppermute | solution.py:562
  52.1 13.5 %collective-permute-start.7 = (bf16[272,512]{1,0:T(8,128)(2,1)S(1)}, bf16[272,512]{1,0:T(8,128)(2,1)S(1)}, u32[]{:S(2)}, u32[]{:S(2)}) collective-permute-start(bf16[272,512]{1,0:T(8,128)(2,1)S(1)} %get-tuple-element.53.refs_8_), channel_id=1, source_target_pairs={{0,1},{1,0},{2,3},{3,2},{4,5},{5,4},{6,7},{7,6},{8,9},{9,8},{10,11... | collective-permute-start | bytes 835592 | tf_op jit(solution)/shard_map/ppermute | solution.py:147
  53.6 14.7 %collective-permute-start.8 = (bf16[272,512]{1,0:T(8,128)(2,1)S(1)}, bf16[272,512]{1,0:T(8,128)(2,1)S(1)}, u32[]{:S(2)}, u32[]{:S(2)}) collective-permute-start(bf16[272,512]{1,0:T(8,128)(2,1)S(1)} %get-tuple-element.54), channel_id=1, source_target_pairs={{0,2},{1,3},{2,0},{3,1},{4,6},{5,7},{6,4},{7,5},{8,10},{9,11},{10,... | collective-permute-start | bytes 835592 | tf_op jit(solution)/shard_map/ppermute | solution.py:147
  54.1 14.2 %collective-permute-start.9 = (bf16[272,512]{1,0:T(8,128)(2,1)S(1)}, bf16[272,512]{1,0:T(8,128)(2,1)S(1)}, u32[]{:S(2)}, u32[]{:S(2)}) collective-permute-start(bf16[272,512]{1,0:T(8,128)(2,1)S(1)} %get-tuple-element.55), channel_id=1, source_target_pairs={{0,3},{1,2},{2,1},{3,0},{4,7},{5,6},{6,5},{7,4},{8,11},{9,10},{10,... | collective-permute-start | bytes 835592 | tf_op jit(solution)/shard_map/ppermute | solution.py:147
  56.4 4.6 %collective-permute-start.13 = (bf16[4,128,128]{2,1,0:T(8,128)(2,1)S(1)}, bf16[4,128,128]{2,1,0:T(8,128)(2,1)S(1)}, u32[]{:S(2)}, u32[]{:S(2)}) collective-permute-start(bf16[4,128,128]{2,1,0:T(8,128)(2,1)S(1)} %get-tuple-element.64), channel_id=1, source_target_pairs={{0,8},{4,12},{1,9},{5,13},{2,10},{6,14},{3,11},{7,15}} | collective-permute-start | bytes 393224 | tf_op jit(solution)/shard_map/ppermute | solution.py:688
  61.7 2.5 %collective-permute-start.14 = (bf16[4,128,128]{2,1,0:T(8,128)(2,1)S(1)}, bf16[4,128,128]{2,1,0:T(8,128)(2,1)S(1)}, u32[]{:S(2)}, u32[]{:S(2)}) collective-permute-start(bf16[4,128,128]{2,1,0:T(8,128)(2,1)S(1)} %get-tuple-element.65.refs_6_), channel_id=1, source_target_pairs={{8,16},{12,20},{9,17},{13,21},{10,18},{14,22},{11,19},{15,23}} | collective-permute-start | bytes 393224 | tf_op jit(solution)/shard_map/ppermute | solution.py:688
  62.4 9.7 %collective-permute-start.15 = (bf16[2,4,128,128]{3,2,1,0:T(8,128)(2,1)S(1)}, bf16[2,4,128,128]{3,2,1,0:T(8,128)(2,1)S(1)}, u32[]{:S(2)}, u32[]{:S(2)}) collective-permute-start(bf16[2,4,128,128]{3,2,1,0:T(8,128)(2,1)S(1)} %get-tuple-element.70.refs_0_), channel_id=1, source_target_pairs={{0,4},{4,0},{8,12},{12,8},{16,20},{20,16},{24,28},{28,24},{1,5},{5... | collective-permute-start | bytes 786440 | tf_op jit(solution)/shard_map/ppermute | solution.py:562
  64.9 7.1 %collective-permute-start.16 = (bf16[4,128,128]{2,1,0:T(8,128)(2,1)S(1)}, bf16[4,128,128]{2,1,0:T(8,128)(2,1)S(1)}, u32[]{:S(2)}, u32[]{:S(2)}) collective-permute-start(bf16[4,128,128]{2,1,0:T(8,128)(2,1)S(1)} %get-tuple-element.67.refs_27_), channel_id=1, source_target_pairs={{16,24},{20,28},{17,25},{21,29},{18,26},{22,30},{19,27},{23,31}} | collective-permute-start | bytes 393224 | tf_op jit(solution)/shard_map/ppermute | solution.py:688
  65.6 7.8 %copy-start.8 = (f32[128]{0:T(128)S(1)}, f32[128]{0:T(128)}, u32[]{:S(2)}) copy-start(f32[128]{0:T(128)} %param.17) | copy-start | bytes 1540
  65.6 6.5 %collective-permute-start.17 = (bf16[4,128,128]{2,1,0:T(8,128)(2,1)S(1)}, bf16[4,128,128]{2,1,0:T(8,128)(2,1)S(1)}, u32[]{:S(2)}, u32[]{:S(2)}) collective-permute-start(bf16[4,128,128]{2,1,0:T(8,128)(2,1)S(1)} %get-tuple-element.71.refs_5_), channel_id=1, source_target_pairs={{0,4},{4,0},{8,12},{12,8},{16,20},{20,16},{24,28},{28,24},{1,5},{5... | collective-permute-start | bytes 393224 | tf_op jit(solution)/shard_map/ppermute | solution.py:562
  72.1 1.4 %collective-permute-start.18 = (bf16[4,128,128]{2,1,0:T(8,128)(2,1)S(1)}, bf16[4,128,128]{2,1,0:T(8,128)(2,1)S(1)}, u32[]{:S(2)}, u32[]{:S(2)}) collective-permute-start(bf16[4,128,128]{2,1,0:T(8,128)(2,1)S(1)} %collective-permute-done.16.refs_6_), channel_id=1, source_target_pairs={{0,4},{4,0},{8,12},{12,8},{16,20},{20,16},{24,28},{28,24},{1,5},{5... | collective-permute-start | bytes 393224 | tf_op jit(solution)/shard_map/ppermute | solution.py:562

commit v7 on v6

--- a/solution.py
+++ b/solution.py
@@ -382,7 +382,8 @@
             for part, span in zip(taken, (slice(0, half), slice(half, count))):
                 part = packed_left(split(part))
                 gather_ref[j, 0 if span.start == 0 else 1] = part
-                term = fold(part, packed_right(split(right[span])))
+                once = right[span].astype(BF16)
+                term = plain(part, jnp.concatenate([once, once], axis=0))
                 moved = term if moved is None else moved + term
             gone = jnp.exp(row[:, count - 1 :])
             trans_ref[j] = keep * (gone * eye - moved)

time: 76.6 us -> 76.5 us (level)
  no operation moved by 1% of the time
where the time goes in v7:
time: 76.5 us; the launch traced here: 75.9 us
  Pallas kernels  27.9 us (36%)
  waiting for transfers between devices  24.4 us (32%)
  starting transfers between devices  19 us (25%)
  local copies, waits for them, and re-layouts  2.91 us (4%)
  between operations  0.91 us (1%)
    pallas_call x14, Pallas kernels, call(): pl.pallas_call(inner, grid_spec=pltpu.PrefetchScalarGridSpec(num_scalar_p...  27.9 us
    ppermute x8, waiting for transfers between devices, exchange(): received[route].append(lax.ppermute(part, 'head', pairs))  18.5 us
    ppermute x8, starting transfers between devices, exchange(): received[route].append(lax.ppermute(part, 'head', pairs))  8.96 us
    ppermute x3, starting transfers between devices, exchange(): lax.ppermute(part, 'head', [(i, i ^ unit + 1) for i in range(ranks)])  3.55 us
    ppermute x3, starting transfers between devices, per_device(): states.append(lax.ppermute(last, 'ctx', hop))  3.41 us
    unnamed x18, local copies, waits for them, and re-layouts  2.88 us
    ppermute x3, waiting for transfers between devices, per_device(): states.append(lax.ppermute(last, 'ctx', hop))  2.51 us
    ppermute x1, starting transfers between devices, shifted(): lax.ppermute(value, 'ctx', [(i, i + steps) for i in range(count - steps)])  2.35 us
  transfers between devices with their start and end apart: 19, of which 10 were waited for; matrix products, arithmetic and copies ran while one was open for 1% of the time, Pallas kernels for 25%

profile of v7, /device:TPU:0, one launch (start us, length us, event | category | flops | bytes accessed | tf_op | source)
XLA Modules:
  0.0 75.9 jit_solution(18295702775350542862)
XLA Ops:
  0.0 0.0 copy-start
  0.0 1.2 %copy-done = bf16[256,2048]{1,0:T(8,128)(2,1)S(1)} copy-done((bf16[256,2048]{1,0:T(8,128)(2,1)S(1)}, bf16[256,2048]{1,0:T(8,128)(2,1)}, u32[]{:S(2)}) %copy-start) | copy-done | bytes 1048600
  1.2 2.3 %collective-permute-start = (bf16[16,512]{1,0:T(8,128)(2,1)S(1)}, bf16[16,512]{1,0:T(8,128)(2,1)S(1)}, u32[]{:S(2)}, u32[]{:S(2)}) collective-permute-start(bf16[16,512]{1,0:T(8,128)(2,1)S(1)} %constant_dynamic-slice_fusion), channel_id=1, source_target_pairs={{0,4},{4,8},{8,12},{12,16},{16,20},{20,24},{24,28},{1,5},{5,9},{9,... | collective-permute-start | bytes 49160 | tf_op jit(solution)/shard_map/ppermute | solution.py:558
  4.3 0.7 pad_add_fusion.sp_ref
  5.0 0.0 collective-permute-done
  5.0 0.0 copy-start.3
  5.0 1.6 %copy-done.3 = bf16[512,2048]{1,0:T(8,128)(2,1)S(1)} copy-done((bf16[512,2048]{1,0:T(8,128)(2,1)S(1)}, bf16[512,2048]{1,0:T(8,128)(2,1)}, u32[]{:S(2)}) %copy-start.3) | copy-done | bytes 2097176
  6.6 1.5 %shard_map.100 = (bf16[2,272,256]{2,1,0:T(8,128)(2,1)S(1)}, bf16[2,272,256]{2,1,0:T(8,128)(2,1)S(1)}) custom-call(s32[19]{0:T(128)S(1)} %pad_add_fusion.sp_ref, bf16[256,512]{1,0:T(8,128)(2,1)S(1)} %constant_dynamic-slice_fusion.1.refs_0_, bf16[16,512]{1,0:T(8,128)(2,1)S(1)} %broadcast_multiply_fusion.refs_1_, bf16[512,2048]{1,0:T(8,128)(2,1)S(1)} %copy-done.3, ...), custom_call_target="tpu_custom_call" | custom-call | flops 1300000000 | bytes 1000 | tf_op jit(solution)/shard_map/pallas_call | solution.py:87
  8.2 2.4 %collective-permute-start.4 = (bf16[2,272,256]{2,1,0:T(8,128)(2,1)S(1)}, bf16[2,272,256]{2,1,0:T(8,128)(2,1)S(1)}, u32[]{:S(2)}, u32[]{:S(2)}) collective-permute-start(bf16[2,272,256]{2,1,0:T(8,128)(2,1)S(1)} %get-tuple-element.46), channel_id=1, source_target_pairs={{0,2},{1,3},{2,0},{3,1},{4,6},{5,7},{6,4},{7,5},{8,10},{9,11},{10,... | collective-permute-start | bytes 835592 | tf_op jit(solution)/shard_map/ppermute | solution.py:206
  10.6 1.5 %collective-permute-start.3 = (bf16[2,272,256]{2,1,0:T(8,128)(2,1)S(1)}, bf16[2,272,256]{2,1,0:T(8,128)(2,1)S(1)}, u32[]{:S(2)}, u32[]{:S(2)}) collective-permute-start(bf16[2,272,256]{2,1,0:T(8,128)(2,1)S(1)} %get-tuple-element.39.refs_2_), channel_id=1, source_target_pairs={{0,1},{1,0},{2,3},{3,2},{4,5},{5,4},{6,7},{7,6},{8,9},{9,8},{10,11... | collective-permute-start | bytes 835592 | tf_op jit(solution)/shard_map/ppermute | solution.py:206
  12.1 0.0 copy-done.6
  12.1 0.0 copy-done.7
  12.1 1.2 %shard_map.101 = (f32[8,256]{1,0:T(8,128)S(1)}, f32[256,8]{1,0:T(8,128)S(1)}, f32[256,8]{1,0:T(8,128)S(1)}) custom-call(s32[19]{0:T(128)S(1)} %pad_add_fusion.sp_ref, f32[8,256]{1,0:T(8,128)S(1)} %copy-done.6, f32[8,256]{1,0:T(8,128)S(1)} %copy-done.7, bf16[2,272,256]{2,1,0:T(8,128)(2,1)S(1)} %get-tuple-element.39.refs_2_), custom_call_target="tpu_custom_call" | custom-call | flops 1200000000 | bytes 1000 | tf_op jit(solution)/shard_map/pallas_call | solution.py:87
  13.3 0.0 copy-done.1
  13.3 0.0 copy-start.2
  13.3 1.5 %shard_map.102 = (bf16[2,272,512]{2,1,0:T(8,128)(2,1)S(1)}, bf16[2,272,512]{2,1,0:T(8,128)(2,1)S(1)}) custom-call(s32[19]{0:T(128)S(1)} %pad_add_fusion.sp_ref, bf16[256,512]{1,0:T(8,128)(2,1)S(1)} %constant_dynamic-slice_fusion.1.refs_0_, bf16[16,512]{1,0:T(8,128)(2,1)S(1)} %broadcast_multiply_fusion.refs_1_, bf16[512,4096]{1,0:T(8,128)(2,1)S(1)} %copy-done.1, ...), custom_call_target="tpu_custom_call" | custom-call | flops 1300000000 | bytes 1000 | tf_op jit(solution)/shard_map/pallas_call | solution.py:87
  14.9 0.0 copy-done.2
  14.9 1.5 %shard_map.103 = (bf16[272,512]{1,0:T(8,128)(2,1)S(1)}, bf16[272,512]{1,0:T(8,128)(2,1)S(1)}, bf16[272,512]{1,0:T(8,128)(2,1)S(1)}) custom-call(s32[19]{0:T(128)S(1)} %pad_add_fusion.sp_ref, bf16[256,512]{1,0:T(8,128)(2,1)S(1)} %constant_dynamic-slice_fusion.1.refs_0_, bf16[16,512]{1,0:T(8,128)(2,1)S(1)} %broadcast_multiply_fusion.refs_1_, ...), custom_call_target="tpu_custom_call" | custom-call | flops 1300000000 | bytes 1000 | tf_op jit(solution)/shard_map/pallas_call | solution.py:87
  16.4 0.4 collective-permute-done.4.refs_5_.refs_12_.refs_16_
  16.8 2.8 %collective-permute-done.3.refs_2_.refs_4_.refs_8_ = bf16[2,272,256]{2,1,0:T(8,128)(2,1)S(1)} collective-permute-done((bf16[2,272,256]{2,1,0:T(8,128)(2,1)S(1)}, bf16[2,272,256]{2,1,0:T(8,128)(2,1)S(1)}, u32[]{:S(2)}, u32[]{:S(2)}) %collective-permute-start.3) | collective-permute-done | bytes 278560 | tf_op jit(solution)/shard_map/ppermute | solution.py:206
  19.6 1.1 %shard_map.104 = (bf16[1,272,256]{2,1,0:T(8,128)(2,1)S(1)}, bf16[1,272,256]{2,1,0:T(8,128)(2,1)S(1)}) custom-call(s32[19]{0:T(128)S(1)} %pad_add_fusion.sp_ref, bf16[256,512]{1,0:T(8,128)(2,1)S(1)} %constant_dynamic-slice_fusion.1.refs_0_, bf16[16,512]{1,0:T(8,128)(2,1)S(1)} %broadcast_multiply_fusion.refs_1_, ...), custom_call_target="tpu_custom_call" | custom-call | flops 1300000000 | bytes 1000 | tf_op jit(solution)/shard_map/pallas_call | solution.py:87
  20.7 1.6 %collective-permute-start.6 = (bf16[1,272,256]{2,1,0:T(8,128)(2,1)S(1)}, bf16[1,272,256]{2,1,0:T(8,128)(2,1)S(1)}, u32[]{:S(2)}, u32[]{:S(2)}) collective-permute-start(bf16[1,272,256]{2,1,0:T(8,128)(2,1)S(1)} %get-tuple-element.48), channel_id=1, source_target_pairs={{0,1},{1,0},{2,3},{3,2},{4,5},{5,4},{6,7},{7,6},{8,9},{9,8},{10,11... | collective-permute-start | bytes 417800 | tf_op jit(solution)/shard_map/ppermute | solution.py:206
  22.3 0.5 collective-permute-start.5
  22.8 1.6 %collective-permute-start.2 = (bf16[2,272,512]{2,1,0:T(8,128)(2,1)S(1)}, bf16[2,272,512]{2,1,0:T(8,128)(2,1)S(1)}, u32[]{:S(2)}, u32[]{:S(2)}) collective-permute-start(bf16[2,272,512]{2,1,0:T(8,128)(2,1)S(1)} %get-tuple-element.45), channel_id=1, source_target_pairs={{0,2},{1,3},{2,0},{3,1},{4,6},{5,7},{6,4},{7,5},{8,10},{9,11},{10,... | collective-permute-start | bytes 1671176 | tf_op jit(solution)/shard_map/ppermute | solution.py:206
  24.3 0.5 collective-permute-start.1
  24.9 2.1 %collective-permute-done.6.refs_13_.refs_17_ = bf16[1,272,256]{2,1,0:T(8,128)(2,1)S(1)} collective-permute-done((bf16[1,272,256]{2,1,0:T(8,128)(2,1)S(1)}, bf16[1,272,256]{2,1,0:T(8,128)(2,1)S(1)}, u32[]{:S(2)}, u32[]{:S(2)}) %collective-permute-start.6) | collective-permute-done | bytes 139296 | tf_op jit(solution)/shard_map/ppermute | solution.py:206
  27.0 1.9 %collective-permute-done.5.refs_5_.refs_9_ = bf16[1,272,256]{2,1,0:T(8,128)(2,1)S(1)} collective-permute-done((bf16[1,272,256]{2,1,0:T(8,128)(2,1)S(1)}, bf16[1,272,256]{2,1,0:T(8,128)(2,1)S(1)}, u32[]{:S(2)}, u32[]{:S(2)}) %collective-permute-start.5) | collective-permute-done | bytes 139296 | tf_op jit(solution)/shard_map/ppermute | solution.py:206
  28.8 0.0 copy-done.5
  28.8 7.1 %shard_map.105 = (f32[4,256,128]{2,1,0:T(8,128)S(1)}, bf16[8,3,128,256]{3,2,1,0:T(8,128)(2,1)S(1)}, bf16[8,2,128,256]{3,2,1,0:T(8,128)(2,1)S(1)}, f32[8,128,128]{2,1,0:T(8,128)S(1)}) custom-call(s32[19]{0:T(128)S(1)} %pad_add_fusion.sp_ref, bf16[256,512]{1,0:T(8,128)(2,1)S(1)} %constant_dynamic-slice_fusion.1.refs_0_, ...), custom_call_target="tpu_custom_call" | custom-call | flops 5000000000 | bytes 1000 | tf_op jit(solution)/shard_map/pallas_call | solution.py:87
  35.9 4.0 %collective-permute-done.2.refs_5_.refs_12_.refs_16_ = bf16[2,272,512]{2,1,0:T(8,128)(2,1)S(1)} collective-permute-done((bf16[2,272,512]{2,1,0:T(8,128)(2,1)S(1)}, bf16[2,272,512]{2,1,0:T(8,128)(2,1)S(1)}, u32[]{:S(2)}, u32[]{:S(2)}) %collective-permute-start.2) | collective-permute-done | bytes 557088 | tf_op jit(solution)/shard_map/ppermute | solution.py:206
  39.9 0.0 collective-permute-done.1.refs_2_.refs_4_.refs_8_
  39.9 1.1 %shard_map.106 = (bf16[1,272,512]{2,1,0:T(8,128)(2,1)S(1)}, bf16[1,272,512]{2,1,0:T(8,128)(2,1)S(1)}) custom-call(s32[19]{0:T(128)S(1)} %pad_add_fusion.sp_ref, bf16[256,512]{1,0:T(8,128)(2,1)S(1)} %constant_dynamic-slice_fusion.1.refs_0_, bf16[16,512]{1,0:T(8,128)(2,1)S(1)} %broadcast_multiply_fusion.refs_1_, ...), custom_call_target="tpu_custom_call" | custom-call | flops 1300000000 | bytes 1000 | tf_op jit(solution)/shard_map/pallas_call | solution.py:87
  41.0 0.6 collective-permute-start.11
  41.6 0.3 collective-permute-start.10
  41.9 7.0 %collective-permute-done.11.refs_13_.refs_17_ = bf16[1,272,512]{2,1,0:T(8,128)(2,1)S(1)} collective-permute-done((bf16[1,272,512]{2,1,0:T(8,128)(2,1)S(1)}, bf16[1,272,512]{2,1,0:T(8,128)(2,1)S(1)}, u32[]{:S(2)}, u32[]{:S(2)}) %collective-permute-start.11) | collective-permute-done | bytes 278560 | tf_op jit(solution)/shard_map/ppermute | solution.py:206
  48.9 0.3 collective-permute-done.10.refs_5_.refs_9_
  49.2 2.8 %shard_map.107 = (f32[8,256,128]{2,1,0:T(8,128)S(1)}, bf16[2,4,128,128]{3,2,1,0:T(8,128)(2,1)S(1)}, bf16[2,4,128,128]{3,2,1,0:T(8,128)(2,1)S(1)}) custom-call(s32[19]{0:T(128)S(1)} %pad_add_fusion.sp_ref, bf16[256,512]{1,0:T(8,128)(2,1)S(1)} %constant_dynamic-slice_fusion.1.refs_0_, bf16[16,512]{1,0:T(8,128)(2,1)S(1)} %broadcast_multiply_fusion.refs_1_, ...), custom_call_target="tpu_custom_call" | custom-call | flops 50000000 | bytes 1000 | tf_op jit(solution)/shard_map/pallas_call | solution.py:87
  52.0 0.1 collective-permute-start.12
  52.1 1.5 %collective-permute-start.7 = (bf16[272,512]{1,0:T(8,128)(2,1)S(1)}, bf16[272,512]{1,0:T(8,128)(2,1)S(1)}, u32[]{:S(2)}, u32[]{:S(2)}) collective-permute-start(bf16[272,512]{1,0:T(8,128)(2,1)S(1)} %get-tuple-element.53.refs_8_), channel_id=1, source_target_pairs={{0,1},{1,0},{2,3},{3,2},{4,5},{5,4},{6,7},{7,6},{8,9},{9,8},{10,11... | collective-permute-start | bytes 835592 | tf_op jit(solution)/shard_map/ppermute | solution.py:147
  53.6 0.5 collective-permute-start.8
  54.1 1.6 %collective-permute-start.9 = (bf16[272,512]{1,0:T(8,128)(2,1)S(1)}, bf16[272,512]{1,0:T(8,128)(2,1)S(1)}, u32[]{:S(2)}, u32[]{:S(2)}) collective-permute-start(bf16[272,512]{1,0:T(8,128)(2,1)S(1)} %get-tuple-element.55), channel_id=1, source_target_pairs={{0,3},{1,2},{2,1},{3,0},{4,7},{5,6},{6,5},{7,4},{8,11},{9,10},{10,... | collective-permute-start | bytes 835592 | tf_op jit(solution)/shard_map/ppermute | solution.py:147
  55.7 0.0 collective-permute-done.12.refs_1_.refs_3_
  55.7 0.8 %shard_map.108 = (bf16[2,4,128,128]{3,2,1,0:T(8,128)(2,1)S(1)}, bf16[4,128,128]{2,1,0:T(8,128)(2,1)S(1)}) custom-call(s32[19]{0:T(128)S(1)} %pad_add_fusion.sp_ref, bf16[2,4,128,128]{3,2,1,0:T(8,128)(2,1)S(1)} %get-tuple-element.70.refs_0_, bf16[2,4,128,128]{3,2,1,0:T(8,128)(2,1)S(1)} %collective-permute-done.12.refs_1_.refs_3_), custom_call_target="tpu_custom_call" | custom-call | flops 50000000 | bytes 1000 | tf_op jit(solution)/shard_map/pallas_call | solution.py:87
  56.5 2.1 %collective-permute-start.13 = (bf16[4,128,128]{2,1,0:T(8,128)(2,1)S(1)}, bf16[4,128,128]{2,1,0:T(8,128)(2,1)S(1)}, u32[]{:S(2)}, u32[]{:S(2)}) collective-permute-start(bf16[4,128,128]{2,1,0:T(8,128)(2,1)S(1)} %get-tuple-element.64), channel_id=1, source_target_pairs={{0,8},{4,12},{1,9},{5,13},{2,10},{6,14},{3,11},{7,15}} | collective-permute-start | bytes 393224 | tf_op jit(solution)/shard_map/ppermute | solution.py:689
  58.5 2.5 %collective-permute-done.13.refs_1_ = bf16[4,128,128]{2,1,0:T(8,128)(2,1)S(1)} collective-permute-done((bf16[4,128,128]{2,1,0:T(8,128)(2,1)S(1)}, bf16[4,128,128]{2,1,0:T(8,128)(2,1)S(1)}, u32[]{:S(2)}, u32[]{:S(2)}) %collective-permute-start.13) | collective-permute-done | bytes 131104 | tf_op jit(solution)/shard_map/ppermute | solution.py:689
  61.0 0.7 shard_map.109
  61.8 0.7 collective-permute-start.14
  62.4 0.1 collective-permute-start.15
  62.5 1.7 %shard_map.110.refs_3_.refs_26_ = f32[8,256,256]{2,1,0:T(8,128)S(1)} custom-call(s32[19]{0:T(128)S(1)} %pad_add_fusion.sp_ref, f32[8,256,128]{2,1,0:T(8,128)S(1)} %get-tuple-element.59.refs_0_, f32[4,256,128]{2,1,0:T(8,128)S(1)} %get-tuple-element.56.refs_1_.refs_25_, f32[8,256]{1,0:T(8,128)S(1)} %get-tuple-element.40.refs_10_.refs_18_.refs_2_.refs_22_, ...), custom_call_target="tpu_custom_call" | custom-call | flops 50000000 | bytes 1000 | tf_op jit(solution)/shard_map/pallas_call | solution.py:87
  64.2 0.0 collective-permute-done.14.refs_2_
  64.2 0.7 shard_map.111
  65.0 0.7 collective-permute-start.16
  65.6 0.0 collective-permute-done.7.refs_4_.refs_9_.refs_14_.refs_19_
  65.7 0.0 copy-start.8
  65.7 0.6 collective-permute-start.17
  66.2 2.1 %collective-permute-done.8.refs_5_.refs_10_.refs_15_.refs_20_ = bf16[272,512]{1,0:T(8,128)(2,1)S(1)} collective-permute-done((bf16[272,512]{1,0:T(8,128)(2,1)S(1)}, bf16[272,512]{1,0:T(8,128)(2,1)S(1)}, u32[]{:S(2)}, u32[]{:S(2)}) %collective-permute-start.8) | collective-permute-done | bytes 278560 | tf_op jit(solution)/shard_map/ppermute | solution.py:147
  68.3 0.0 collective-permute-done.9.refs_6_.refs_11_.refs_16_.refs_21_
  68.3 3.7 %shard_map.112 = (f32[8,256,128]{2,1,0:T(8,128)S(1)}, bf16[8,256,128]{2,1,0:T(8,128)(2,1)S(1)}) custom-call(s32[19]{0:T(128)S(1)} %pad_add_fusion.sp_ref, bf16[256,512]{1,0:T(8,128)(2,1)S(1)} %constant_dynamic-slice_fusion.1.refs_0_, bf16[16,512]{1,0:T(8,128)(2,1)S(1)} %broadcast_multiply_fusion.refs_1_, bf16[512,2048]{1,0:T(8,128)(2,1)S(1)} %copy-done.2, ...), custom_call_target="tpu_custom_call" | custom-call | flops 3700000000 | bytes 1000 | tf_op jit(solution)/shard_map/pallas_call | solution.py:87
  72.1 0.0 collective-permute-done.16.refs_6_
  72.1 0.1 collective-permute-start.18
  72.1 0.0 collective-permute-done.15.refs_2_
  72.2 0.0 collective-permute-done.17.refs_7_
  72.2 1.3 %collective-permute-done.18.refs_8_ = bf16[4,128,128]{2,1,0:T(8,128)(2,1)S(1)} collective-permute-done((bf16[4,128,128]{2,1,0:T(8,128)(2,1)S(1)}, bf16[4,128,128]{2,1,0:T(8,128)(2,1)S(1)}, u32[]{:S(2)}, u32[]{:S(2)}) %collective-permute-start.18) | collective-permute-done | bytes 131104 | tf_op jit(solution)/shard_map/ppermute | solution.py:563
  73.5 2.4 %shard_map.113 = bf16[256,1024]{1,0:T(8,128)(2,1)} custom-call(s32[19]{0:T(128)S(1)} %pad_add_fusion.sp_ref, f32[8,256,128]{2,1,0:T(8,128)S(1)} %get-tuple-element.68.refs_0_, bf16[8,256,128]{2,1,0:T(8,128)(2,1)S(1)} %get-tuple-element.69.refs_1_, bf16[2,4,128,128]{3,2,1,0:T(8,128)(2,1)S(1)} %collective-permute-done.15.refs_2_, ...), custom_call_target="tpu_custom_call" | custom-call | flops 2700000000 | bytes 1000 | tf_op jit(solution)/shard_map/pallas_call | solution.py:87
  (10 shorter events, 0.0 us)
Async XLA Ops:
  0.0 1.2 %copy-start = (bf16[256,2048]{1,0:T(8,128)(2,1)S(1)}, bf16[256,2048]{1,0:T(8,128)(2,1)}, u32[]{:S(2)}) copy-start(bf16[256,2048]{1,0:T(8,128)(2,1)} %param.10) | copy-start | bytes 3145732
  1.2 3.8 %collective-permute-start = (bf16[16,512]{1,0:T(8,128)(2,1)S(1)}, bf16[16,512]{1,0:T(8,128)(2,1)S(1)}, u32[]{:S(2)}, u32[]{:S(2)}) collective-permute-start(bf16[16,512]{1,0:T(8,128)(2,1)S(1)} %constant_dynamic-slice_fusion), channel_id=1, source_target_pairs={{0,4},{4,8},{8,12},{12,16},{16,20},{20,24},{24,28},{1,5},{5,9},{9,... | collective-permute-start | bytes 49160 | tf_op jit(solution)/shard_map/ppermute | solution.py:558
  5.0 1.6 %copy-start.3 = (bf16[512,2048]{1,0:T(8,128)(2,1)S(1)}, bf16[512,2048]{1,0:T(8,128)(2,1)}, u32[]{:S(2)}) copy-start(bf16[512,2048]{1,0:T(8,128)(2,1)} %refs_14_.2) | copy-start | bytes 6291460
  6.6 5.5 %copy-start.6 = (f32[8,256]{1,0:T(8,128)S(1)}, f32[8,256]{1,0:T(8,128)}, u32[]{:S(2)}) copy-start(f32[8,256]{1,0:T(8,128)} %refs_0_.1) | copy-start | bytes 24580
  6.6 5.5 %copy-start.7 = (f32[8,256]{1,0:T(8,128)S(1)}, f32[8,256]{1,0:T(8,128)}, u32[]{:S(2)}) copy-start(f32[8,256]{1,0:T(8,128)} %refs_1_.1) | copy-start | bytes 24580
  8.2 8.6 %collective-permute-start.4 = (bf16[2,272,256]{2,1,0:T(8,128)(2,1)S(1)}, bf16[2,272,256]{2,1,0:T(8,128)(2,1)S(1)}, u32[]{:S(2)}, u32[]{:S(2)}) collective-permute-start(bf16[2,272,256]{2,1,0:T(8,128)(2,1)S(1)} %get-tuple-element.46), channel_id=1, source_target_pairs={{0,2},{1,3},{2,0},{3,1},{4,6},{5,7},{6,4},{7,5},{8,10},{9,11},{10,... | collective-permute-start | bytes 835592 | tf_op jit(solution)/shard_map/ppermute | solution.py:206
  10.6 2.7 %copy-start.1 = (bf16[512,4096]{1,0:T(8,128)(2,1)S(1)}, bf16[512,4096]{1,0:T(8,128)(2,1)}, u32[]{:S(2)}) copy-start(bf16[512,4096]{1,0:T(8,128)(2,1)} %refs_14_.3) | copy-start | bytes 12582916
  10.6 9.0 %collective-permute-start.3 = (bf16[2,272,256]{2,1,0:T(8,128)(2,1)S(1)}, bf16[2,272,256]{2,1,0:T(8,128)(2,1)S(1)}, u32[]{:S(2)}, u32[]{:S(2)}) collective-permute-start(bf16[2,272,256]{2,1,0:T(8,128)(2,1)S(1)} %get-tuple-element.39.refs_2_), channel_id=1, source_target_pairs={{0,1},{1,0},{2,3},{3,2},{4,5},{5,4},{6,7},{7,6},{8,9},{9,8},{10,11... | collective-permute-start | bytes 835592 | tf_op jit(solution)/shard_map/ppermute | solution.py:206
  13.3 1.6 %copy-start.2 = (bf16[512,2048]{1,0:T(8,128)(2,1)S(1)}, bf16[512,2048]{1,0:T(8,128)(2,1)}, u32[]{:S(2)}) copy-start(bf16[512,2048]{1,0:T(8,128)(2,1)} %refs_17_.1) | copy-start | bytes 6291460
  14.9 4.7 %copy-start.4 = (bf16[512,2048]{1,0:T(8,128)(2,1)S(1)}, bf16[512,2048]{1,0:T(8,128)(2,1)}, u32[]{:S(2)}) copy-start(bf16[512,2048]{1,0:T(8,128)(2,1)} %refs_14_.2) | copy-start | bytes 6291460
  19.6 9.2 %copy-start.5 = (bf16[4,8192]{1,0:T(4,128)(2,1)S(1)}, bf16[4,8192]{1,0:T(4,128)(2,1)}, u32[]{:S(2)}) copy-start(bf16[4,8192]{1,0:T(4,128)(2,1)} %refs_18_.1) | copy-start | bytes 196612
  20.7 6.2 %collective-permute-start.6 = (bf16[1,272,256]{2,1,0:T(8,128)(2,1)S(1)}, bf16[1,272,256]{2,1,0:T(8,128)(2,1)S(1)}, u32[]{:S(2)}, u32[]{:S(2)}) collective-permute-start(bf16[1,272,256]{2,1,0:T(8,128)(2,1)S(1)} %get-tuple-element.48), channel_id=1, source_target_pairs={{0,1},{1,0},{2,3},{3,2},{4,5},{5,4},{6,7},{7,6},{8,9},{9,8},{10,11... | collective-permute-start | bytes 417800 | tf_op jit(solution)/shard_map/ppermute | solution.py:206
  22.3 6.5 %collective-permute-start.5 = (bf16[1,272,256]{2,1,0:T(8,128)(2,1)S(1)}, bf16[1,272,256]{2,1,0:T(8,128)(2,1)S(1)}, u32[]{:S(2)}, u32[]{:S(2)}) collective-permute-start(bf16[1,272,256]{2,1,0:T(8,128)(2,1)S(1)} %get-tuple-element.47.refs_21_), channel_id=1, source_target_pairs={{0,2},{1,3},{2,0},{3,1},{4,6},{5,7},{6,4},{7,5},{8,10},{9,11},{10,... | collective-permute-start | bytes 417800 | tf_op jit(solution)/shard_map/ppermute | solution.py:206
  22.8 17.1 %collective-permute-start.2 = (bf16[2,272,512]{2,1,0:T(8,128)(2,1)S(1)}, bf16[2,272,512]{2,1,0:T(8,128)(2,1)S(1)}, u32[]{:S(2)}, u32[]{:S(2)}) collective-permute-start(bf16[2,272,512]{2,1,0:T(8,128)(2,1)S(1)} %get-tuple-element.45), channel_id=1, source_target_pairs={{0,2},{1,3},{2,0},{3,1},{4,6},{5,7},{6,4},{7,5},{8,10},{9,11},{10,... | collective-permute-start | bytes 1671176 | tf_op jit(solution)/shard_map/ppermute | solution.py:206
  24.3 15.6 %collective-permute-start.1 = (bf16[2,272,512]{2,1,0:T(8,128)(2,1)S(1)}, bf16[2,272,512]{2,1,0:T(8,128)(2,1)S(1)}, u32[]{:S(2)}, u32[]{:S(2)}) collective-permute-start(bf16[2,272,512]{2,1,0:T(8,128)(2,1)S(1)} %get-tuple-element.41.refs_14_), channel_id=1, source_target_pairs={{0,1},{1,0},{2,3},{3,2},{4,5},{5,4},{6,7},{7,6},{8,9},{9,8},{10,11... | collective-permute-start | bytes 1671176 | tf_op jit(solution)/shard_map/ppermute | solution.py:206
  41.0 7.9 %collective-permute-start.11 = (bf16[1,272,512]{2,1,0:T(8,128)(2,1)S(1)}, bf16[1,272,512]{2,1,0:T(8,128)(2,1)S(1)}, u32[]{:S(2)}, u32[]{:S(2)}) collective-permute-start(bf16[1,272,512]{2,1,0:T(8,128)(2,1)S(1)} %get-tuple-element.57), channel_id=1, source_target_pairs={{0,1},{1,0},{2,3},{3,2},{4,5},{5,4},{6,7},{7,6},{8,9},{9,8},{10,11... | collective-permute-start | bytes 835592 | tf_op jit(solution)/shard_map/ppermute | solution.py:206
  41.6 7.6 %collective-permute-start.10 = (bf16[1,272,512]{2,1,0:T(8,128)(2,1)S(1)}, bf16[1,272,512]{2,1,0:T(8,128)(2,1)S(1)}, u32[]{:S(2)}, u32[]{:S(2)}) collective-permute-start(bf16[1,272,512]{2,1,0:T(8,128)(2,1)S(1)} %get-tuple-element.52.refs_23_), channel_id=1, source_target_pairs={{0,2},{1,3},{2,0},{3,1},{4,6},{5,7},{6,4},{7,5},{8,10},{9,11},{10,... | collective-permute-start | bytes 835592 | tf_op jit(solution)/shard_map/ppermute | solution.py:206
  52.0 3.6 %collective-permute-start.12 = (bf16[2,4,128,128]{3,2,1,0:T(8,128)(2,1)S(1)}, bf16[2,4,128,128]{3,2,1,0:T(8,128)(2,1)S(1)}, u32[]{:S(2)}, u32[]{:S(2)}) collective-permute-start(bf16[2,4,128,128]{3,2,1,0:T(8,128)(2,1)S(1)} %get-tuple-element.62), channel_id=1, source_target_pairs={{0,4},{4,0},{8,12},{12,8},{16,20},{20,16},{24,28},{28,24},{1,5},{5... | collective-permute-start | bytes 786440 | tf_op jit(solution)/shard_map/ppermute | solution.py:563
  52.1 13.5 %collective-permute-start.7 = (bf16[272,512]{1,0:T(8,128)(2,1)S(1)}, bf16[272,512]{1,0:T(8,128)(2,1)S(1)}, u32[]{:S(2)}, u32[]{:S(2)}) collective-permute-start(bf16[272,512]{1,0:T(8,128)(2,1)S(1)} %get-tuple-element.53.refs_8_), channel_id=1, source_target_pairs={{0,1},{1,0},{2,3},{3,2},{4,5},{5,4},{6,7},{7,6},{8,9},{9,8},{10,11... | collective-permute-start | bytes 835592 | tf_op jit(solution)/shard_map/ppermute | solution.py:147
  53.6 14.7 %collective-permute-start.8 = (bf16[272,512]{1,0:T(8,128)(2,1)S(1)}, bf16[272,512]{1,0:T(8,128)(2,1)S(1)}, u32[]{:S(2)}, u32[]{:S(2)}) collective-permute-start(bf16[272,512]{1,0:T(8,128)(2,1)S(1)} %get-tuple-element.54), channel_id=1, source_target_pairs={{0,2},{1,3},{2,0},{3,1},{4,6},{5,7},{6,4},{7,5},{8,10},{9,11},{10,... | collective-permute-start | bytes 835592 | tf_op jit(solution)/shard_map/ppermute | solution.py:147
  54.1 14.2 %collective-permute-start.9 = (bf16[272,512]{1,0:T(8,128)(2,1)S(1)}, bf16[272,512]{1,0:T(8,128)(2,1)S(1)}, u32[]{:S(2)}, u32[]{:S(2)}) collective-permute-start(bf16[272,512]{1,0:T(8,128)(2,1)S(1)} %get-tuple-element.55), channel_id=1, source_target_pairs={{0,3},{1,2},{2,1},{3,0},{4,7},{5,6},{6,5},{7,4},{8,11},{9,10},{10,... | collective-permute-start | bytes 835592 | tf_op jit(solution)/shard_map/ppermute | solution.py:147
  56.5 4.6 %collective-permute-start.13 = (bf16[4,128,128]{2,1,0:T(8,128)(2,1)S(1)}, bf16[4,128,128]{2,1,0:T(8,128)(2,1)S(1)}, u32[]{:S(2)}, u32[]{:S(2)}) collective-permute-start(bf16[4,128,128]{2,1,0:T(8,128)(2,1)S(1)} %get-tuple-element.64), channel_id=1, source_target_pairs={{0,8},{4,12},{1,9},{5,13},{2,10},{6,14},{3,11},{7,15}} | collective-permute-start | bytes 393224 | tf_op jit(solution)/shard_map/ppermute | solution.py:689
  61.8 2.5 %collective-permute-start.14 = (bf16[4,128,128]{2,1,0:T(8,128)(2,1)S(1)}, bf16[4,128,128]{2,1,0:T(8,128)(2,1)S(1)}, u32[]{:S(2)}, u32[]{:S(2)}) collective-permute-start(bf16[4,128,128]{2,1,0:T(8,128)(2,1)S(1)} %get-tuple-element.65.refs_6_), channel_id=1, source_target_pairs={{8,16},{12,20},{9,17},{13,21},{10,18},{14,22},{11,19},{15,23}} | collective-permute-start | bytes 393224 | tf_op jit(solution)/shard_map/ppermute | solution.py:689
  62.4 9.7 %collective-permute-start.15 = (bf16[2,4,128,128]{3,2,1,0:T(8,128)(2,1)S(1)}, bf16[2,4,128,128]{3,2,1,0:T(8,128)(2,1)S(1)}, u32[]{:S(2)}, u32[]{:S(2)}) collective-permute-start(bf16[2,4,128,128]{3,2,1,0:T(8,128)(2,1)S(1)} %get-tuple-element.70.refs_0_), channel_id=1, source_target_pairs={{0,4},{4,0},{8,12},{12,8},{16,20},{20,16},{24,28},{28,24},{1,5},{5... | collective-permute-start | bytes 786440 | tf_op jit(solution)/shard_map/ppermute | solution.py:563
  65.0 7.1 %collective-permute-start.16 = (bf16[4,128,128]{2,1,0:T(8,128)(2,1)S(1)}, bf16[4,128,128]{2,1,0:T(8,128)(2,1)S(1)}, u32[]{:S(2)}, u32[]{:S(2)}) collective-permute-start(bf16[4,128,128]{2,1,0:T(8,128)(2,1)S(1)} %get-tuple-element.67.refs_27_), channel_id=1, source_target_pairs={{16,24},{20,28},{17,25},{21,29},{18,26},{22,30},{19,27},{23,31}} | collective-permute-start | bytes 393224 | tf_op jit(solution)/shard_map/ppermute | solution.py:689
  65.7 7.8 %copy-start.8 = (f32[128]{0:T(128)S(1)}, f32[128]{0:T(128)}, u32[]{:S(2)}) copy-start(f32[128]{0:T(128)} %param.17) | copy-start | bytes 1540
  65.7 6.5 %collective-permute-start.17 = (bf16[4,128,128]{2,1,0:T(8,128)(2,1)S(1)}, bf16[4,128,128]{2,1,0:T(8,128)(2,1)S(1)}, u32[]{:S(2)}, u32[]{:S(2)}) collective-permute-start(bf16[4,128,128]{2,1,0:T(8,128)(2,1)S(1)} %get-tuple-element.71.refs_5_), channel_id=1, source_target_pairs={{0,4},{4,0},{8,12},{12,8},{16,20},{20,16},{24,28},{28,24},{1,5},{5... | collective-permute-start | bytes 393224 | tf_op jit(solution)/shard_map/ppermute | solution.py:563
  72.1 1.4 %collective-permute-start.18 = (bf16[4,128,128]{2,1,0:T(8,128)(2,1)S(1)}, bf16[4,128,128]{2,1,0:T(8,128)(2,1)S(1)}, u32[]{:S(2)}, u32[]{:S(2)}) collective-permute-start(bf16[4,128,128]{2,1,0:T(8,128)(2,1)S(1)} %collective-permute-done.16.refs_6_), channel_id=1, source_target_pairs={{0,4},{4,0},{8,12},{12,8},{16,20},{20,16},{24,28},{28,24},{1,5},{5... | collective-permute-start | bytes 393224 | tf_op jit(solution)/shard_map/ppermute | solution.py:563
